TPU v7x, 32 devices: a whole 2x2x4 slice. The times are simulated.
32 devices in a mesh: seq: 16 (over z, y, x), dp: 2 (over core).
Axes of the slice: x: 2, y: 2, z: 4, core: 2. Of those that a mesh axis runs over, the one named last changes fastest.
Arguments:
- teacher_rows: bfloat16 [4096, 8192], P('seq', 'dp'), may hold values from -6 to 6
- teacher_next: bfloat16 [4096, 8192], P('seq', 'dp'), may hold values from -9 to 9
- state_proj: bfloat16 [8192, 256], replicated, may hold values from -0.015625 to 0.015625
- step_proj: bfloat16 [8192, 64], replicated, may hold values from -0.0625 to 0.0625
- rate_log: float32 [64], replicated, may hold values from -12 to 1.2
- step_bias: float32 [64], replicated, may hold values from -1 to 0
- skip_gain: float32 [64], replicated, may hold values from 0.5 to 1.5
Outputs:
- loss_value: float32 [], replicated
- state_proj_grad: float32 [8192, 256], P('dp')
- step_proj_grad: float32 [8192, 64], P('dp')
- rate_log_grad: float32 [64], replicated
- step_bias_grad: float32 [64], replicated
- skip_gain_grad: float32 [64], replicated
All inputs are finite; a program needn't handle non-finite values.
Results may differ from a plain program's by a relative error of at most 0.011.
Values may be sent and summed in bfloat16 or wider, within the bound.
No kernel may reach another device: no remote copies, remote signals or barrier semaphores. Data moves between devices by JAX's collectives and lax.ppermute only.
A program may use at most 128 MiB of HBM per device.

v0:
```python
import jax
import jax.numpy as jnp
from jax import lax
from jax.sharding import PartitionSpec as P

BLOCK = 256


def entering_2(value, axis, combine, identity, reverse):
    length, position = (lax.axis_size(axis), lax.axis_index(axis))
    everything = jax.tree.map(lambda part: lax.all_gather(part, axis), value)
    start = jax.tree.map(
        lambda part, zero: jnp.broadcast_to(jnp.asarray(zero, part.dtype), part.shape),
        value,
        identity,
    )

    def lap(k, before):
        at = length - 1 - k if reverse else k
        reached = at > position if reverse else at < position
        new = combine(before, jax.tree.map(lambda part: part[at], everything))
        return jax.tree.map(lambda a, b: jnp.where(reached, a, b), new, before)

    return lax.fori_loop(0, length, lap, start)


def block_terms(bc_block, dt_block, rate_log, step_bias):
    state_width = bc_block.shape[1] // 2
    rounded = bc_block.astype(jnp.bfloat16)
    dt_steps = jax.nn.softplus(dt_block + step_bias)
    log_decay = jnp.cumsum(-jnp.exp(rate_log) * dt_steps, axis=0)
    return (rounded[:, :state_width], rounded[:, state_width:], dt_steps, log_decay)


def block_state(rows_block, b_input, dt_steps, log_decay, head_count):
    block_rows, model_width = rows_block.shape
    decay_total = log_decay[-1]
    weighting = dt_steps * jnp.exp(decay_total - log_decay)
    scaled_rows = (
        (rows_block.reshape(block_rows, head_count, -1) * weighting[:, :, None])
        .reshape(block_rows, model_width)
        .astype(jnp.bfloat16)
    )
    increment = lax.dot_general(
        scaled_rows, b_input, (((0,), (0,)), ((), ())), preferred_element_type=jnp.float32
    )
    return (jnp.exp(decay_total), increment)


def block_output(
    rows_block, b_input, c_output, dt_steps, log_decay, skip_gain, carry_state, head_count
):
    block_rows, model_width = rows_block.shape
    scores = lax.dot_general(
        c_output, b_input, (((1,), (1,)), ((), ())), preferred_element_type=jnp.float32
    )
    row_index = lax.broadcasted_iota(jnp.int32, (block_rows, block_rows), 0)
    col_index = lax.broadcasted_iota(jnp.int32, (block_rows, block_rows), 1)
    causal = (row_index >= col_index)[None]
    log_gap = log_decay.T[:, :, None] - log_decay.T[:, None, :]
    weights = (
        jnp.where(causal, jnp.exp(jnp.where(causal, log_gap, 0.0)), 0.0)
        * scores[None]
        * dt_steps.T[:, None, :]
    )
    weights = weights.astype(jnp.bfloat16)
    inputs = rows_block.reshape(block_rows, head_count, -1)
    inner_term = jnp.einsum("hts,shp->thp", weights, inputs, preferred_element_type=jnp.float32)
    carried = lax.dot_general(
        c_output.astype(jnp.float32),
        carry_state,
        (((1,), (1,)), ((), ())),
        precision=lax.Precision.HIGHEST,
    )
    output = (
        inner_term
        + carried.reshape(inner_term.shape) * jnp.exp(log_decay)[:, :, None]
        + skip_gain[None, :, None] * inputs
    )
    return output.reshape(block_rows, model_width)


def spread(decays, carry_state):
    return jnp.repeat(decays, carry_state.shape[0] // decays.shape[0])[:, None] * carry_state


def combine(earlier, later):
    return (earlier[0] * later[0], spread(later[0], earlier[1]) + later[1])


def chain_states(decays, increments, start_state):

    def advance(carry, block_items):
        carry_state, decay_total = carry
        return (
            (spread(block_items[0], carry_state) + block_items[1], decay_total * block_items[0]),
            carry_state,
        )

    (end_state, decay_total), incoming = lax.scan(
        advance, (start_state, jnp.ones_like(decays[0])), (decays, increments)
    )
    return (incoming, end_state, decay_total)


def shards(teacher_rows, teacher_next, state_proj, step_proj, rate_log, step_bias, skip_gain):
    seq_rows, local_width = teacher_rows.shape
    dp_count = lax.axis_size("dp")
    member = lax.axis_index("dp")
    head_count = rate_log.shape[0]
    local_heads = head_count // dp_count
    state_width = state_proj.shape[1] // 2
    block_rows = min(BLOCK, seq_rows)
    block_count = seq_rows // block_rows
    tokens_all = seq_rows * lax.axis_size("seq")
    joined = jnp.concatenate([state_proj, step_proj], axis=1)
    proj_all = jnp.dot(
        lax.all_gather(teacher_rows, "dp", axis=1, tiled=True),
        joined,
        preferred_element_type=jnp.float32,
    )
    proj_bc = proj_all[:, : 2 * state_width]
    proj_dt = proj_all[:, 2 * state_width :]
    head_start = member * local_heads
    own_dt = lax.dynamic_slice_in_dim(proj_dt, head_start, local_heads, 1)
    own_rate = lax.dynamic_slice_in_dim(rate_log, head_start, local_heads, 0)
    own_bias = lax.dynamic_slice_in_dim(step_bias, head_start, local_heads, 0)
    own_skip = lax.dynamic_slice_in_dim(skip_gain, head_start, local_heads, 0)
    pieces_rows = teacher_rows.reshape(block_count, block_rows, local_width)
    pieces_target = teacher_next.reshape(block_count, block_rows, local_width)

    def summaries(proj_bc, own_dt, own_rate, own_bias):

        def summaries_per_block(block_items):
            rows_block, bc_block, dt_block = block_items
            b_input, c_output, dt_steps, log_decay = block_terms(
                bc_block, dt_block, own_rate, own_bias
            )
            return block_state(rows_block, b_input, dt_steps, log_decay, local_heads)

        return lax.map(
            summaries_per_block,
            (
                pieces_rows,
                proj_bc.reshape(block_count, block_rows, -1),
                own_dt.reshape(block_count, block_rows, local_heads),
            ),
        )

    def local_end(decays, increments):
        _, end_state, decay_total = chain_states(
            decays, increments, jnp.zeros((local_width, state_width), jnp.float32)
        )
        return (end_state, decay_total)

    def entering(decays, increments, start_state):
        return chain_states(decays, increments, start_state)[0]

    def errors(proj_bc, own_dt, own_rate, own_bias, own_skip, incoming):

        def errors_per_block(block_items):
            rows_block, target_block, bc_block, dt_block, carry_state = block_items
            b_input, c_output, dt_steps, log_decay = block_terms(
                bc_block, dt_block, own_rate, own_bias
            )
            output = block_output(
                rows_block,
                b_input,
                c_output,
                dt_steps,
                log_decay,
                own_skip,
                carry_state,
                local_heads,
            )
            residual = output - target_block.astype(jnp.float32)
            return jnp.sum(residual * residual)

        block_sums = lax.map(
            errors_per_block,
            (
                pieces_rows,
                pieces_target,
                proj_bc.reshape(block_count, block_rows, -1),
                own_dt.reshape(block_count, block_rows, local_heads),
                incoming,
            ),
        )
        return jnp.sum(block_sums) / (2.0 * tokens_all)

    (decays, increments), pull_summary = jax.vjp(summaries, proj_bc, own_dt, own_rate, own_bias)
    (end_state, decay_total), pull_end = jax.vjp(local_end, decays, increments)
    identity = (jnp.ones_like(decay_total), jnp.zeros_like(end_state))
    _, state_before = entering_2((decay_total, end_state), "seq", combine, identity, False)
    incoming, pull_entering = jax.vjp(entering, decays, increments, state_before)
    partial_loss, pull_errors = jax.vjp(
        errors, proj_bc, own_dt, own_rate, own_bias, own_skip, incoming
    )
    err_grad_bc, err_grad_dt, err_grad_rate, err_grad_bias, err_grad_skip, grad_incoming = (
        pull_errors(jnp.ones((), jnp.float32))
    )
    in_grad_decays, in_grad_increments, grad_before = pull_entering(grad_incoming)
    _, grad_after = entering_2((decay_total, grad_before), "seq", combine, identity, True)
    grad_decay_total = jnp.sum((grad_after * state_before).reshape(local_heads, -1), axis=1)
    end_grad_decays, end_grad_increments = pull_end((grad_after, grad_decay_total))
    sum_grad_bc, sum_grad_dt, sum_grad_rate, sum_grad_bias = pull_summary(
        (in_grad_decays + end_grad_decays, in_grad_increments + end_grad_increments)
    )
    grad_dt_cols = lax.dynamic_update_slice_in_dim(
        jnp.zeros((seq_rows, head_count), jnp.float32), err_grad_dt + sum_grad_dt, head_start, 1
    )
    head_partial = jnp.concatenate([err_grad_bc + sum_grad_bc, grad_dt_cols], axis=1)
    proj_grads = lax.psum(head_partial, "dp").astype(jnp.bfloat16)
    weight_part = lax.dot_general(
        teacher_rows, proj_grads, (((0,), (0,)), ((), ())), preferred_element_type=jnp.float32
    )
    summed = lax.psum(weight_part, "seq")
    empty_heads = jnp.zeros((head_count,), jnp.float32)
    rate_part = lax.dynamic_update_slice_in_dim(
        empty_heads, err_grad_rate + sum_grad_rate, head_start, 0
    )
    bias_part = lax.dynamic_update_slice_in_dim(
        empty_heads, err_grad_bias + sum_grad_bias, head_start, 0
    )
    skip_part = lax.dynamic_update_slice_in_dim(empty_heads, err_grad_skip, head_start, 0)
    loss_total, total_rate, total_bias, total_skip = lax.psum(
        (partial_loss, rate_part, bias_part, skip_part), ("seq", "dp")
    )
    model_width = local_width * dp_count
    return (
        loss_total / model_width,
        summed[:, : 2 * state_width],
        summed[:, 2 * state_width :],
        total_rate,
        total_bias,
        total_skip,
    )


def solution(mesh):
    placed = (P("seq", "dp"), P("seq", "dp"), P(), P(), P(), P(), P())
    return jax.shard_map(
        shards,
        mesh=mesh,
        in_specs=placed,
        out_specs=(P(), P("dp", None), P("dp", None), P(), P(), P()),
        check_vma=False,
    )
```

profile of v0, /device:TPU:0, one launch (start us, length us, event | category | flops | bytes accessed | tf_op | source)
XLA Modules:
  0.0 1084.9 jit_solution(17986296282966292676)
XLA Ops:
  10.2 15.8 %all-gather.7.cloned.1.call-done = bf16[256,8192]{1,0:T(8,128)(2,1)} async-done(((bf16[256,4096]{1,0:T(8,128)(2,1)}), bf16[256,8192]{1,0:T(8,128)(2,1)}) %all-gather.7.cloned.1.call-update) | async-done | bytes 4194320 | tf_op jit(solution)/shard_map/all_gather | solution.py:118
  26.0 5.3 fusion.71
  36.0 6.2 convolution_add_fusion.1
  42.2 4.1 copy.78
  46.4 4.3 copy.81
  50.8 41.3 %all-gather.2 = f32[16,1,32]{2,1,0:T(1,128)S(1)} all-gather(f32[1,1,32]{2,1,0:T(1,128)S(1)} %bitcast.227), channel_id=1, replica_groups=mesh['seq'=16,'dp'=2] {'seq'}, dimensions={0}, use_global_device_ids=true | all-gather | bytes 2176 | tf_op jit(solution)/shard_map/all_gather | solution.py:11
  92.2 302.0 %all-gather.9.cloned.1.call-done = f32[65536,128]{1,0:T(8,128)} async-done(((f32[4096,128]{1,0:T(8,128)}), f32[65536,128]{1,0:T(8,128)}) %all-gather.9.cloned.1.call-update) | async-done | bytes 33554448 | tf_op jit(solution)/shard_map/all_gather | solution.py:11
  394.3 35.9 %while.25 = (s32[]{:T(128)}, f32[4096,128]{1,0:T(8,128)S(1)}, s32[]{:T(128)}, f32[16,32]{1,0:T(8,128)S(1)}, f32[16,4096,128]{2,1,0:T(8,128)}, /*index=5*/s32[]{:T(128)}, s32[]{:T(128)}) while((s32[]{:T(128)}, f32[4096,128]{1,0:T(8,128)S(1)}, s32[]{:T(128)}, f32[16,32]{1,0:T(8,128)S(1)}, f32[16,4096,128]{2,1,0:T(8,128)}, ...), condition=%wide.region_3.5_spmd.clone, body=%wide.region_2.4_spmd.clone.sunk | while | flops 2097156 | bytes 6324713 | solution.py:24
  432.5 2.7 copy-done.12
  435.3 5.8 multiply_reduce_fusion.1
  441.1 5.8 copy.82
  449.9 8.8 convolution_add_fusion
  459.0 6.8 fusion.20
  465.8 6.0 copy.84
  471.8 4.4 multiply_reduce_fusion
  477.2 6.5 fusion.12
  483.7 2.5 reduce-window.48
  486.6 10.7 convolution_convert_fusion.3
  497.5 310.5 %all-gather.11.cloned.1.call-done = f32[65536,128]{1,0:T(8,128)} async-done(((f32[4096,128]{1,0:T(8,128)}), f32[65536,128]{1,0:T(8,128)}) %all-gather.11.cloned.1.call-update) | async-done | bytes 33554448 | tf_op jit(solution)/shard_map/all_gather | solution.py:11
  808.0 36.3 %while.26 = (s32[]{:T(128)}, f32[4096,128]{1,0:T(8,128)S(1)}, s32[]{:T(128)}, f32[16,32]{1,0:T(8,128)S(1)}, f32[16,4096,128]{2,1,0:T(8,128)}, /*index=5*/s32[]{:T(128)}, s32[]{:T(128)}, s32[]{:T(128)}, s32[]{:T(128)}) while((s32[]{:T(128)}, f32[4096,128]{1,0:T(8,128)S(1)}, s32[]{:T(128)}, f32[16,32]{1,0:T(8,128)S(1)}, ...), condition=%wide.region_8.10_spmd.clone, body=%wide.region_7.9_spmd.clone.sunk | while | flops 2097160 | bytes 6324775 | solution.py:24
  844.3 5.5 convolution_convert_fusion.2
  851.5 2.7 fusion.17
  854.5 5.6 copy.89
  860.1 3.7 fusion.22
  864.3 2.5 reduce-window.50
  867.2 4.3 all-reduce.9
  871.5 3.2 convolution_bitcast_fusion
  876.3 42.5 %all-reduce.4 = (f32[]{:T(128)}, f32[64]{0:T(128)}, f32[64]{0:T(128)}, f32[64]{0:T(128)}) all-reduce(f32[]{:T(128)S(6)} %div.6, f32[64]{0:T(128)S(1)} %multiply_dynamic-update-slice_fusion, f32[64]{0:T(128)S(1)} %add_dynamic-update-slice_fusion.1, f32[64]{0:T(128)S(1)} %dynamic_update_slice.109), channel_id=1, replica_groups=mesh['seq'=16,'dp'=2] {'seq','dp'}, use_global_device_ids=true, to_apply=%region_5.7 | all-reduce | flops 193 | bytes 1544 | tf_op jit(solution)/shard_map/psum | solution.py:226
  919.4 144.9 %all-reduce.8.cloned.1.call-done = f32[4096,320]{0,1:T(8,128)} async-done(((f32[4096,320]{0,1:T(8,128)}), f32[4096,320]{0,1:T(8,128)}) %all-reduce.8.cloned.1.call-update) | async-done | bytes 5242896 | tf_op jit(solution)/shard_map/psum | solution.py:217
  1064.3 4.7 slice.92
  1068.9 5.6 copy.94
  1074.5 2.3 slice.93
  (189 shorter events, 89.9 us)
Async XLA Ops:
  7.2 2.8 copy-start.14
  7.2 2.9 copy-start.13
  7.2 18.8 %all-gather.7.cloned.1.call-start = ((), (), s32[]{:S(2)}) async-start(), calls=%async_computation | async-start | bytes 6291456 | tf_op jit(solution)/shard_map/all_gather | solution.py:118
  7.9 386.3 %all-gather.9.cloned.1.call-start = ((), (), s32[]{:S(2)}) async-start(), calls=%async_computation.2 | async-start | bytes 35651584 | tf_op jit(solution)/shard_map/all_gather | solution.py:11
  31.3 4.7 copy-start.2
  33.9 2.1 copy-start.6
  42.1 4.2 copy-start.15
  42.2 765.8 %all-gather.11.cloned.1.call-start = ((), (), s32[]{:S(2)}) async-start(), calls=%async_computation.3 | async-start | bytes 35651584 | tf_op jit(solution)/shard_map/all_gather | solution.py:11
  430.2 10.9 %copy-start = (f32[4096,128]{1,0:T(8,128)}, f32[4096,128]{1,0:T(8,128)S(1)}, u32[]{:S(2)}) copy-start(f32[4096,128]{1,0:T(8,128)S(1)} %get-tuple-element.806) | copy-start | bytes 6291460
  430.2 2.3 copy-start.10
  430.2 5.1 copy-start.12
  432.1 9.0 copy-start.8
  441.1 8.9 copy-start.7
  446.9 3.1 copy-start.4
  448.0 1.9 copy-start.5
  458.8 605.5 %all-reduce.8.cloned.1.call-start = ((), (), s32[]{:S(2)}) async-start(), calls=%async_computation.1 | async-start | bytes 10485760 | tf_op jit(solution)/shard_map/psum | solution.py:217
  471.8 4.7 copy-start.9
  471.8 5.3 copy-start.11
  844.2 5.5 copy-start.1
  860.1 11.4 %copy-start.3 = (bf16[256,4096]{1,0:T(8,128)(2,1)S(1)}, bf16[256,4096]{1,0:T(8,128)(2,1)}, u32[]{:S(2)}) copy-start(bf16[256,4096]{1,0:T(8,128)(2,1)} %param.14) | copy-start | bytes 6291460
Sparse Core Ops, SparseCore 0:
  9.6 16.3 all-gather.6
  42.3 351.9 all-gather.8
  458.9 349.0 all-gather.10
  874.9 189.3 all-reduce.7
where the time goes:
time: 1090 us; the launch traced here: 1080 us
  waiting for transfers between devices  774 us (71%)
  other arithmetic  92.8 us (9%)
  blocking collectives  88 us (8%)
  matrix products  57.1 us (5%)
  local copies, waits for them, and re-layouts  54.4 us (5%)
  between operations  17 us (2%)
    all_gather x2, waiting for transfers between devices, entering_2(): everything = jax.tree.map(lambda part: lax.all_gather(part, axis), value)  613 us
    psum x1, waiting for transfers between devices, shards(): summed = lax.psum(weight_part, 'seq')  145 us
    select_n x32, other arithmetic, lap(): return jax.tree.map(lambda a, b: jnp.where(reached, a, b), new, before)  68.3 us
    psum x1, blocking collectives, shards(): lax.psum((partial_loss, rate_part, bias_part, skip_part), ('seq', 'dp'))  42.5 us
    all_gather x1, blocking collectives, entering_2(): everything = jax.tree.map(lambda part: lax.all_gather(part, axis), value)  41.3 us
  transfers between devices with their start and end apart: 4, of which 4 were waited for; matrix products, arithmetic and copies ran while one was open for 5% of the time, Pallas kernels for 0%

commit v1 on v0

v1 whole, which is shorter than its diff:
```python
import functools

import jax
import jax.numpy as jnp
from jax import lax
from jax.experimental import pallas as pl
from jax.experimental.pallas import tpu as pltpu
from jax.sharding import PartitionSpec as P

F32 = jnp.float32
BF16 = jnp.bfloat16
HEADS = 8
LANE = 128
TAIL = 16
CUM, STEP, GROWN, LEFT, SLOPE, HALF = 0, 8, 16, 24, 32, 40
TABLE = 48
KINDS = 8
VMEM_LIMIT = 20 * 1024 * 1024
VMEM_WIDE = 56 * 1024 * 1024
FLOPS_US = 1100000000


def dot_00(a, b, **kw):
    return lax.dot_general(a, b, (((0,), (0,)), ((), ())), preferred_element_type=F32, **kw)


def dot_11(a, b, **kw):
    return lax.dot_general(a, b, (((1,), (1,)), ((), ())), preferred_element_type=F32, **kw)


def dot_10(a, b, **kw):
    return lax.dot_general(a, b, (((1,), (0,)), ((), ())), preferred_element_type=F32, **kw)


def whole(shape):
    zeros = (0,) * len(shape)
    return pl.BlockSpec(shape, lambda *_: zeros)


def call(body, grid, in_specs, out_specs, out_shape, scratch=(), us=1, vmem=VMEM_LIMIT, aliases=None):
    return pl.pallas_call(
        body,
        grid_spec=pltpu.PrefetchScalarGridSpec(
            num_scalar_prefetch=1,
            grid=grid,
            in_specs=in_specs,
            out_specs=out_specs,
            scratch_shapes=list(scratch),
        ),
        out_shape=out_shape,
        input_output_aliases=aliases or {},
        cost_estimate=pl.CostEstimate(flops=us * FLOPS_US, bytes_accessed=0, transcendentals=0),
        compiler_params=pltpu.CompilerParams(vmem_limit_bytes=vmem),
    )


ORDER = (8, LANE)
AFTER = pl.BlockSpec(memory_space=pl.ANY)


def shape_of(shape, dtype):
    return jax.ShapeDtypeStruct(shape, dtype)


def head_lanes(h):
    return slice(h * LANE, (h + 1) * LANE)


def transposed(rows):
    count, length = rows.shape
    if count < LANE:
        rows = jnp.concatenate([rows, jnp.zeros((LANE - count, length), F32)], axis=0)
    return rows.T


def rounded_parts(value):
    high = value.astype(BF16).astype(F32)
    middle = (value - high).astype(BF16).astype(F32)
    return high, middle, value - high - middle


def tree_sum(parts):
    while len(parts) > 1:
        parts = [parts[i] + parts[i + 1] for i in range(0, len(parts), 2)]
    return parts[0]


def project_body(direct, sp, u_ref, wb_ref, wd_ref, out_ref, *copies):
    k = pl.program_id(0)

    @pl.when(k == 0)
    def _():
        out_ref[...] = jnp.zeros_like(out_ref)

    u = u_ref[...]
    bc_width = wb_ref.shape[1]
    head_count = wd_ref.shape[0]
    out_ref[:, :bc_width] += dot_10(u, wb_ref[...])
    out_ref[:, bc_width : bc_width + head_count] += dot_11(u, wd_ref[...])
    for o, copy in zip(direct, copies):

        @pl.when(k == o)
        def _():
            copy[...] = u


def running_sum(rows, keep):
    count = rows.shape[0]
    parts = jnp.concatenate(rounded_parts(rows), axis=0).astype(BF16)
    sums = dot_10(parts, jnp.where(keep, 1.0, 0.0).astype(BF16))
    return sums[:count] + sums[count : 2 * count] + sums[2 * count :]


def table_body(groups, local_heads, members, sp, *refs):
    projs = refs[:members]
    u_ref, par_ref, bc_ref, rows_ref, cols_ref = refs[members : members + 5]
    messages, dt_all, table_ref = refs[members + 5 : -2], refs[-2], refs[-1]
    o = pl.program_id(0)
    q = o ^ sp[1]
    length = u_ref.shape[0]
    states = bc_ref.shape[1] // 2

    @pl.when(o == 0)
    def _():
        proj = tree_sum([part[...] for part in projs])
        bc_ref[...] = proj[:, : 2 * states].astype(BF16)
        dt_all[...] = proj[:, 2 * states :].T
        own = pl.ds(pl.multiple_of(sp[0] * local_heads, HEADS), local_heads)
        raw = dt_all[own, :] + par_ref[own, 1:2]
        rate = jnp.exp(par_ref[own, 0:1])
        small = jnp.exp(-jnp.abs(raw))
        dt = jnp.maximum(raw, 0.0) + jnp.log1p(small)
        from_pos = lax.broadcasted_iota(jnp.int32, (length, length), 0)
        to_pos = lax.broadcasted_iota(jnp.int32, (length, length), 1)
        cum = running_sum(-rate * dt, from_pos <= to_pos)
        end = cum[:, length - 1 : length]
        middle = cum[:, LANE - 1 : LANE]
        kinds = {
            CUM: cum,
            STEP: dt,
            GROWN: jnp.exp(cum),
            LEFT: dt * jnp.exp(jnp.minimum(end - cum, 0.0)),
            SLOPE: jnp.where(raw >= 0, 1.0, small) / (1.0 + small),
            HALF: jnp.exp(-jnp.abs(cum - middle)),
        }
        for at, kind in kinds.items():
            for g in range(groups):
                table_ref[g, at : at + HEADS, :] = kind[g * HEADS : (g + 1) * HEADS]

    table = table_ref[q]
    rows_ref[0] = table
    cols = transposed(table)
    cols_ref[0] = cols
    u = u_ref[...]
    scaled = jnp.concatenate(
        [
            (u[:, head_lanes(h)].astype(F32) * cols[:, LEFT + h : LEFT + h + 1]).astype(BF16)
            for h in range(HEADS)
        ],
        axis=1,
    )
    gained = dot_00(bc_ref[:, :states], scaled).astype(BF16)
    decay = table[GROWN : GROWN + HEADS, length - 1 : length]
    high, middle, low = rounded_parts(decay)
    spare = jnp.zeros((HEADS, LANE), F32)
    tail = [
        jnp.concatenate([jnp.broadcast_to(part, (HEADS, LANE)), spare], axis=0).astype(BF16)
        for part in (high, middle, low)
    ]
    for k in range(groups):

        @pl.when(o == k)
        def _():
            out = messages[k]
            out[:states, :] = gained
            out[states:, :] = jnp.zeros((TAIL, out.shape[1]), BF16)
            for i in range(3):
                out[states:, head_lanes(i)] = tail[i]


def causal_scores(b_input, c_output):
    scores = dot_11(c_output, b_input)
    row = lax.broadcasted_iota(jnp.int32, scores.shape, 0)
    col = lax.broadcasted_iota(jnp.int32, scores.shape, 1)
    return jnp.where(row >= col, scores, 0.0)


def decays_of(cols, rows, h, at, back=False):
    here = slice(at, at + LANE)
    gap = cols[here, CUM + h : CUM + h + 1] - rows[CUM + h : CUM + h + 1, here]
    return jnp.exp(jnp.minimum(-gap if back else gap, 0.0))


def local_body(groups, local_heads, sp, bc_ref, rows_ref, cols_ref, u_ref, target_ref, par_ref, err_ref, *rest):
    outs, scores_ref = rest[:groups], rest[groups]
    o = pl.program_id(0)
    q = o ^ sp[1]
    length = bc_ref.shape[0]
    states = bc_ref.shape[1] // 2

    @pl.when(o == 0)
    def _():
        scores_ref[...] = causal_scores(bc_ref[:, :states], bc_ref[:, states:])

    start = pl.multiple_of(sp[0] * local_heads + q * HEADS, HEADS)
    skip = par_ref[pl.ds(start, HEADS), 2:3]
    rows = rows_ref[0]
    cols = cols_ref[0]
    weighted = []
    for h in range(HEADS):
        x = u_ref[:, head_lanes(h)].astype(F32)
        stepped = (x * cols[:, STEP + h : STEP + h + 1]).astype(BF16)
        blocks = []
        for at in range(0, length, LANE):
            here = slice(at, at + LANE)
            row = [decays_of(cols, rows, h, at) * scores_ref[here, here]]
            if at:
                across = cols[here, HALF + h : HALF + h + 1] * rows[HALF + h : HALF + h + 1, :at]
                row.insert(0, across * scores_ref[here, :at])
            if at + LANE < length:
                row.append(jnp.zeros((LANE, length - at - LANE), F32))
            blocks.append(jnp.concatenate(row, axis=1).astype(BF16))
        inner = dot_10(jnp.concatenate(blocks, axis=0), stepped)
        err = inner + skip[h : h + 1, :] * x - target_ref[:, head_lanes(h)].astype(F32)
        err_ref[:, head_lanes(h)] = err
        weighted.append((err * cols[:, GROWN + h : GROWN + h + 1]).astype(BF16))
    grads = dot_00(bc_ref[:, states:], jnp.concatenate(weighted, axis=1)).astype(BF16)
    grown = rows[GROWN : GROWN + HEADS]
    grown = jnp.concatenate([grown, jnp.zeros_like(grown)], axis=0)
    piece = length // HEADS
    for k in range(groups):

        @pl.when(o == k)
        def _():
            out = outs[k]
            out[:states, :] = grads
            base = states + piece
            for i in range(HEADS):
                out[states:base, head_lanes(i)] = bc_ref[i * piece : (i + 1) * piece, states:]
            out[base:, :] = jnp.zeros((TAIL, out.shape[1]), BF16)
            out[base:, :length] = grown.astype(BF16)


def moment_body(groups, far, length, states, sp, *refs):
    messages, rows = refs[:groups], refs[groups : groups + far]
    out_ref = refs[groups + far + 1]
    for row, copy in zip(rows, refs[groups + far + 2 :]):
        copy[...] = row[...]
    piece = length // HEADS
    base = states + piece
    for o in range(groups):
        message = messages[o]
        c_output = jnp.concatenate(
            [message[states:base, head_lanes(i)] for i in range(HEADS)], axis=0
        )
        grown = message[base : base + TAIL, :length].astype(F32)[:HEADS]
        cols = transposed(grown * grown)
        wide = c_output.astype(F32)
        scaled = jnp.concatenate(
            [(wide * cols[:, h : h + 1]).astype(BF16) for h in range(HEADS)], axis=1
        )
        out_ref[o ^ sp[1]] = dot_00(c_output, scaled).astype(BF16)


def gather_body(groups, states, planes, count, sp, *refs):
    messages = refs[:groups]
    inc_ref, decay_ref, total_ref, span_ref = refs[-4 - count : -count]
    sent = refs[-count:]
    for o in range(groups):
        message = messages[o]
        parts = [message[states:, head_lanes(i)].astype(F32)[:HEADS] for i in range(3)]
        decay = (parts[0] + parts[1]) + parts[2]
        decay = jnp.concatenate([decay[h : h + 1] for h in range(HEADS)], axis=1)
        inc_ref[o ^ sp[1]] = message[:states, :]
        decay_ref[o ^ sp[1]] = jnp.broadcast_to(decay, decay_ref.shape[1:])
    total = inc_ref[0].astype(F32)
    span = decay_ref[0]
    for j in range(1, groups):
        total = decay_ref[j][:1] * total + inc_ref[j].astype(F32)
        span = span * decay_ref[j]
    total_ref[...] = total
    span_ref[...] = span
    if len(sent) == 1:
        sent[0][...] = total.astype(BF16)
        return
    piece = states // planes
    high, middle, _ = rounded_parts(span)
    tail = jnp.concatenate([high, middle], axis=0).astype(BF16)
    for m in range(planes):
        at = pl.multiple_of((sp[2] ^ m) * piece, TAIL)
        sent[m][:piece, :] = total_ref[pl.ds(at, piece), :].astype(BF16)
        sent[m][piece:, :] = tail


def ahead_body(planes, sp, *refs):
    messages, outs = refs[:planes], refs[-3 - planes : -3]
    span_ref, hold_ref, state_ref = refs[-3:]
    piece = state_ref.shape[1]
    for m in range(planes):
        tail = messages[m][piece:, :].astype(F32)
        span_ref[sp[2] ^ m] = tail[:HEADS] + tail[HEADS:]
        hold_ref[sp[2] ^ m] = messages[m][:piece, :]
    state = jnp.zeros(state_ref.shape[1:], F32)
    for k in range(planes):
        state_ref[k] = state.astype(BF16)
        state = span_ref[k][:1] * state + hold_ref[k].astype(F32)
    for m in range(planes):
        outs[m][...] = state_ref[sp[2] ^ m]


def behind_body(planes, sp, span_ref, *refs):
    messages, outs = refs[:planes], refs[-2 - planes : -2]
    hold_ref, state_ref = refs[-2:]
    for m in range(planes):
        hold_ref[sp[2] ^ m] = messages[m][...]
    state = jnp.zeros(state_ref.shape[1:], F32)
    for k in range(planes - 1, -1, -1):
        state_ref[k] = state.astype(BF16)
        state = span_ref[k][:1] * state + hold_ref[k].astype(F32)
    for m in range(planes):
        outs[m][...] = state_ref[sp[2] ^ m]


def assembled(pieces, hold_ref, sp):
    if len(pieces) == 1:
        hold_ref[...] = pieces[0][...]
    else:
        piece = pieces[0].shape[0]
        for m, part in enumerate(pieces):
            at = pl.multiple_of((sp[2] ^ m) * piece, TAIL)
            hold_ref[pl.ds(at, piece), :] = part[...]
    return hold_ref[...].astype(F32)


def forward_body(groups, pieces, sent_count, sp, inc_ref, decay_ref, moment_ref, *refs):
    before, locals_ = refs[:pieces], refs[pieces : pieces + groups]
    outs = refs[-4 - sent_count - groups : -4 - sent_count]
    grad_ref, total_ref = refs[-4 - sent_count : -2 - sent_count]
    sent = refs[-2 - sent_count : -2]
    states_ref, hold_ref = refs[-2:]
    states = hold_ref.shape[0]
    state = assembled(before, hold_ref, sp)
    for j in range(groups):
        states_ref[j] = state.astype(BF16)
        state = decay_ref[j][:1] * state + inc_ref[j].astype(F32)
    for o in range(groups):
        outs[o][...] = states_ref[o ^ sp[1]]
        grad_ref[o ^ sp[1]] = locals_[o][:states, :].astype(F32)
    for j in range(groups):
        moved = [
            dot_10(moment_ref[j, :, head_lanes(h)], states_ref[j, :, head_lanes(h)])
            for h in range(HEADS)
        ]
        grad_ref[j] = grad_ref[j] + jnp.concatenate(moved, axis=1)
    total = grad_ref[groups - 1]
    for j in range(groups - 2, -1, -1):
        total = decay_ref[j][:1] * total + grad_ref[j]
    total_ref[...] = total
    if sent_count == 1:
        sent[0][...] = total.astype(BF16)
        return
    piece = states // sent_count
    for m in range(sent_count):
        at = pl.multiple_of((sp[2] ^ m) * piece, TAIL)
        sent[m][...] = total_ref[pl.ds(at, piece), :].astype(BF16)


def backward_body(groups, pieces, sp, grad_ref, decay_ref, *refs):
    outs, hold_ref, join_ref = refs[-2 - groups : -2], refs[-2], refs[-1]
    after = assembled(refs[:pieces], join_ref, sp)
    for j in range(groups - 1, -1, -1):
        hold_ref[j] = after.astype(BF16)
        after = decay_ref[j][:1] * after + grad_ref[j]
    for o in range(groups):
        outs[o][...] = hold_ref[o ^ sp[1]]


def folded(values):
    return jnp.sum(values, axis=0, keepdims=True)


def head_sums(values):
    row = lax.broadcasted_iota(jnp.int32, (values.shape[1], LANE), 0)
    col = lax.broadcasted_iota(jnp.int32, (values.shape[1], LANE), 1)
    pick = jnp.where((row >= col * LANE) & (row < (col + 1) * LANE), 1.0, 0.0)
    return dot_10(values, pick.astype(BF16))


def error_body(first, local_heads, offset, sp, bc_ref, rows_ref, cols_ref, u_ref, target_ref, err_ref, par_ref, state_ref, *refs):
    sums_ref, head_ref, total_ref, order_ref, scores_ref = refs[-5:]
    length = bc_ref.shape[0]
    states = bc_ref.shape[1] // 2
    c_output = bc_ref[:, states:]
    scores = dot_11(bc_ref[:, :states], c_output)
    from_pos = lax.broadcasted_iota(jnp.int32, scores.shape, 0)
    to_pos = lax.broadcasted_iota(jnp.int32, scores.shape, 1)
    scores_ref[...] = jnp.where(from_pos <= to_pos, scores, 0.0)
    order_ref[...] = jnp.zeros_like(order_ref)
    if first:
        total_ref[...] = jnp.zeros_like(total_ref)
    else:
        total_ref[...] = refs[0][...]
    start = pl.multiple_of(sp[0] * local_heads + (sp[1] ^ offset) * HEADS, HEADS)
    skip = par_ref[pl.ds(start, HEADS), 2:3]
    rows = rows_ref[0]
    cols = cols_ref[0]
    carried = dot_10(c_output, state_ref[...])
    weighted, row_parts, col_parts = [], [], []
    for h in range(HEADS):
        x = u_ref[:, head_lanes(h)].astype(F32)
        grown = cols[:, GROWN + h : GROWN + h + 1]
        stepped = (x * cols[:, STEP + h : STEP + h + 1]).astype(BF16)
        err = err_ref[:, head_lanes(h)] + carried[:, head_lanes(h)] * grown
        short = err.astype(BF16)
        weighted.append((err * grown).astype(BF16))
        head_ref[h : h + 1, :] = folded(err * x)
        head_ref[HEADS + h : HEADS + h + 1, :] = folded(err * err)
        through = err - skip[h : h + 1, :] * x + target_ref[:, head_lanes(h)].astype(F32)
        row_parts.append((err * through).astype(BF16))
        pairs = dot_11(stepped, short)
        blocks = []
        for at in range(0, length, LANE):
            here = slice(at, at + LANE)
            decay = decays_of(cols, rows, h, at, back=True)
            total_ref[here, here] += pairs[here, here] * decay
            row = [decay * scores_ref[here, here]]
            if at:
                row.insert(0, jnp.zeros((LANE, at), F32))
            if at + LANE < length:
                late = slice(at + LANE, length)
                decay = cols[here, HALF + h : HALF + h + 1] * rows[HALF + h : HALF + h + 1, late]
                total_ref[here, late] += pairs[here, late] * decay
                row.append(decay * scores_ref[here, late])
            blocks.append(jnp.concatenate(row, axis=1).astype(BF16))
        pulled = dot_10(jnp.concatenate(blocks, axis=0), short)
        col_parts.append((pulled * x).astype(BF16))
    sums_ref[:HEADS, :] = head_sums(jnp.concatenate(row_parts, axis=1)).T[:HEADS]
    sums_ref[HEADS:, :] = head_sums(jnp.concatenate(col_parts, axis=1)).T[:HEADS]
    total_ref[:, length:] += dot_11(jnp.concatenate(weighted, axis=1), state_ref[...])


def input_body(first, sp, bc_ref, cols_ref, u_ref, state_ref, after_ref, *refs):
    sums_ref, met_ref, grad_ref = refs[-3:]
    states = bc_ref.shape[1] // 2
    cols = cols_ref[0]
    after = after_ref[...]
    pulled = dot_10(bc_ref[:, :states], after)
    met = folded(after.astype(F32) * state_ref[...].astype(F32))
    scaled, parts = [], []
    for h in range(HEADS):
        x = u_ref[:, head_lanes(h)].astype(F32)
        scaled.append((x * cols[:, LEFT + h : LEFT + h + 1]).astype(BF16))
        parts.append((pulled[:, head_lanes(h)] * x).astype(BF16))
        met_ref[h : h + 1, :] = met[:, head_lanes(h)]
    grad = dot_11(jnp.concatenate(scaled, axis=1), after)
    if not first:
        grad = grad + refs[0][...]
    grad_ref[...] = grad
    sums_ref[...] = head_sums(jnp.concatenate(parts, axis=1)).T[:HEADS]


def finish_body(groups, local_heads, scale, sp, bc_ref, rows_ref, par_ref, total_ref, grad_ref, *refs):
    sums, heads, pulls, mets = [refs[i * groups : (i + 1) * groups] for i in range(4)]
    out_ref, small_ref = refs[4 * groups :]
    length = bc_ref.shape[0]
    states = bc_ref.shape[1] // 2
    head_count = par_ref.shape[0]
    from_pos = lax.broadcasted_iota(jnp.int32, (length, length), 0)
    to_pos = lax.broadcasted_iota(jnp.int32, (length, length), 1)
    causal = from_pos >= to_pos
    spread = jnp.where(from_pos <= to_pos, total_ref[:, :length], 0.0).astype(BF16)
    c_grad = total_ref[:, length:] + dot_00(spread, bc_ref[:, :states])
    b_grad = grad_ref[...] + dot_10(spread, bc_ref[:, states:])
    out_ref[:states, :] = b_grad.T * scale
    out_ref[states : 2 * states, :] = c_grad.T * scale
    out_ref[2 * states :, :] = jnp.zeros((out_ref.shape[0] - 2 * states, length), F32)
    small_ref[...] = jnp.zeros_like(small_ref)
    starts = [
        pl.multiple_of(sp[0] * local_heads + (o ^ sp[1]) * HEADS, HEADS) for o in range(groups)
    ]

    def kind(at):
        return jnp.concatenate(
            [rows_ref[o ^ sp[1], at : at + HEADS, :] for o in range(groups)], axis=0
        )

    def stacked(refs, at=0):
        return jnp.concatenate([ref[at : at + HEADS, :] for ref in refs], axis=0)

    rate = jnp.exp(jnp.concatenate([par_ref[pl.ds(at, HEADS), 0:1] for at in starts], axis=0))
    cum, dt, grown, left, slope = [kind(at) for at in (CUM, STEP, GROWN, LEFT, SLOPE)]
    place = lax.broadcasted_iota(jnp.int32, cum.shape, 1)
    lane = lax.broadcasted_iota(jnp.int32, (cum.shape[0], LANE), 1)
    end = cum[:, length - 1 : length]
    row_sum = stacked(sums)
    col_sum = stacked(sums, HEADS)
    pulled = stacked(pulls)
    met = jnp.sum(stacked(mets), axis=1, keepdims=True)
    gain = pulled * left
    at_end = jnp.sum(gain, axis=1, keepdims=True) + met * grown[:, length - 1 : length]
    cum_grad = row_sum - dt * col_sum - gain + jnp.where(place == length - 1, at_end, 0.0)
    log_grad = running_sum(cum_grad, causal)
    dt_grad = col_sum + pulled * jnp.exp(jnp.minimum(end - cum, 0.0)) - rate * log_grad
    raw_grad = dt_grad * slope * scale
    rate_grad = jnp.sum(-rate * dt * log_grad, axis=1, keepdims=True)
    bias_grad = jnp.sum(raw_grad, axis=1, keepdims=True)
    skip_grad = jnp.sum(stacked(heads), axis=1, keepdims=True)
    loss = jnp.sum(stacked(heads, HEADS), axis=1, keepdims=True)
    small = jnp.where(lane == 0, rate_grad * scale, 0.0)
    small = jnp.where(lane == 1, bias_grad, small)
    small = jnp.where(lane == 2, skip_grad * scale, small)
    small = jnp.where(lane == 3, 0.5 * loss * scale, small)
    for o in range(groups):
        here = slice(o * HEADS, (o + 1) * HEADS)
        at = pl.multiple_of(2 * states + starts[o], HEADS)
        out_ref[pl.ds(at, HEADS), :] = raw_grad[here]
        small_ref[pl.ds(starts[o], HEADS), :] = small[here]
    out_ref[2 * states + head_count : 2 * states + head_count + KINDS, :LANE] = small_ref[...].T[:KINDS]


def merge_body(members, width, sp, *refs):
    out_ref = refs[members]
    total = tree_sum([part[...] for part in refs[:members]])
    out_ref[:width, :] = total[:width].astype(BF16)
    parts = rounded_parts(total[width : width + KINDS])
    parts = jnp.concatenate(list(parts) + [jnp.zeros_like(parts[0])], axis=0)
    out_ref[width:, :] = parts.astype(BF16)


def weight_body(groups, planes, width, sp, *refs):
    grads, rows = refs[:groups], refs[groups : 2 * groups]
    own_ref, small_ref = refs[2 * groups : 2 * groups + 2]
    sent, hold_ref = refs[2 * groups + 2 : -1], refs[-1]
    piece = own_ref.shape[0]
    total = dot_10(grads[0][:width, :], rows[0][...])
    for o in range(1, groups):
        total = total + dot_10(grads[o][:width, :], rows[o][...])
    hold_ref[:width, :] = total
    if hold_ref.shape[0] > width:
        hold_ref[width:, :] = jnp.zeros((hold_ref.shape[0] - width, hold_ref.shape[1]), F32)
    for m in range(planes):
        at = pl.multiple_of((sp[2] ^ m) * piece, TAIL)
        value = hold_ref[pl.ds(at, piece), :]
        if m == 0:
            own_ref[...] = value
        else:
            sent[m - 1][...] = value.astype(BF16)
    parts = []
    for o in range(groups):
        small = grads[o][width:, :].astype(F32)
        parts.append((small[:KINDS] + small[KINDS : 2 * KINDS]) + small[2 * KINDS : 3 * KINDS])
    small_ref[...] = tree_sum(parts)[:, :LANE]


def spread_body(planes, sp, *refs):
    pieces = refs[:planes]
    state_ref, step_ref, hold_ref = refs[-3:]
    piece = hold_ref.shape[0] // planes
    for m in range(planes):
        at = pl.multiple_of((m ^ sp[2]) * piece, TAIL)
        hold_ref[pl.ds(at, piece), :] = pieces[m][...]
    width = state_ref.shape[1]
    steps = step_ref.shape[0]
    state_ref[...] = hold_ref[:width, :].astype(F32).T
    step_ref[...] = hold_ref[width : width + steps, :].astype(F32)


def shards(seq_count, dp_count, teacher_rows, teacher_next, state_proj, step_proj, rate_log, step_bias, skip_gain):
    length, local_width = teacher_rows.shape
    bc_width = state_proj.shape[1]
    states = bc_width // 2
    head_count = rate_log.shape[0]
    local_heads = head_count // dp_count
    groups = local_heads // HEADS
    planes = seq_count // groups
    span = local_width // groups
    member = lax.axis_index("dp")
    position = lax.axis_index("seq")
    mine, plane = position % groups, position // groups
    sp = jnp.stack([member, mine, plane]).astype(jnp.int32)
    params = jnp.stack([rate_log, step_bias, skip_gain], axis=1)
    proj_width = bc_width + LANE
    scale = 1.0 / (length * seq_count)

    def in_plane(value, o):
        pairs = [(i, (i // groups) * groups + ((i % groups) ^ o)) for i in range(seq_count)]
        return lax.ppermute(value, "seq", pairs)

    def over_planes(value, m):
        pairs = [(i, ((i // groups) ^ m) * groups + i % groups) for i in range(seq_count)]
        return lax.ppermute(value, "seq", pairs)

    def next_plane(value, step):
        pairs = [
            (i, i + step * groups) for i in range(seq_count) if 0 <= i + step * groups < seq_count
        ]
        return lax.ppermute(value, "seq", pairs)

    def exchanged(parts):
        return [parts[0]] + [in_plane(parts[o], o) for o in range(1, groups)]

    def members_of(value):
        pairs = [[(i, i ^ k) for i in range(dp_count)] for k in range(1, dp_count)]
        return [value] + [lax.ppermute(value, "dp", pair) for pair in pairs]

    direct = [o for o in range(1, groups) if o & (o - 1) == 0]
    far = [o for o in range(1, groups) if o & (o - 1)]
    partial, *near_copies = call(
        functools.partial(project_body, direct),
        (groups,),
        [
            pl.BlockSpec((length, span), lambda o, sp: (0, o ^ sp[1])),
            pl.BlockSpec((span, bc_width), lambda o, sp: (sp[0] * groups + (o ^ sp[1]), 0)),
            pl.BlockSpec((head_count, span), lambda o, sp: (0, sp[0] * groups + (o ^ sp[1]))),
        ],
        [whole((length, proj_width))] + [whole((length, span))] * len(direct),
        [shape_of((length, proj_width), F32)] + [shape_of((length, span), BF16)] * len(direct),
        us=3,
        vmem=VMEM_WIDE,
    )(sp, teacher_rows, state_proj, step_proj.T)
    projs = members_of(partial)
    moved_rows = {o: in_plane(copy, o) for o, copy in zip(direct, near_copies)}

    message_shape = (states + TAIL, span)
    local_shape = (states + length // HEADS + TAIL, span)
    group_rows = pl.BlockSpec((1, TABLE, length), lambda o, sp: (o ^ sp[1], 0, 0))
    group_cols = pl.BlockSpec((1, length, LANE), lambda o, sp: (o ^ sp[1], 0, 0))
    group_wide = pl.BlockSpec((length, span), lambda o, sp: (0, o ^ sp[1]))
    state_shape = (states, span)
    bc, rows, cols, *messages = call(
        functools.partial(table_body, groups, local_heads, dp_count),
        (groups,),
        [whole((length, proj_width))] * dp_count + [group_wide, whole(params.shape)],
        [whole((length, bc_width)), group_rows, group_cols] + [whole(message_shape)] * groups,
        [
            shape_of((length, bc_width), BF16),
            shape_of((groups, TABLE, length), F32),
            shape_of((groups, length, LANE), F32),
        ]
        + [shape_of(message_shape, BF16)] * groups,
        [pltpu.VMEM((LANE, length), F32), pltpu.VMEM((groups, TABLE, length), F32)],
        us=5,
    )(sp, *projs, teacher_rows, params)
    messages = exchanged(messages)

    err, *outs = call(
        functools.partial(local_body, groups, local_heads),
        (groups,),
        [whole((length, bc_width)), group_rows, group_cols, group_wide, group_wide, whole(params.shape)],
        [group_wide] + [whole(local_shape)] * groups,
        [shape_of((length, local_width), F32)]
        + [shape_of(local_shape, BF16)] * groups,
        [pltpu.VMEM((length, length), F32)],
        us=7,
    )(sp, bc, rows, cols, teacher_rows, teacher_next, params)
    local_grads = exchanged(outs)

    stack_shape = (groups,) + state_shape
    decay_shape = (groups, HEADS, span)
    shared = planes > 1 and states % (planes * TAIL) == 0
    piece_shape = (states // planes, span) if shared else state_shape
    sent_shape = (piece_shape[0] + TAIL, span) if shared else state_shape
    count = planes if shared else 1
    inc, decays, total, total_decay, *sent = call(
        functools.partial(gather_body, groups, states, planes, count),
        (1,),
        [whole(message_shape)] * groups + [AFTER] * (1 + len(direct)),
        [whole(stack_shape), whole(decay_shape), whole(state_shape), whole((HEADS, span))]
        + [whole(sent_shape)] * count,
        [
            shape_of(stack_shape, BF16),
            shape_of(decay_shape, F32),
            shape_of(state_shape, F32),
            shape_of((HEADS, span), F32),
        ]
        + [shape_of(sent_shape, BF16)] * count,
    )(sp, *messages, err, *moved_rows.values())
    def hop(before, total):
        return (total_decay[:1] * before.astype(F32) + total).astype(BF16)

    def exchanged_planes(parts):
        return [parts[0]] + [over_planes(parts[m], m) for m in range(1, planes)]

    spans_shape = (planes, HEADS, span)
    if shared:
        *parts, spans = call(
            functools.partial(ahead_body, planes),
            (1,),
            [whole(sent_shape)] * planes,
            [whole(piece_shape)] * planes + [whole(spans_shape)],
            [shape_of(piece_shape, BF16)] * planes + [shape_of(spans_shape, F32)],
            [pltpu.VMEM((planes,) + piece_shape, BF16)] * 2,
        )(sp, *exchanged_planes(sent))
        before = exchanged_planes(parts)
    else:
        before = jnp.zeros(state_shape, BF16)
        for step in range(planes - 1):
            before = next_plane(hop(before, total), 1)
        before, spans = [before], decays

    far_blocks = [
        pl.BlockSpec((length, span), functools.partial(lambda o, _, sp: (0, o ^ sp[1]), o))
        for o in far
    ]
    moments, *far_copies = call(
        functools.partial(moment_body, groups, len(far), length, states),
        (1,),
        [whole(local_shape)] * groups + far_blocks + [AFTER],
        [whole(stack_shape)] + [whole((length, span))] * len(far),
        [shape_of(stack_shape, BF16)] + [shape_of((length, span), BF16)] * len(far),
        us=2,
    )(sp, *local_grads, *[teacher_rows] * len(far), spans)
    far_rows = {o: in_plane(copy, o) for o, copy in zip(far, far_copies)}

    outs = call(
        functools.partial(forward_body, groups, count, count),
        (1,),
        [whole(stack_shape), whole(decay_shape), whole(stack_shape)]
        + [whole(piece_shape)] * count
        + [whole(local_shape)] * groups
        + [AFTER] * len(far),
        [whole(state_shape)] * groups
        + [whole(stack_shape), whole(state_shape)]
        + [whole(piece_shape)] * count,
        [shape_of(state_shape, BF16)] * groups
        + [shape_of(stack_shape, F32), shape_of(state_shape, F32)]
        + [shape_of(piece_shape, BF16)] * count,
        [pltpu.VMEM(stack_shape, BF16), pltpu.VMEM(state_shape, BF16)],
        us=2,
    )(
        sp,
        inc,
        decays,
        moments,
        *before,
        *local_grads,
        *far_rows.values(),
    )
    moved_rows = [(moved_rows | far_rows)[o] for o in range(1, groups)]
    entering = exchanged(outs[:groups])
    grads, grad_total, *grad_sent = outs[groups:]

    totals, sums, heads, orders = [], [], [], []
    total_shape = (length, length + states)
    for o in range(groups):
        fixed = functools.partial(lambda o, _, sp: (o ^ sp[1], 0, 0), o)
        fixed_wide = functools.partial(lambda o, _, sp: (0, o ^ sp[1]), o)
        one_sum, one_head, one_total, one_order = call(
            functools.partial(error_body, o == 0, local_heads, o),
            (1,),
            [
                whole((length, bc_width)),
                pl.BlockSpec((1, TABLE, length), fixed),
                pl.BlockSpec((1, length, LANE), fixed),
                pl.BlockSpec((length, span), fixed_wide),
                pl.BlockSpec((length, span), fixed_wide),
                pl.BlockSpec((length, span), fixed_wide),
                whole(params.shape),
                whole(state_shape),
            ]
            + [whole(total_shape)] * (o > 0),
            [
                whole((2 * HEADS, length)),
                whole((2 * HEADS, LANE)),
                whole(total_shape),
                whole(ORDER),
            ],
            [
                shape_of((2 * HEADS, length), F32),
                shape_of((2 * HEADS, LANE), F32),
                shape_of(total_shape, F32),
                shape_of(ORDER, F32),
            ],
            [pltpu.VMEM((length, length), F32)],
            us=4,
        )(sp, bc, rows, cols, teacher_rows, teacher_next, err, params, entering[o], *totals[-1:])
        orders.append(one_order)
        totals.append(one_total)
        sums.append(one_sum)
        heads.append(one_head)

    if shared:
        parts = call(
            functools.partial(behind_body, planes),
            (1,),
            [whole(spans_shape)] + [whole(piece_shape)] * planes,
            [whole(piece_shape)] * planes,
            [shape_of(piece_shape, BF16)] * planes,
            [pltpu.VMEM((planes,) + piece_shape, BF16)] * 2,
        )(sp, spans, *exchanged_planes(grad_sent))
        after = exchanged_planes(parts)
    else:
        after = jnp.zeros(state_shape, BF16)
        for step in range(planes - 1):
            after = next_plane(hop(after, grad_total), -1)
        after = [after]

    leaving = call(
        functools.partial(backward_body, groups, count),
        (1,),
        [whole(stack_shape), whole(decay_shape)] + [whole(piece_shape)] * count + [AFTER],
        [whole(state_shape)] * groups,
        [shape_of(state_shape, BF16)] * groups,
        [pltpu.VMEM(stack_shape, BF16), pltpu.VMEM(state_shape, BF16)],
    )(sp, grads, decays, *after, orders[min(1, groups - 1)])
    leaving = exchanged(leaving)

    pulls, mets, input_grads = [], [], []
    for o in range(groups):
        fixed = functools.partial(lambda o, _, sp: (o ^ sp[1], 0, 0), o)
        fixed_wide = functools.partial(lambda o, _, sp: (0, o ^ sp[1]), o)
        one_pull, one_met, one_grad = call(
            functools.partial(input_body, o == 0),
            (1,),
            [
                whole((length, bc_width)),
                pl.BlockSpec((1, length, LANE), fixed),
                pl.BlockSpec((length, span), fixed_wide),
                whole(state_shape),
                whole(state_shape),
            ]
            + [whole((length, states))] * (o > 0),
            [whole((HEADS, length)), whole((HEADS, LANE)), whole((length, states))],
            [
                shape_of((HEADS, length), F32),
                shape_of((HEADS, LANE), F32),
                shape_of((length, states), F32),
            ],
            us=2,
        )(sp, bc, cols, teacher_rows, entering[o], leaving[o], *input_grads[-1:])
        pulls.append(one_pull)
        mets.append(one_met)
        input_grads.append(one_grad)

    width = bc_width + head_count
    grad_rows = (width + TAIL, length)
    partial_grads = call(
        functools.partial(finish_body, groups, local_heads, scale),
        (1,),
        [
            whole((length, bc_width)),
            whole((groups, TABLE, length)),
            whole(params.shape),
            whole(total_shape),
            whole((length, states)),
        ]
        + [whole((2 * HEADS, length))] * groups
        + [whole((2 * HEADS, LANE))] * groups
        + [whole((HEADS, length))] * groups
        + [whole((HEADS, LANE))] * groups,
        whole(grad_rows),
        shape_of(grad_rows, F32),
        [pltpu.VMEM((LANE, LANE), F32)],
        us=2,
    )(sp, bc, rows, params, totals[-1], input_grads[-1], *sums, *heads, *pulls, *mets)
    grad_shape = (width + 4 * KINDS, length)
    merged = call(
        functools.partial(merge_body, dp_count, width),
        (1,),
        [whole(grad_rows)] * dp_count,
        whole(grad_shape),
        shape_of(grad_shape, BF16),
    )(sp, *members_of(partial_grads))
    merged = [merged] + [in_plane(merged, o) for o in range(1, groups)]

    unit = TAIL * planes
    padded = -(-width // unit) * unit
    piece = padded // planes
    share_shape = (piece, span)
    own, small, *sent = call(
        functools.partial(weight_body, groups, planes, width),
        (1,),
        [whole(grad_shape)] * groups
        + [pl.BlockSpec((length, span), lambda _, sp: (0, sp[1]))]
        + [whole((length, span))] * (groups - 1),
        [whole(share_shape), whole((KINDS, LANE))] + [whole(share_shape)] * (planes - 1),
        [shape_of(share_shape, F32), shape_of((KINDS, LANE), F32)]
        + [shape_of(share_shape, BF16)] * (planes - 1),
        [pltpu.VMEM((padded, span), F32)],
        us=3,
    )(sp, *merged, teacher_rows, *moved_rows)
    for m in range(1, planes):
        own = own + over_planes(sent[m - 1], m).astype(F32)
    own = own.astype(BF16)
    def all_over(value, send, count):
        parts, step = {0: value}, 1
        while step < count:
            step *= 2
        while step > 1:
            step //= 2
            parts |= {k | step: send(part, step) for k, part in parts.items()}
        return [parts[k] for k in range(count)]

    gathered = all_over(own, over_planes, planes)
    pieces = []
    for k, part in enumerate(gathered):
        spread = {0: part}
        steps = [1 << i for i in range(groups.bit_length() - 1)]
        for step in steps if k % 2 else steps[::-1]:
            spread |= {o | step: in_plane(value, step) for o, value in spread.items()}
        pieces.append(spread)
    step = 1
    while step < planes:
        small = small + over_planes(small, step)
        step *= 2
    results = []
    for o in range(groups):
        results = call(
            functools.partial(spread_body, planes),
            (1,),
            [whole(share_shape)] * planes + [AFTER] * len(results),
            [
                pl.BlockSpec((span, bc_width), functools.partial(lambda o, _, sp: (o ^ sp[1], 0), o)),
                pl.BlockSpec((head_count, span), functools.partial(lambda o, _, sp: (0, o ^ sp[1]), o)),
            ],
            [shape_of((local_width, bc_width), F32), shape_of((head_count, local_width), F32)],
            [pltpu.VMEM((padded, span), BF16)],
            aliases={1 + planes + i: i for i in range(len(results))},
        )(sp, *[part[o] for part in pieces], *results)
    state_grad, step_grad = results

    model_width = local_width * dp_count
    return (
        jnp.sum(small[3, :head_count]) / model_width,
        state_grad,
        step_grad.T,
        small[0, :head_count],
        small[1, :head_count],
        small[2, :head_count],
    )


def solution(mesh):
    placed = (P("seq", "dp"), P("seq", "dp"), P(), P(), P(), P(), P())
    return jax.shard_map(
        functools.partial(shards, mesh.shape["seq"], mesh.shape["dp"]),
        mesh=mesh,
        in_specs=placed,
        out_specs=(P(), P("dp", None), P("dp", None), P(), P(), P()),
        check_vma=False,
    )
```

time: 1090 us -> 187 us (0.17)
  waiting for transfers between devices: 774 us -> 55.7 us
  other arithmetic: 92.8 us -> 1.8 us
  blocking collectives: 88 us -> 0 us
  starting transfers between devices: 0.37 us -> 70.7 us
  matrix products: 57.1 us -> 0 us
  Pallas kernels: 0 us -> 54 us
  local copies, waits for them, and re-layouts: 54.4 us -> 1.25 us
  between operations: 17 us -> 2.84 us
    all_gather x3 -> x0, waiting for transfers between devices: 628 us -> none  [the longest x2 613 us: entering_2(): everything = jax.tree.map(lambda part: lax.all_gather(part, axis), value)]
    psum x1 -> x0, waiting for transfers between devices: 145 us -> none  [shards(): summed = lax.psum(weight_part, 'seq')]
    ppermute x0 -> x52, starting transfers between devices: none -> 70.7 us  [the longest x20 35.2 us: over_planes(): return lax.ppermute(value, 'seq', pairs)]
    select_n x32 -> x0, other arithmetic: 68.3 us -> none  [lap(): return jax.tree.map(lambda a, b: jnp.where(reached, a, b), new, before)]
    dot_general x13 -> x0, matrix products: 57.1 us -> none  [the longest x3 21.4 us: block_output(): lax.dot_general(c_output.astype(jnp.float32), carry_state, (((1,), (1,)),...]
    ppermute x0 -> x52, waiting for transfers between devices: none -> 55.7 us  [the longest x20 33.6 us: over_planes(): return lax.ppermute(value, 'seq', pairs)]
    pallas_call x0 -> x24, Pallas kernels: none -> 54 us  [the longest x4 11.7 us: shards(): call(functools.partial(error_body, o == 0, local_heads, o), (1,), [whole(...]
    psum x2 -> x0, blocking collectives: 46.8 us -> none  [the longest x1 42.5 us: shards(): lax.psum((partial_loss, rate_part, bias_part, skip_part), ('seq', 'dp'))]
  transfers between devices with their start and end apart: 4 -> 52, of which waited for: 4 -> 21; matrix products, arithmetic and copies ran while one was open for 5% -> 1% of each run, Pallas kernels for 0% -> 20%
where the time goes in v1:
time: 187 us; the launch traced here: 186 us
  starting transfers between devices  70.7 us (38%)
  waiting for transfers between devices  55.7 us (30%)
  Pallas kernels  54 us (29%)
  between operations  2.84 us (2%)
    ppermute x20, starting transfers between devices, over_planes(): return lax.ppermute(value, 'seq', pairs)  35.2 us
    ppermute x30, starting transfers between devices, in_plane(): return lax.ppermute(value, 'seq', pairs)  35 us
    ppermute x20, waiting for transfers between devices, over_planes(): return lax.ppermute(value, 'seq', pairs)  33.6 us
    ppermute x30, waiting for transfers between devices, in_plane(): return lax.ppermute(value, 'seq', pairs)  20.5 us
    pallas_call x4, Pallas kernels, shards(): call(functools.partial(error_body, o == 0, local_heads, o), (1,), [whole(...  11.7 us
    pallas_call x1, Pallas kernels, shards(): call(functools.partial(local_body, groups, local_heads), (groups,), [whol...  7.55 us
    pallas_call x4, Pallas kernels, shards(): call(functools.partial(spread_body, planes), (1,), [whole(share_shape)] *...  7.22 us
    pallas_call x1, Pallas kernels, shards(): call(functools.partial(project_body, direct), (groups,), [pl.BlockSpec((l...  5.85 us
  transfers between devices with their start and end apart: 52, of which 21 were waited for; matrix products, arithmetic and copies ran while one was open for 1% of the time, Pallas kernels for 20%

profile of v1, /device:TPU:0, one launch (start us, length us, event | category | flops | bytes accessed | tf_op | source)
XLA Modules:
  0.0 186.3 jit_solution(11420148093857669944)
XLA Ops:
  1.3 5.9 %shard_map.118 = (f32[256,384]{1,0:T(8,128)}, bf16[256,1024]{1,0:T(8,128)(2,1)}, bf16[256,1024]{1,0:T(8,128)(2,1)}) custom-call(s32[3]{0:T(128)} %pad_add_fusion.sp, bf16[256,4096]{1,0:T(8,128)(2,1)} %refs_4_.3, bf16[8192,256]{1,0:T(8,128)(2,1)} %wb_ref.1, bf16[64,8192]{1,0:T(8,128)(2,1)} %bitcast.18), custom_call_target="tpu_custom_call" | custom-call | flops 3300000000 | tf_op jit(solution)/shard_map/pallas_call | solution.py:608
  7.6 2.5 %collective-permute-start.4 = (bf16[256,1024]{1,0:T(8,128)(2,1)}, bf16[256,1024]{1,0:T(8,128)(2,1)S(1)}, u32[]{:S(2)}, u32[]{:S(2)}) collective-permute-start(bf16[256,1024]{1,0:T(8,128)(2,1)} %get-tuple-element.98), channel_id=1, source_target_pairs={{0,2},{2,0},{4,6},{6,4},{8,10},{10,8},{12,14},{14,12},{16,18},{18,... | collective-permute-start | bytes 1572872 | tf_op jit(solution)/shard_map/ppermute | solution.py:587
  12.9 4.8 %shard_map.119 = (bf16[256,256]{1,0:T(8,128)(2,1)S(1)}, f32[4,48,256]{2,1,0:T(8,128)S(1)}, f32[4,256,128]{2,1,0:T(8,128)S(1)}, bf16[144,1024]{1,0:T(8,128)(2,1)S...) custom-call(s32[3]{0:T(128)S(1)} %copy-done, ...), custom_call_target="tpu_custom_call" | custom-call | flops 5500000256 | tf_op jit(solution)/shard_map/pallas_call | solution.py:630
  21.3 7.6 %shard_map.120 = (f32[256,4096]{1,0:T(8,128)S(1)}, bf16[176,1024]{1,0:T(8,128)(2,1)S(1)}, bf16[176,1024]{1,0:T(8,128)(2,1)S(1)}, bf16[176,1024]{1,0:T(8,128)(2,1)S(1)}, bf16[176,1024]{1,0:T(8,128)(2,1)S(1)}) custom-call(s32[3]{0:T(128)S(1)} %copy-done, bf16[256,256]{1,0:T(8,128)(2,1)S(1)} %get-tuple-element.90.bc_ref, ...), custom_call_target="tpu_custom_call" | custom-call | flops 7699999744 | tf_op jit(solution)/shard_map/pallas_call | solution.py:646
  32.4 4.6 %collective-permute-done.2.refs_2_ = bf16[144,1024]{1,0:T(8,128)(2,1)S(1)} collective-permute-done((bf16[144,1024]{1,0:T(8,128)(2,1)S(1)}, bf16[144,1024]{1,0:T(8,128)(2,1)S(1)}, u32[]{:S(2)}, u32[]{:S(2)}) %collective-permute-start.2) | collective-permute-done | bytes 294944 | tf_op jit(solution)/shard_map/ppermute | solution.py:587
  40.4 2.6 %collective-permute-start.10 = (bf16[48,1024]{1,0:T(8,128)(2,1)S(1)}, bf16[48,1024]{1,0:T(8,128)(2,1)S(1)}, u32[]{:S(2)}, u32[]{:S(2)}) collective-permute-start(bf16[48,1024]{1,0:T(8,128)(2,1)S(1)} %get-tuple-element.108), channel_id=1, source_target_pairs={{0,16},{2,18},{4,20},{6,22},{8,24},{10,26},{12,28},{14,30},{16,0},... | collective-permute-start | bytes 294920 | tf_op jit(solution)/shard_map/ppermute | solution.py:591
  44.4 3.1 %collective-permute-start.11 = (bf16[48,1024]{1,0:T(8,128)(2,1)S(1)}, bf16[48,1024]{1,0:T(8,128)(2,1)S(1)}, u32[]{:S(2)}, u32[]{:S(2)}) collective-permute-start(bf16[48,1024]{1,0:T(8,128)(2,1)S(1)} %get-tuple-element.109), channel_id=1, source_target_pairs={{0,24},{2,26},{4,28},{6,30},{8,16},{10,18},{12,20},{14,22},{16,8},... | collective-permute-start | bytes 294920 | tf_op jit(solution)/shard_map/ppermute | solution.py:591
  48.9 2.1 %collective-permute-done.11.refs_3_ = bf16[48,1024]{1,0:T(8,128)(2,1)S(1)} collective-permute-done((bf16[48,1024]{1,0:T(8,128)(2,1)S(1)}, bf16[48,1024]{1,0:T(8,128)(2,1)S(1)}, u32[]{:S(2)}, u32[]{:S(2)}) %collective-permute-start.11) | collective-permute-done | bytes 98336 | tf_op jit(solution)/shard_map/ppermute | solution.py:591
  52.4 2.2 %shard_map.123 = (bf16[4,128,1024]{2,1,0:T(8,128)(2,1)S(1)}, bf16[256,1024]{1,0:T(8,128)(2,1)S(1)}) custom-call(s32[3]{0:T(128)S(1)} %copy-done, bf16[176,1024]{1,0:T(8,128)(2,1)S(1)} %get-tuple-element.102.refs_0_.refs_4_, bf16[176,1024]{1,0:T(8,128)(2,1)S(1)} %collective-permute-done.6.refs_1_.refs_5_, ...), custom_call_target="tpu_custom_call" | custom-call | flops 2200000000 | tf_op jit(solution)/shard_map/pallas_call | solution.py:705
  57.8 2.6 %collective-permute-start.13 = (bf16[32,1024]{1,0:T(8,128)(2,1)S(1)}, bf16[32,1024]{1,0:T(8,128)(2,1)S(1)}, u32[]{:S(2)}, u32[]{:S(2)}) collective-permute-start(bf16[32,1024]{1,0:T(8,128)(2,1)S(1)} %get-tuple-element.114), channel_id=1, source_target_pairs={{0,16},{2,18},{4,20},{6,22},{8,24},{10,26},{12,28},{14,30},{16,0},... | collective-permute-start | bytes 196616 | tf_op jit(solution)/shard_map/ppermute | solution.py:591
  60.6 4.3 %collective-permute-done.13.refs_2_ = bf16[32,1024]{1,0:T(8,128)(2,1)S(1)} collective-permute-done((bf16[32,1024]{1,0:T(8,128)(2,1)S(1)}, bf16[32,1024]{1,0:T(8,128)(2,1)S(1)}, u32[]{:S(2)}, u32[]{:S(2)}) %collective-permute-start.13) | collective-permute-done | bytes 65568 | tf_op jit(solution)/shard_map/ppermute | solution.py:591
  66.4 3.0 %collective-permute-done.15.refs_8_.refs_7_ = bf16[256,1024]{1,0:T(8,128)(2,1)S(1)} collective-permute-done((bf16[256,1024]{1,0:T(8,128)(2,1)S(1)}, bf16[256,1024]{1,0:T(8,128)(2,1)S(1)}, u32[]{:S(2)}, u32[]{:S(2)}) %collective-permute-start.15) | collective-permute-done | bytes 524320 | tf_op jit(solution)/shard_map/ppermute | solution.py:587
  69.5 2.5 %shard_map.124 = (bf16[128,1024]{1,0:T(8,128)(2,1)S(1)}, bf16[128,1024]{1,0:T(8,128)(2,1)S(1)}, bf16[128,1024]{1,0:T(8,128)(2,1)S(1)}, bf16[128,1024]{1,0:T(8,12...) custom-call(s32[3]{0:T(128)S(1)} %copy-done, ...), custom_call_target="tpu_custom_call" | custom-call | flops 2200000000 | tf_op jit(solution)/shard_map/pallas_call | solution.py:715
  73.5 2.6 %collective-permute-start.20 = (bf16[32,1024]{1,0:T(8,128)(2,1)S(1)}, bf16[32,1024]{1,0:T(8,128)(2,1)S(1)}, u32[]{:S(2)}, u32[]{:S(2)}) collective-permute-start(bf16[32,1024]{1,0:T(8,128)(2,1)S(1)} %get-tuple-element.128), channel_id=1, source_target_pairs={{0,16},{2,18},{4,20},{6,22},{8,24},{10,26},{12,28},{14,30},{16,0},... | collective-permute-start | bytes 196616 | tf_op jit(solution)/shard_map/ppermute | solution.py:591
  78.7 2.9 %shard_map.125 = (f32[16,256]{1,0:T(8,128)S(1)}, f32[16,128]{1,0:T(8,128)S(1)}, f32[256,384]{1,0:T(8,128)S(1)}, f32[8,128]{1,0:T(8,128)}) custom-call(s32[3]{0:T(128)S(1)} %copy-done, bf16[256,256]{1,0:T(8,128)(2,1)S(1)} %get-tuple-element.90.bc_ref, f32[4,48,256]{2,1,0:T(8,128)S(1)} %get-tuple-element.91.rows_ref, ...), custom_call_target="tpu_custom_call" | custom-call | flops 4400000000 | tf_op jit(solution)/shard_map/pallas_call | solution.py:748
  84.2 3.5 %collective-permute-start.23 = (bf16[32,1024]{1,0:T(8,128)(2,1)S(1)}, bf16[32,1024]{1,0:T(8,128)(2,1)S(1)}, u32[]{:S(2)}, u32[]{:S(2)}) collective-permute-start(bf16[32,1024]{1,0:T(8,128)(2,1)S(1)} %get-tuple-element.132), channel_id=1, source_target_pairs={{0,16},{2,18},{4,20},{6,22},{8,24},{10,26},{12,28},{14,30},{16,0},... | collective-permute-start | bytes 196616 | tf_op jit(solution)/shard_map/ppermute | solution.py:591
  88.2 3.5 %collective-permute-start.24 = (bf16[32,1024]{1,0:T(8,128)(2,1)S(1)}, bf16[32,1024]{1,0:T(8,128)(2,1)S(1)}, u32[]{:S(2)}, u32[]{:S(2)}) collective-permute-start(bf16[32,1024]{1,0:T(8,128)(2,1)S(1)} %get-tuple-element.133), channel_id=1, source_target_pairs={{0,24},{2,26},{4,28},{6,30},{8,16},{10,18},{12,20},{14,22},{16,8},... | collective-permute-start | bytes 196616 | tf_op jit(solution)/shard_map/ppermute | solution.py:591
  91.8 2.9 %shard_map.126 = (f32[16,256]{1,0:T(8,128)S(1)}, f32[16,128]{1,0:T(8,128)S(1)}, f32[256,384]{1,0:T(8,128)S(1)}, f32[8,128]{1,0:T(8,128)S(1)}) custom-call(s32[3]{0:T(128)S(1)} %copy-done, bf16[256,256]{1,0:T(8,128)(2,1)S(1)} %get-tuple-element.90.bc_ref, f32[4,48,256]{2,1,0:T(8,128)S(1)} %get-tuple-element.91.rows_ref, ...), custom_call_target="tpu_custom_call" | custom-call | flops 4400000000 | tf_op jit(solution)/shard_map/pallas_call | solution.py:748
  95.7 2.0 %collective-permute-start.25 = (bf16[128,1024]{1,0:T(8,128)(2,1)S(1)}, bf16[128,1024]{1,0:T(8,128)(2,1)S(1)}, u32[]{:S(2)}, u32[]{:S(2)}) collective-permute-start(bf16[128,1024]{1,0:T(8,128)(2,1)S(1)} %get-tuple-element.135), channel_id=1, source_target_pairs={{0,6},{2,4},{4,2},{6,0},{8,14},{10,12},{12,10},{14,8},{16,22},{18,... | collective-permute-start | bytes 786440 | tf_op jit(solution)/shard_map/ppermute | solution.py:587
  99.2 3.0 %shard_map.127 = (f32[16,256]{1,0:T(8,128)S(1)}, f32[16,128]{1,0:T(8,128)S(1)}, f32[256,384]{1,0:T(8,128)S(1)}, f32[8,128]{1,0:T(8,128)}) custom-call(s32[3]{0:T(128)S(1)} %copy-done, bf16[256,256]{1,0:T(8,128)(2,1)S(1)} %get-tuple-element.90.bc_ref, f32[4,48,256]{2,1,0:T(8,128)S(1)} %get-tuple-element.91.rows_ref, ...), custom_call_target="tpu_custom_call" | custom-call | flops 4400000000 | tf_op jit(solution)/shard_map/pallas_call | solution.py:748
  102.4 3.0 %shard_map.128 = (f32[16,256]{1,0:T(8,128)S(1)}, f32[16,128]{1,0:T(8,128)S(1)}, f32[256,384]{1,0:T(8,128)S(1)}, f32[8,128]{1,0:T(8,128)}) custom-call(s32[3]{0:T(128)S(1)} %copy-done, bf16[256,256]{1,0:T(8,128)(2,1)S(1)} %get-tuple-element.90.bc_ref, f32[4,48,256]{2,1,0:T(8,128)S(1)} %get-tuple-element.91.rows_ref, ...), custom_call_target="tpu_custom_call" | custom-call | flops 4400000000 | tf_op jit(solution)/shard_map/pallas_call | solution.py:748
  118.7 4.8 %collective-permute-done.31.refs_3_ = bf16[352,256]{1,0:T(8,128)(2,1)S(1)} collective-permute-done((bf16[352,256]{1,0:T(8,128)(2,1)S(1)}, bf16[352,256]{1,0:T(8,128)(2,1)S(1)}, u32[]{:S(2)}, u32[]{:S(2)}) %collective-permute-start.31) | collective-permute-done | bytes 180256 | tf_op jit(solution)/shard_map/ppermute | solution.py:587
  123.6 3.0 %collective-permute-done.30.refs_2_ = bf16[352,256]{1,0:T(8,128)(2,1)S(1)} collective-permute-done((bf16[352,256]{1,0:T(8,128)(2,1)S(1)}, bf16[352,256]{1,0:T(8,128)(2,1)S(1)}, u32[]{:S(2)}, u32[]{:S(2)}) %collective-permute-start.30) | collective-permute-done | bytes 180256 | tf_op jit(solution)/shard_map/ppermute | solution.py:587
  128.1 2.8 %collective-permute-start.35 = (bf16[80,1024]{1,0:T(8,128)(2,1)S(1)}, bf16[80,1024]{1,0:T(8,128)(2,1)S(1)}, u32[]{:S(2)}, u32[]{:S(2)}) collective-permute-start(bf16[80,1024]{1,0:T(8,128)(2,1)S(1)} %get-tuple-element.162), channel_id=1, source_target_pairs={{0,16},{2,18},{4,20},{6,22},{8,24},{10,26},{12,28},{14,30},{16,0},... | collective-permute-start | bytes 491528 | tf_op jit(solution)/shard_map/ppermute | solution.py:591
  132.5 4.6 %collective-permute-done.34 = bf16[80,1024]{1,0:T(8,128)(2,1)S(1)} collective-permute-done((bf16[80,1024]{1,0:T(8,128)(2,1)S(1)}, bf16[80,1024]{1,0:T(8,128)(2,1)S(1)}, u32[]{:S(2)}, u32[]{:S(2)}) %collective-permute-start.34) | collective-permute-done | bytes 163872 | tf_op jit(solution)/shard_map/ppermute | solution.py:591
  137.1 6.1 %collective-permute-done.35 = bf16[80,1024]{1,0:T(8,128)(2,1)S(1)} collective-permute-done((bf16[80,1024]{1,0:T(8,128)(2,1)S(1)}, bf16[80,1024]{1,0:T(8,128)(2,1)S(1)}, u32[]{:S(2)}, u32[]{:S(2)}) %collective-permute-start.35) | collective-permute-done | bytes 163872 | tf_op jit(solution)/shard_map/ppermute | solution.py:591
  143.3 4.0 %collective-permute-start.42 = (bf16[80,1024]{1,0:T(8,128)(2,1)S(1)}, bf16[80,1024]{1,0:T(8,128)(2,1)S(1)}, u32[]{:S(2)}, u32[]{:S(2)}) collective-permute-start(bf16[80,1024]{1,0:T(8,128)(2,1)S(1)} %add_convert_fusion.refs_0_), channel_id=1, source_target_pairs={{0,16},{2,18},{4,20},{6,22},{8,24},{10,26},{12,28},{14,30},{16,0},... | collective-permute-start | bytes 491528 | tf_op jit(solution)/shard_map/ppermute | solution.py:591
  149.2 5.2 %collective-permute-done.42.refs_2_ = bf16[80,1024]{1,0:T(8,128)(2,1)S(1)} collective-permute-done((bf16[80,1024]{1,0:T(8,128)(2,1)S(1)}, bf16[80,1024]{1,0:T(8,128)(2,1)S(1)}, u32[]{:S(2)}, u32[]{:S(2)}) %collective-permute-start.42) | collective-permute-done | bytes 163872 | tf_op jit(solution)/shard_map/ppermute | solution.py:591
  154.6 1.9 %collective-permute-start.32 = (f32[8,128]{1,0:T(8,128)S(1)}, f32[8,128]{1,0:T(8,128)S(1)}, u32[]{:S(2)}, u32[]{:S(2)}) collective-permute-start(f32[8,128]{1,0:T(8,128)S(1)} %get-tuple-element.159), channel_id=1, source_target_pairs={{0,8},{2,10},{4,12},{6,14},{8,0},{10,2},{12,4},{14,6},{16,24},{18,... | collective-permute-start | bytes 12296 | tf_op jit(solution)/shard_map/ppermute | solution.py:591
  156.4 3.3 %collective-permute-done.32 = f32[8,128]{1,0:T(8,128)S(1)} collective-permute-done((f32[8,128]{1,0:T(8,128)S(1)}, f32[8,128]{1,0:T(8,128)S(1)}, u32[]{:S(2)}, u32[]{:S(2)}) %collective-permute-start.32) | collective-permute-done | bytes 4128 | tf_op jit(solution)/shard_map/ppermute | solution.py:591
  160.7 3.6 %collective-permute-done.33 = f32[8,128]{1,0:T(8,128)S(1)} collective-permute-done((f32[8,128]{1,0:T(8,128)S(1)}, f32[8,128]{1,0:T(8,128)S(1)}, u32[]{:S(2)}, u32[]{:S(2)}) %collective-permute-start.33) | collective-permute-done | bytes 4128 | tf_op jit(solution)/shard_map/ppermute | solution.py:591
  180.3 1.8 shard_map.140
  (117 shorter events, 71.2 us)
Async XLA Ops:
  7.6 21.3 %collective-permute-start.4 = (bf16[256,1024]{1,0:T(8,128)(2,1)}, bf16[256,1024]{1,0:T(8,128)(2,1)S(1)}, u32[]{:S(2)}, u32[]{:S(2)}) collective-permute-start(bf16[256,1024]{1,0:T(8,128)(2,1)} %get-tuple-element.98), channel_id=1, source_target_pairs={{0,2},{2,0},{4,6},{6,4},{8,10},{10,8},{12,14},{14,12},{16,18},{18,... | collective-permute-start | bytes 1572872 | tf_op jit(solution)/shard_map/ppermute | solution.py:587
  10.1 19.4 %collective-permute-start.5 = (bf16[256,1024]{1,0:T(8,128)(2,1)}, bf16[256,1024]{1,0:T(8,128)(2,1)S(1)}, u32[]{:S(2)}, u32[]{:S(2)}) collective-permute-start(bf16[256,1024]{1,0:T(8,128)(2,1)} %get-tuple-element.99), channel_id=1, source_target_pairs={{0,4},{2,6},{4,0},{6,2},{8,12},{10,14},{12,8},{14,10},{16,20},{18,... | collective-permute-start | bytes 1572872 | tf_op jit(solution)/shard_map/ppermute | solution.py:587
  17.7 13.0 %collective-permute-start.1 = (bf16[144,1024]{1,0:T(8,128)(2,1)S(1)}, bf16[144,1024]{1,0:T(8,128)(2,1)S(1)}, u32[]{:S(2)}, u32[]{:S(2)}) collective-permute-start(bf16[144,1024]{1,0:T(8,128)(2,1)S(1)} %get-tuple-element.95), channel_id=1, source_target_pairs={{0,2},{2,0},{4,6},{6,4},{8,10},{10,8},{12,14},{14,12},{16,18},{18,... | collective-permute-start | bytes 884744 | tf_op jit(solution)/shard_map/ppermute | solution.py:587
  18.3 18.7 %collective-permute-start.2 = (bf16[144,1024]{1,0:T(8,128)(2,1)S(1)}, bf16[144,1024]{1,0:T(8,128)(2,1)S(1)}, u32[]{:S(2)}, u32[]{:S(2)}) collective-permute-start(bf16[144,1024]{1,0:T(8,128)(2,1)S(1)} %get-tuple-element.96), channel_id=1, source_target_pairs={{0,4},{2,6},{4,0},{6,2},{8,12},{10,14},{12,8},{14,10},{16,20},{18,... | collective-permute-start | bytes 884744 | tf_op jit(solution)/shard_map/ppermute | solution.py:587
  19.6 17.6 %collective-permute-start.3 = (bf16[144,1024]{1,0:T(8,128)(2,1)S(1)}, bf16[144,1024]{1,0:T(8,128)(2,1)S(1)}, u32[]{:S(2)}, u32[]{:S(2)}) collective-permute-start(bf16[144,1024]{1,0:T(8,128)(2,1)S(1)} %get-tuple-element.97), channel_id=1, source_target_pairs={{0,6},{2,4},{4,2},{6,0},{8,14},{10,12},{12,10},{14,8},{16,22},{18,... | collective-permute-start | bytes 884744 | tf_op jit(solution)/shard_map/ppermute | solution.py:587
  28.8 22.8 %collective-permute-start.6 = (bf16[176,1024]{1,0:T(8,128)(2,1)S(1)}, bf16[176,1024]{1,0:T(8,128)(2,1)S(1)}, u32[]{:S(2)}, u32[]{:S(2)}) collective-permute-start(bf16[176,1024]{1,0:T(8,128)(2,1)S(1)} %get-tuple-element.103), channel_id=1, source_target_pairs={{0,2},{2,0},{4,6},{6,4},{8,10},{10,8},{12,14},{14,12},{16,18},{18,... | collective-permute-start | bytes 1081352 | tf_op jit(solution)/shard_map/ppermute | solution.py:587
  29.4 23.0 %collective-permute-start.7 = (bf16[176,1024]{1,0:T(8,128)(2,1)S(1)}, bf16[176,1024]{1,0:T(8,128)(2,1)S(1)}, u32[]{:S(2)}, u32[]{:S(2)}) collective-permute-start(bf16[176,1024]{1,0:T(8,128)(2,1)S(1)} %get-tuple-element.104), channel_id=1, source_target_pairs={{0,4},{2,6},{4,0},{6,2},{8,12},{10,14},{12,8},{14,10},{16,20},{18,... | collective-permute-start | bytes 1081352 | tf_op jit(solution)/shard_map/ppermute | solution.py:587
  30.7 21.7 %collective-permute-start.8 = (bf16[176,1024]{1,0:T(8,128)(2,1)S(1)}, bf16[176,1024]{1,0:T(8,128)(2,1)S(1)}, u32[]{:S(2)}, u32[]{:S(2)}) collective-permute-start(bf16[176,1024]{1,0:T(8,128)(2,1)S(1)} %get-tuple-element.105), channel_id=1, source_target_pairs={{0,6},{2,4},{4,2},{6,0},{8,14},{10,12},{12,10},{14,8},{16,22},{18,... | collective-permute-start | bytes 1081352 | tf_op jit(solution)/shard_map/ppermute | solution.py:587
  54.6 14.8 %collective-permute-start.15 = (bf16[256,1024]{1,0:T(8,128)(2,1)S(1)}, bf16[256,1024]{1,0:T(8,128)(2,1)S(1)}, u32[]{:S(2)}, u32[]{:S(2)}) collective-permute-start(bf16[256,1024]{1,0:T(8,128)(2,1)S(1)} %get-tuple-element.116), channel_id=1, source_target_pairs={{0,6},{2,4},{4,2},{6,0},{8,14},{10,12},{12,10},{14,8},{16,22},{18,... | collective-permute-start | bytes 1572872 | tf_op jit(solution)/shard_map/ppermute | solution.py:587
  72.0 9.6 %collective-permute-start.19 = (bf16[32,1024]{1,0:T(8,128)(2,1)S(1)}, bf16[32,1024]{1,0:T(8,128)(2,1)S(1)}, u32[]{:S(2)}, u32[]{:S(2)}) collective-permute-start(bf16[32,1024]{1,0:T(8,128)(2,1)S(1)} %get-tuple-element.127), channel_id=1, source_target_pairs={{0,8},{2,10},{4,12},{6,14},{8,0},{10,2},{12,4},{14,6},{16,24},{18,... | collective-permute-start | bytes 196616 | tf_op jit(solution)/shard_map/ppermute | solution.py:591
  73.5 9.3 %collective-permute-start.20 = (bf16[32,1024]{1,0:T(8,128)(2,1)S(1)}, bf16[32,1024]{1,0:T(8,128)(2,1)S(1)}, u32[]{:S(2)}, u32[]{:S(2)}) collective-permute-start(bf16[32,1024]{1,0:T(8,128)(2,1)S(1)} %get-tuple-element.128), channel_id=1, source_target_pairs={{0,16},{2,18},{4,20},{6,22},{8,24},{10,26},{12,28},{14,30},{16,0},... | collective-permute-start | bytes 196616 | tf_op jit(solution)/shard_map/ppermute | solution.py:591
  76.3 25.9 %collective-permute-start.16 = (bf16[128,1024]{1,0:T(8,128)(2,1)S(1)}, bf16[128,1024]{1,0:T(8,128)(2,1)S(1)}, u32[]{:S(2)}, u32[]{:S(2)}) collective-permute-start(bf16[128,1024]{1,0:T(8,128)(2,1)S(1)} %get-tuple-element.117), channel_id=1, source_target_pairs={{0,6},{2,4},{4,2},{6,0},{8,14},{10,12},{12,10},{14,8},{16,22},{18,... | collective-permute-start | bytes 786440 | tf_op jit(solution)/shard_map/ppermute | solution.py:587
  77.8 10.4 %collective-permute-start.18 = (bf16[128,1024]{1,0:T(8,128)(2,1)S(1)}, bf16[128,1024]{1,0:T(8,128)(2,1)S(1)}, u32[]{:S(2)}, u32[]{:S(2)}) collective-permute-start(bf16[128,1024]{1,0:T(8,128)(2,1)S(1)} %get-tuple-element.119), channel_id=1, source_target_pairs={{0,2},{2,0},{4,6},{6,4},{8,10},{10,8},{12,14},{14,12},{16,18},{18,... | collective-permute-start | bytes 786440 | tf_op jit(solution)/shard_map/ppermute | solution.py:587
  81.6 17.6 %collective-permute-start.17 = (bf16[128,1024]{1,0:T(8,128)(2,1)S(1)}, bf16[128,1024]{1,0:T(8,128)(2,1)S(1)}, u32[]{:S(2)}, u32[]{:S(2)}) collective-permute-start(bf16[128,1024]{1,0:T(8,128)(2,1)S(1)} %get-tuple-element.118), channel_id=1, source_target_pairs={{0,4},{2,6},{4,0},{6,2},{8,12},{10,14},{12,8},{14,10},{16,20},{18,... | collective-permute-start | bytes 786440 | tf_op jit(solution)/shard_map/ppermute | solution.py:587
  83.4 11.2 %collective-permute-start.22 = (bf16[32,1024]{1,0:T(8,128)(2,1)S(1)}, bf16[32,1024]{1,0:T(8,128)(2,1)S(1)}, u32[]{:S(2)}, u32[]{:S(2)}) collective-permute-start(bf16[32,1024]{1,0:T(8,128)(2,1)S(1)} %get-tuple-element.131), channel_id=1, source_target_pairs={{0,8},{2,10},{4,12},{6,14},{8,0},{10,2},{12,4},{14,6},{16,24},{18,... | collective-permute-start | bytes 196616 | tf_op jit(solution)/shard_map/ppermute | solution.py:591
  84.2 10.5 %collective-permute-start.23 = (bf16[32,1024]{1,0:T(8,128)(2,1)S(1)}, bf16[32,1024]{1,0:T(8,128)(2,1)S(1)}, u32[]{:S(2)}, u32[]{:S(2)}) collective-permute-start(bf16[32,1024]{1,0:T(8,128)(2,1)S(1)} %get-tuple-element.132), channel_id=1, source_target_pairs={{0,16},{2,18},{4,20},{6,22},{8,24},{10,26},{12,28},{14,30},{16,0},... | collective-permute-start | bytes 196616 | tf_op jit(solution)/shard_map/ppermute | solution.py:591
  95.7 14.9 %collective-permute-start.25 = (bf16[128,1024]{1,0:T(8,128)(2,1)S(1)}, bf16[128,1024]{1,0:T(8,128)(2,1)S(1)}, u32[]{:S(2)}, u32[]{:S(2)}) collective-permute-start(bf16[128,1024]{1,0:T(8,128)(2,1)S(1)} %get-tuple-element.135), channel_id=1, source_target_pairs={{0,6},{2,4},{4,2},{6,0},{8,14},{10,12},{12,10},{14,8},{16,22},{18,... | collective-permute-start | bytes 786440 | tf_op jit(solution)/shard_map/ppermute | solution.py:587
  97.6 11.7 %collective-permute-start.26 = (bf16[128,1024]{1,0:T(8,128)(2,1)S(1)}, bf16[128,1024]{1,0:T(8,128)(2,1)S(1)}, u32[]{:S(2)}, u32[]{:S(2)}) collective-permute-start(bf16[128,1024]{1,0:T(8,128)(2,1)S(1)} %get-tuple-element.136), channel_id=1, source_target_pairs={{0,4},{2,6},{4,0},{6,2},{8,12},{10,14},{12,8},{14,10},{16,20},{18,... | collective-permute-start | bytes 786440 | tf_op jit(solution)/shard_map/ppermute | solution.py:587
  98.9 9.1 %collective-permute-start.27 = (bf16[128,1024]{1,0:T(8,128)(2,1)S(1)}, bf16[128,1024]{1,0:T(8,128)(2,1)S(1)}, u32[]{:S(2)}, u32[]{:S(2)}) collective-permute-start(bf16[128,1024]{1,0:T(8,128)(2,1)S(1)} %get-tuple-element.137), channel_id=1, source_target_pairs={{0,2},{2,0},{4,6},{6,4},{8,10},{10,8},{12,14},{14,12},{16,18},{18,... | collective-permute-start | bytes 786440 | tf_op jit(solution)/shard_map/ppermute | solution.py:587
  116.5 10.1 %collective-permute-start.30 = (bf16[352,256]{1,0:T(8,128)(2,1)S(1)}, bf16[352,256]{1,0:T(8,128)(2,1)S(1)}, u32[]{:S(2)}, u32[]{:S(2)}) collective-permute-start(bf16[352,256]{1,0:T(8,128)(2,1)S(1)} %shard_map.136.refs_0_), channel_id=1, source_target_pairs={{0,4},{2,6},{4,0},{6,2},{8,12},{10,14},{12,8},{14,10},{16,20},{18,... | collective-permute-start | bytes 540680 | tf_op jit(solution)/shard_map/ppermute | solution.py:587
  117.0 9.6 %collective-permute-start.29 = (bf16[352,256]{1,0:T(8,128)(2,1)S(1)}, bf16[352,256]{1,0:T(8,128)(2,1)S(1)}, u32[]{:S(2)}, u32[]{:S(2)}) collective-permute-start(bf16[352,256]{1,0:T(8,128)(2,1)S(1)} %shard_map.136.refs_0_), channel_id=1, source_target_pairs={{0,2},{2,0},{4,6},{6,4},{8,10},{10,8},{12,14},{14,12},{16,18},{18,... | collective-permute-start | bytes 540680 | tf_op jit(solution)/shard_map/ppermute | solution.py:587
  128.1 9.0 %collective-permute-start.34 = (bf16[80,1024]{1,0:T(8,128)(2,1)S(1)}, bf16[80,1024]{1,0:T(8,128)(2,1)S(1)}, u32[]{:S(2)}, u32[]{:S(2)}) collective-permute-start(bf16[80,1024]{1,0:T(8,128)(2,1)S(1)} %get-tuple-element.161), channel_id=1, source_target_pairs={{0,8},{2,10},{4,12},{6,14},{8,0},{10,2},{12,4},{14,6},{16,24},{18,... | collective-permute-start | bytes 491528 | tf_op jit(solution)/shard_map/ppermute | solution.py:591
  128.1 15.1 %collective-permute-start.35 = (bf16[80,1024]{1,0:T(8,128)(2,1)S(1)}, bf16[80,1024]{1,0:T(8,128)(2,1)S(1)}, u32[]{:S(2)}, u32[]{:S(2)}) collective-permute-start(bf16[80,1024]{1,0:T(8,128)(2,1)S(1)} %get-tuple-element.162), channel_id=1, source_target_pairs={{0,16},{2,18},{4,20},{6,22},{8,24},{10,26},{12,28},{14,30},{16,0},... | collective-permute-start | bytes 491528 | tf_op jit(solution)/shard_map/ppermute | solution.py:591
  131.0 12.3 %collective-permute-start.36 = (bf16[80,1024]{1,0:T(8,128)(2,1)S(1)}, bf16[80,1024]{1,0:T(8,128)(2,1)S(1)}, u32[]{:S(2)}, u32[]{:S(2)}) collective-permute-start(bf16[80,1024]{1,0:T(8,128)(2,1)S(1)} %get-tuple-element.163), channel_id=1, source_target_pairs={{0,24},{2,26},{4,28},{6,30},{8,16},{10,18},{12,20},{14,22},{16,8},... | collective-permute-start | bytes 491528 | tf_op jit(solution)/shard_map/ppermute | solution.py:591
  143.3 11.1 %collective-permute-start.42 = (bf16[80,1024]{1,0:T(8,128)(2,1)S(1)}, bf16[80,1024]{1,0:T(8,128)(2,1)S(1)}, u32[]{:S(2)}, u32[]{:S(2)}) collective-permute-start(bf16[80,1024]{1,0:T(8,128)(2,1)S(1)} %add_convert_fusion.refs_0_), channel_id=1, source_target_pairs={{0,16},{2,18},{4,20},{6,22},{8,24},{10,26},{12,28},{14,30},{16,0},... | collective-permute-start | bytes 491528 | tf_op jit(solution)/shard_map/ppermute | solution.py:591
  147.3 18.1 %collective-permute-start.50 = (bf16[80,1024]{1,0:T(8,128)(2,1)S(1)}, bf16[80,1024]{1,0:T(8,128)(2,1)S(1)}, u32[]{:S(2)}, u32[]{:S(2)}) collective-permute-start(bf16[80,1024]{1,0:T(8,128)(2,1)S(1)} %add_convert_fusion.refs_0_), channel_id=1, source_target_pairs={{0,2},{2,0},{4,6},{6,4},{8,10},{10,8},{12,14},{14,12},{16,18},{18,... | collective-permute-start | bytes 491528 | tf_op jit(solution)/shard_map/ppermute | solution.py:587
  148.5 17.7 %collective-permute-start.39 = (bf16[80,1024]{1,0:T(8,128)(2,1)S(1)}, bf16[80,1024]{1,0:T(8,128)(2,1)S(1)}, u32[]{:S(2)}, u32[]{:S(2)}) collective-permute-start(bf16[80,1024]{1,0:T(8,128)(2,1)S(1)} %add_convert_fusion.refs_0_), channel_id=1, source_target_pairs={{0,8},{2,10},{4,12},{6,14},{8,0},{10,2},{12,4},{14,6},{16,24},{18,... | collective-permute-start | bytes 491528 | tf_op jit(solution)/shard_map/ppermute | solution.py:591
  148.5 19.0 %collective-permute-start.37 = (bf16[80,1024]{1,0:T(8,128)(2,1)S(1)}, bf16[80,1024]{1,0:T(8,128)(2,1)S(1)}, u32[]{:S(2)}, u32[]{:S(2)}) collective-permute-start(bf16[80,1024]{1,0:T(8,128)(2,1)S(1)} %add_convert_fusion.refs_0_), channel_id=1, source_target_pairs={{0,4},{2,6},{4,0},{6,2},{8,12},{10,14},{12,8},{14,10},{16,20},{18,... | collective-permute-start | bytes 491528 | tf_op jit(solution)/shard_map/ppermute | solution.py:587
  154.4 13.9 %collective-permute-start.45 = (bf16[80,1024]{1,0:T(8,128)(2,1)S(1)}, bf16[80,1024]{1,0:T(8,128)(2,1)S(1)}, u32[]{:S(2)}, u32[]{:S(2)}) collective-permute-start(bf16[80,1024]{1,0:T(8,128)(2,1)S(1)} %collective-permute-done.42.refs_2_), channel_id=1, source_target_pairs={{0,8},{2,10},{4,12},{6,14},{8,0},{10,2},{12,4},{14,6},{16,24},{18,... | collective-permute-start | bytes 491528 | tf_op jit(solution)/shard_map/ppermute | solution.py:591
  166.2 9.1 %collective-permute-start.48 = (bf16[80,1024]{1,0:T(8,128)(2,1)S(1)}, bf16[80,1024]{1,0:T(8,128)(2,1)S(1)}, u32[]{:S(2)}, u32[]{:S(2)}) collective-permute-start(bf16[80,1024]{1,0:T(8,128)(2,1)S(1)} %collective-permute-done.39.refs_1_), channel_id=1, source_target_pairs={{0,4},{2,6},{4,0},{6,2},{8,12},{10,14},{12,8},{14,10},{16,20},{18,... | collective-permute-start | bytes 491528 | tf_op jit(solution)/shard_map/ppermute | solution.py:587
  168.4 9.7 %collective-permute-start.46 = (bf16[80,1024]{1,0:T(8,128)(2,1)S(1)}, bf16[80,1024]{1,0:T(8,128)(2,1)S(1)}, u32[]{:S(2)}, u32[]{:S(2)}) collective-permute-start(bf16[80,1024]{1,0:T(8,128)(2,1)S(1)} %collective-permute-done.45.refs_3_), channel_id=1, source_target_pairs={{0,2},{2,0},{4,6},{6,4},{8,10},{10,8},{12,14},{14,12},{16,18},{18,... | collective-permute-start | bytes 491528 | tf_op jit(solution)/shard_map/ppermute | solution.py:587
  171.3 9.0 %collective-permute-start.49 = (bf16[80,1024]{1,0:T(8,128)(2,1)S(1)}, bf16[80,1024]{1,0:T(8,128)(2,1)S(1)}, u32[]{:S(2)}, u32[]{:S(2)}) collective-permute-start(bf16[80,1024]{1,0:T(8,128)(2,1)S(1)} %collective-permute-done.45.refs_3_), channel_id=1, source_target_pairs={{0,4},{2,6},{4,0},{6,2},{8,12},{10,14},{12,8},{14,10},{16,20},{18,... | collective-permute-start | bytes 491528 | tf_op jit(solution)/shard_map/ppermute | solution.py:587
  (27 other events, 188.8 us)

commit v2 on v1

--- a/solution.py
+++ b/solution.py
@@ -85,10 +85,8 @@
     return parts[0]
 
 
-def project_body(direct, sp, u_ref, wb_ref, wd_ref, out_ref, *copies):
-    k = pl.program_id(0)
-
-    @pl.when(k == 0)
+def project_body(sp, u_ref, wb_ref, wd_ref, out_ref):
+    @pl.when(pl.program_id(0) == 0)
     def _():
         out_ref[...] = jnp.zeros_like(out_ref)
 
@@ -97,11 +95,6 @@
     head_count = wd_ref.shape[0]
     out_ref[:, :bc_width] += dot_10(u, wb_ref[...])
     out_ref[:, bc_width : bc_width + head_count] += dot_11(u, wd_ref[...])
-    for o, copy in zip(direct, copies):
-
-        @pl.when(k == o)
-        def _():
-            copy[...] = u
 
 
 def running_sum(rows, keep):
@@ -241,11 +234,8 @@
             out[base:, :length] = grown.astype(BF16)
 
 
-def moment_body(groups, far, length, states, sp, *refs):
-    messages, rows = refs[:groups], refs[groups : groups + far]
-    out_ref = refs[groups + far + 1]
-    for row, copy in zip(rows, refs[groups + far + 2 :]):
-        copy[...] = row[...]
+def moment_body(groups, length, states, sp, *refs):
+    messages, out_ref = refs[:groups], refs[-1]
     piece = length // HEADS
     base = states + piece
     for o in range(groups):
@@ -260,6 +250,11 @@
             [(wide * cols[:, h : h + 1]).astype(BF16) for h in range(HEADS)], axis=1
         )
         out_ref[o ^ sp[1]] = dot_00(c_output, scaled).astype(BF16)
+
+
+def plane_lanes(sp, m, ref, planes):
+    piece = ref.shape[1] // planes
+    return pl.ds(pl.multiple_of((sp[2] ^ m) * piece, LANE), piece)
 
 
 def gather_body(groups, states, planes, count, sp, *refs):
@@ -283,23 +278,23 @@
     if len(sent) == 1:
         sent[0][...] = total.astype(BF16)
         return
-    piece = states // planes
-    high, middle, _ = rounded_parts(span)
-    tail = jnp.concatenate([high, middle], axis=0).astype(BF16)
     for m in range(planes):
-        at = pl.multiple_of((sp[2] ^ m) * piece, TAIL)
-        sent[m][:piece, :] = total_ref[pl.ds(at, piece), :].astype(BF16)
-        sent[m][piece:, :] = tail
-
-
-def ahead_body(planes, sp, *refs):
-    messages, outs = refs[:planes], refs[-3 - planes : -3]
-    span_ref, hold_ref, state_ref = refs[-3:]
-    piece = state_ref.shape[1]
+        here = plane_lanes(sp, m, total_ref, planes)
+        high, middle, _ = rounded_parts(span_ref[:, here])
+        sent[m][:states, :] = total_ref[:, here].astype(BF16)
+        sent[m][states:, :] = jnp.concatenate([high, middle], axis=0).astype(BF16)
+
+
+def ahead_body(planes, near, sp, *refs):
+    for row, copy in zip(refs[planes : planes + near], refs[2 * planes + 1 + near :]):
+        copy[...] = row[...]
+    messages, outs = refs[:planes], refs[planes + near : 2 * planes + near]
+    span_ref, hold_ref, state_ref = refs[2 * planes + near], refs[-2], refs[-1]
+    states = state_ref.shape[1]
     for m in range(planes):
-        tail = messages[m][piece:, :].astype(F32)
+        tail = messages[m][states:, :].astype(F32)
         span_ref[sp[2] ^ m] = tail[:HEADS] + tail[HEADS:]
-        hold_ref[sp[2] ^ m] = messages[m][:piece, :]
+        hold_ref[sp[2] ^ m] = messages[m][:states, :]
     state = jnp.zeros(state_ref.shape[1:], F32)
     for k in range(planes):
         state_ref[k] = state.astype(BF16)
@@ -325,19 +320,19 @@
     if len(pieces) == 1:
         hold_ref[...] = pieces[0][...]
     else:
-        piece = pieces[0].shape[0]
         for m, part in enumerate(pieces):
-            at = pl.multiple_of((sp[2] ^ m) * piece, TAIL)
-            hold_ref[pl.ds(at, piece), :] = part[...]
+            hold_ref[:, plane_lanes(sp, m, hold_ref, len(pieces))] = part[...]
     return hold_ref[...].astype(F32)
 
 
-def forward_body(groups, pieces, sent_count, sp, inc_ref, decay_ref, moment_ref, *refs):
+def forward_body(groups, pieces, far, sp, inc_ref, decay_ref, moment_ref, *refs):
+    states_ref, hold_ref = refs[-2:]
     before, locals_ = refs[:pieces], refs[pieces : pieces + groups]
-    outs = refs[-4 - sent_count - groups : -4 - sent_count]
-    grad_ref, total_ref = refs[-4 - sent_count : -2 - sent_count]
-    sent = refs[-2 - sent_count : -2]
-    states_ref, hold_ref = refs[-2:]
+    refs = refs[pieces + groups : -2]
+    for row, copy in zip(refs[:far], refs[len(refs) - far :]):
+        copy[...] = row[...]
+    outs, refs = refs[far : far + groups], refs[far + groups : len(refs) - far]
+    grad_ref, total_ref, sent = refs[0], refs[1], refs[2:]
     states = hold_ref.shape[0]
     state = assembled(before, hold_ref, sp)
     for j in range(groups):
@@ -356,13 +351,12 @@
     for j in range(groups - 2, -1, -1):
         total = decay_ref[j][:1] * total + grad_ref[j]
     total_ref[...] = total
-    if sent_count == 1:
+    if pieces == 1:
         sent[0][...] = total.astype(BF16)
         return
-    piece = states // sent_count
-    for m in range(sent_count):
-        at = pl.multiple_of((sp[2] ^ m) * piece, TAIL)
-        sent[m][...] = total_ref[pl.ds(at, piece), :].astype(BF16)
+    for m in range(pieces):
+        here = plane_lanes(sp, m, total_ref, pieces)
+        sent[m][...] = total_ref[:, here].astype(BF16)
 
 
 def backward_body(groups, pieces, sp, grad_ref, decay_ref, *refs):
@@ -521,20 +515,17 @@
 def merge_body(members, width, sp, *refs):
     out_ref = refs[members]
     total = tree_sum([part[...] for part in refs[:members]])
-    out_ref[:width, :] = total[:width].astype(BF16)
-    parts = rounded_parts(total[width : width + KINDS])
-    parts = jnp.concatenate(list(parts) + [jnp.zeros_like(parts[0])], axis=0)
-    out_ref[width:, :] = parts.astype(BF16)
+    out_ref[...] = total[:width].astype(BF16)
+    refs[members + 1][...] = total[width : width + KINDS, :LANE]
 
 
 def weight_body(groups, planes, width, sp, *refs):
     grads, rows = refs[:groups], refs[groups : 2 * groups]
-    own_ref, small_ref = refs[2 * groups : 2 * groups + 2]
-    sent, hold_ref = refs[2 * groups + 2 : -1], refs[-1]
+    own_ref, sent, hold_ref = refs[2 * groups + 1], refs[2 * groups + 2 : -1], refs[-1]
     piece = own_ref.shape[0]
-    total = dot_10(grads[0][:width, :], rows[0][...])
+    total = dot_10(grads[0][...], rows[0][...])
     for o in range(1, groups):
-        total = total + dot_10(grads[o][:width, :], rows[o][...])
+        total = total + dot_10(grads[o][...], rows[o][...])
     hold_ref[:width, :] = total
     if hold_ref.shape[0] > width:
         hold_ref[width:, :] = jnp.zeros((hold_ref.shape[0] - width, hold_ref.shape[1]), F32)
@@ -545,11 +536,13 @@
             own_ref[...] = value
         else:
             sent[m - 1][...] = value.astype(BF16)
-    parts = []
-    for o in range(groups):
-        small = grads[o][width:, :].astype(F32)
-        parts.append((small[:KINDS] + small[KINDS : 2 * KINDS]) + small[2 * KINDS : 3 * KINDS])
-    small_ref[...] = tree_sum(parts)[:, :LANE]
+
+
+def total_body(planes, sp, own_ref, *refs):
+    total = own_ref[...]
+    for other in refs[: planes - 1]:
+        total = total + other[...].astype(F32)
+    refs[-1][...] = total.astype(BF16)
 
 
 def spread_body(planes, sp, *refs):
@@ -605,21 +598,29 @@
 
     direct = [o for o in range(1, groups) if o & (o - 1) == 0]
     far = [o for o in range(1, groups) if o & (o - 1)]
-    partial, *near_copies = call(
-        functools.partial(project_body, direct),
+    partial = call(
+        project_body,
         (groups,),
         [
             pl.BlockSpec((length, span), lambda o, sp: (0, o ^ sp[1])),
             pl.BlockSpec((span, bc_width), lambda o, sp: (sp[0] * groups + (o ^ sp[1]), 0)),
             pl.BlockSpec((head_count, span), lambda o, sp: (0, sp[0] * groups + (o ^ sp[1]))),
         ],
-        [whole((length, proj_width))] + [whole((length, span))] * len(direct),
-        [shape_of((length, proj_width), F32)] + [shape_of((length, span), BF16)] * len(direct),
+        whole((length, proj_width)),
+        shape_of((length, proj_width), F32),
         us=3,
         vmem=VMEM_WIDE,
     )(sp, teacher_rows, state_proj, step_proj.T)
     projs = members_of(partial)
-    moved_rows = {o: in_plane(copy, o) for o, copy in zip(direct, near_copies)}
+
+    def row_blocks(offsets):
+        return [
+            pl.BlockSpec((length, span), functools.partial(lambda o, _, sp: (0, o ^ sp[1]), o))
+            for o in offsets
+        ]
+
+    copy_shape = shape_of((length, span), BF16)
+    copy_spec = whole((length, span))
 
     message_shape = (states + TAIL, span)
     local_shape = (states + length // HEADS + TAIL, span)
@@ -657,14 +658,14 @@
 
     stack_shape = (groups,) + state_shape
     decay_shape = (groups, HEADS, span)
-    shared = planes > 1 and states % (planes * TAIL) == 0
-    piece_shape = (states // planes, span) if shared else state_shape
-    sent_shape = (piece_shape[0] + TAIL, span) if shared else state_shape
+    shared = planes > 1 and span % (planes * LANE) == 0
+    piece_shape = (states, span // planes) if shared else state_shape
+    sent_shape = (states + TAIL, span // planes) if shared else state_shape
     count = planes if shared else 1
     inc, decays, total, total_decay, *sent = call(
         functools.partial(gather_body, groups, states, planes, count),
         (1,),
-        [whole(message_shape)] * groups + [AFTER] * (1 + len(direct)),
+        [whole(message_shape)] * groups + [AFTER],
         [whole(stack_shape), whole(decay_shape), whole(state_shape), whole((HEADS, span))]
         + [whole(sent_shape)] * count,
         [
@@ -674,75 +675,91 @@
             shape_of((HEADS, span), F32),
         ]
         + [shape_of(sent_shape, BF16)] * count,
-    )(sp, *messages, err, *moved_rows.values())
+    )(sp, *messages, err)
+    moments = call(
+        functools.partial(moment_body, groups, length, states),
+        (1,),
+        [whole(local_shape)] * groups + [AFTER],
+        whole(stack_shape),
+        shape_of(stack_shape, BF16),
+        us=2,
+    )(sp, *local_grads, decays)
+
     def hop(before, total):
         return (total_decay[:1] * before.astype(F32) + total).astype(BF16)
 
     def exchanged_planes(parts):
         return [parts[0]] + [over_planes(parts[m], m) for m in range(1, planes)]
 
-    spans_shape = (planes, HEADS, span)
+    spans_shape = (planes, HEADS, piece_shape[1])
     if shared:
-        *parts, spans = call(
-            functools.partial(ahead_body, planes),
+        outs = call(
+            functools.partial(ahead_body, planes, len(direct)),
             (1,),
-            [whole(sent_shape)] * planes,
-            [whole(piece_shape)] * planes + [whole(spans_shape)],
-            [shape_of(piece_shape, BF16)] * planes + [shape_of(spans_shape, F32)],
+            [whole(sent_shape)] * planes + row_blocks(direct),
+            [whole(piece_shape)] * planes
+            + [whole(spans_shape)]
+            + [copy_spec] * len(direct),
+            [shape_of(piece_shape, BF16)] * planes
+            + [shape_of(spans_shape, F32)]
+            + [copy_shape] * len(direct),
             [pltpu.VMEM((planes,) + piece_shape, BF16)] * 2,
-        )(sp, *exchanged_planes(sent))
+        )(sp, *exchanged_planes(sent), *[teacher_rows] * len(direct))
+        parts, spans, copies = outs[:planes], outs[planes], outs[planes + 1 :]
         before = exchanged_planes(parts)
     else:
         before = jnp.zeros(state_shape, BF16)
         for step in range(planes - 1):
             before = next_plane(hop(before, total), 1)
-        before, spans = [before], decays
-
-    far_blocks = [
-        pl.BlockSpec((length, span), functools.partial(lambda o, _, sp: (0, o ^ sp[1]), o))
-        for o in far
-    ]
-    moments, *far_copies = call(
-        functools.partial(moment_body, groups, len(far), length, states),
-        (1,),
-        [whole(local_shape)] * groups + far_blocks + [AFTER],
-        [whole(stack_shape)] + [whole((length, span))] * len(far),
-        [shape_of(stack_shape, BF16)] + [shape_of((length, span), BF16)] * len(far),
-        us=2,
-    )(sp, *local_grads, *[teacher_rows] * len(far), spans)
-    far_rows = {o: in_plane(copy, o) for o, copy in zip(far, far_copies)}
+        before = [before]
+        copies = [
+            lax.dynamic_slice_in_dim(teacher_rows, (mine ^ o) * span, span, 1) for o in direct
+        ]
+    moved_rows = {o: in_plane(copy, o) for o, copy in zip(direct, copies)}
 
     outs = call(
-        functools.partial(forward_body, groups, count, count),
+        functools.partial(forward_body, groups, count, len(far)),
         (1,),
         [whole(stack_shape), whole(decay_shape), whole(stack_shape)]
         + [whole(piece_shape)] * count
         + [whole(local_shape)] * groups
-        + [AFTER] * len(far),
+        + row_blocks(far),
         [whole(state_shape)] * groups
         + [whole(stack_shape), whole(state_shape)]
-        + [whole(piece_shape)] * count,
+        + [whole(piece_shape)] * count
+        + [copy_spec] * len(far),
         [shape_of(state_shape, BF16)] * groups
         + [shape_of(stack_shape, F32), shape_of(state_shape, F32)]
-        + [shape_of(piece_shape, BF16)] * count,
+        + [shape_of(piece_shape, BF16)] * count
+        + [copy_shape] * len(far),
         [pltpu.VMEM(stack_shape, BF16), pltpu.VMEM(state_shape, BF16)],
         us=2,
-    )(
-        sp,
-        inc,
-        decays,
-        moments,
-        *before,
-        *local_grads,
-        *far_rows.values(),
-    )
+    )(sp, inc, decays, moments, *before, *local_grads, *[teacher_rows] * len(far))
+    entering = exchanged(outs[:groups])
+    grads, grad_total, *grad_sent = outs[groups : groups + 2 + count]
+    far_rows = {o: in_plane(copy, o) for o, copy in zip(far, outs[groups + 2 + count :])}
     moved_rows = [(moved_rows | far_rows)[o] for o in range(1, groups)]
-    entering = exchanged(outs[:groups])
-    grads, grad_total, *grad_sent = outs[groups:]
+
+    if shared:
+        parts = call(
+            functools.partial(behind_body, planes),
+            (1,),
+            [whole(spans_shape)] + [whole(piece_shape)] * planes + [AFTER] * len(direct),
+            [whole(piece_shape)] * planes,
+            [shape_of(piece_shape, BF16)] * planes,
+            [pltpu.VMEM((planes,) + piece_shape, BF16)] * 2,
+        )(sp, spans, *exchanged_planes(grad_sent), *[moved_rows[o - 1] for o in direct])
+        after = exchanged_planes(parts)
+    else:
+        after = jnp.zeros(state_shape, BF16)
+        for step in range(planes - 1):
+            after = next_plane(hop(after, grad_total), -1)
+        after, parts = [after], [grad_total]
 
     totals, sums, heads, orders = [], [], [], []
     total_shape = (length, length + states)
-    for o in range(groups):
+
+    def error_part(o, order):
         fixed = functools.partial(lambda o, _, sp: (o ^ sp[1], 0, 0), o)
         fixed_wide = functools.partial(lambda o, _, sp: (0, o ^ sp[1]), o)
         one_sum, one_head, one_total, one_order = call(
@@ -758,7 +775,7 @@
                 whole(params.shape),
                 whole(state_shape),
             ]
-            + [whole(total_shape)] * (o > 0),
+            + [whole(total_shape), AFTER] * (o > 0),
             [
                 whole((2 * HEADS, length)),
                 whole((2 * HEADS, LANE)),
@@ -773,36 +790,27 @@
             ],
             [pltpu.VMEM((length, length), F32)],
             us=4,
-        )(sp, bc, rows, cols, teacher_rows, teacher_next, err, params, entering[o], *totals[-1:])
+        )(sp, bc, rows, cols, teacher_rows, teacher_next, err, params, entering[o], *totals[-1:], *[order] * (o > 0))
         orders.append(one_order)
         totals.append(one_total)
         sums.append(one_sum)
         heads.append(one_head)
 
-    if shared:
-        parts = call(
-            functools.partial(behind_body, planes),
-            (1,),
-            [whole(spans_shape)] + [whole(piece_shape)] * planes,
-            [whole(piece_shape)] * planes,
-            [shape_of(piece_shape, BF16)] * planes,
-            [pltpu.VMEM((planes,) + piece_shape, BF16)] * 2,
-        )(sp, spans, *exchanged_planes(grad_sent))
-        after = exchanged_planes(parts)
-    else:
-        after = jnp.zeros(state_shape, BF16)
-        for step in range(planes - 1):
-            after = next_plane(hop(after, grad_total), -1)
-        after = [after]
-
+    error_part(0, None)
+    if groups > 1:
+        error_part(1, parts[0])
     leaving = call(
         functools.partial(backward_body, groups, count),
         (1,),
-        [whole(stack_shape), whole(decay_shape)] + [whole(piece_shape)] * count + [AFTER],
+        [whole(stack_shape), whole(decay_shape)]
+        + [whole(piece_shape)] * count
+        + [AFTER] * (1 + len(far)),
         [whole(state_shape)] * groups,
         [shape_of(state_shape, BF16)] * groups,
         [pltpu.VMEM(stack_shape, BF16), pltpu.VMEM(state_shape, BF16)],
-    )(sp, grads, decays, *after, orders[min(1, groups - 1)])
+    )(sp, grads, decays, *after, orders[0], *[moved_rows[o - 1] for o in far])
+    for o in range(2, groups):
+        error_part(o, leaving[0])
     leaving = exchanged(leaving)
 
     pulls, mets, input_grads = [], [], []
@@ -853,35 +861,48 @@
         [pltpu.VMEM((LANE, LANE), F32)],
         us=2,
     )(sp, bc, rows, params, totals[-1], input_grads[-1], *sums, *heads, *pulls, *mets)
-    grad_shape = (width + 4 * KINDS, length)
-    merged = call(
+    grad_shape = (width, length)
+    merged, small = call(
         functools.partial(merge_body, dp_count, width),
         (1,),
         [whole(grad_rows)] * dp_count,
-        whole(grad_shape),
-        shape_of(grad_shape, BF16),
+        [whole(grad_shape), whole((KINDS, LANE))],
+        [shape_of(grad_shape, BF16), shape_of((KINDS, LANE), F32)],
     )(sp, *members_of(partial_grads))
+    step = 1
+    while step < planes:
+        small = small + over_planes(small, step)
+        step *= 2
     merged = [merged] + [in_plane(merged, o) for o in range(1, groups)]
 
     unit = TAIL * planes
     padded = -(-width // unit) * unit
     piece = padded // planes
     share_shape = (piece, span)
-    own, small, *sent = call(
+    own, *sent = call(
         functools.partial(weight_body, groups, planes, width),
         (1,),
         [whole(grad_shape)] * groups
         + [pl.BlockSpec((length, span), lambda _, sp: (0, sp[1]))]
-        + [whole((length, span))] * (groups - 1),
-        [whole(share_shape), whole((KINDS, LANE))] + [whole(share_shape)] * (planes - 1),
-        [shape_of(share_shape, F32), shape_of((KINDS, LANE), F32)]
-        + [shape_of(share_shape, BF16)] * (planes - 1),
+        + [whole((length, span))] * (groups - 1)
+        + [AFTER],
+        [whole(share_shape)] * planes,
+        [shape_of(share_shape, F32)] + [shape_of(share_shape, BF16)] * (planes - 1),
         [pltpu.VMEM((padded, span), F32)],
         us=3,
-    )(sp, *merged, teacher_rows, *moved_rows)
-    for m in range(1, planes):
-        own = own + over_planes(sent[m - 1], m).astype(F32)
-    own = own.astype(BF16)
+    )(sp, *merged, teacher_rows, *moved_rows, small)
+    step = 1
+    while step < groups:
+        small = small + in_plane(small, step)
+        step *= 2
+    own = call(
+        functools.partial(total_body, planes),
+        (1,),
+        [whole(share_shape)] * planes + [AFTER],
+        whole(share_shape),
+        shape_of(share_shape, BF16),
+    )(sp, own, *[over_planes(sent[m - 1], m) for m in range(1, planes)], small)
+
     def all_over(value, send, count):
         parts, step = {0: value}, 1
         while step < count:
@@ -899,10 +920,6 @@
         for step in steps if k % 2 else steps[::-1]:
             spread |= {o | step: in_plane(value, step) for o, value in spread.items()}
         pieces.append(spread)
-    step = 1
-    while step < planes:
-        small = small + over_planes(small, step)
-        step *= 2
     results = []
     for o in range(groups):
         results = call(

time: 187 us -> 174 us (0.930)
  waiting for transfers between devices: 55.7 us -> 46.8 us
  starting transfers between devices: 70.7 us -> 67.5 us
    ppermute x20, waiting for transfers between devices: 33.6 us -> 20.9 us  [over_planes(): return lax.ppermute(value, 'seq', pairs)]
    ppermute x20, starting transfers between devices: 35.2 us -> 31.9 us  [over_planes(): return lax.ppermute(value, 'seq', pairs)]
    ppermute x30 -> x32, waiting for transfers between devices: 20.5 us -> 22.9 us  [in_plane(): return lax.ppermute(value, 'seq', pairs)]
    pallas_call x8 -> x9, Pallas kernels: 22.9 us -> 23.6 us  [the longest x4 12 us: error_part(): call(functools.partial(error_body, o == 0, local_heads, o), (1,), [whole(...]
    ppermute x30 -> x32, starting transfers between devices: 35 us -> 35 us  [in_plane(): return lax.ppermute(value, 'seq', pairs)]
  transfers between devices with their start and end apart: 52 -> 54, of which waited for: 21 -> 21; matrix products, arithmetic and copies ran while one was open for 1% -> 1% of each run, Pallas kernels for 20% -> 22%
where the time goes in v2:
time: 174 us; the launch traced here: 173 us
  starting transfers between devices  67.5 us (39%)
  Pallas kernels  53.7 us (31%)
  waiting for transfers between devices  46.8 us (27%)
  between operations  2.63 us (2%)
    ppermute x32, starting transfers between devices, in_plane(): return lax.ppermute(value, 'seq', pairs)  35 us
    ppermute x20, starting transfers between devices, over_planes(): return lax.ppermute(value, 'seq', pairs)  31.9 us
    ppermute x32, waiting for transfers between devices, in_plane(): return lax.ppermute(value, 'seq', pairs)  22.9 us
    ppermute x20, waiting for transfers between devices, over_planes(): return lax.ppermute(value, 'seq', pairs)  20.9 us
    pallas_call x4, Pallas kernels, error_part(): call(functools.partial(error_body, o == 0, local_heads, o), (1,), [whole(...  12 us
    pallas_call x1, Pallas kernels, shards(): call(functools.partial(local_body, groups, local_heads), (groups,), [whol...  7.56 us
    pallas_call x4, Pallas kernels, shards(): call(functools.partial(spread_body, planes), (1,), [whole(share_shape)] *...  7.22 us
    pallas_call x1, Pallas kernels, shards(): call(project_body, (groups,), [pl.BlockSpec((length, span), lambda o, sp:...  5.46 us
  transfers between devices with their start and end apart: 54, of which 21 were waited for; matrix products, arithmetic and copies ran while one was open for 1% of the time, Pallas kernels for 22%

profile of v2, /device:TPU:0, one launch (start us, length us, event | category | flops | bytes accessed | tf_op | source)
XLA Modules:
  0.0 173.5 jit_solution(12949925153950583434)
XLA Ops:
  1.3 5.5 %shard_map.118.refs_0_ = f32[256,384]{1,0:T(8,128)} custom-call(s32[3]{0:T(128)} %pad_add_fusion.sp, bf16[256,4096]{1,0:T(8,128)(2,1)} %refs_4_.3, bf16[8192,256]{1,0:T(8,128)(2,1)} %wb_ref.1, bf16[64,8192]{1,0:T(8,128)(2,1)} %bitcast.18), custom_call_target="tpu_custom_call" | custom-call | flops 3300000000 | tf_op jit(solution)/shard_map/pallas_call | solution.py:601
  9.7 3.9 %shard_map.119 = (bf16[256,256]{1,0:T(8,128)(2,1)S(1)}, f32[4,48,256]{2,1,0:T(8,128)S(1)}, f32[4,256,128]{2,1,0:T(8,128)S(1)}, bf16[144,1024]{1,0:T(8,128)(2,1)S...) custom-call(s32[3]{0:T(128)S(1)} %copy-done.1, ...), custom_call_target="tpu_custom_call" | custom-call | flops 5500000256 | tf_op jit(solution)/shard_map/pallas_call | solution.py:631
  13.6 2.9 %collective-permute-start.1 = (bf16[144,1024]{1,0:T(8,128)(2,1)S(1)}, bf16[144,1024]{1,0:T(8,128)(2,1)S(1)}, u32[]{:S(2)}, u32[]{:S(2)}) collective-permute-start(bf16[144,1024]{1,0:T(8,128)(2,1)S(1)} %get-tuple-element.93), channel_id=1, source_target_pairs={{0,2},{2,0},{4,6},{6,4},{8,10},{10,8},{12,14},{14,12},{16,18},{18,... | collective-permute-start | bytes 884744 | tf_op jit(solution)/shard_map/ppermute | solution.py:580
  18.1 7.6 %shard_map.120 = (f32[256,4096]{1,0:T(8,128)S(1)}, bf16[176,1024]{1,0:T(8,128)(2,1)S(1)}, bf16[176,1024]{1,0:T(8,128)(2,1)S(1)}, bf16[176,1024]{1,0:T(8,128)(2,1)S(1)}, bf16[176,1024]{1,0:T(8,128)(2,1)S(1)}) custom-call(s32[3]{0:T(128)S(1)} %copy-done.1, bf16[256,256]{1,0:T(8,128)(2,1)S(1)} %get-tuple-element.88.bc_ref, ...), custom_call_target="tpu_custom_call" | custom-call | flops 7699999744 | tf_op jit(solution)/shard_map/pallas_call | solution.py:647
  25.7 2.0 %collective-permute-start.4 = (bf16[176,1024]{1,0:T(8,128)(2,1)S(1)}, bf16[176,1024]{1,0:T(8,128)(2,1)S(1)}, u32[]{:S(2)}, u32[]{:S(2)}) collective-permute-start(bf16[176,1024]{1,0:T(8,128)(2,1)S(1)} %get-tuple-element.99), channel_id=1, source_target_pairs={{0,2},{2,0},{4,6},{6,4},{8,10},{10,8},{12,14},{14,12},{16,18},{18,... | collective-permute-start | bytes 1081352 | tf_op jit(solution)/shard_map/ppermute | solution.py:580
  29.2 2.6 %collective-permute-done.2.refs_2_ = bf16[144,1024]{1,0:T(8,128)(2,1)S(1)} collective-permute-done((bf16[144,1024]{1,0:T(8,128)(2,1)S(1)}, bf16[144,1024]{1,0:T(8,128)(2,1)S(1)}, u32[]{:S(2)}, u32[]{:S(2)}) %collective-permute-start.2) | collective-permute-done | bytes 294944 | tf_op jit(solution)/shard_map/ppermute | solution.py:580
  35.5 2.6 %collective-permute-start.8 = (bf16[144,256]{1,0:T(8,128)(2,1)S(1)}, bf16[144,256]{1,0:T(8,128)(2,1)S(1)}, u32[]{:S(2)}, u32[]{:S(2)}) collective-permute-start(bf16[144,256]{1,0:T(8,128)(2,1)S(1)} %get-tuple-element.104), channel_id=1, source_target_pairs={{0,16},{2,18},{4,20},{6,22},{8,24},{10,26},{12,28},{14,30},{16,0},... | collective-permute-start | bytes 221192 | tf_op jit(solution)/shard_map/ppermute | solution.py:584
  38.7 3.2 %collective-permute-start.9 = (bf16[144,256]{1,0:T(8,128)(2,1)S(1)}, bf16[144,256]{1,0:T(8,128)(2,1)S(1)}, u32[]{:S(2)}, u32[]{:S(2)}) collective-permute-start(bf16[144,256]{1,0:T(8,128)(2,1)S(1)} %get-tuple-element.105), channel_id=1, source_target_pairs={{0,24},{2,26},{4,28},{6,30},{8,16},{10,18},{12,20},{14,22},{16,8},... | collective-permute-start | bytes 221192 | tf_op jit(solution)/shard_map/ppermute | solution.py:584
  42.7 2.3 %collective-permute-done.9.refs_3_ = bf16[144,256]{1,0:T(8,128)(2,1)S(1)} collective-permute-done((bf16[144,256]{1,0:T(8,128)(2,1)S(1)}, bf16[144,256]{1,0:T(8,128)(2,1)S(1)}, u32[]{:S(2)}, u32[]{:S(2)}) %collective-permute-start.9) | collective-permute-done | bytes 73760 | tf_op jit(solution)/shard_map/ppermute | solution.py:584
  46.4 3.0 %collective-permute-start.11 = (bf16[128,256]{1,0:T(8,128)(2,1)S(1)}, bf16[128,256]{1,0:T(8,128)(2,1)S(1)}, u32[]{:S(2)}, u32[]{:S(2)}) collective-permute-start(bf16[128,256]{1,0:T(8,128)(2,1)S(1)} %get-tuple-element.108), channel_id=1, source_target_pairs={{0,16},{2,18},{4,20},{6,22},{8,24},{10,26},{12,28},{14,30},{16,0},... | collective-permute-start | bytes 196616 | tf_op jit(solution)/shard_map/ppermute | solution.py:584
  50.2 2.2 %shard_map.122.moment_ref = bf16[4,128,1024]{2,1,0:T(8,128)(2,1)S(1)} custom-call(s32[3]{0:T(128)S(1)} %copy-done.1, bf16[176,1024]{1,0:T(8,128)(2,1)S(1)} %get-tuple-element.98.refs_0_.refs_4_, bf16[176,1024]{1,0:T(8,128)(2,1)S(1)} %collective-permute-done.4.refs_1_.refs_5_, bf16[176,1024]{1,0:T(8,128)(2,1)S(1)} %collective-permute-done.5.refs_2_.refs_6_, ...), custom_call_target="tpu_custom_call" | custom-call | flops 2200000000 | tf_op jit(solution)/shard_map/pallas_call | solution.py:679
  55.4 2.6 %shard_map.124 = (bf16[128,1024]{1,0:T(8,128)(2,1)S(1)}, bf16[128,1024]{1,0:T(8,128)(2,1)S(1)}, bf16[128,1024]{1,0:T(8,128)(2,1)S(1)}, bf16[128,1024]{1,0:T(8,12...) custom-call(s32[3]{0:T(128)S(1)} %copy-done.1, ...), custom_call_target="tpu_custom_call" | custom-call | flops 2200000000 | tf_op jit(solution)/shard_map/pallas_call | solution.py:720
  58.0 2.9 %collective-permute-start.17 = (bf16[128,256]{1,0:T(8,128)(2,1)S(1)}, bf16[128,256]{1,0:T(8,128)(2,1)S(1)}, u32[]{:S(2)}, u32[]{:S(2)}) collective-permute-start(bf16[128,256]{1,0:T(8,128)(2,1)S(1)} %get-tuple-element.118), channel_id=1, source_target_pairs={{0,16},{2,18},{4,20},{6,22},{8,24},{10,26},{12,28},{14,30},{16,0},... | collective-permute-start | bytes 196616 | tf_op jit(solution)/shard_map/ppermute | solution.py:584
  63.9 2.3 %collective-permute-start.24 = (bf16[256,1024]{1,0:T(8,128)(2,1)S(1)}, bf16[256,1024]{1,0:T(8,128)(2,1)S(1)}, u32[]{:S(2)}, u32[]{:S(2)}) collective-permute-start(bf16[256,1024]{1,0:T(8,128)(2,1)S(1)} %get-tuple-element.129), channel_id=1, source_target_pairs={{0,6},{2,4},{4,2},{6,0},{8,14},{10,12},{12,10},{14,8},{16,22},{18,... | collective-permute-start | bytes 1572872 | tf_op jit(solution)/shard_map/ppermute | solution.py:580
  66.2 2.9 %shard_map.125 = (f32[16,256]{1,0:T(8,128)S(1)}, f32[16,128]{1,0:T(8,128)S(1)}, f32[256,384]{1,0:T(8,128)S(1)}, f32[8,128]{1,0:T(8,128)S(1)}) custom-call(s32[3]{0:T(128)S(1)} %copy-done.1, bf16[256,256]{1,0:T(8,128)(2,1)S(1)} %get-tuple-element.88.bc_ref, f32[4,48,256]{2,1,0:T(8,128)S(1)} %get-tuple-element.89.rows_ref, ...), custom_call_target="tpu_custom_call" | custom-call | flops 4400000000 | tf_op jit(solution)/shard_map/pallas_call | solution.py:765
  73.3 2.7 %collective-permute-start.23 = (bf16[128,256]{1,0:T(8,128)(2,1)S(1)}, bf16[128,256]{1,0:T(8,128)(2,1)S(1)}, u32[]{:S(2)}, u32[]{:S(2)}) collective-permute-start(bf16[128,256]{1,0:T(8,128)(2,1)S(1)} %get-tuple-element.127), channel_id=1, source_target_pairs={{0,24},{2,26},{4,28},{6,30},{8,16},{10,18},{12,20},{14,22},{16,8},... | collective-permute-start | bytes 196616 | tf_op jit(solution)/shard_map/ppermute | solution.py:584
  76.0 3.0 %shard_map.127 = (f32[16,256]{1,0:T(8,128)S(1)}, f32[16,128]{1,0:T(8,128)S(1)}, f32[256,384]{1,0:T(8,128)S(1)}, f32[8,128]{1,0:T(8,128)}) custom-call(s32[3]{0:T(128)S(1)} %copy-done.1, bf16[256,256]{1,0:T(8,128)(2,1)S(1)} %get-tuple-element.88.bc_ref, f32[4,48,256]{2,1,0:T(8,128)S(1)} %get-tuple-element.89.rows_ref, ...), custom_call_target="tpu_custom_call" | custom-call | flops 4400000000 | tf_op jit(solution)/shard_map/pallas_call | solution.py:765
  79.0 2.0 %collective-permute-done.24.refs_5_.refs_7_ = bf16[256,1024]{1,0:T(8,128)(2,1)S(1)} collective-permute-done((bf16[256,1024]{1,0:T(8,128)(2,1)S(1)}, bf16[256,1024]{1,0:T(8,128)(2,1)S(1)}, u32[]{:S(2)}, u32[]{:S(2)}) %collective-permute-start.24) | collective-permute-done | bytes 524320 | tf_op jit(solution)/shard_map/ppermute | solution.py:580
  82.7 2.3 %collective-permute-start.25 = (bf16[128,1024]{1,0:T(8,128)(2,1)S(1)}, bf16[128,1024]{1,0:T(8,128)(2,1)S(1)}, u32[]{:S(2)}, u32[]{:S(2)}) collective-permute-start(bf16[128,1024]{1,0:T(8,128)(2,1)S(1)} %get-tuple-element.133), channel_id=1, source_target_pairs={{0,6},{2,4},{4,2},{6,0},{8,14},{10,12},{12,10},{14,8},{16,22},{18,... | collective-permute-start | bytes 786440 | tf_op jit(solution)/shard_map/ppermute | solution.py:580
  86.2 10.4 %collective-permute-done.14.state_ref = bf16[128,1024]{1,0:T(8,128)(2,1)S(1)} collective-permute-done((bf16[128,1024]{1,0:T(8,128)(2,1)S(1)}, bf16[128,1024]{1,0:T(8,128)(2,1)S(1)}, u32[]{:S(2)}, u32[]{:S(2)}) %collective-permute-start.14) | collective-permute-done | bytes 262176 | tf_op jit(solution)/shard_map/ppermute | solution.py:580
  96.6 3.2 %shard_map.129 = (f32[16,256]{1,0:T(8,128)S(1)}, f32[16,128]{1,0:T(8,128)S(1)}, f32[256,384]{1,0:T(8,128)S(1)}, f32[8,128]{1,0:T(8,128)}) custom-call(s32[3]{0:T(128)S(1)} %copy-done.1, bf16[256,256]{1,0:T(8,128)(2,1)S(1)} %get-tuple-element.88.bc_ref, f32[4,48,256]{2,1,0:T(8,128)S(1)} %get-tuple-element.89.rows_ref, ...), custom_call_target="tpu_custom_call" | custom-call | flops 4400000000 | tf_op jit(solution)/shard_map/pallas_call | solution.py:765
  99.8 3.0 %shard_map.130 = (f32[16,256]{1,0:T(8,128)S(1)}, f32[16,128]{1,0:T(8,128)S(1)}, f32[256,384]{1,0:T(8,128)S(1)}, f32[8,128]{1,0:T(8,128)}) custom-call(s32[3]{0:T(128)S(1)} %copy-done.1, bf16[256,256]{1,0:T(8,128)(2,1)S(1)} %get-tuple-element.88.bc_ref, f32[4,48,256]{2,1,0:T(8,128)S(1)} %get-tuple-element.89.rows_ref, ...), custom_call_target="tpu_custom_call" | custom-call | flops 4400000000 | tf_op jit(solution)/shard_map/pallas_call | solution.py:765
  115.8 2.6 %collective-permute-done.29 = f32[8,128]{1,0:T(8,128)S(1)} collective-permute-done((f32[8,128]{1,0:T(8,128)S(1)}, f32[8,128]{1,0:T(8,128)S(1)}, u32[]{:S(2)}, u32[]{:S(2)}) %collective-permute-start.29) | collective-permute-done | bytes 4128 | tf_op jit(solution)/shard_map/ppermute | solution.py:584
  120.1 2.7 %collective-permute-done.30 = f32[8,128]{1,0:T(8,128)S(1)} collective-permute-done((f32[8,128]{1,0:T(8,128)S(1)}, f32[8,128]{1,0:T(8,128)S(1)}, u32[]{:S(2)}, u32[]{:S(2)}) %collective-permute-start.30) | collective-permute-done | bytes 4128 | tf_op jit(solution)/shard_map/ppermute | solution.py:584
  126.7 2.1 %collective-permute-start.38 = (bf16[80,1024]{1,0:T(8,128)(2,1)S(1)}, bf16[80,1024]{1,0:T(8,128)(2,1)S(1)}, u32[]{:S(2)}, u32[]{:S(2)}) collective-permute-start(bf16[80,1024]{1,0:T(8,128)(2,1)S(1)} %get-tuple-element.161), channel_id=1, source_target_pairs={{0,24},{2,26},{4,28},{6,30},{8,16},{10,18},{12,20},{14,22},{16,8},... | collective-permute-start | bytes 491528 | tf_op jit(solution)/shard_map/ppermute | solution.py:584
  129.8 2.6 %collective-permute-done.31 = f32[8,128]{1,0:T(8,128)S(1)} collective-permute-done((f32[8,128]{1,0:T(8,128)S(1)}, f32[8,128]{1,0:T(8,128)S(1)}, u32[]{:S(2)}, u32[]{:S(2)}) %collective-permute-start.31) | collective-permute-done | bytes 4128 | tf_op jit(solution)/shard_map/ppermute | solution.py:580
  133.4 2.6 %collective-permute-done.32 = f32[8,128]{1,0:T(8,128)S(1)} collective-permute-done((f32[8,128]{1,0:T(8,128)S(1)}, f32[8,128]{1,0:T(8,128)S(1)}, u32[]{:S(2)}, u32[]{:S(2)}) %collective-permute-start.32) | collective-permute-done | bytes 4128 | tf_op jit(solution)/shard_map/ppermute | solution.py:580
  136.0 3.9 %collective-permute-done.37.refs_1_ = bf16[80,1024]{1,0:T(8,128)(2,1)S(1)} collective-permute-done((bf16[80,1024]{1,0:T(8,128)(2,1)S(1)}, bf16[80,1024]{1,0:T(8,128)(2,1)S(1)}, u32[]{:S(2)}, u32[]{:S(2)}) %collective-permute-start.37) | collective-permute-done | bytes 163872 | tf_op jit(solution)/shard_map/ppermute | solution.py:584
  140.5 3.2 %collective-permute-start.44 = (bf16[80,1024]{1,0:T(8,128)(2,1)S(1)}, bf16[80,1024]{1,0:T(8,128)(2,1)S(1)}, u32[]{:S(2)}, u32[]{:S(2)}) collective-permute-start(bf16[80,1024]{1,0:T(8,128)(2,1)S(1)} %shard_map.138.refs_0_), channel_id=1, source_target_pairs={{0,16},{2,18},{4,20},{6,22},{8,24},{10,26},{12,28},{14,30},{16,0},... | collective-permute-start | bytes 491528 | tf_op jit(solution)/shard_map/ppermute | solution.py:584
  145.8 4.5 %collective-permute-done.44.refs_2_ = bf16[80,1024]{1,0:T(8,128)(2,1)S(1)} collective-permute-done((bf16[80,1024]{1,0:T(8,128)(2,1)S(1)}, bf16[80,1024]{1,0:T(8,128)(2,1)S(1)}, u32[]{:S(2)}, u32[]{:S(2)}) %collective-permute-start.44) | collective-permute-done | bytes 163872 | tf_op jit(solution)/shard_map/ppermute | solution.py:584
  150.8 1.8 %collective-permute-start.45 = (bf16[80,1024]{1,0:T(8,128)(2,1)S(1)}, bf16[80,1024]{1,0:T(8,128)(2,1)S(1)}, u32[]{:S(2)}, u32[]{:S(2)}) collective-permute-start(bf16[80,1024]{1,0:T(8,128)(2,1)S(1)} %collective-permute-done.44.refs_2_), channel_id=1, source_target_pairs={{0,4},{2,6},{4,0},{6,2},{8,12},{10,14},{12,8},{14,10},{16,20},{18,... | collective-permute-start | bytes 491528 | tf_op jit(solution)/shard_map/ppermute | solution.py:580
  157.8 1.8 %collective-permute-start.51 = (bf16[80,1024]{1,0:T(8,128)(2,1)S(1)}, bf16[80,1024]{1,0:T(8,128)(2,1)S(1)}, u32[]{:S(2)}, u32[]{:S(2)}) collective-permute-start(bf16[80,1024]{1,0:T(8,128)(2,1)S(1)} %collective-permute-done.47.refs_3_), channel_id=1, source_target_pairs={{0,4},{2,6},{4,0},{6,2},{8,12},{10,14},{12,8},{14,10},{16,20},{18,... | collective-permute-start | bytes 491528 | tf_op jit(solution)/shard_map/ppermute | solution.py:580
  (123 shorter events, 68.1 us)
Async XLA Ops:
  13.6 15.6 %collective-permute-start.1 = (bf16[144,1024]{1,0:T(8,128)(2,1)S(1)}, bf16[144,1024]{1,0:T(8,128)(2,1)S(1)}, u32[]{:S(2)}, u32[]{:S(2)}) collective-permute-start(bf16[144,1024]{1,0:T(8,128)(2,1)S(1)} %get-tuple-element.93), channel_id=1, source_target_pairs={{0,2},{2,0},{4,6},{6,4},{8,10},{10,8},{12,14},{14,12},{16,18},{18,... | collective-permute-start | bytes 884744 | tf_op jit(solution)/shard_map/ppermute | solution.py:580
  16.5 15.2 %collective-permute-start.2 = (bf16[144,1024]{1,0:T(8,128)(2,1)S(1)}, bf16[144,1024]{1,0:T(8,128)(2,1)S(1)}, u32[]{:S(2)}, u32[]{:S(2)}) collective-permute-start(bf16[144,1024]{1,0:T(8,128)(2,1)S(1)} %get-tuple-element.94), channel_id=1, source_target_pairs={{0,4},{2,6},{4,0},{6,2},{8,12},{10,14},{12,8},{14,10},{16,20},{18,... | collective-permute-start | bytes 884744 | tf_op jit(solution)/shard_map/ppermute | solution.py:580
  18.1 14.2 %collective-permute-start.3 = (bf16[144,1024]{1,0:T(8,128)(2,1)S(1)}, bf16[144,1024]{1,0:T(8,128)(2,1)S(1)}, u32[]{:S(2)}, u32[]{:S(2)}) collective-permute-start(bf16[144,1024]{1,0:T(8,128)(2,1)S(1)} %get-tuple-element.95), channel_id=1, source_target_pairs={{0,6},{2,4},{4,2},{6,0},{8,14},{10,12},{12,10},{14,8},{16,22},{18,... | collective-permute-start | bytes 884744 | tf_op jit(solution)/shard_map/ppermute | solution.py:580
  25.7 23.7 %collective-permute-start.4 = (bf16[176,1024]{1,0:T(8,128)(2,1)S(1)}, bf16[176,1024]{1,0:T(8,128)(2,1)S(1)}, u32[]{:S(2)}, u32[]{:S(2)}) collective-permute-start(bf16[176,1024]{1,0:T(8,128)(2,1)S(1)} %get-tuple-element.99), channel_id=1, source_target_pairs={{0,2},{2,0},{4,6},{6,4},{8,10},{10,8},{12,14},{14,12},{16,18},{18,... | collective-permute-start | bytes 1081352 | tf_op jit(solution)/shard_map/ppermute | solution.py:580
  27.7 22.5 %collective-permute-start.5 = (bf16[176,1024]{1,0:T(8,128)(2,1)S(1)}, bf16[176,1024]{1,0:T(8,128)(2,1)S(1)}, u32[]{:S(2)}, u32[]{:S(2)}) collective-permute-start(bf16[176,1024]{1,0:T(8,128)(2,1)S(1)} %get-tuple-element.100), channel_id=1, source_target_pairs={{0,4},{2,6},{4,0},{6,2},{8,12},{10,14},{12,8},{14,10},{16,20},{18,... | collective-permute-start | bytes 1081352 | tf_op jit(solution)/shard_map/ppermute | solution.py:580
  29.2 21.0 %collective-permute-start.6 = (bf16[176,1024]{1,0:T(8,128)(2,1)S(1)}, bf16[176,1024]{1,0:T(8,128)(2,1)S(1)}, u32[]{:S(2)}, u32[]{:S(2)}) collective-permute-start(bf16[176,1024]{1,0:T(8,128)(2,1)S(1)} %get-tuple-element.101), channel_id=1, source_target_pairs={{0,6},{2,4},{4,2},{6,0},{8,14},{10,12},{12,10},{14,8},{16,22},{18,... | collective-permute-start | bytes 1081352 | tf_op jit(solution)/shard_map/ppermute | solution.py:580
  45.7 8.8 %collective-permute-start.10 = (bf16[128,256]{1,0:T(8,128)(2,1)S(1)}, bf16[128,256]{1,0:T(8,128)(2,1)S(1)}, u32[]{:S(2)}, u32[]{:S(2)}) collective-permute-start(bf16[128,256]{1,0:T(8,128)(2,1)S(1)} %get-tuple-element.107), channel_id=1, source_target_pairs={{0,8},{2,10},{4,12},{6,14},{8,0},{10,2},{12,4},{14,6},{16,24},{18,... | collective-permute-start | bytes 196616 | tf_op jit(solution)/shard_map/ppermute | solution.py:584
  52.4 17.6 %collective-permute-start.19 = (bf16[256,1024]{1,0:T(8,128)(2,1)S(1)}, bf16[256,1024]{1,0:T(8,128)(2,1)S(1)}, u32[]{:S(2)}, u32[]{:S(2)}) collective-permute-start(bf16[256,1024]{1,0:T(8,128)(2,1)S(1)} %get-tuple-element.120), channel_id=1, source_target_pairs={{0,2},{2,0},{4,6},{6,4},{8,10},{10,8},{12,14},{14,12},{16,18},{18,... | collective-permute-start | bytes 1572872 | tf_op jit(solution)/shard_map/ppermute | solution.py:580
  53.9 16.1 %collective-permute-start.20 = (bf16[256,1024]{1,0:T(8,128)(2,1)S(1)}, bf16[256,1024]{1,0:T(8,128)(2,1)S(1)}, u32[]{:S(2)}, u32[]{:S(2)}) collective-permute-start(bf16[256,1024]{1,0:T(8,128)(2,1)S(1)} %get-tuple-element.121), channel_id=1, source_target_pairs={{0,4},{2,6},{4,0},{6,2},{8,12},{10,14},{12,8},{14,10},{16,20},{18,... | collective-permute-start | bytes 1572872 | tf_op jit(solution)/shard_map/ppermute | solution.py:580
  63.5 9.8 %collective-permute-start.15 = (bf16[128,1024]{1,0:T(8,128)(2,1)S(1)}, bf16[128,1024]{1,0:T(8,128)(2,1)S(1)}, u32[]{:S(2)}, u32[]{:S(2)}) collective-permute-start(bf16[128,1024]{1,0:T(8,128)(2,1)S(1)} %get-tuple-element.112), channel_id=1, source_target_pairs={{0,2},{2,0},{4,6},{6,4},{8,10},{10,8},{12,14},{14,12},{16,18},{18,... | collective-permute-start | bytes 786440 | tf_op jit(solution)/shard_map/ppermute | solution.py:580
  63.9 17.1 %collective-permute-start.24 = (bf16[256,1024]{1,0:T(8,128)(2,1)S(1)}, bf16[256,1024]{1,0:T(8,128)(2,1)S(1)}, u32[]{:S(2)}, u32[]{:S(2)}) collective-permute-start(bf16[256,1024]{1,0:T(8,128)(2,1)S(1)} %get-tuple-element.129), channel_id=1, source_target_pairs={{0,6},{2,4},{4,2},{6,0},{8,14},{10,12},{12,10},{14,8},{16,22},{18,... | collective-permute-start | bytes 1572872 | tf_op jit(solution)/shard_map/ppermute | solution.py:580
  69.1 27.5 %collective-permute-start.14 = (bf16[128,1024]{1,0:T(8,128)(2,1)S(1)}, bf16[128,1024]{1,0:T(8,128)(2,1)S(1)}, u32[]{:S(2)}, u32[]{:S(2)}) collective-permute-start(bf16[128,1024]{1,0:T(8,128)(2,1)S(1)} %get-tuple-element.111), channel_id=1, source_target_pairs={{0,4},{2,6},{4,0},{6,2},{8,12},{10,14},{12,8},{14,10},{16,20},{18,... | collective-permute-start | bytes 786440 | tf_op jit(solution)/shard_map/ppermute | solution.py:580
  70.7 11.0 %collective-permute-start.21 = (bf16[128,256]{1,0:T(8,128)(2,1)S(1)}, bf16[128,256]{1,0:T(8,128)(2,1)S(1)}, u32[]{:S(2)}, u32[]{:S(2)}) collective-permute-start(bf16[128,256]{1,0:T(8,128)(2,1)S(1)} %get-tuple-element.125), channel_id=1, source_target_pairs={{0,8},{2,10},{4,12},{6,14},{8,0},{10,2},{12,4},{14,6},{16,24},{18,... | collective-permute-start | bytes 196616 | tf_op jit(solution)/shard_map/ppermute | solution.py:584
  71.9 9.8 %collective-permute-start.22 = (bf16[128,256]{1,0:T(8,128)(2,1)S(1)}, bf16[128,256]{1,0:T(8,128)(2,1)S(1)}, u32[]{:S(2)}, u32[]{:S(2)}) collective-permute-start(bf16[128,256]{1,0:T(8,128)(2,1)S(1)} %get-tuple-element.126), channel_id=1, source_target_pairs={{0,16},{2,18},{4,20},{6,22},{8,24},{10,26},{12,28},{14,30},{16,0},... | collective-permute-start | bytes 196616 | tf_op jit(solution)/shard_map/ppermute | solution.py:584
  81.0 18.8 %collective-permute-start.13 = (bf16[128,1024]{1,0:T(8,128)(2,1)S(1)}, bf16[128,1024]{1,0:T(8,128)(2,1)S(1)}, u32[]{:S(2)}, u32[]{:S(2)}) collective-permute-start(bf16[128,1024]{1,0:T(8,128)(2,1)S(1)} %get-tuple-element.110), channel_id=1, source_target_pairs={{0,6},{2,4},{4,2},{6,0},{8,14},{10,12},{12,10},{14,8},{16,22},{18,... | collective-permute-start | bytes 786440 | tf_op jit(solution)/shard_map/ppermute | solution.py:580
  82.7 23.9 %collective-permute-start.25 = (bf16[128,1024]{1,0:T(8,128)(2,1)S(1)}, bf16[128,1024]{1,0:T(8,128)(2,1)S(1)}, u32[]{:S(2)}, u32[]{:S(2)}) collective-permute-start(bf16[128,1024]{1,0:T(8,128)(2,1)S(1)} %get-tuple-element.133), channel_id=1, source_target_pairs={{0,6},{2,4},{4,2},{6,0},{8,14},{10,12},{12,10},{14,8},{16,22},{18,... | collective-permute-start | bytes 786440 | tf_op jit(solution)/shard_map/ppermute | solution.py:580
  85.0 20.3 %collective-permute-start.26 = (bf16[128,1024]{1,0:T(8,128)(2,1)S(1)}, bf16[128,1024]{1,0:T(8,128)(2,1)S(1)}, u32[]{:S(2)}, u32[]{:S(2)}) collective-permute-start(bf16[128,1024]{1,0:T(8,128)(2,1)S(1)} %get-tuple-element.134), channel_id=1, source_target_pairs={{0,4},{2,6},{4,0},{6,2},{8,12},{10,14},{12,8},{14,10},{16,20},{18,... | collective-permute-start | bytes 786440 | tf_op jit(solution)/shard_map/ppermute | solution.py:580
  85.8 18.2 %collective-permute-start.27 = (bf16[128,1024]{1,0:T(8,128)(2,1)S(1)}, bf16[128,1024]{1,0:T(8,128)(2,1)S(1)}, u32[]{:S(2)}, u32[]{:S(2)}) collective-permute-start(bf16[128,1024]{1,0:T(8,128)(2,1)S(1)} %get-tuple-element.135), channel_id=1, source_target_pairs={{0,2},{2,0},{4,6},{6,4},{8,10},{10,8},{12,14},{14,12},{16,18},{18,... | collective-permute-start | bytes 786440 | tf_op jit(solution)/shard_map/ppermute | solution.py:580
  111.2 11.7 %collective-permute-start.35 = (bf16[320,256]{1,0:T(8,128)(2,1)S(1)}, bf16[320,256]{1,0:T(8,128)(2,1)S(1)}, u32[]{:S(2)}, u32[]{:S(2)}) collective-permute-start(bf16[320,256]{1,0:T(8,128)(2,1)S(1)} %get-tuple-element.157.refs_0_), channel_id=1, source_target_pairs={{0,6},{2,4},{4,2},{6,0},{8,14},{10,12},{12,10},{14,8},{16,22},{18,... | collective-permute-start | bytes 491528 | tf_op jit(solution)/shard_map/ppermute | solution.py:580
  112.8 10.1 %collective-permute-start.34 = (bf16[320,256]{1,0:T(8,128)(2,1)S(1)}, bf16[320,256]{1,0:T(8,128)(2,1)S(1)}, u32[]{:S(2)}, u32[]{:S(2)}) collective-permute-start(bf16[320,256]{1,0:T(8,128)(2,1)S(1)} %get-tuple-element.157.refs_0_), channel_id=1, source_target_pairs={{0,4},{2,6},{4,0},{6,2},{8,12},{10,14},{12,8},{14,10},{16,20},{18,... | collective-permute-start | bytes 491528 | tf_op jit(solution)/shard_map/ppermute | solution.py:580
  113.7 9.1 %collective-permute-start.33 = (bf16[320,256]{1,0:T(8,128)(2,1)S(1)}, bf16[320,256]{1,0:T(8,128)(2,1)S(1)}, u32[]{:S(2)}, u32[]{:S(2)}) collective-permute-start(bf16[320,256]{1,0:T(8,128)(2,1)S(1)} %get-tuple-element.157.refs_0_), channel_id=1, source_target_pairs={{0,2},{2,0},{4,6},{6,4},{8,10},{10,8},{12,14},{14,12},{16,18},{18,... | collective-permute-start | bytes 491528 | tf_op jit(solution)/shard_map/ppermute | solution.py:580
  124.3 11.7 %collective-permute-start.36 = (bf16[80,1024]{1,0:T(8,128)(2,1)S(1)}, bf16[80,1024]{1,0:T(8,128)(2,1)S(1)}, u32[]{:S(2)}, u32[]{:S(2)}) collective-permute-start(bf16[80,1024]{1,0:T(8,128)(2,1)S(1)} %get-tuple-element.159), channel_id=1, source_target_pairs={{0,8},{2,10},{4,12},{6,14},{8,0},{10,2},{12,4},{14,6},{16,24},{18,... | collective-permute-start | bytes 491528 | tf_op jit(solution)/shard_map/ppermute | solution.py:584
  125.4 14.5 %collective-permute-start.37 = (bf16[80,1024]{1,0:T(8,128)(2,1)S(1)}, bf16[80,1024]{1,0:T(8,128)(2,1)S(1)}, u32[]{:S(2)}, u32[]{:S(2)}) collective-permute-start(bf16[80,1024]{1,0:T(8,128)(2,1)S(1)} %get-tuple-element.160), channel_id=1, source_target_pairs={{0,16},{2,18},{4,20},{6,22},{8,24},{10,26},{12,28},{14,30},{16,0},... | collective-permute-start | bytes 491528 | tf_op jit(solution)/shard_map/ppermute | solution.py:584
  126.7 13.2 %collective-permute-start.38 = (bf16[80,1024]{1,0:T(8,128)(2,1)S(1)}, bf16[80,1024]{1,0:T(8,128)(2,1)S(1)}, u32[]{:S(2)}, u32[]{:S(2)}) collective-permute-start(bf16[80,1024]{1,0:T(8,128)(2,1)S(1)} %get-tuple-element.161), channel_id=1, source_target_pairs={{0,24},{2,26},{4,28},{6,30},{8,16},{10,18},{12,20},{14,22},{16,8},... | collective-permute-start | bytes 491528 | tf_op jit(solution)/shard_map/ppermute | solution.py:584
  140.5 9.8 %collective-permute-start.44 = (bf16[80,1024]{1,0:T(8,128)(2,1)S(1)}, bf16[80,1024]{1,0:T(8,128)(2,1)S(1)}, u32[]{:S(2)}, u32[]{:S(2)}) collective-permute-start(bf16[80,1024]{1,0:T(8,128)(2,1)S(1)} %shard_map.138.refs_0_), channel_id=1, source_target_pairs={{0,16},{2,18},{4,20},{6,22},{8,24},{10,26},{12,28},{14,30},{16,0},... | collective-permute-start | bytes 491528 | tf_op jit(solution)/shard_map/ppermute | solution.py:584
  144.1 8.6 %collective-permute-start.41 = (bf16[80,1024]{1,0:T(8,128)(2,1)S(1)}, bf16[80,1024]{1,0:T(8,128)(2,1)S(1)}, u32[]{:S(2)}, u32[]{:S(2)}) collective-permute-start(bf16[80,1024]{1,0:T(8,128)(2,1)S(1)} %shard_map.138.refs_0_), channel_id=1, source_target_pairs={{0,8},{2,10},{4,12},{6,14},{8,0},{10,2},{12,4},{14,6},{16,24},{18,... | collective-permute-start | bytes 491528 | tf_op jit(solution)/shard_map/ppermute | solution.py:584
  144.1 9.4 %collective-permute-start.39 = (bf16[80,1024]{1,0:T(8,128)(2,1)S(1)}, bf16[80,1024]{1,0:T(8,128)(2,1)S(1)}, u32[]{:S(2)}, u32[]{:S(2)}) collective-permute-start(bf16[80,1024]{1,0:T(8,128)(2,1)S(1)} %shard_map.138.refs_0_), channel_id=1, source_target_pairs={{0,4},{2,6},{4,0},{6,2},{8,12},{10,14},{12,8},{14,10},{16,20},{18,... | collective-permute-start | bytes 491528 | tf_op jit(solution)/shard_map/ppermute | solution.py:580
  150.8 10.6 %collective-permute-start.45 = (bf16[80,1024]{1,0:T(8,128)(2,1)S(1)}, bf16[80,1024]{1,0:T(8,128)(2,1)S(1)}, u32[]{:S(2)}, u32[]{:S(2)}) collective-permute-start(bf16[80,1024]{1,0:T(8,128)(2,1)S(1)} %collective-permute-done.44.refs_2_), channel_id=1, source_target_pairs={{0,4},{2,6},{4,0},{6,2},{8,12},{10,14},{12,8},{14,10},{16,20},{18,... | collective-permute-start | bytes 491528 | tf_op jit(solution)/shard_map/ppermute | solution.py:580
  152.7 9.4 %collective-permute-start.50 = (bf16[80,1024]{1,0:T(8,128)(2,1)S(1)}, bf16[80,1024]{1,0:T(8,128)(2,1)S(1)}, u32[]{:S(2)}, u32[]{:S(2)}) collective-permute-start(bf16[80,1024]{1,0:T(8,128)(2,1)S(1)} %collective-permute-done.41.refs_1_), channel_id=1, source_target_pairs={{0,4},{2,6},{4,0},{6,2},{8,12},{10,14},{12,8},{14,10},{16,20},{18,... | collective-permute-start | bytes 491528 | tf_op jit(solution)/shard_map/ppermute | solution.py:580
  153.4 10.0 %collective-permute-start.42 = (bf16[80,1024]{1,0:T(8,128)(2,1)S(1)}, bf16[80,1024]{1,0:T(8,128)(2,1)S(1)}, u32[]{:S(2)}, u32[]{:S(2)}) collective-permute-start(bf16[80,1024]{1,0:T(8,128)(2,1)S(1)} %collective-permute-done.41.refs_1_), channel_id=1, source_target_pairs={{0,2},{2,0},{4,6},{6,4},{8,10},{10,8},{12,14},{14,12},{16,18},{18,... | collective-permute-start | bytes 491528 | tf_op jit(solution)/shard_map/ppermute | solution.py:580
  155.7 8.8 %collective-permute-start.48 = (bf16[80,1024]{1,0:T(8,128)(2,1)S(1)}, bf16[80,1024]{1,0:T(8,128)(2,1)S(1)}, u32[]{:S(2)}, u32[]{:S(2)}) collective-permute-start(bf16[80,1024]{1,0:T(8,128)(2,1)S(1)} %collective-permute-done.47.refs_3_), channel_id=1, source_target_pairs={{0,2},{2,0},{4,6},{6,4},{8,10},{10,8},{12,14},{14,12},{16,18},{18,... | collective-permute-start | bytes 491528 | tf_op jit(solution)/shard_map/ppermute | solution.py:580
  157.8 9.5 %collective-permute-start.51 = (bf16[80,1024]{1,0:T(8,128)(2,1)S(1)}, bf16[80,1024]{1,0:T(8,128)(2,1)S(1)}, u32[]{:S(2)}, u32[]{:S(2)}) collective-permute-start(bf16[80,1024]{1,0:T(8,128)(2,1)S(1)} %collective-permute-done.47.refs_3_), channel_id=1, source_target_pairs={{0,4},{2,6},{4,0},{6,2},{8,12},{10,14},{12,8},{14,10},{16,20},{18,... | collective-permute-start | bytes 491528 | tf_op jit(solution)/shard_map/ppermute | solution.py:580
  (29 other events, 171.4 us)

commit v3 on v2

--- a/solution.py
+++ b/solution.py
@@ -85,8 +85,10 @@
     return parts[0]
 
 
-def project_body(sp, u_ref, wb_ref, wd_ref, out_ref):
-    @pl.when(pl.program_id(0) == 0)
+def project_body(far, sp, u_ref, wb_ref, wd_ref, out_ref, *copies):
+    k = pl.program_id(0)
+
+    @pl.when(k == 0)
     def _():
         out_ref[...] = jnp.zeros_like(out_ref)
 
@@ -95,6 +97,11 @@
     head_count = wd_ref.shape[0]
     out_ref[:, :bc_width] += dot_10(u, wb_ref[...])
     out_ref[:, bc_width : bc_width + head_count] += dot_11(u, wd_ref[...])
+    for o, copy in zip(far, copies):
+
+        @pl.when(k == o)
+        def _():
+            copy[...] = u
 
 
 def running_sum(rows, keep):
@@ -184,8 +191,8 @@
     return jnp.exp(jnp.minimum(-gap if back else gap, 0.0))
 
 
-def local_body(groups, local_heads, sp, bc_ref, rows_ref, cols_ref, u_ref, target_ref, par_ref, err_ref, *rest):
-    outs, scores_ref = rest[:groups], rest[groups]
+def local_body(groups, local_heads, sp, bc_ref, rows_ref, cols_ref, u_ref, target_ref, par_ref, *rest):
+    err_ref, outs, scores_ref = rest[-2 - groups], rest[-1 - groups : -1], rest[-1]
     o = pl.program_id(0)
     q = o ^ sp[1]
     length = bc_ref.shape[0]
@@ -325,14 +332,11 @@
     return hold_ref[...].astype(F32)
 
 
-def forward_body(groups, pieces, far, sp, inc_ref, decay_ref, moment_ref, *refs):
+def forward_body(groups, pieces, sp, inc_ref, decay_ref, moment_ref, *refs):
     states_ref, hold_ref = refs[-2:]
     before, locals_ = refs[:pieces], refs[pieces : pieces + groups]
     refs = refs[pieces + groups : -2]
-    for row, copy in zip(refs[:far], refs[len(refs) - far :]):
-        copy[...] = row[...]
-    outs, refs = refs[far : far + groups], refs[far + groups : len(refs) - far]
-    grad_ref, total_ref, sent = refs[0], refs[1], refs[2:]
+    outs, grad_ref, total_ref, sent = refs[:groups], refs[groups], refs[groups + 1], refs[groups + 2 :]
     states = hold_ref.shape[0]
     state = assembled(before, hold_ref, sp)
     for j in range(groups):
@@ -455,7 +459,7 @@
 
 def finish_body(groups, local_heads, scale, sp, bc_ref, rows_ref, par_ref, total_ref, grad_ref, *refs):
     sums, heads, pulls, mets = [refs[i * groups : (i + 1) * groups] for i in range(4)]
-    out_ref, small_ref = refs[4 * groups :]
+    out_ref, sent_ref, small_ref = refs[4 * groups :]
     length = bc_ref.shape[0]
     states = bc_ref.shape[1] // 2
     head_count = par_ref.shape[0]
@@ -467,7 +471,7 @@
     b_grad = grad_ref[...] + dot_10(spread, bc_ref[:, states:])
     out_ref[:states, :] = b_grad.T * scale
     out_ref[states : 2 * states, :] = c_grad.T * scale
-    out_ref[2 * states :, :] = jnp.zeros((out_ref.shape[0] - 2 * states, length), F32)
+    out_ref[2 * states :, :] = jnp.zeros((head_count, length), F32)
     small_ref[...] = jnp.zeros_like(small_ref)
     starts = [
         pl.multiple_of(sp[0] * local_heads + (o ^ sp[1]) * HEADS, HEADS) for o in range(groups)
@@ -509,14 +513,13 @@
         at = pl.multiple_of(2 * states + starts[o], HEADS)
         out_ref[pl.ds(at, HEADS), :] = raw_grad[here]
         small_ref[pl.ds(starts[o], HEADS), :] = small[here]
-    out_ref[2 * states + head_count : 2 * states + head_count + KINDS, :LANE] = small_ref[...].T[:KINDS]
-
-
-def merge_body(members, width, sp, *refs):
+    sent_ref[...] = small_ref[...].T[:KINDS]
+
+
+def merge_body(members, sp, *refs):
     out_ref = refs[members]
     total = tree_sum([part[...] for part in refs[:members]])
-    out_ref[...] = total[:width].astype(BF16)
-    refs[members + 1][...] = total[width : width + KINDS, :LANE]
+    out_ref[...] = total.astype(BF16)
 
 
 def weight_body(groups, planes, width, sp, *refs):
@@ -598,17 +601,19 @@
 
     direct = [o for o in range(1, groups) if o & (o - 1) == 0]
     far = [o for o in range(1, groups) if o & (o - 1)]
-    partial = call(
-        project_body,
+    copy_shape = shape_of((length, span), BF16)
+    copy_spec = whole((length, span))
+    partial, *copies = call(
+        functools.partial(project_body, far),
         (groups,),
         [
             pl.BlockSpec((length, span), lambda o, sp: (0, o ^ sp[1])),
             pl.BlockSpec((span, bc_width), lambda o, sp: (sp[0] * groups + (o ^ sp[1]), 0)),
             pl.BlockSpec((head_count, span), lambda o, sp: (0, sp[0] * groups + (o ^ sp[1]))),
         ],
-        whole((length, proj_width)),
-        shape_of((length, proj_width), F32),
-        us=3,
+        [whole((length, proj_width))] + [copy_spec] * len(far),
+        [shape_of((length, proj_width), F32)] + [copy_shape] * len(far),
+        us=1,
         vmem=VMEM_WIDE,
     )(sp, teacher_rows, state_proj, step_proj.T)
     projs = members_of(partial)
@@ -619,8 +624,7 @@
             for o in offsets
         ]
 
-    copy_shape = shape_of((length, span), BF16)
-    copy_spec = whole((length, span))
+    far_rows = {o: in_plane(copy, o) for o, copy in zip(far, copies)}
 
     message_shape = (states + TAIL, span)
     local_shape = (states + length // HEADS + TAIL, span)
@@ -640,20 +644,21 @@
         ]
         + [shape_of(message_shape, BF16)] * groups,
         [pltpu.VMEM((LANE, length), F32), pltpu.VMEM((groups, TABLE, length), F32)],
-        us=5,
+        us=1,
     )(sp, *projs, teacher_rows, params)
     messages = exchanged(messages)
 
     err, *outs = call(
         functools.partial(local_body, groups, local_heads),
         (groups,),
-        [whole((length, bc_width)), group_rows, group_cols, group_wide, group_wide, whole(params.shape)],
+        [whole((length, bc_width)), group_rows, group_cols, group_wide, group_wide, whole(params.shape)]
+        + [AFTER] * len(far),
         [group_wide] + [whole(local_shape)] * groups,
         [shape_of((length, local_width), F32)]
         + [shape_of(local_shape, BF16)] * groups,
         [pltpu.VMEM((length, length), F32)],
         us=7,
-    )(sp, bc, rows, cols, teacher_rows, teacher_next, params)
+    )(sp, bc, rows, cols, teacher_rows, teacher_next, params, *far_rows.values())
     local_grads = exchanged(outs)
 
     stack_shape = (groups,) + state_shape
@@ -718,26 +723,22 @@
     moved_rows = {o: in_plane(copy, o) for o, copy in zip(direct, copies)}
 
     outs = call(
-        functools.partial(forward_body, groups, count, len(far)),
+        functools.partial(forward_body, groups, count),
         (1,),
         [whole(stack_shape), whole(decay_shape), whole(stack_shape)]
         + [whole(piece_shape)] * count
-        + [whole(local_shape)] * groups
-        + row_blocks(far),
+        + [whole(local_shape)] * groups,
         [whole(state_shape)] * groups
         + [whole(stack_shape), whole(state_shape)]
-        + [whole(piece_shape)] * count
-        + [copy_spec] * len(far),
+        + [whole(piece_shape)] * count,
         [shape_of(state_shape, BF16)] * groups
         + [shape_of(stack_shape, F32), shape_of(state_shape, F32)]
-        + [shape_of(piece_shape, BF16)] * count
-        + [copy_shape] * len(far),
+        + [shape_of(piece_shape, BF16)] * count,
         [pltpu.VMEM(stack_shape, BF16), pltpu.VMEM(state_shape, BF16)],
         us=2,
-    )(sp, inc, decays, moments, *before, *local_grads, *[teacher_rows] * len(far))
+    )(sp, inc, decays, moments, *before, *local_grads)
     entering = exchanged(outs[:groups])
-    grads, grad_total, *grad_sent = outs[groups : groups + 2 + count]
-    far_rows = {o: in_plane(copy, o) for o, copy in zip(far, outs[groups + 2 + count :])}
+    grads, grad_total, *grad_sent = outs[groups:]
     moved_rows = [(moved_rows | far_rows)[o] for o in range(1, groups)]
 
     if shared:
@@ -804,11 +805,11 @@
         (1,),
         [whole(stack_shape), whole(decay_shape)]
         + [whole(piece_shape)] * count
-        + [AFTER] * (1 + len(far)),
+        + [AFTER],
         [whole(state_shape)] * groups,
         [shape_of(state_shape, BF16)] * groups,
         [pltpu.VMEM(stack_shape, BF16), pltpu.VMEM(state_shape, BF16)],
-    )(sp, grads, decays, *after, orders[0], *[moved_rows[o - 1] for o in far])
+    )(sp, grads, decays, *after, orders[0])
     for o in range(2, groups):
         error_part(o, leaving[0])
     leaving = exchanged(leaving)
@@ -841,8 +842,8 @@
         input_grads.append(one_grad)
 
     width = bc_width + head_count
-    grad_rows = (width + TAIL, length)
-    partial_grads = call(
+    grad_shape = (width, length)
+    partial_grads, small = call(
         functools.partial(finish_body, groups, local_heads, scale),
         (1,),
         [
@@ -856,18 +857,17 @@
         + [whole((2 * HEADS, LANE))] * groups
         + [whole((HEADS, length))] * groups
         + [whole((HEADS, LANE))] * groups,
-        whole(grad_rows),
-        shape_of(grad_rows, F32),
+        [whole(grad_shape), whole((KINDS, LANE))],
+        [shape_of(grad_shape, F32), shape_of((KINDS, LANE), F32)],
         [pltpu.VMEM((LANE, LANE), F32)],
         us=2,
     )(sp, bc, rows, params, totals[-1], input_grads[-1], *sums, *heads, *pulls, *mets)
-    grad_shape = (width, length)
-    merged, small = call(
-        functools.partial(merge_body, dp_count, width),
+    merged = call(
+        functools.partial(merge_body, dp_count),
         (1,),
-        [whole(grad_rows)] * dp_count,
-        [whole(grad_shape), whole((KINDS, LANE))],
-        [shape_of(grad_shape, BF16), shape_of((KINDS, LANE), F32)],
+        [whole(grad_shape)] * dp_count,
+        whole(grad_shape),
+        shape_of(grad_shape, BF16),
     )(sp, *members_of(partial_grads))
     step = 1
     while step < planes:
@@ -895,6 +895,7 @@
     while step < groups:
         small = small + in_plane(small, step)
         step *= 2
+    small = tree_sum(members_of(small))
     own = call(
         functools.partial(total_body, planes),
         (1,),
@@ -915,6 +916,9 @@
     gathered = all_over(own, over_planes, planes)
     pieces = []
     for k, part in enumerate(gathered):
+        if k == planes - 1:
+            pieces.append({o: in_plane(part, o) if o else part for o in range(groups)})
+            continue
         spread = {0: part}
         steps = [1 << i for i in range(groups.bit_length() - 1)]
         for step in steps if k % 2 else steps[::-1]:

time: 174 us -> 167 us (0.960)
  waiting for transfers between devices: 46.8 us -> 37 us
    ppermute x32, waiting for transfers between devices: 22.9 us -> 11.6 us  [in_plane(): return lax.ppermute(value, 'seq', pairs)]
    ppermute x32, starting transfers between devices: 35 us -> 39.5 us  [in_plane(): return lax.ppermute(value, 'seq', pairs)]
    ppermute x20, starting transfers between devices: 31.9 us -> 29 us  [over_planes(): return lax.ppermute(value, 'seq', pairs)]
    ppermute x2 -> x3, waiting for transfers between devices: 3.08 us -> 4.58 us  [members_of(): return [value] + [lax.ppermute(value, 'dp', pair) for pair in pairs]]
  transfers between devices with their start and end apart: 54 -> 55, of which waited for: 21 -> 17; matrix products, arithmetic and copies ran while one was open for 1% -> 1% of each run, Pallas kernels for 22% -> 25%
where the time goes in v3:
time: 167 us; the launch traced here: 166 us
  starting transfers between devices  68.6 us (41%)
  Pallas kernels  53.7 us (32%)
  waiting for transfers between devices  37 us (22%)
  local copies, waits for them, and re-layouts  2.71 us (2%)
  between operations  2.7 us (2%)
  other arithmetic  1.73 us (1%)
    ppermute x32, starting transfers between devices, in_plane(): return lax.ppermute(value, 'seq', pairs)  39.5 us
    ppermute x20, starting transfers between devices, over_planes(): return lax.ppermute(value, 'seq', pairs)  29 us
    ppermute x20, waiting for transfers between devices, over_planes(): return lax.ppermute(value, 'seq', pairs)  20.8 us
    pallas_call x4, Pallas kernels, error_part(): call(functools.partial(error_body, o == 0, local_heads, o), (1,), [whole(...  11.9 us
    ppermute x32, waiting for transfers between devices, in_plane(): return lax.ppermute(value, 'seq', pairs)  11.6 us
    pallas_call x1, Pallas kernels, shards(): call(functools.partial(local_body, groups, local_heads), (groups,), [whol...  7.55 us
    pallas_call x4, Pallas kernels, shards(): call(functools.partial(spread_body, planes), (1,), [whole(share_shape)] *...  7.22 us
    pallas_call x1, Pallas kernels, shards(): call(functools.partial(project_body, far), (groups,), [pl.BlockSpec((leng...  5.66 us
  transfers between devices with their start and end apart: 55, of which 17 were waited for; matrix products, arithmetic and copies ran while one was open for 1% of the time, Pallas kernels for 25%

profile of v3, /device:TPU:0, one launch (start us, length us, event | category | flops | bytes accessed | tf_op | source)
XLA Modules:
  0.0 166.4 jit_solution(10349819998054986567)
XLA Ops:
  1.3 5.7 %shard_map.118 = (f32[256,384]{1,0:T(8,128)}, bf16[256,1024]{1,0:T(8,128)(2,1)}) custom-call(s32[3]{0:T(128)} %pad_add_fusion.sp, bf16[256,4096]{1,0:T(8,128)(2,1)} %refs_4_.3, bf16[8192,256]{1,0:T(8,128)(2,1)} %wb_ref.1, bf16[64,8192]{1,0:T(8,128)(2,1)} %bitcast.15), custom_call_target="tpu_custom_call" | custom-call | flops 1100000000 | tf_op jit(solution)/shard_map/pallas_call | solution.py:606
  6.9 3.9 %collective-permute-start.1 = (bf16[256,1024]{1,0:T(8,128)(2,1)}, bf16[256,1024]{1,0:T(8,128)(2,1)S(1)}, u32[]{:S(2)}, u32[]{:S(2)}) collective-permute-start(bf16[256,1024]{1,0:T(8,128)(2,1)} %get-tuple-element.93), channel_id=1, source_target_pairs={{0,6},{2,4},{4,2},{6,0},{8,14},{10,12},{12,10},{14,8},{16,22},{18,... | collective-permute-start | bytes 1572872 | tf_op jit(solution)/shard_map/ppermute | solution.py:583
  13.8 3.9 %shard_map.119 = (bf16[256,256]{1,0:T(8,128)(2,1)S(1)}, f32[4,48,256]{2,1,0:T(8,128)S(1)}, f32[4,256,128]{2,1,0:T(8,128)S(1)}, bf16[144,1024]{1,0:T(8,128)(2,1)S...) custom-call(s32[3]{0:T(128)S(1)} %copy-done.1, ...), custom_call_target="tpu_custom_call" | custom-call | flops 1100000000 | tf_op jit(solution)/shard_map/pallas_call | solution.py:635
  18.3 2.9 %collective-permute-start.4 = (bf16[144,1024]{1,0:T(8,128)(2,1)S(1)}, bf16[144,1024]{1,0:T(8,128)(2,1)S(1)}, u32[]{:S(2)}, u32[]{:S(2)}) collective-permute-start(bf16[144,1024]{1,0:T(8,128)(2,1)S(1)} %get-tuple-element.98), channel_id=1, source_target_pairs={{0,6},{2,4},{4,2},{6,0},{8,14},{10,12},{12,10},{14,8},{16,22},{18,... | collective-permute-start | bytes 884744 | tf_op jit(solution)/shard_map/ppermute | solution.py:583
  21.2 2.6 %collective-permute-done.1.rest_0_.refs_7_ = bf16[256,1024]{1,0:T(8,128)(2,1)S(1)} collective-permute-done((bf16[256,1024]{1,0:T(8,128)(2,1)}, bf16[256,1024]{1,0:T(8,128)(2,1)S(1)}, u32[]{:S(2)}, u32[]{:S(2)}) %collective-permute-start.1) | collective-permute-done | bytes 524320 | tf_op jit(solution)/shard_map/ppermute | solution.py:583
  25.4 7.6 %shard_map.120 = (f32[256,4096]{1,0:T(8,128)S(1)}, bf16[176,1024]{1,0:T(8,128)(2,1)S(1)}, bf16[176,1024]{1,0:T(8,128)(2,1)S(1)}, bf16[176,1024]{1,0:T(8,128)(2,1)S(1)}, bf16[176,1024]{1,0:T(8,128)(2,1)S(1)}) custom-call(s32[3]{0:T(128)S(1)} %copy-done.1, bf16[256,256]{1,0:T(8,128)(2,1)S(1)} %get-tuple-element.90.bc_ref, ...), custom_call_target="tpu_custom_call" | custom-call | flops 7699999744 | tf_op jit(solution)/shard_map/pallas_call | solution.py:651
  33.0 2.1 %collective-permute-start.5 = (bf16[176,1024]{1,0:T(8,128)(2,1)S(1)}, bf16[176,1024]{1,0:T(8,128)(2,1)S(1)}, u32[]{:S(2)}, u32[]{:S(2)}) collective-permute-start(bf16[176,1024]{1,0:T(8,128)(2,1)S(1)} %get-tuple-element.102), channel_id=1, source_target_pairs={{0,2},{2,0},{4,6},{6,4},{8,10},{10,8},{12,14},{14,12},{16,18},{18,... | collective-permute-start | bytes 1081352 | tf_op jit(solution)/shard_map/ppermute | solution.py:583
  38.3 2.0 %collective-permute-start.8 = (bf16[144,256]{1,0:T(8,128)(2,1)S(1)}, bf16[144,256]{1,0:T(8,128)(2,1)S(1)}, u32[]{:S(2)}, u32[]{:S(2)}) collective-permute-start(bf16[144,256]{1,0:T(8,128)(2,1)S(1)} %get-tuple-element.106), channel_id=1, source_target_pairs={{0,8},{2,10},{4,12},{6,14},{8,0},{10,2},{12,4},{14,6},{16,24},{18,... | collective-permute-start | bytes 221192 | tf_op jit(solution)/shard_map/ppermute | solution.py:587
  40.3 2.6 %collective-permute-start.9 = (bf16[144,256]{1,0:T(8,128)(2,1)S(1)}, bf16[144,256]{1,0:T(8,128)(2,1)S(1)}, u32[]{:S(2)}, u32[]{:S(2)}) collective-permute-start(bf16[144,256]{1,0:T(8,128)(2,1)S(1)} %get-tuple-element.107), channel_id=1, source_target_pairs={{0,16},{2,18},{4,20},{6,22},{8,24},{10,26},{12,28},{14,30},{16,0},... | collective-permute-start | bytes 221192 | tf_op jit(solution)/shard_map/ppermute | solution.py:587
  42.9 3.8 %collective-permute-start.10 = (bf16[144,256]{1,0:T(8,128)(2,1)S(1)}, bf16[144,256]{1,0:T(8,128)(2,1)S(1)}, u32[]{:S(2)}, u32[]{:S(2)}) collective-permute-start(bf16[144,256]{1,0:T(8,128)(2,1)S(1)} %get-tuple-element.108), channel_id=1, source_target_pairs={{0,24},{2,26},{4,28},{6,30},{8,16},{10,18},{12,20},{14,22},{16,8},... | collective-permute-start | bytes 221192 | tf_op jit(solution)/shard_map/ppermute | solution.py:587
  47.0 2.2 %collective-permute-done.10.refs_3_ = bf16[144,256]{1,0:T(8,128)(2,1)S(1)} collective-permute-done((bf16[144,256]{1,0:T(8,128)(2,1)S(1)}, bf16[144,256]{1,0:T(8,128)(2,1)S(1)}, u32[]{:S(2)}, u32[]{:S(2)}) %collective-permute-start.10) | collective-permute-done | bytes 73760 | tf_op jit(solution)/shard_map/ppermute | solution.py:587
  50.8 3.5 %collective-permute-start.12 = (bf16[128,256]{1,0:T(8,128)(2,1)S(1)}, bf16[128,256]{1,0:T(8,128)(2,1)S(1)}, u32[]{:S(2)}, u32[]{:S(2)}) collective-permute-start(bf16[128,256]{1,0:T(8,128)(2,1)S(1)} %get-tuple-element.111), channel_id=1, source_target_pairs={{0,16},{2,18},{4,20},{6,22},{8,24},{10,26},{12,28},{14,30},{16,0},... | collective-permute-start | bytes 196616 | tf_op jit(solution)/shard_map/ppermute | solution.py:587
  57.6 2.2 %shard_map.122.moment_ref = bf16[4,128,1024]{2,1,0:T(8,128)(2,1)S(1)} custom-call(s32[3]{0:T(128)S(1)} %copy-done.1, bf16[176,1024]{1,0:T(8,128)(2,1)S(1)} %get-tuple-element.101.refs_0_.refs_4_, bf16[176,1024]{1,0:T(8,128)(2,1)S(1)} %collective-permute-done.5.refs_1_.refs_5_, bf16[176,1024]{1,0:T(8,128)(2,1)S(1)} %collective-permute-done.6.refs_2_.refs_6_, ...), custom_call_target="tpu_custom_call" | custom-call | flops 2200000000 | tf_op jit(solution)/shard_map/pallas_call | solution.py:684
  60.4 2.5 %shard_map.124 = (bf16[128,1024]{1,0:T(8,128)(2,1)S(1)}, bf16[128,1024]{1,0:T(8,128)(2,1)S(1)}, bf16[128,1024]{1,0:T(8,128)(2,1)S(1)}, bf16[128,1024]{1,0:T(8,12...) custom-call(s32[3]{0:T(128)S(1)} %copy-done.1, ...), custom_call_target="tpu_custom_call" | custom-call | flops 2200000000 | tf_op jit(solution)/shard_map/pallas_call | solution.py:725
  62.9 3.6 %collective-permute-start.18 = (bf16[128,256]{1,0:T(8,128)(2,1)S(1)}, bf16[128,256]{1,0:T(8,128)(2,1)S(1)}, u32[]{:S(2)}, u32[]{:S(2)}) collective-permute-start(bf16[128,256]{1,0:T(8,128)(2,1)S(1)} %get-tuple-element.121), channel_id=1, source_target_pairs={{0,16},{2,18},{4,20},{6,22},{8,24},{10,26},{12,28},{14,30},{16,0},... | collective-permute-start | bytes 196616 | tf_op jit(solution)/shard_map/ppermute | solution.py:587
  68.8 2.9 %shard_map.125 = (f32[16,256]{1,0:T(8,128)S(1)}, f32[16,128]{1,0:T(8,128)S(1)}, f32[256,384]{1,0:T(8,128)S(1)}, f32[8,128]{1,0:T(8,128)S(1)}) custom-call(s32[3]{0:T(128)S(1)} %copy-done.1, bf16[256,256]{1,0:T(8,128)(2,1)S(1)} %get-tuple-element.90.bc_ref, f32[4,48,256]{2,1,0:T(8,128)S(1)} %get-tuple-element.91.rows_ref, ...), custom_call_target="tpu_custom_call" | custom-call | flops 4400000000 | tf_op jit(solution)/shard_map/pallas_call | solution.py:766
  74.8 3.3 %collective-permute-start.23 = (bf16[128,256]{1,0:T(8,128)(2,1)S(1)}, bf16[128,256]{1,0:T(8,128)(2,1)S(1)}, u32[]{:S(2)}, u32[]{:S(2)}) collective-permute-start(bf16[128,256]{1,0:T(8,128)(2,1)S(1)} %get-tuple-element.129), channel_id=1, source_target_pairs={{0,16},{2,18},{4,20},{6,22},{8,24},{10,26},{12,28},{14,30},{16,0},... | collective-permute-start | bytes 196616 | tf_op jit(solution)/shard_map/ppermute | solution.py:587
  79.2 3.0 %shard_map.127 = (f32[16,256]{1,0:T(8,128)S(1)}, f32[16,128]{1,0:T(8,128)S(1)}, f32[256,384]{1,0:T(8,128)S(1)}, f32[8,128]{1,0:T(8,128)}) custom-call(s32[3]{0:T(128)S(1)} %copy-done.1, bf16[256,256]{1,0:T(8,128)(2,1)S(1)} %get-tuple-element.90.bc_ref, f32[4,48,256]{2,1,0:T(8,128)S(1)} %get-tuple-element.91.rows_ref, ...), custom_call_target="tpu_custom_call" | custom-call | flops 4400000000 | tf_op jit(solution)/shard_map/pallas_call | solution.py:766
  82.2 2.0 %collective-permute-done.24.refs_3_ = bf16[128,256]{1,0:T(8,128)(2,1)S(1)} collective-permute-done((bf16[128,256]{1,0:T(8,128)(2,1)S(1)}, bf16[128,256]{1,0:T(8,128)(2,1)S(1)}, u32[]{:S(2)}, u32[]{:S(2)}) %collective-permute-start.24) | collective-permute-done | bytes 65568 | tf_op jit(solution)/shard_map/ppermute | solution.py:587
  88.7 3.1 %shard_map.129 = (f32[16,256]{1,0:T(8,128)S(1)}, f32[16,128]{1,0:T(8,128)S(1)}, f32[256,384]{1,0:T(8,128)S(1)}, f32[8,128]{1,0:T(8,128)}) custom-call(s32[3]{0:T(128)S(1)} %copy-done.1, bf16[256,256]{1,0:T(8,128)(2,1)S(1)} %get-tuple-element.90.bc_ref, f32[4,48,256]{2,1,0:T(8,128)S(1)} %get-tuple-element.91.rows_ref, ...), custom_call_target="tpu_custom_call" | custom-call | flops 4400000000 | tf_op jit(solution)/shard_map/pallas_call | solution.py:766
  91.8 3.0 %shard_map.130 = (f32[16,256]{1,0:T(8,128)S(1)}, f32[16,128]{1,0:T(8,128)S(1)}, f32[256,384]{1,0:T(8,128)S(1)}, f32[8,128]{1,0:T(8,128)}) custom-call(s32[3]{0:T(128)S(1)} %copy-done.1, bf16[256,256]{1,0:T(8,128)(2,1)S(1)} %get-tuple-element.90.bc_ref, f32[4,48,256]{2,1,0:T(8,128)S(1)} %get-tuple-element.91.rows_ref, ...), custom_call_target="tpu_custom_call" | custom-call | flops 4400000000 | tf_op jit(solution)/shard_map/pallas_call | solution.py:766
  106.7 3.6 %collective-permute-done.28 = f32[8,128]{1,0:T(8,128)S(1)} collective-permute-done((f32[8,128]{1,0:T(8,128)S(1)}, f32[8,128]{1,0:T(8,128)S(1)}, u32[]{:S(2)}, u32[]{:S(2)}) %collective-permute-start.28) | collective-permute-done | bytes 4128 | tf_op jit(solution)/shard_map/ppermute | solution.py:587
  110.3 4.5 %collective-permute-done.29 = f32[8,128]{1,0:T(8,128)S(1)} collective-permute-done((f32[8,128]{1,0:T(8,128)S(1)}, f32[8,128]{1,0:T(8,128)S(1)}, u32[]{:S(2)}, u32[]{:S(2)}) %collective-permute-start.29) | collective-permute-done | bytes 4128 | tf_op jit(solution)/shard_map/ppermute | solution.py:587
  118.0 2.7 %collective-permute-start.39 = (bf16[80,1024]{1,0:T(8,128)(2,1)S(1)}, bf16[80,1024]{1,0:T(8,128)(2,1)S(1)}, u32[]{:S(2)}, u32[]{:S(2)}) collective-permute-start(bf16[80,1024]{1,0:T(8,128)(2,1)S(1)} %get-tuple-element.163), channel_id=1, source_target_pairs={{0,24},{2,26},{4,28},{6,30},{8,16},{10,18},{12,20},{14,22},{16,8},... | collective-permute-start | bytes 491528 | tf_op jit(solution)/shard_map/ppermute | solution.py:587
  121.8 2.6 %collective-permute-done.30 = f32[8,128]{1,0:T(8,128)S(1)} collective-permute-done((f32[8,128]{1,0:T(8,128)S(1)}, f32[8,128]{1,0:T(8,128)S(1)}, u32[]{:S(2)}, u32[]{:S(2)}) %collective-permute-start.30) | collective-permute-done | bytes 4128 | tf_op jit(solution)/shard_map/ppermute | solution.py:583
  124.8 3.2 %collective-permute-done.31 = f32[8,128]{1,0:T(8,128)S(1)} collective-permute-done((f32[8,128]{1,0:T(8,128)S(1)}, f32[8,128]{1,0:T(8,128)S(1)}, u32[]{:S(2)}, u32[]{:S(2)}) %collective-permute-start.31) | collective-permute-done | bytes 4128 | tf_op jit(solution)/shard_map/ppermute | solution.py:583
  131.3 2.9 %collective-permute-start.45 = (bf16[80,1024]{1,0:T(8,128)(2,1)S(1)}, bf16[80,1024]{1,0:T(8,128)(2,1)S(1)}, u32[]{:S(2)}, u32[]{:S(2)}) collective-permute-start(bf16[80,1024]{1,0:T(8,128)(2,1)S(1)} %shard_map.138.refs_0_), channel_id=1, source_target_pairs={{0,16},{2,18},{4,20},{6,22},{8,24},{10,26},{12,28},{14,30},{16,0},... | collective-permute-start | bytes 491528 | tf_op jit(solution)/shard_map/ppermute | solution.py:587
  135.9 5.0 %collective-permute-done.45.refs_2_ = bf16[80,1024]{1,0:T(8,128)(2,1)S(1)} collective-permute-done((bf16[80,1024]{1,0:T(8,128)(2,1)S(1)}, bf16[80,1024]{1,0:T(8,128)(2,1)S(1)}, u32[]{:S(2)}, u32[]{:S(2)}) %collective-permute-start.45) | collective-permute-done | bytes 163872 | tf_op jit(solution)/shard_map/ppermute | solution.py:587
  152.7 1.9 %collective-permute-start.49 = (bf16[80,1024]{1,0:T(8,128)(2,1)S(1)}, bf16[80,1024]{1,0:T(8,128)(2,1)S(1)}, u32[]{:S(2)}, u32[]{:S(2)}) collective-permute-start(bf16[80,1024]{1,0:T(8,128)(2,1)S(1)} %collective-permute-done.48.refs_3_), channel_id=1, source_target_pairs={{0,6},{2,4},{4,2},{6,0},{8,14},{10,12},{12,10},{14,8},{16,22},{18,... | collective-permute-start | bytes 491528 | tf_op jit(solution)/shard_map/ppermute | solution.py:583
  158.5 1.8 %shard_map.141 = (f32[4096,256]{1,0:T(8,128)}, f32[64,4096]{1,0:T(8,128)}) custom-call(s32[3]{0:T(128)S(1)} %copy-done.1, bf16[80,1024]{1,0:T(8,128)(2,1)S(1)} %collective-permute-done.40.refs_0_, bf16[80,1024]{1,0:T(8,128)(2,1)S(1)} %collective-permute-done.50.refs_1_, ...), custom_call_target="tpu_custom_call", output_to_operand_aliasing={{0}: (5, {}), {1}: (6, {})} | custom-call | flops 1100000000 | tf_op jit(solution)/shard_map/pallas_call | solution.py:929
  160.3 2.6 %collective-permute-done.49.refs_3_ = bf16[80,1024]{1,0:T(8,128)(2,1)S(1)} collective-permute-done((bf16[80,1024]{1,0:T(8,128)(2,1)S(1)}, bf16[80,1024]{1,0:T(8,128)(2,1)S(1)}, u32[]{:S(2)}, u32[]{:S(2)}) %collective-permute-start.49) | collective-permute-done | bytes 163872 | tf_op jit(solution)/shard_map/ppermute | solution.py:583
  163.5 1.8 %shard_map.142 = (f32[4096,256]{1,0:T(8,128)}, f32[64,4096]{1,0:T(8,128)}) custom-call(s32[3]{0:T(128)S(1)} %copy-done.1, bf16[80,1024]{1,0:T(8,128)(2,1)S(1)} %collective-permute-done.41.refs_0_, bf16[80,1024]{1,0:T(8,128)(2,1)S(1)} %collective-permute-done.44.refs_1_, ...), custom_call_target="tpu_custom_call", output_to_operand_aliasing={{0}: (5, {}), {1}: (6, {})} | custom-call | flops 1100000000 | tf_op jit(solution)/shard_map/pallas_call | solution.py:929
  (128 shorter events, 63.0 us)
Async XLA Ops:
  6.9 16.9 %collective-permute-start.1 = (bf16[256,1024]{1,0:T(8,128)(2,1)}, bf16[256,1024]{1,0:T(8,128)(2,1)S(1)}, u32[]{:S(2)}, u32[]{:S(2)}) collective-permute-start(bf16[256,1024]{1,0:T(8,128)(2,1)} %get-tuple-element.93), channel_id=1, source_target_pairs={{0,6},{2,4},{4,2},{6,0},{8,14},{10,12},{12,10},{14,8},{16,22},{18,... | collective-permute-start | bytes 1572872 | tf_op jit(solution)/shard_map/ppermute | solution.py:583
  17.7 18.9 %collective-permute-start.2 = (bf16[144,1024]{1,0:T(8,128)(2,1)S(1)}, bf16[144,1024]{1,0:T(8,128)(2,1)S(1)}, u32[]{:S(2)}, u32[]{:S(2)}) collective-permute-start(bf16[144,1024]{1,0:T(8,128)(2,1)S(1)} %get-tuple-element.96), channel_id=1, source_target_pairs={{0,2},{2,0},{4,6},{6,4},{8,10},{10,8},{12,14},{14,12},{16,18},{18,... | collective-permute-start | bytes 884744 | tf_op jit(solution)/shard_map/ppermute | solution.py:583
  18.3 18.3 %collective-permute-start.3 = (bf16[144,1024]{1,0:T(8,128)(2,1)S(1)}, bf16[144,1024]{1,0:T(8,128)(2,1)S(1)}, u32[]{:S(2)}, u32[]{:S(2)}) collective-permute-start(bf16[144,1024]{1,0:T(8,128)(2,1)S(1)} %get-tuple-element.97), channel_id=1, source_target_pairs={{0,4},{2,6},{4,0},{6,2},{8,12},{10,14},{12,8},{14,10},{16,20},{18,... | collective-permute-start | bytes 884744 | tf_op jit(solution)/shard_map/ppermute | solution.py:583
  18.3 18.3 %collective-permute-start.4 = (bf16[144,1024]{1,0:T(8,128)(2,1)S(1)}, bf16[144,1024]{1,0:T(8,128)(2,1)S(1)}, u32[]{:S(2)}, u32[]{:S(2)}) collective-permute-start(bf16[144,1024]{1,0:T(8,128)(2,1)S(1)} %get-tuple-element.98), channel_id=1, source_target_pairs={{0,6},{2,4},{4,2},{6,0},{8,14},{10,12},{12,10},{14,8},{16,22},{18,... | collective-permute-start | bytes 884744 | tf_op jit(solution)/shard_map/ppermute | solution.py:583
  33.0 21.3 %collective-permute-start.5 = (bf16[176,1024]{1,0:T(8,128)(2,1)S(1)}, bf16[176,1024]{1,0:T(8,128)(2,1)S(1)}, u32[]{:S(2)}, u32[]{:S(2)}) collective-permute-start(bf16[176,1024]{1,0:T(8,128)(2,1)S(1)} %get-tuple-element.102), channel_id=1, source_target_pairs={{0,2},{2,0},{4,6},{6,4},{8,10},{10,8},{12,14},{14,12},{16,18},{18,... | collective-permute-start | bytes 1081352 | tf_op jit(solution)/shard_map/ppermute | solution.py:583
  35.0 19.3 %collective-permute-start.6 = (bf16[176,1024]{1,0:T(8,128)(2,1)S(1)}, bf16[176,1024]{1,0:T(8,128)(2,1)S(1)}, u32[]{:S(2)}, u32[]{:S(2)}) collective-permute-start(bf16[176,1024]{1,0:T(8,128)(2,1)S(1)} %get-tuple-element.103), channel_id=1, source_target_pairs={{0,4},{2,6},{4,0},{6,2},{8,12},{10,14},{12,8},{14,10},{16,20},{18,... | collective-permute-start | bytes 1081352 | tf_op jit(solution)/shard_map/ppermute | solution.py:583
  36.6 19.5 %collective-permute-start.7 = (bf16[176,1024]{1,0:T(8,128)(2,1)S(1)}, bf16[176,1024]{1,0:T(8,128)(2,1)S(1)}, u32[]{:S(2)}, u32[]{:S(2)}) collective-permute-start(bf16[176,1024]{1,0:T(8,128)(2,1)S(1)} %get-tuple-element.104), channel_id=1, source_target_pairs={{0,6},{2,4},{4,2},{6,0},{8,14},{10,12},{12,10},{14,8},{16,22},{18,... | collective-permute-start | bytes 1081352 | tf_op jit(solution)/shard_map/ppermute | solution.py:583
  49.9 10.0 %collective-permute-start.11 = (bf16[128,256]{1,0:T(8,128)(2,1)S(1)}, bf16[128,256]{1,0:T(8,128)(2,1)S(1)}, u32[]{:S(2)}, u32[]{:S(2)}) collective-permute-start(bf16[128,256]{1,0:T(8,128)(2,1)S(1)} %get-tuple-element.110), channel_id=1, source_target_pairs={{0,8},{2,10},{4,12},{6,14},{8,0},{10,2},{12,4},{14,6},{16,24},{18,... | collective-permute-start | bytes 196616 | tf_op jit(solution)/shard_map/ppermute | solution.py:587
  50.8 9.1 %collective-permute-start.12 = (bf16[128,256]{1,0:T(8,128)(2,1)S(1)}, bf16[128,256]{1,0:T(8,128)(2,1)S(1)}, u32[]{:S(2)}, u32[]{:S(2)}) collective-permute-start(bf16[128,256]{1,0:T(8,128)(2,1)S(1)} %get-tuple-element.111), channel_id=1, source_target_pairs={{0,16},{2,18},{4,20},{6,22},{8,24},{10,26},{12,28},{14,30},{16,0},... | collective-permute-start | bytes 196616 | tf_op jit(solution)/shard_map/ppermute | solution.py:587
  54.3 19.8 %collective-permute-start.20 = (bf16[256,1024]{1,0:T(8,128)(2,1)S(1)}, bf16[256,1024]{1,0:T(8,128)(2,1)S(1)}, u32[]{:S(2)}, u32[]{:S(2)}) collective-permute-start(bf16[256,1024]{1,0:T(8,128)(2,1)S(1)} %get-tuple-element.123), channel_id=1, source_target_pairs={{0,2},{2,0},{4,6},{6,4},{8,10},{10,8},{12,14},{14,12},{16,18},{18,... | collective-permute-start | bytes 1572872 | tf_op jit(solution)/shard_map/ppermute | solution.py:583
  56.1 18.0 %collective-permute-start.21 = (bf16[256,1024]{1,0:T(8,128)(2,1)S(1)}, bf16[256,1024]{1,0:T(8,128)(2,1)S(1)}, u32[]{:S(2)}, u32[]{:S(2)}) collective-permute-start(bf16[256,1024]{1,0:T(8,128)(2,1)S(1)} %get-tuple-element.124), channel_id=1, source_target_pairs={{0,4},{2,6},{4,0},{6,2},{8,12},{10,14},{12,8},{14,10},{16,20},{18,... | collective-permute-start | bytes 1572872 | tf_op jit(solution)/shard_map/ppermute | solution.py:583
  62.9 8.8 %collective-permute-start.18 = (bf16[128,256]{1,0:T(8,128)(2,1)S(1)}, bf16[128,256]{1,0:T(8,128)(2,1)S(1)}, u32[]{:S(2)}, u32[]{:S(2)}) collective-permute-start(bf16[128,256]{1,0:T(8,128)(2,1)S(1)} %get-tuple-element.121), channel_id=1, source_target_pairs={{0,16},{2,18},{4,20},{6,22},{8,24},{10,26},{12,28},{14,30},{16,0},... | collective-permute-start | bytes 196616 | tf_op jit(solution)/shard_map/ppermute | solution.py:587
  67.3 10.8 %collective-permute-start.16 = (bf16[128,1024]{1,0:T(8,128)(2,1)S(1)}, bf16[128,1024]{1,0:T(8,128)(2,1)S(1)}, u32[]{:S(2)}, u32[]{:S(2)}) collective-permute-start(bf16[128,1024]{1,0:T(8,128)(2,1)S(1)} %get-tuple-element.115), channel_id=1, source_target_pairs={{0,2},{2,0},{4,6},{6,4},{8,10},{10,8},{12,14},{14,12},{16,18},{18,... | collective-permute-start | bytes 786440 | tf_op jit(solution)/shard_map/ppermute | solution.py:583
  71.7 20.1 %collective-permute-start.14 = (bf16[128,1024]{1,0:T(8,128)(2,1)S(1)}, bf16[128,1024]{1,0:T(8,128)(2,1)S(1)}, u32[]{:S(2)}, u32[]{:S(2)}) collective-permute-start(bf16[128,1024]{1,0:T(8,128)(2,1)S(1)} %get-tuple-element.113), channel_id=1, source_target_pairs={{0,6},{2,4},{4,2},{6,0},{8,14},{10,12},{12,10},{14,8},{16,22},{18,... | collective-permute-start | bytes 786440 | tf_op jit(solution)/shard_map/ppermute | solution.py:583
  73.5 15.3 %collective-permute-start.15 = (bf16[128,1024]{1,0:T(8,128)(2,1)S(1)}, bf16[128,1024]{1,0:T(8,128)(2,1)S(1)}, u32[]{:S(2)}, u32[]{:S(2)}) collective-permute-start(bf16[128,1024]{1,0:T(8,128)(2,1)S(1)} %get-tuple-element.114), channel_id=1, source_target_pairs={{0,4},{2,6},{4,0},{6,2},{8,12},{10,14},{12,8},{14,10},{16,20},{18,... | collective-permute-start | bytes 786440 | tf_op jit(solution)/shard_map/ppermute | solution.py:583
  85.2 13.4 %collective-permute-start.25 = (bf16[128,1024]{1,0:T(8,128)(2,1)S(1)}, bf16[128,1024]{1,0:T(8,128)(2,1)S(1)}, u32[]{:S(2)}, u32[]{:S(2)}) collective-permute-start(bf16[128,1024]{1,0:T(8,128)(2,1)S(1)} %get-tuple-element.135), channel_id=1, source_target_pairs={{0,6},{2,4},{4,2},{6,0},{8,14},{10,12},{12,10},{14,8},{16,22},{18,... | collective-permute-start | bytes 786440 | tf_op jit(solution)/shard_map/ppermute | solution.py:583
  86.1 11.3 %collective-permute-start.26 = (bf16[128,1024]{1,0:T(8,128)(2,1)S(1)}, bf16[128,1024]{1,0:T(8,128)(2,1)S(1)}, u32[]{:S(2)}, u32[]{:S(2)}) collective-permute-start(bf16[128,1024]{1,0:T(8,128)(2,1)S(1)} %get-tuple-element.136), channel_id=1, source_target_pairs={{0,4},{2,6},{4,0},{6,2},{8,12},{10,14},{12,8},{14,10},{16,20},{18,... | collective-permute-start | bytes 786440 | tf_op jit(solution)/shard_map/ppermute | solution.py:583
  103.2 11.7 %collective-permute-start.36 = (bf16[320,256]{1,0:T(8,128)(2,1)S(1)}, bf16[320,256]{1,0:T(8,128)(2,1)S(1)}, u32[]{:S(2)}, u32[]{:S(2)}) collective-permute-start(bf16[320,256]{1,0:T(8,128)(2,1)S(1)} %shard_map.136.refs_0_), channel_id=1, source_target_pairs={{0,6},{2,4},{4,2},{6,0},{8,14},{10,12},{12,10},{14,8},{16,22},{18,... | collective-permute-start | bytes 491528 | tf_op jit(solution)/shard_map/ppermute | solution.py:583
  104.1 10.8 %collective-permute-start.35 = (bf16[320,256]{1,0:T(8,128)(2,1)S(1)}, bf16[320,256]{1,0:T(8,128)(2,1)S(1)}, u32[]{:S(2)}, u32[]{:S(2)}) collective-permute-start(bf16[320,256]{1,0:T(8,128)(2,1)S(1)} %shard_map.136.refs_0_), channel_id=1, source_target_pairs={{0,4},{2,6},{4,0},{6,2},{8,12},{10,14},{12,8},{14,10},{16,20},{18,... | collective-permute-start | bytes 491528 | tf_op jit(solution)/shard_map/ppermute | solution.py:583
  105.7 9.1 %collective-permute-start.34 = (bf16[320,256]{1,0:T(8,128)(2,1)S(1)}, bf16[320,256]{1,0:T(8,128)(2,1)S(1)}, u32[]{:S(2)}, u32[]{:S(2)}) collective-permute-start(bf16[320,256]{1,0:T(8,128)(2,1)S(1)} %shard_map.136.refs_0_), channel_id=1, source_target_pairs={{0,2},{2,0},{4,6},{6,4},{8,10},{10,8},{12,14},{14,12},{16,18},{18,... | collective-permute-start | bytes 491528 | tf_op jit(solution)/shard_map/ppermute | solution.py:583
  116.3 12.8 %collective-permute-start.37 = (bf16[80,1024]{1,0:T(8,128)(2,1)S(1)}, bf16[80,1024]{1,0:T(8,128)(2,1)S(1)}, u32[]{:S(2)}, u32[]{:S(2)}) collective-permute-start(bf16[80,1024]{1,0:T(8,128)(2,1)S(1)} %get-tuple-element.161), channel_id=1, source_target_pairs={{0,8},{2,10},{4,12},{6,14},{8,0},{10,2},{12,4},{14,6},{16,24},{18,... | collective-permute-start | bytes 491528 | tf_op jit(solution)/shard_map/ppermute | solution.py:587
  116.4 14.2 %collective-permute-start.38 = (bf16[80,1024]{1,0:T(8,128)(2,1)S(1)}, bf16[80,1024]{1,0:T(8,128)(2,1)S(1)}, u32[]{:S(2)}, u32[]{:S(2)}) collective-permute-start(bf16[80,1024]{1,0:T(8,128)(2,1)S(1)} %get-tuple-element.162), channel_id=1, source_target_pairs={{0,16},{2,18},{4,20},{6,22},{8,24},{10,26},{12,28},{14,30},{16,0},... | collective-permute-start | bytes 491528 | tf_op jit(solution)/shard_map/ppermute | solution.py:587
  118.0 12.6 %collective-permute-start.39 = (bf16[80,1024]{1,0:T(8,128)(2,1)S(1)}, bf16[80,1024]{1,0:T(8,128)(2,1)S(1)}, u32[]{:S(2)}, u32[]{:S(2)}) collective-permute-start(bf16[80,1024]{1,0:T(8,128)(2,1)S(1)} %get-tuple-element.163), channel_id=1, source_target_pairs={{0,24},{2,26},{4,28},{6,30},{8,16},{10,18},{12,20},{14,22},{16,8},... | collective-permute-start | bytes 491528 | tf_op jit(solution)/shard_map/ppermute | solution.py:587
  131.3 9.6 %collective-permute-start.45 = (bf16[80,1024]{1,0:T(8,128)(2,1)S(1)}, bf16[80,1024]{1,0:T(8,128)(2,1)S(1)}, u32[]{:S(2)}, u32[]{:S(2)}) collective-permute-start(bf16[80,1024]{1,0:T(8,128)(2,1)S(1)} %shard_map.138.refs_0_), channel_id=1, source_target_pairs={{0,16},{2,18},{4,20},{6,22},{8,24},{10,26},{12,28},{14,30},{16,0},... | collective-permute-start | bytes 491528 | tf_op jit(solution)/shard_map/ppermute | solution.py:587
  142.1 9.4 %collective-permute-start.46 = (bf16[80,1024]{1,0:T(8,128)(2,1)S(1)}, bf16[80,1024]{1,0:T(8,128)(2,1)S(1)}, u32[]{:S(2)}, u32[]{:S(2)}) collective-permute-start(bf16[80,1024]{1,0:T(8,128)(2,1)S(1)} %collective-permute-done.45.refs_2_), channel_id=1, source_target_pairs={{0,4},{2,6},{4,0},{6,2},{8,12},{10,14},{12,8},{14,10},{16,20},{18,... | collective-permute-start | bytes 491528 | tf_op jit(solution)/shard_map/ppermute | solution.py:583
  143.2 9.4 %collective-permute-start.50 = (bf16[80,1024]{1,0:T(8,128)(2,1)S(1)}, bf16[80,1024]{1,0:T(8,128)(2,1)S(1)}, u32[]{:S(2)}, u32[]{:S(2)}) collective-permute-start(bf16[80,1024]{1,0:T(8,128)(2,1)S(1)} %collective-permute-done.42.refs_1_), channel_id=1, source_target_pairs={{0,4},{2,6},{4,0},{6,2},{8,12},{10,14},{12,8},{14,10},{16,20},{18,... | collective-permute-start | bytes 491528 | tf_op jit(solution)/shard_map/ppermute | solution.py:583
  144.1 10.4 %collective-permute-start.43 = (bf16[80,1024]{1,0:T(8,128)(2,1)S(1)}, bf16[80,1024]{1,0:T(8,128)(2,1)S(1)}, u32[]{:S(2)}, u32[]{:S(2)}) collective-permute-start(bf16[80,1024]{1,0:T(8,128)(2,1)S(1)} %collective-permute-done.42.refs_1_), channel_id=1, source_target_pairs={{0,2},{2,0},{4,6},{6,4},{8,10},{10,8},{12,14},{14,12},{16,18},{18,... | collective-permute-start | bytes 491528 | tf_op jit(solution)/shard_map/ppermute | solution.py:583
  146.2 9.2 %collective-permute-start.54 = (bf16[80,1024]{1,0:T(8,128)(2,1)S(1)}, bf16[80,1024]{1,0:T(8,128)(2,1)S(1)}, u32[]{:S(2)}, u32[]{:S(2)}) collective-permute-start(bf16[80,1024]{1,0:T(8,128)(2,1)S(1)} %collective-permute-done.48.refs_3_), channel_id=1, source_target_pairs={{0,2},{2,0},{4,6},{6,4},{8,10},{10,8},{12,14},{14,12},{16,18},{18,... | collective-permute-start | bytes 491528 | tf_op jit(solution)/shard_map/ppermute | solution.py:583
  149.2 9.3 %collective-permute-start.51 = (bf16[80,1024]{1,0:T(8,128)(2,1)S(1)}, bf16[80,1024]{1,0:T(8,128)(2,1)S(1)}, u32[]{:S(2)}, u32[]{:S(2)}) collective-permute-start(bf16[80,1024]{1,0:T(8,128)(2,1)S(1)} %collective-permute-done.48.refs_3_), channel_id=1, source_target_pairs={{0,4},{2,6},{4,0},{6,2},{8,12},{10,14},{12,8},{14,10},{16,20},{18,... | collective-permute-start | bytes 491528 | tf_op jit(solution)/shard_map/ppermute | solution.py:583
  151.4 8.8 %collective-permute-start.41 = (bf16[80,1024]{1,0:T(8,128)(2,1)S(1)}, bf16[80,1024]{1,0:T(8,128)(2,1)S(1)}, u32[]{:S(2)}, u32[]{:S(2)}) collective-permute-start(bf16[80,1024]{1,0:T(8,128)(2,1)S(1)} %collective-permute-done.40.refs_0_), channel_id=1, source_target_pairs={{0,2},{2,0},{4,6},{6,4},{8,10},{10,8},{12,14},{14,12},{16,18},{18,... | collective-permute-start | bytes 491528 | tf_op jit(solution)/shard_map/ppermute | solution.py:583
  152.7 10.2 %collective-permute-start.49 = (bf16[80,1024]{1,0:T(8,128)(2,1)S(1)}, bf16[80,1024]{1,0:T(8,128)(2,1)S(1)}, u32[]{:S(2)}, u32[]{:S(2)}) collective-permute-start(bf16[80,1024]{1,0:T(8,128)(2,1)S(1)} %collective-permute-done.48.refs_3_), channel_id=1, source_target_pairs={{0,6},{2,4},{4,2},{6,0},{8,14},{10,12},{12,10},{14,8},{16,22},{18,... | collective-permute-start | bytes 491528 | tf_op jit(solution)/shard_map/ppermute | solution.py:583
  154.6 8.9 %collective-permute-start.47 = (bf16[80,1024]{1,0:T(8,128)(2,1)S(1)}, bf16[80,1024]{1,0:T(8,128)(2,1)S(1)}, u32[]{:S(2)}, u32[]{:S(2)}) collective-permute-start(bf16[80,1024]{1,0:T(8,128)(2,1)S(1)} %collective-permute-done.46.refs_2_), channel_id=1, source_target_pairs={{0,2},{2,0},{4,6},{6,4},{8,10},{10,8},{12,14},{14,12},{16,18},{18,... | collective-permute-start | bytes 491528 | tf_op jit(solution)/shard_map/ppermute | solution.py:583
  (31 other events, 196.1 us)

commit v4 on v3

--- a/solution.py
+++ b/solution.py
@@ -85,23 +85,24 @@
     return parts[0]
 
 
-def project_body(far, sp, u_ref, wb_ref, wd_ref, out_ref, *copies):
+def project_body(copies, sp, u_ref, wb_ref, wd_ref, *refs):
     k = pl.program_id(0)
+    out_ref = refs[-1 - copies]
 
     @pl.when(k == 0)
     def _():
-        out_ref[...] = jnp.zeros_like(out_ref)
+        out_ref[...] = refs[0][...] if len(refs) > 1 + copies else jnp.zeros_like(out_ref)
 
     u = u_ref[...]
     bc_width = wb_ref.shape[1]
     head_count = wd_ref.shape[0]
     out_ref[:, :bc_width] += dot_10(u, wb_ref[...])
     out_ref[:, bc_width : bc_width + head_count] += dot_11(u, wd_ref[...])
-    for o, copy in zip(far, copies):
-
-        @pl.when(k == o)
+    for i in range(copies):
+
+        @pl.when(k == i)
         def _():
-            copy[...] = u
+            refs[len(refs) - copies + i][...] = u
 
 
 def running_sum(rows, keep):
@@ -573,7 +574,10 @@
     member = lax.axis_index("dp")
     position = lax.axis_index("seq")
     mine, plane = position % groups, position // groups
-    sp = jnp.stack([member, mine, plane]).astype(jnp.int32)
+    far = [o for o in range(1, groups) if o & (o - 1)]
+    direct = [o for o in range(1, groups) if o & (o - 1) == 0]
+    order = far + [0] + direct
+    sp = jnp.stack([member, mine, plane] + [mine ^ o for o in order]).astype(jnp.int32)
     params = jnp.stack([rate_log, step_bias, skip_gain], axis=1)
     proj_width = bc_width + LANE
     scale = 1.0 / (length * seq_count)
@@ -599,23 +603,30 @@
         pairs = [[(i, i ^ k) for i in range(dp_count)] for k in range(1, dp_count)]
         return [value] + [lax.ppermute(value, "dp", pair) for pair in pairs]
 
-    direct = [o for o in range(1, groups) if o & (o - 1) == 0]
-    far = [o for o in range(1, groups) if o & (o - 1)]
     copy_shape = shape_of((length, span), BF16)
     copy_spec = whole((length, span))
-    partial, *copies = call(
-        functools.partial(project_body, far),
-        (groups,),
-        [
-            pl.BlockSpec((length, span), lambda o, sp: (0, o ^ sp[1])),
-            pl.BlockSpec((span, bc_width), lambda o, sp: (sp[0] * groups + (o ^ sp[1]), 0)),
-            pl.BlockSpec((head_count, span), lambda o, sp: (0, sp[0] * groups + (o ^ sp[1]))),
-        ],
-        [whole((length, proj_width))] + [copy_spec] * len(far),
-        [shape_of((length, proj_width), F32)] + [copy_shape] * len(far),
-        us=1,
-        vmem=VMEM_WIDE,
-    )(sp, teacher_rows, state_proj, step_proj.T)
+
+    def project(first, count, copies, *before):
+        return call(
+            functools.partial(project_body, copies),
+            (count,),
+            [
+                pl.BlockSpec((length, span), lambda k, sp: (0, sp[3 + first + k])),
+                pl.BlockSpec((span, bc_width), lambda k, sp: (sp[0] * groups + sp[3 + first + k], 0)),
+                pl.BlockSpec((head_count, span), lambda k, sp: (0, sp[0] * groups + sp[3 + first + k])),
+            ]
+            + [whole((length, proj_width))] * len(before),
+            [whole((length, proj_width))] + [copy_spec] * copies,
+            [shape_of((length, proj_width), F32)] + [copy_shape] * copies,
+            us=1,
+            vmem=VMEM_WIDE,
+        )(sp, teacher_rows, state_proj, step_proj.T, *before)
+
+    partial, copies = [], []
+    if far:
+        first, *copies = project(0, len(far), len(far))
+        partial = [first]
+    (partial,) = project(len(far), groups - len(far), 0, *partial)
     projs = members_of(partial)
 
     def row_blocks(offsets):
@@ -916,9 +927,6 @@
     gathered = all_over(own, over_planes, planes)
     pieces = []
     for k, part in enumerate(gathered):
-        if k == planes - 1:
-            pieces.append({o: in_plane(part, o) if o else part for o in range(groups)})
-            continue
         spread = {0: part}
         steps = [1 << i for i in range(groups.bit_length() - 1)]
         for step in steps if k % 2 else steps[::-1]:

time: 167 us -> 163 us (0.976)
  waiting for transfers between devices: 37 us -> 30.7 us
  Pallas kernels: 53.7 us -> 55.5 us
    ppermute x32, waiting for transfers between devices: 11.6 us -> 6.31 us  [in_plane(): return lax.ppermute(value, 'seq', pairs)]
    pallas_call x1 -> x2, Pallas kernels: 5.66 us -> 8.16 us  [project(): call(functools.partial(project_body, copies), (count,), [pl.BlockSpec((le...]
  transfers between devices with their start and end apart: 55 -> 55, of which waited for: 17 -> 18; matrix products, arithmetic and copies ran while one was open for 1% -> 1% of each run, Pallas kernels for 25% -> 28%
where the time goes in v4:
time: 163 us; the launch traced here: 162 us
  starting transfers between devices  69 us (42%)
  Pallas kernels  55.5 us (34%)
  waiting for transfers between devices  30.7 us (19%)
  local copies, waits for them, and re-layouts  3.34 us (2%)
  between operations  2.7 us (2%)
    ppermute x32, starting transfers between devices, in_plane(): return lax.ppermute(value, 'seq', pairs)  39.3 us
    ppermute x20, starting transfers between devices, over_planes(): return lax.ppermute(value, 'seq', pairs)  29.6 us
    ppermute x20, waiting for transfers between devices, over_planes(): return lax.ppermute(value, 'seq', pairs)  19.8 us
    pallas_call x4, Pallas kernels, error_part(): call(functools.partial(error_body, o == 0, local_heads, o), (1,), [whole(...  11.5 us
    pallas_call x2, Pallas kernels, project(): call(functools.partial(project_body, copies), (count,), [pl.BlockSpec((le...  8.16 us
    pallas_call x1, Pallas kernels, shards(): call(functools.partial(local_body, groups, local_heads), (groups,), [whol...  7.45 us
    pallas_call x4, Pallas kernels, shards(): call(functools.partial(spread_body, planes), (1,), [whole(share_shape)] *...  7.22 us
    ppermute x32, waiting for transfers between devices, in_plane(): return lax.ppermute(value, 'seq', pairs)  6.31 us
  transfers between devices with their start and end apart: 55, of which 18 were waited for; matrix products, arithmetic and copies ran while one was open for 1% of the time, Pallas kernels for 28%

profile of v4, /device:TPU:0, one launch (start us, length us, event | category | flops | bytes accessed | tf_op | source)
XLA Modules:
  0.0 162.3 jit_solution(5570758816167287412)
XLA Ops:
  1.3 3.1 %shard_map.118 = (f32[256,384]{1,0:T(8,128)}, bf16[256,1024]{1,0:T(8,128)(2,1)}) custom-call(s32[7]{0:T(128)} %stack.40.sp, bf16[256,4096]{1,0:T(8,128)(2,1)} %refs_4_.3, bf16[8192,256]{1,0:T(8,128)(2,1)} %wb_ref.3, bf16[64,8192]{1,0:T(8,128)(2,1)} %bitcast.18), custom_call_target="tpu_custom_call" | custom-call | flops 1100000000 | tf_op jit(solution)/shard_map/pallas_call | solution.py:610
  4.4 4.0 %collective-permute-start.1 = (bf16[256,1024]{1,0:T(8,128)(2,1)}, bf16[256,1024]{1,0:T(8,128)(2,1)S(1)}, u32[]{:S(2)}, u32[]{:S(2)}) collective-permute-start(bf16[256,1024]{1,0:T(8,128)(2,1)} %get-tuple-element.93), channel_id=1, source_target_pairs={{0,6},{2,4},{4,2},{6,0},{8,14},{10,12},{12,10},{14,8},{16,22},{18,... | collective-permute-start | bytes 1572872 | tf_op jit(solution)/shard_map/ppermute | solution.py:587
  8.3 5.1 %shard_map.119.refs_0_ = f32[256,384]{1,0:T(8,128)} custom-call(s32[7]{0:T(128)} %stack.40.sp, bf16[256,4096]{1,0:T(8,128)(2,1)} %refs_4_.3, bf16[8192,256]{1,0:T(8,128)(2,1)} %wb_ref.3, bf16[64,8192]{1,0:T(8,128)(2,1)} %bitcast.19, f32[256,384]{1,0:T(8,128)} %get-tuple-element.89.refs_0_), custom_call_target="tpu_custom_call" | custom-call | flops 1100000000 | tf_op jit(solution)/shard_map/pallas_call | solution.py:610
  16.4 3.9 %shard_map.120 = (bf16[256,256]{1,0:T(8,128)(2,1)S(1)}, f32[4,48,256]{2,1,0:T(8,128)S(1)}, f32[4,256,128]{2,1,0:T(8,128)S(1)}, bf16[144,1024]{1,0:T(8,128)(2,1)S...) custom-call(s32[7]{0:T(128)S(1)} %copy-done.2, ...), custom_call_target="tpu_custom_call" | custom-call | flops 1100000000 | tf_op jit(solution)/shard_map/pallas_call | solution.py:646
  21.0 2.8 %collective-permute-start.4 = (bf16[144,1024]{1,0:T(8,128)(2,1)S(1)}, bf16[144,1024]{1,0:T(8,128)(2,1)S(1)}, u32[]{:S(2)}, u32[]{:S(2)}) collective-permute-start(bf16[144,1024]{1,0:T(8,128)(2,1)S(1)} %get-tuple-element.98), channel_id=1, source_target_pairs={{0,6},{2,4},{4,2},{6,0},{8,14},{10,12},{12,10},{14,8},{16,22},{18,... | collective-permute-start | bytes 884744 | tf_op jit(solution)/shard_map/ppermute | solution.py:587
  25.4 7.4 %shard_map.121 = (f32[256,4096]{1,0:T(8,128)S(1)}, bf16[176,1024]{1,0:T(8,128)(2,1)S(1)}, bf16[176,1024]{1,0:T(8,128)(2,1)S(1)}, bf16[176,1024]{1,0:T(8,128)(2,1)S(1)}, bf16[176,1024]{1,0:T(8,128)(2,1)S(1)}) custom-call(s32[7]{0:T(128)S(1)} %copy-done.2, bf16[256,256]{1,0:T(8,128)(2,1)S(1)} %get-tuple-element.90.bc_ref, ...), custom_call_target="tpu_custom_call" | custom-call | flops 7699999744 | tf_op jit(solution)/shard_map/pallas_call | solution.py:662
  33.6 2.8 %collective-permute-start.7 = (bf16[176,1024]{1,0:T(8,128)(2,1)S(1)}, bf16[176,1024]{1,0:T(8,128)(2,1)S(1)}, u32[]{:S(2)}, u32[]{:S(2)}) collective-permute-start(bf16[176,1024]{1,0:T(8,128)(2,1)S(1)} %get-tuple-element.104), channel_id=1, source_target_pairs={{0,6},{2,4},{4,2},{6,0},{8,14},{10,12},{12,10},{14,8},{16,22},{18,... | collective-permute-start | bytes 1081352 | tf_op jit(solution)/shard_map/ppermute | solution.py:587
  39.7 2.6 %collective-permute-start.9 = (bf16[144,256]{1,0:T(8,128)(2,1)S(1)}, bf16[144,256]{1,0:T(8,128)(2,1)S(1)}, u32[]{:S(2)}, u32[]{:S(2)}) collective-permute-start(bf16[144,256]{1,0:T(8,128)(2,1)S(1)} %get-tuple-element.107), channel_id=1, source_target_pairs={{0,16},{2,18},{4,20},{6,22},{8,24},{10,26},{12,28},{14,30},{16,0},... | collective-permute-start | bytes 221192 | tf_op jit(solution)/shard_map/ppermute | solution.py:591
  43.0 3.1 %collective-permute-start.10 = (bf16[144,256]{1,0:T(8,128)(2,1)S(1)}, bf16[144,256]{1,0:T(8,128)(2,1)S(1)}, u32[]{:S(2)}, u32[]{:S(2)}) collective-permute-start(bf16[144,256]{1,0:T(8,128)(2,1)S(1)} %get-tuple-element.108), channel_id=1, source_target_pairs={{0,24},{2,26},{4,28},{6,30},{8,16},{10,18},{12,20},{14,22},{16,8},... | collective-permute-start | bytes 221192 | tf_op jit(solution)/shard_map/ppermute | solution.py:591
  46.9 2.3 %collective-permute-done.10.refs_3_ = bf16[144,256]{1,0:T(8,128)(2,1)S(1)} collective-permute-done((bf16[144,256]{1,0:T(8,128)(2,1)S(1)}, bf16[144,256]{1,0:T(8,128)(2,1)S(1)}, u32[]{:S(2)}, u32[]{:S(2)}) %collective-permute-start.10) | collective-permute-done | bytes 73760 | tf_op jit(solution)/shard_map/ppermute | solution.py:591
  50.6 3.0 %collective-permute-start.12 = (bf16[128,256]{1,0:T(8,128)(2,1)S(1)}, bf16[128,256]{1,0:T(8,128)(2,1)S(1)}, u32[]{:S(2)}, u32[]{:S(2)}) collective-permute-start(bf16[128,256]{1,0:T(8,128)(2,1)S(1)} %get-tuple-element.111), channel_id=1, source_target_pairs={{0,16},{2,18},{4,20},{6,22},{8,24},{10,26},{12,28},{14,30},{16,0},... | collective-permute-start | bytes 196616 | tf_op jit(solution)/shard_map/ppermute | solution.py:591
  56.5 2.2 %shard_map.123.moment_ref = bf16[4,128,1024]{2,1,0:T(8,128)(2,1)S(1)} custom-call(s32[7]{0:T(128)S(1)} %copy-done.2, bf16[176,1024]{1,0:T(8,128)(2,1)S(1)} %get-tuple-element.101.refs_0_.refs_4_, bf16[176,1024]{1,0:T(8,128)(2,1)S(1)} %collective-permute-done.5.refs_1_.refs_5_, bf16[176,1024]{1,0:T(8,128)(2,1)S(1)} %collective-permute-done.6.refs_2_.refs_6_, ...), custom_call_target="tpu_custom_call" | custom-call | flops 2200000000 | tf_op jit(solution)/shard_map/pallas_call | solution.py:695
  59.7 2.4 %shard_map.125 = (bf16[128,1024]{1,0:T(8,128)(2,1)S(1)}, bf16[128,1024]{1,0:T(8,128)(2,1)S(1)}, bf16[128,1024]{1,0:T(8,128)(2,1)S(1)}, bf16[128,1024]{1,0:T(8,12...) custom-call(s32[7]{0:T(128)S(1)} %copy-done.2, ...), custom_call_target="tpu_custom_call" | custom-call | flops 2200000000 | tf_op jit(solution)/shard_map/pallas_call | solution.py:736
  62.1 2.7 %collective-permute-start.18 = (bf16[128,256]{1,0:T(8,128)(2,1)S(1)}, bf16[128,256]{1,0:T(8,128)(2,1)S(1)}, u32[]{:S(2)}, u32[]{:S(2)}) collective-permute-start(bf16[128,256]{1,0:T(8,128)(2,1)S(1)} %get-tuple-element.121), channel_id=1, source_target_pairs={{0,16},{2,18},{4,20},{6,22},{8,24},{10,26},{12,28},{14,30},{16,0},... | collective-permute-start | bytes 196616 | tf_op jit(solution)/shard_map/ppermute | solution.py:591
  68.2 2.8 %shard_map.126 = (f32[16,256]{1,0:T(8,128)S(1)}, f32[16,128]{1,0:T(8,128)S(1)}, f32[256,384]{1,0:T(8,128)S(1)}, f32[8,128]{1,0:T(8,128)S(1)}) custom-call(s32[7]{0:T(128)S(1)} %copy-done.2, bf16[256,256]{1,0:T(8,128)(2,1)S(1)} %get-tuple-element.90.bc_ref, f32[4,48,256]{2,1,0:T(8,128)S(1)} %get-tuple-element.91.rows_ref, ...), custom_call_target="tpu_custom_call" | custom-call | flops 4400000000 | tf_op jit(solution)/shard_map/pallas_call | solution.py:777
  73.6 2.6 %collective-permute-start.23 = (bf16[128,256]{1,0:T(8,128)(2,1)S(1)}, bf16[128,256]{1,0:T(8,128)(2,1)S(1)}, u32[]{:S(2)}, u32[]{:S(2)}) collective-permute-start(bf16[128,256]{1,0:T(8,128)(2,1)S(1)} %get-tuple-element.129), channel_id=1, source_target_pairs={{0,16},{2,18},{4,20},{6,22},{8,24},{10,26},{12,28},{14,30},{16,0},... | collective-permute-start | bytes 196616 | tf_op jit(solution)/shard_map/ppermute | solution.py:591
  78.0 2.8 %shard_map.128 = (f32[16,256]{1,0:T(8,128)S(1)}, f32[16,128]{1,0:T(8,128)S(1)}, f32[256,384]{1,0:T(8,128)S(1)}, f32[8,128]{1,0:T(8,128)}) custom-call(s32[7]{0:T(128)S(1)} %copy-done.2, bf16[256,256]{1,0:T(8,128)(2,1)S(1)} %get-tuple-element.90.bc_ref, f32[4,48,256]{2,1,0:T(8,128)S(1)} %get-tuple-element.91.rows_ref, ...), custom_call_target="tpu_custom_call" | custom-call | flops 4400000000 | tf_op jit(solution)/shard_map/pallas_call | solution.py:777
  86.8 3.0 %shard_map.130 = (f32[16,256]{1,0:T(8,128)S(1)}, f32[16,128]{1,0:T(8,128)S(1)}, f32[256,384]{1,0:T(8,128)S(1)}, f32[8,128]{1,0:T(8,128)}) custom-call(s32[7]{0:T(128)S(1)} %copy-done.2, bf16[256,256]{1,0:T(8,128)(2,1)S(1)} %get-tuple-element.90.bc_ref, f32[4,48,256]{2,1,0:T(8,128)S(1)} %get-tuple-element.91.rows_ref, ...), custom_call_target="tpu_custom_call" | custom-call | flops 4400000000 | tf_op jit(solution)/shard_map/pallas_call | solution.py:777
  89.8 2.8 %shard_map.131 = (f32[16,256]{1,0:T(8,128)S(1)}, f32[16,128]{1,0:T(8,128)S(1)}, f32[256,384]{1,0:T(8,128)S(1)}, f32[8,128]{1,0:T(8,128)}) custom-call(s32[7]{0:T(128)S(1)} %copy-done.2, bf16[256,256]{1,0:T(8,128)(2,1)S(1)} %get-tuple-element.90.bc_ref, f32[4,48,256]{2,1,0:T(8,128)S(1)} %get-tuple-element.91.rows_ref, ...), custom_call_target="tpu_custom_call" | custom-call | flops 4400000000 | tf_op jit(solution)/shard_map/pallas_call | solution.py:777
  104.5 3.6 %collective-permute-done.28 = f32[8,128]{1,0:T(8,128)S(1)} collective-permute-done((f32[8,128]{1,0:T(8,128)S(1)}, f32[8,128]{1,0:T(8,128)S(1)}, u32[]{:S(2)}, u32[]{:S(2)}) %collective-permute-start.28) | collective-permute-done | bytes 4128 | tf_op jit(solution)/shard_map/ppermute | solution.py:591
  108.4 4.3 %collective-permute-done.29 = f32[8,128]{1,0:T(8,128)S(1)} collective-permute-done((f32[8,128]{1,0:T(8,128)S(1)}, f32[8,128]{1,0:T(8,128)S(1)}, u32[]{:S(2)}, u32[]{:S(2)}) %collective-permute-start.29) | collective-permute-done | bytes 4128 | tf_op jit(solution)/shard_map/ppermute | solution.py:591
  114.2 2.3 %collective-permute-start.38 = (bf16[80,1024]{1,0:T(8,128)(2,1)S(1)}, bf16[80,1024]{1,0:T(8,128)(2,1)S(1)}, u32[]{:S(2)}, u32[]{:S(2)}) collective-permute-start(bf16[80,1024]{1,0:T(8,128)(2,1)S(1)} %get-tuple-element.162), channel_id=1, source_target_pairs={{0,16},{2,18},{4,20},{6,22},{8,24},{10,26},{12,28},{14,30},{16,0},... | collective-permute-start | bytes 491528 | tf_op jit(solution)/shard_map/ppermute | solution.py:591
  116.5 2.1 %collective-permute-start.39 = (bf16[80,1024]{1,0:T(8,128)(2,1)S(1)}, bf16[80,1024]{1,0:T(8,128)(2,1)S(1)}, u32[]{:S(2)}, u32[]{:S(2)}) collective-permute-start(bf16[80,1024]{1,0:T(8,128)(2,1)S(1)} %get-tuple-element.163), channel_id=1, source_target_pairs={{0,24},{2,26},{4,28},{6,30},{8,16},{10,18},{12,20},{14,22},{16,8},... | collective-permute-start | bytes 491528 | tf_op jit(solution)/shard_map/ppermute | solution.py:591
  120.0 2.2 %collective-permute-done.30 = f32[8,128]{1,0:T(8,128)S(1)} collective-permute-done((f32[8,128]{1,0:T(8,128)S(1)}, f32[8,128]{1,0:T(8,128)S(1)}, u32[]{:S(2)}, u32[]{:S(2)}) %collective-permute-start.30) | collective-permute-done | bytes 4128 | tf_op jit(solution)/shard_map/ppermute | solution.py:587
  123.8 2.0 %collective-permute-done.31 = f32[8,128]{1,0:T(8,128)S(1)} collective-permute-done((f32[8,128]{1,0:T(8,128)S(1)}, f32[8,128]{1,0:T(8,128)S(1)}, u32[]{:S(2)}, u32[]{:S(2)}) %collective-permute-start.31) | collective-permute-done | bytes 4128 | tf_op jit(solution)/shard_map/ppermute | solution.py:587
  127.0 1.9 %collective-permute-done.38.refs_1_ = bf16[80,1024]{1,0:T(8,128)(2,1)S(1)} collective-permute-done((bf16[80,1024]{1,0:T(8,128)(2,1)S(1)}, bf16[80,1024]{1,0:T(8,128)(2,1)S(1)}, u32[]{:S(2)}, u32[]{:S(2)}) %collective-permute-start.38) | collective-permute-done | bytes 163872 | tf_op jit(solution)/shard_map/ppermute | solution.py:591
  129.5 2.9 %collective-permute-start.45 = (bf16[80,1024]{1,0:T(8,128)(2,1)S(1)}, bf16[80,1024]{1,0:T(8,128)(2,1)S(1)}, u32[]{:S(2)}, u32[]{:S(2)}) collective-permute-start(bf16[80,1024]{1,0:T(8,128)(2,1)S(1)} %shard_map.139.refs_0_), channel_id=1, source_target_pairs={{0,16},{2,18},{4,20},{6,22},{8,24},{10,26},{12,28},{14,30},{16,0},... | collective-permute-start | bytes 491528 | tf_op jit(solution)/shard_map/ppermute | solution.py:591
  134.5 3.8 %collective-permute-done.45.refs_2_ = bf16[80,1024]{1,0:T(8,128)(2,1)S(1)} collective-permute-done((bf16[80,1024]{1,0:T(8,128)(2,1)S(1)}, bf16[80,1024]{1,0:T(8,128)(2,1)S(1)}, u32[]{:S(2)}, u32[]{:S(2)}) %collective-permute-start.45) | collective-permute-done | bytes 163872 | tf_op jit(solution)/shard_map/ppermute | solution.py:591
  147.9 1.8 %shard_map.140 = (f32[4096,256]{1,0:T(8,128)}, f32[64,4096]{1,0:T(8,128)}) custom-call(s32[7]{0:T(128)S(1)} %copy-done.2, bf16[80,1024]{1,0:T(8,128)(2,1)S(1)} %shard_map.139.refs_0_, bf16[80,1024]{1,0:T(8,128)(2,1)S(1)} %collective-permute-done.42.refs_1_, bf16[80,1024]{1,0:T(8,128)(2,1)S(1)} %collective-permute-done.45.refs_2_, ...), custom_call_target="tpu_custom_call" | custom-call | flops 1100000000 | tf_op jit(solution)/shard_map/pallas_call | solution.py:937
  153.8 1.8 %shard_map.141 = (f32[4096,256]{1,0:T(8,128)}, f32[64,4096]{1,0:T(8,128)}) custom-call(s32[7]{0:T(128)S(1)} %copy-done.2, bf16[80,1024]{1,0:T(8,128)(2,1)S(1)} %collective-permute-done.53.refs_0_, bf16[80,1024]{1,0:T(8,128)(2,1)S(1)} %collective-permute-done.43.refs_1_, ...), custom_call_target="tpu_custom_call", output_to_operand_aliasing={{0}: (5, {}), {1}: (6, {})} | custom-call | flops 1100000000 | tf_op jit(solution)/shard_map/pallas_call | solution.py:937
  155.6 1.8 %shard_map.142 = (f32[4096,256]{1,0:T(8,128)}, f32[64,4096]{1,0:T(8,128)}) custom-call(s32[7]{0:T(128)S(1)} %copy-done.2, bf16[80,1024]{1,0:T(8,128)(2,1)S(1)} %collective-permute-done.40.refs_0_, bf16[80,1024]{1,0:T(8,128)(2,1)S(1)} %collective-permute-done.51.refs_1_, ...), custom_call_target="tpu_custom_call", output_to_operand_aliasing={{0}: (5, {}), {1}: (6, {})} | custom-call | flops 1100000000 | tf_op jit(solution)/shard_map/pallas_call | solution.py:937
  159.4 1.8 %shard_map.143 = (f32[4096,256]{1,0:T(8,128)}, f32[64,4096]{1,0:T(8,128)}) custom-call(s32[7]{0:T(128)S(1)} %copy-done.2, bf16[80,1024]{1,0:T(8,128)(2,1)S(1)} %collective-permute-done.41.refs_0_, bf16[80,1024]{1,0:T(8,128)(2,1)S(1)} %collective-permute-done.44.refs_1_, ...), custom_call_target="tpu_custom_call", output_to_operand_aliasing={{0}: (5, {}), {1}: (6, {})} | custom-call | flops 1100000000 | tf_op jit(solution)/shard_map/pallas_call | solution.py:937
  (129 shorter events, 66.0 us)
Async XLA Ops:
  4.4 19.4 %collective-permute-start.1 = (bf16[256,1024]{1,0:T(8,128)(2,1)}, bf16[256,1024]{1,0:T(8,128)(2,1)S(1)}, u32[]{:S(2)}, u32[]{:S(2)}) collective-permute-start(bf16[256,1024]{1,0:T(8,128)(2,1)} %get-tuple-element.93), channel_id=1, source_target_pairs={{0,6},{2,4},{4,2},{6,0},{8,14},{10,12},{12,10},{14,8},{16,22},{18,... | collective-permute-start | bytes 1572872 | tf_op jit(solution)/shard_map/ppermute | solution.py:587
  20.2 13.4 %collective-permute-start.2 = (bf16[144,1024]{1,0:T(8,128)(2,1)S(1)}, bf16[144,1024]{1,0:T(8,128)(2,1)S(1)}, u32[]{:S(2)}, u32[]{:S(2)}) collective-permute-start(bf16[144,1024]{1,0:T(8,128)(2,1)S(1)} %get-tuple-element.96), channel_id=1, source_target_pairs={{0,2},{2,0},{4,6},{6,4},{8,10},{10,8},{12,14},{14,12},{16,18},{18,... | collective-permute-start | bytes 884744 | tf_op jit(solution)/shard_map/ppermute | solution.py:587
  20.8 15.6 %collective-permute-start.3 = (bf16[144,1024]{1,0:T(8,128)(2,1)S(1)}, bf16[144,1024]{1,0:T(8,128)(2,1)S(1)}, u32[]{:S(2)}, u32[]{:S(2)}) collective-permute-start(bf16[144,1024]{1,0:T(8,128)(2,1)S(1)} %get-tuple-element.97), channel_id=1, source_target_pairs={{0,4},{2,6},{4,0},{6,2},{8,12},{10,14},{12,8},{14,10},{16,20},{18,... | collective-permute-start | bytes 884744 | tf_op jit(solution)/shard_map/ppermute | solution.py:587
  21.0 15.4 %collective-permute-start.4 = (bf16[144,1024]{1,0:T(8,128)(2,1)S(1)}, bf16[144,1024]{1,0:T(8,128)(2,1)S(1)}, u32[]{:S(2)}, u32[]{:S(2)}) collective-permute-start(bf16[144,1024]{1,0:T(8,128)(2,1)S(1)} %get-tuple-element.98), channel_id=1, source_target_pairs={{0,6},{2,4},{4,2},{6,0},{8,14},{10,12},{12,10},{14,8},{16,22},{18,... | collective-permute-start | bytes 884744 | tf_op jit(solution)/shard_map/ppermute | solution.py:587
  32.9 20.8 %collective-permute-start.5 = (bf16[176,1024]{1,0:T(8,128)(2,1)S(1)}, bf16[176,1024]{1,0:T(8,128)(2,1)S(1)}, u32[]{:S(2)}, u32[]{:S(2)}) collective-permute-start(bf16[176,1024]{1,0:T(8,128)(2,1)S(1)} %get-tuple-element.102), channel_id=1, source_target_pairs={{0,2},{2,0},{4,6},{6,4},{8,10},{10,8},{12,14},{14,12},{16,18},{18,... | collective-permute-start | bytes 1081352 | tf_op jit(solution)/shard_map/ppermute | solution.py:587
  33.5 20.9 %collective-permute-start.6 = (bf16[176,1024]{1,0:T(8,128)(2,1)S(1)}, bf16[176,1024]{1,0:T(8,128)(2,1)S(1)}, u32[]{:S(2)}, u32[]{:S(2)}) collective-permute-start(bf16[176,1024]{1,0:T(8,128)(2,1)S(1)} %get-tuple-element.103), channel_id=1, source_target_pairs={{0,4},{2,6},{4,0},{6,2},{8,12},{10,14},{12,8},{14,10},{16,20},{18,... | collective-permute-start | bytes 1081352 | tf_op jit(solution)/shard_map/ppermute | solution.py:587
  33.6 22.0 %collective-permute-start.7 = (bf16[176,1024]{1,0:T(8,128)(2,1)S(1)}, bf16[176,1024]{1,0:T(8,128)(2,1)S(1)}, u32[]{:S(2)}, u32[]{:S(2)}) collective-permute-start(bf16[176,1024]{1,0:T(8,128)(2,1)S(1)} %get-tuple-element.104), channel_id=1, source_target_pairs={{0,6},{2,4},{4,2},{6,0},{8,14},{10,12},{12,10},{14,8},{16,22},{18,... | collective-permute-start | bytes 1081352 | tf_op jit(solution)/shard_map/ppermute | solution.py:587
  49.9 8.8 %collective-permute-start.11 = (bf16[128,256]{1,0:T(8,128)(2,1)S(1)}, bf16[128,256]{1,0:T(8,128)(2,1)S(1)}, u32[]{:S(2)}, u32[]{:S(2)}) collective-permute-start(bf16[128,256]{1,0:T(8,128)(2,1)S(1)} %get-tuple-element.110), channel_id=1, source_target_pairs={{0,8},{2,10},{4,12},{6,14},{8,0},{10,2},{12,4},{14,6},{16,24},{18,... | collective-permute-start | bytes 196616 | tf_op jit(solution)/shard_map/ppermute | solution.py:591
  50.6 8.1 %collective-permute-start.12 = (bf16[128,256]{1,0:T(8,128)(2,1)S(1)}, bf16[128,256]{1,0:T(8,128)(2,1)S(1)}, u32[]{:S(2)}, u32[]{:S(2)}) collective-permute-start(bf16[128,256]{1,0:T(8,128)(2,1)S(1)} %get-tuple-element.111), channel_id=1, source_target_pairs={{0,16},{2,18},{4,20},{6,22},{8,24},{10,26},{12,28},{14,30},{16,0},... | collective-permute-start | bytes 196616 | tf_op jit(solution)/shard_map/ppermute | solution.py:591
  54.4 18.5 %collective-permute-start.20 = (bf16[256,1024]{1,0:T(8,128)(2,1)S(1)}, bf16[256,1024]{1,0:T(8,128)(2,1)S(1)}, u32[]{:S(2)}, u32[]{:S(2)}) collective-permute-start(bf16[256,1024]{1,0:T(8,128)(2,1)S(1)} %get-tuple-element.123), channel_id=1, source_target_pairs={{0,2},{2,0},{4,6},{6,4},{8,10},{10,8},{12,14},{14,12},{16,18},{18,... | collective-permute-start | bytes 1572872 | tf_op jit(solution)/shard_map/ppermute | solution.py:587
  55.6 17.2 %collective-permute-start.21 = (bf16[256,1024]{1,0:T(8,128)(2,1)S(1)}, bf16[256,1024]{1,0:T(8,128)(2,1)S(1)}, u32[]{:S(2)}, u32[]{:S(2)}) collective-permute-start(bf16[256,1024]{1,0:T(8,128)(2,1)S(1)} %get-tuple-element.124), channel_id=1, source_target_pairs={{0,4},{2,6},{4,0},{6,2},{8,12},{10,14},{12,8},{14,10},{16,20},{18,... | collective-permute-start | bytes 1572872 | tf_op jit(solution)/shard_map/ppermute | solution.py:587
  62.1 8.9 %collective-permute-start.18 = (bf16[128,256]{1,0:T(8,128)(2,1)S(1)}, bf16[128,256]{1,0:T(8,128)(2,1)S(1)}, u32[]{:S(2)}, u32[]{:S(2)}) collective-permute-start(bf16[128,256]{1,0:T(8,128)(2,1)S(1)} %get-tuple-element.121), channel_id=1, source_target_pairs={{0,16},{2,18},{4,20},{6,22},{8,24},{10,26},{12,28},{14,30},{16,0},... | collective-permute-start | bytes 196616 | tf_op jit(solution)/shard_map/ppermute | solution.py:591
  66.5 9.8 %collective-permute-start.16 = (bf16[128,1024]{1,0:T(8,128)(2,1)S(1)}, bf16[128,1024]{1,0:T(8,128)(2,1)S(1)}, u32[]{:S(2)}, u32[]{:S(2)}) collective-permute-start(bf16[128,1024]{1,0:T(8,128)(2,1)S(1)} %get-tuple-element.115), channel_id=1, source_target_pairs={{0,2},{2,0},{4,6},{6,4},{8,10},{10,8},{12,14},{14,12},{16,18},{18,... | collective-permute-start | bytes 786440 | tf_op jit(solution)/shard_map/ppermute | solution.py:587
  71.0 18.8 %collective-permute-start.14 = (bf16[128,1024]{1,0:T(8,128)(2,1)S(1)}, bf16[128,1024]{1,0:T(8,128)(2,1)S(1)}, u32[]{:S(2)}, u32[]{:S(2)}) collective-permute-start(bf16[128,1024]{1,0:T(8,128)(2,1)S(1)} %get-tuple-element.113), channel_id=1, source_target_pairs={{0,6},{2,4},{4,2},{6,0},{8,14},{10,12},{12,10},{14,8},{16,22},{18,... | collective-permute-start | bytes 786440 | tf_op jit(solution)/shard_map/ppermute | solution.py:587
  72.3 14.5 %collective-permute-start.15 = (bf16[128,1024]{1,0:T(8,128)(2,1)S(1)}, bf16[128,1024]{1,0:T(8,128)(2,1)S(1)}, u32[]{:S(2)}, u32[]{:S(2)}) collective-permute-start(bf16[128,1024]{1,0:T(8,128)(2,1)S(1)} %get-tuple-element.114), channel_id=1, source_target_pairs={{0,4},{2,6},{4,0},{6,2},{8,12},{10,14},{12,8},{14,10},{16,20},{18,... | collective-permute-start | bytes 786440 | tf_op jit(solution)/shard_map/ppermute | solution.py:587
  83.3 13.2 %collective-permute-start.25 = (bf16[128,1024]{1,0:T(8,128)(2,1)S(1)}, bf16[128,1024]{1,0:T(8,128)(2,1)S(1)}, u32[]{:S(2)}, u32[]{:S(2)}) collective-permute-start(bf16[128,1024]{1,0:T(8,128)(2,1)S(1)} %get-tuple-element.135), channel_id=1, source_target_pairs={{0,6},{2,4},{4,2},{6,0},{8,14},{10,12},{12,10},{14,8},{16,22},{18,... | collective-permute-start | bytes 786440 | tf_op jit(solution)/shard_map/ppermute | solution.py:587
  84.8 10.4 %collective-permute-start.26 = (bf16[128,1024]{1,0:T(8,128)(2,1)S(1)}, bf16[128,1024]{1,0:T(8,128)(2,1)S(1)}, u32[]{:S(2)}, u32[]{:S(2)}) collective-permute-start(bf16[128,1024]{1,0:T(8,128)(2,1)S(1)} %get-tuple-element.136), channel_id=1, source_target_pairs={{0,4},{2,6},{4,0},{6,2},{8,12},{10,14},{12,8},{14,10},{16,20},{18,... | collective-permute-start | bytes 786440 | tf_op jit(solution)/shard_map/ppermute | solution.py:587
  101.0 11.7 %collective-permute-start.36 = (bf16[320,256]{1,0:T(8,128)(2,1)S(1)}, bf16[320,256]{1,0:T(8,128)(2,1)S(1)}, u32[]{:S(2)}, u32[]{:S(2)}) collective-permute-start(bf16[320,256]{1,0:T(8,128)(2,1)S(1)} %shard_map.137.refs_0_), channel_id=1, source_target_pairs={{0,6},{2,4},{4,2},{6,0},{8,14},{10,12},{12,10},{14,8},{16,22},{18,... | collective-permute-start | bytes 491528 | tf_op jit(solution)/shard_map/ppermute | solution.py:587
  102.5 10.2 %collective-permute-start.35 = (bf16[320,256]{1,0:T(8,128)(2,1)S(1)}, bf16[320,256]{1,0:T(8,128)(2,1)S(1)}, u32[]{:S(2)}, u32[]{:S(2)}) collective-permute-start(bf16[320,256]{1,0:T(8,128)(2,1)S(1)} %shard_map.137.refs_0_), channel_id=1, source_target_pairs={{0,4},{2,6},{4,0},{6,2},{8,12},{10,14},{12,8},{14,10},{16,20},{18,... | collective-permute-start | bytes 491528 | tf_op jit(solution)/shard_map/ppermute | solution.py:587
  103.9 8.7 %collective-permute-start.34 = (bf16[320,256]{1,0:T(8,128)(2,1)S(1)}, bf16[320,256]{1,0:T(8,128)(2,1)S(1)}, u32[]{:S(2)}, u32[]{:S(2)}) collective-permute-start(bf16[320,256]{1,0:T(8,128)(2,1)S(1)} %shard_map.137.refs_0_), channel_id=1, source_target_pairs={{0,2},{2,0},{4,6},{6,4},{8,10},{10,8},{12,14},{14,12},{16,18},{18,... | collective-permute-start | bytes 491528 | tf_op jit(solution)/shard_map/ppermute | solution.py:587
  114.1 12.8 %collective-permute-start.37 = (bf16[80,1024]{1,0:T(8,128)(2,1)S(1)}, bf16[80,1024]{1,0:T(8,128)(2,1)S(1)}, u32[]{:S(2)}, u32[]{:S(2)}) collective-permute-start(bf16[80,1024]{1,0:T(8,128)(2,1)S(1)} %get-tuple-element.161), channel_id=1, source_target_pairs={{0,8},{2,10},{4,12},{6,14},{8,0},{10,2},{12,4},{14,6},{16,24},{18,... | collective-permute-start | bytes 491528 | tf_op jit(solution)/shard_map/ppermute | solution.py:591
  114.2 14.7 %collective-permute-start.38 = (bf16[80,1024]{1,0:T(8,128)(2,1)S(1)}, bf16[80,1024]{1,0:T(8,128)(2,1)S(1)}, u32[]{:S(2)}, u32[]{:S(2)}) collective-permute-start(bf16[80,1024]{1,0:T(8,128)(2,1)S(1)} %get-tuple-element.162), channel_id=1, source_target_pairs={{0,16},{2,18},{4,20},{6,22},{8,24},{10,26},{12,28},{14,30},{16,0},... | collective-permute-start | bytes 491528 | tf_op jit(solution)/shard_map/ppermute | solution.py:591
  116.5 12.4 %collective-permute-start.39 = (bf16[80,1024]{1,0:T(8,128)(2,1)S(1)}, bf16[80,1024]{1,0:T(8,128)(2,1)S(1)}, u32[]{:S(2)}, u32[]{:S(2)}) collective-permute-start(bf16[80,1024]{1,0:T(8,128)(2,1)S(1)} %get-tuple-element.163), channel_id=1, source_target_pairs={{0,24},{2,26},{4,28},{6,30},{8,16},{10,18},{12,20},{14,22},{16,8},... | collective-permute-start | bytes 491528 | tf_op jit(solution)/shard_map/ppermute | solution.py:591
  129.5 8.8 %collective-permute-start.45 = (bf16[80,1024]{1,0:T(8,128)(2,1)S(1)}, bf16[80,1024]{1,0:T(8,128)(2,1)S(1)}, u32[]{:S(2)}, u32[]{:S(2)}) collective-permute-start(bf16[80,1024]{1,0:T(8,128)(2,1)S(1)} %shard_map.139.refs_0_), channel_id=1, source_target_pairs={{0,16},{2,18},{4,20},{6,22},{8,24},{10,26},{12,28},{14,30},{16,0},... | collective-permute-start | bytes 491528 | tf_op jit(solution)/shard_map/ppermute | solution.py:591
  132.4 9.1 %collective-permute-start.53 = (bf16[80,1024]{1,0:T(8,128)(2,1)S(1)}, bf16[80,1024]{1,0:T(8,128)(2,1)S(1)}, u32[]{:S(2)}, u32[]{:S(2)}) collective-permute-start(bf16[80,1024]{1,0:T(8,128)(2,1)S(1)} %shard_map.139.refs_0_), channel_id=1, source_target_pairs={{0,2},{2,0},{4,6},{6,4},{8,10},{10,8},{12,14},{14,12},{16,18},{18,... | collective-permute-start | bytes 491528 | tf_op jit(solution)/shard_map/ppermute | solution.py:587
  134.1 7.7 %collective-permute-start.42 = (bf16[80,1024]{1,0:T(8,128)(2,1)S(1)}, bf16[80,1024]{1,0:T(8,128)(2,1)S(1)}, u32[]{:S(2)}, u32[]{:S(2)}) collective-permute-start(bf16[80,1024]{1,0:T(8,128)(2,1)S(1)} %shard_map.139.refs_0_), channel_id=1, source_target_pairs={{0,8},{2,10},{4,12},{6,14},{8,0},{10,2},{12,4},{14,6},{16,24},{18,... | collective-permute-start | bytes 491528 | tf_op jit(solution)/shard_map/ppermute | solution.py:591
  134.1 9.4 %collective-permute-start.40 = (bf16[80,1024]{1,0:T(8,128)(2,1)S(1)}, bf16[80,1024]{1,0:T(8,128)(2,1)S(1)}, u32[]{:S(2)}, u32[]{:S(2)}) collective-permute-start(bf16[80,1024]{1,0:T(8,128)(2,1)S(1)} %shard_map.139.refs_0_), channel_id=1, source_target_pairs={{0,4},{2,6},{4,0},{6,2},{8,12},{10,14},{12,8},{14,10},{16,20},{18,... | collective-permute-start | bytes 491528 | tf_op jit(solution)/shard_map/ppermute | solution.py:587
  141.4 8.2 %collective-permute-start.46 = (bf16[80,1024]{1,0:T(8,128)(2,1)S(1)}, bf16[80,1024]{1,0:T(8,128)(2,1)S(1)}, u32[]{:S(2)}, u32[]{:S(2)}) collective-permute-start(bf16[80,1024]{1,0:T(8,128)(2,1)S(1)} %collective-permute-done.45.refs_2_), channel_id=1, source_target_pairs={{0,4},{2,6},{4,0},{6,2},{8,12},{10,14},{12,8},{14,10},{16,20},{18,... | collective-permute-start | bytes 491528 | tf_op jit(solution)/shard_map/ppermute | solution.py:587
  141.8 9.1 %collective-permute-start.51 = (bf16[80,1024]{1,0:T(8,128)(2,1)S(1)}, bf16[80,1024]{1,0:T(8,128)(2,1)S(1)}, u32[]{:S(2)}, u32[]{:S(2)}) collective-permute-start(bf16[80,1024]{1,0:T(8,128)(2,1)S(1)} %collective-permute-done.42.refs_1_), channel_id=1, source_target_pairs={{0,4},{2,6},{4,0},{6,2},{8,12},{10,14},{12,8},{14,10},{16,20},{18,... | collective-permute-start | bytes 491528 | tf_op jit(solution)/shard_map/ppermute | solution.py:587
  143.5 8.2 %collective-permute-start.43 = (bf16[80,1024]{1,0:T(8,128)(2,1)S(1)}, bf16[80,1024]{1,0:T(8,128)(2,1)S(1)}, u32[]{:S(2)}, u32[]{:S(2)}) collective-permute-start(bf16[80,1024]{1,0:T(8,128)(2,1)S(1)} %collective-permute-done.42.refs_1_), channel_id=1, source_target_pairs={{0,2},{2,0},{4,6},{6,4},{8,10},{10,8},{12,14},{14,12},{16,18},{18,... | collective-permute-start | bytes 491528 | tf_op jit(solution)/shard_map/ppermute | solution.py:587
  143.8 9.5 %collective-permute-start.49 = (bf16[80,1024]{1,0:T(8,128)(2,1)S(1)}, bf16[80,1024]{1,0:T(8,128)(2,1)S(1)}, u32[]{:S(2)}, u32[]{:S(2)}) collective-permute-start(bf16[80,1024]{1,0:T(8,128)(2,1)S(1)} %collective-permute-done.48.refs_3_), channel_id=1, source_target_pairs={{0,2},{2,0},{4,6},{6,4},{8,10},{10,8},{12,14},{14,12},{16,18},{18,... | collective-permute-start | bytes 491528 | tf_op jit(solution)/shard_map/ppermute | solution.py:587
  147.3 8.2 %collective-permute-start.52 = (bf16[80,1024]{1,0:T(8,128)(2,1)S(1)}, bf16[80,1024]{1,0:T(8,128)(2,1)S(1)}, u32[]{:S(2)}, u32[]{:S(2)}) collective-permute-start(bf16[80,1024]{1,0:T(8,128)(2,1)S(1)} %collective-permute-done.48.refs_3_), channel_id=1, source_target_pairs={{0,4},{2,6},{4,0},{6,2},{8,12},{10,14},{12,8},{14,10},{16,20},{18,... | collective-permute-start | bytes 491528 | tf_op jit(solution)/shard_map/ppermute | solution.py:587
  (31 other events, 185.6 us)

commit v5 on v4

--- a/solution.py
+++ b/solution.py
@@ -16,7 +16,7 @@
 TABLE = 48
 KINDS = 8
 VMEM_LIMIT = 20 * 1024 * 1024
-VMEM_WIDE = 56 * 1024 * 1024
+VMEM_WIDE = 53 * 1024 * 1024
 FLOPS_US = 1100000000
 
 

time: 163 us -> 161 us (0.988)
  waiting for transfers between devices: 30.7 us -> 35.6 us
  starting transfers between devices: 69 us -> 64.3 us
    ppermute x32, starting transfers between devices: 39.3 us -> 35.7 us  [in_plane(): return lax.ppermute(value, 'seq', pairs)]
    ppermute x32, waiting for transfers between devices: 6.31 us -> 9.03 us  [in_plane(): return lax.ppermute(value, 'seq', pairs)]
    ppermute x20, waiting for transfers between devices: 19.8 us -> 22.2 us  [over_planes(): return lax.ppermute(value, 'seq', pairs)]
  transfers between devices with their start and end apart: 55 -> 55, of which waited for: 18 -> 19; matrix products, arithmetic and copies ran while one was open for 1% -> 1% of each run, Pallas kernels for 28% -> 28%
where the time goes in v5:
time: 161 us; the launch traced here: 160 us
  starting transfers between devices  64.3 us (40%)
  Pallas kernels  54.8 us (34%)
  waiting for transfers between devices  35.6 us (22%)
  between operations  2.7 us (2%)
  local copies, waits for them, and re-layouts  1.79 us (1%)
    ppermute x32, starting transfers between devices, in_plane(): return lax.ppermute(value, 'seq', pairs)  35.7 us
    ppermute x20, starting transfers between devices, over_planes(): return lax.ppermute(value, 'seq', pairs)  28.4 us
    ppermute x20, waiting for transfers between devices, over_planes(): return lax.ppermute(value, 'seq', pairs)  22.2 us
    pallas_call x4, Pallas kernels, error_part(): call(functools.partial(error_body, o == 0, local_heads, o), (1,), [whole(...  11.9 us
    ppermute x32, waiting for transfers between devices, in_plane(): return lax.ppermute(value, 'seq', pairs)  9.03 us
    pallas_call x1, Pallas kernels, shards(): call(functools.partial(local_body, groups, local_heads), (groups,), [whol...  7.55 us
    pallas_call x4, Pallas kernels, shards(): call(functools.partial(spread_body, planes), (1,), [whole(share_shape)] *...  7.22 us
    pallas_call x2, Pallas kernels, project(): call(functools.partial(project_body, copies), (count,), [pl.BlockSpec((le...  6.73 us
  transfers between devices with their start and end apart: 55, of which 19 were waited for; matrix products, arithmetic and copies ran while one was open for 1% of the time, Pallas kernels for 28%

profile of v5, /device:TPU:0, one launch (start us, length us, event | category | flops | bytes accessed | tf_op | source)
XLA Modules:
  0.0 160.3 jit_solution(3940475667457862337)
XLA Ops:
  0.7 2.8 %shard_map.118 = (f32[256,384]{1,0:T(8,128)S(1)}, bf16[256,1024]{1,0:T(8,128)(2,1)}) custom-call(s32[7]{0:T(128)S(1)} %stack.40.sp, bf16[256,4096]{1,0:T(8,128)(2,1)} %refs_4_.3, bf16[8192,256]{1,0:T(8,128)(2,1)} %wb_ref.3, bf16[64,8192]{1,0:T(8,128)(2,1)} %bitcast.18), custom_call_target="tpu_custom_call" | custom-call | flops 1100000000 | tf_op jit(solution)/shard_map/pallas_call | solution.py:610
  3.5 4.0 %collective-permute-start.1 = (bf16[256,1024]{1,0:T(8,128)(2,1)}, bf16[256,1024]{1,0:T(8,128)(2,1)S(1)}, u32[]{:S(2)}, u32[]{:S(2)}) collective-permute-start(bf16[256,1024]{1,0:T(8,128)(2,1)} %get-tuple-element.93), channel_id=1, source_target_pairs={{0,6},{2,4},{4,2},{6,0},{8,14},{10,12},{12,10},{14,8},{16,22},{18,... | collective-permute-start | bytes 1572872 | tf_op jit(solution)/shard_map/ppermute | solution.py:587
  7.5 3.9 %shard_map.119.refs_0_ = f32[256,384]{1,0:T(8,128)S(1)} custom-call(s32[7]{0:T(128)S(1)} %stack.40.sp, bf16[256,4096]{1,0:T(8,128)(2,1)} %refs_4_.3, bf16[8192,256]{1,0:T(8,128)(2,1)} %wb_ref.3, bf16[64,8192]{1,0:T(8,128)(2,1)} %bitcast.19, f32[256,384]{1,0:T(8,128)S(1)} %get-tuple-element.89.refs_0_), custom_call_target="tpu_custom_call" | custom-call | flops 1100000000 | tf_op jit(solution)/shard_map/pallas_call | solution.py:610
  13.2 3.9 %shard_map.120 = (bf16[256,256]{1,0:T(8,128)(2,1)S(1)}, f32[4,48,256]{2,1,0:T(8,128)S(1)}, f32[4,256,128]{2,1,0:T(8,128)S(1)}, bf16[144,1024]{1,0:T(8,128)(2,1)S...) custom-call(s32[7]{0:T(128)S(1)} %stack.40.sp, ...), custom_call_target="tpu_custom_call" | custom-call | flops 1100000000 | tf_op jit(solution)/shard_map/pallas_call | solution.py:646
  17.8 2.9 %collective-permute-start.4 = (bf16[144,1024]{1,0:T(8,128)(2,1)S(1)}, bf16[144,1024]{1,0:T(8,128)(2,1)S(1)}, u32[]{:S(2)}, u32[]{:S(2)}) collective-permute-start(bf16[144,1024]{1,0:T(8,128)(2,1)S(1)} %get-tuple-element.98), channel_id=1, source_target_pairs={{0,6},{2,4},{4,2},{6,0},{8,14},{10,12},{12,10},{14,8},{16,22},{18,... | collective-permute-start | bytes 884744 | tf_op jit(solution)/shard_map/ppermute | solution.py:587
  22.3 7.6 %shard_map.121 = (f32[256,4096]{1,0:T(8,128)S(1)}, bf16[176,1024]{1,0:T(8,128)(2,1)S(1)}, bf16[176,1024]{1,0:T(8,128)(2,1)S(1)}, bf16[176,1024]{1,0:T(8,128)(2,1)S(1)}, bf16[176,1024]{1,0:T(8,128)(2,1)S(1)}) custom-call(s32[7]{0:T(128)S(1)} %stack.40.sp, bf16[256,256]{1,0:T(8,128)(2,1)S(1)} %get-tuple-element.90.bc_ref, ...), custom_call_target="tpu_custom_call" | custom-call | flops 7699999744 | tf_op jit(solution)/shard_map/pallas_call | solution.py:662
  29.8 1.8 %collective-permute-start.5 = (bf16[176,1024]{1,0:T(8,128)(2,1)S(1)}, bf16[176,1024]{1,0:T(8,128)(2,1)S(1)}, u32[]{:S(2)}, u32[]{:S(2)}) collective-permute-start(bf16[176,1024]{1,0:T(8,128)(2,1)S(1)} %get-tuple-element.102), channel_id=1, source_target_pairs={{0,2},{2,0},{4,6},{6,4},{8,10},{10,8},{12,14},{14,12},{16,18},{18,... | collective-permute-start | bytes 1081352 | tf_op jit(solution)/shard_map/ppermute | solution.py:587
  36.7 2.6 %collective-permute-start.9 = (bf16[144,256]{1,0:T(8,128)(2,1)S(1)}, bf16[144,256]{1,0:T(8,128)(2,1)S(1)}, u32[]{:S(2)}, u32[]{:S(2)}) collective-permute-start(bf16[144,256]{1,0:T(8,128)(2,1)S(1)} %get-tuple-element.107), channel_id=1, source_target_pairs={{0,16},{2,18},{4,20},{6,22},{8,24},{10,26},{12,28},{14,30},{16,0},... | collective-permute-start | bytes 221192 | tf_op jit(solution)/shard_map/ppermute | solution.py:591
  39.9 3.2 %collective-permute-start.10 = (bf16[144,256]{1,0:T(8,128)(2,1)S(1)}, bf16[144,256]{1,0:T(8,128)(2,1)S(1)}, u32[]{:S(2)}, u32[]{:S(2)}) collective-permute-start(bf16[144,256]{1,0:T(8,128)(2,1)S(1)} %get-tuple-element.108), channel_id=1, source_target_pairs={{0,24},{2,26},{4,28},{6,30},{8,16},{10,18},{12,20},{14,22},{16,8},... | collective-permute-start | bytes 221192 | tf_op jit(solution)/shard_map/ppermute | solution.py:591
  43.8 2.3 %collective-permute-done.10.refs_3_ = bf16[144,256]{1,0:T(8,128)(2,1)S(1)} collective-permute-done((bf16[144,256]{1,0:T(8,128)(2,1)S(1)}, bf16[144,256]{1,0:T(8,128)(2,1)S(1)}, u32[]{:S(2)}, u32[]{:S(2)}) %collective-permute-start.10) | collective-permute-done | bytes 73760 | tf_op jit(solution)/shard_map/ppermute | solution.py:591
  47.5 3.0 %collective-permute-start.12 = (bf16[128,256]{1,0:T(8,128)(2,1)S(1)}, bf16[128,256]{1,0:T(8,128)(2,1)S(1)}, u32[]{:S(2)}, u32[]{:S(2)}) collective-permute-start(bf16[128,256]{1,0:T(8,128)(2,1)S(1)} %get-tuple-element.111), channel_id=1, source_target_pairs={{0,16},{2,18},{4,20},{6,22},{8,24},{10,26},{12,28},{14,30},{16,0},... | collective-permute-start | bytes 196616 | tf_op jit(solution)/shard_map/ppermute | solution.py:591
  54.2 2.2 %shard_map.123.moment_ref = bf16[4,128,1024]{2,1,0:T(8,128)(2,1)S(1)} custom-call(s32[7]{0:T(128)S(1)} %stack.40.sp, bf16[176,1024]{1,0:T(8,128)(2,1)S(1)} %get-tuple-element.101.refs_0_.refs_4_, bf16[176,1024]{1,0:T(8,128)(2,1)S(1)} %collective-permute-done.5.refs_1_.refs_5_, bf16[176,1024]{1,0:T(8,128)(2,1)S(1)} %collective-permute-done.6.refs_2_.refs_6_, ...), custom_call_target="tpu_custom_call" | custom-call | flops 2200000000 | tf_op jit(solution)/shard_map/pallas_call | solution.py:695
  56.6 2.5 %shard_map.125 = (bf16[128,1024]{1,0:T(8,128)(2,1)S(1)}, bf16[128,1024]{1,0:T(8,128)(2,1)S(1)}, bf16[128,1024]{1,0:T(8,128)(2,1)S(1)}, bf16[128,1024]{1,0:T(8,12...) custom-call(s32[7]{0:T(128)S(1)} %stack.40.sp, ...), custom_call_target="tpu_custom_call" | custom-call | flops 2200000000 | tf_op jit(solution)/shard_map/pallas_call | solution.py:736
  59.1 3.8 %collective-permute-start.18 = (bf16[128,256]{1,0:T(8,128)(2,1)S(1)}, bf16[128,256]{1,0:T(8,128)(2,1)S(1)}, u32[]{:S(2)}, u32[]{:S(2)}) collective-permute-start(bf16[128,256]{1,0:T(8,128)(2,1)S(1)} %get-tuple-element.121), channel_id=1, source_target_pairs={{0,16},{2,18},{4,20},{6,22},{8,24},{10,26},{12,28},{14,30},{16,0},... | collective-permute-start | bytes 196616 | tf_op jit(solution)/shard_map/ppermute | solution.py:591
  65.1 2.9 %shard_map.126 = (f32[16,256]{1,0:T(8,128)S(1)}, f32[16,128]{1,0:T(8,128)S(1)}, f32[256,384]{1,0:T(8,128)S(1)}, f32[8,128]{1,0:T(8,128)S(1)}) custom-call(s32[7]{0:T(128)S(1)} %stack.40.sp, bf16[256,256]{1,0:T(8,128)(2,1)S(1)} %get-tuple-element.90.bc_ref, f32[4,48,256]{2,1,0:T(8,128)S(1)} %get-tuple-element.91.rows_ref, ...), custom_call_target="tpu_custom_call" | custom-call | flops 4400000000 | tf_op jit(solution)/shard_map/pallas_call | solution.py:777
  70.8 3.7 %collective-permute-start.23 = (bf16[128,256]{1,0:T(8,128)(2,1)S(1)}, bf16[128,256]{1,0:T(8,128)(2,1)S(1)}, u32[]{:S(2)}, u32[]{:S(2)}) collective-permute-start(bf16[128,256]{1,0:T(8,128)(2,1)S(1)} %get-tuple-element.129), channel_id=1, source_target_pairs={{0,16},{2,18},{4,20},{6,22},{8,24},{10,26},{12,28},{14,30},{16,0},... | collective-permute-start | bytes 196616 | tf_op jit(solution)/shard_map/ppermute | solution.py:591
  75.2 3.0 %shard_map.128 = (f32[16,256]{1,0:T(8,128)S(1)}, f32[16,128]{1,0:T(8,128)S(1)}, f32[256,384]{1,0:T(8,128)S(1)}, f32[8,128]{1,0:T(8,128)}) custom-call(s32[7]{0:T(128)S(1)} %stack.40.sp, bf16[256,256]{1,0:T(8,128)(2,1)S(1)} %get-tuple-element.90.bc_ref, f32[4,48,256]{2,1,0:T(8,128)S(1)} %get-tuple-element.91.rows_ref, ...), custom_call_target="tpu_custom_call" | custom-call | flops 4400000000 | tf_op jit(solution)/shard_map/pallas_call | solution.py:777
  78.1 2.4 %collective-permute-done.24.refs_3_ = bf16[128,256]{1,0:T(8,128)(2,1)S(1)} collective-permute-done((bf16[128,256]{1,0:T(8,128)(2,1)S(1)}, bf16[128,256]{1,0:T(8,128)(2,1)S(1)}, u32[]{:S(2)}, u32[]{:S(2)}) %collective-permute-start.24) | collective-permute-done | bytes 65568 | tf_op jit(solution)/shard_map/ppermute | solution.py:591
  83.2 1.8 %collective-permute-start.27 = (bf16[128,1024]{1,0:T(8,128)(2,1)S(1)}, bf16[128,1024]{1,0:T(8,128)(2,1)S(1)}, u32[]{:S(2)}, u32[]{:S(2)}) collective-permute-start(bf16[128,1024]{1,0:T(8,128)(2,1)S(1)} %get-tuple-element.137), channel_id=1, source_target_pairs={{0,2},{2,0},{4,6},{6,4},{8,10},{10,8},{12,14},{14,12},{16,18},{18,... | collective-permute-start | bytes 786440 | tf_op jit(solution)/shard_map/ppermute | solution.py:587
  85.1 3.1 %shard_map.130 = (f32[16,256]{1,0:T(8,128)S(1)}, f32[16,128]{1,0:T(8,128)S(1)}, f32[256,384]{1,0:T(8,128)S(1)}, f32[8,128]{1,0:T(8,128)}) custom-call(s32[7]{0:T(128)S(1)} %stack.40.sp, bf16[256,256]{1,0:T(8,128)(2,1)S(1)} %get-tuple-element.90.bc_ref, f32[4,48,256]{2,1,0:T(8,128)S(1)} %get-tuple-element.91.rows_ref, ...), custom_call_target="tpu_custom_call" | custom-call | flops 4400000000 | tf_op jit(solution)/shard_map/pallas_call | solution.py:777
  88.2 3.0 %shard_map.131 = (f32[16,256]{1,0:T(8,128)S(1)}, f32[16,128]{1,0:T(8,128)S(1)}, f32[256,384]{1,0:T(8,128)S(1)}, f32[8,128]{1,0:T(8,128)}) custom-call(s32[7]{0:T(128)S(1)} %stack.40.sp, bf16[256,256]{1,0:T(8,128)(2,1)S(1)} %get-tuple-element.90.bc_ref, f32[4,48,256]{2,1,0:T(8,128)S(1)} %get-tuple-element.91.rows_ref, ...), custom_call_target="tpu_custom_call" | custom-call | flops 4400000000 | tf_op jit(solution)/shard_map/pallas_call | solution.py:777
  101.2 1.8 %collective-permute-start.34 = (bf16[320,256]{1,0:T(8,128)(2,1)S(1)}, bf16[320,256]{1,0:T(8,128)(2,1)S(1)}, u32[]{:S(2)}, u32[]{:S(2)}) collective-permute-start(bf16[320,256]{1,0:T(8,128)(2,1)S(1)} %shard_map.137.refs_0_), channel_id=1, source_target_pairs={{0,2},{2,0},{4,6},{6,4},{8,10},{10,8},{12,14},{14,12},{16,18},{18,... | collective-permute-start | bytes 491528 | tf_op jit(solution)/shard_map/ppermute | solution.py:587
  103.1 3.6 %collective-permute-done.28 = f32[8,128]{1,0:T(8,128)S(1)} collective-permute-done((f32[8,128]{1,0:T(8,128)S(1)}, f32[8,128]{1,0:T(8,128)S(1)}, u32[]{:S(2)}, u32[]{:S(2)}) %collective-permute-start.28) | collective-permute-done | bytes 4128 | tf_op jit(solution)/shard_map/ppermute | solution.py:591
  106.7 4.5 %collective-permute-done.29 = f32[8,128]{1,0:T(8,128)S(1)} collective-permute-done((f32[8,128]{1,0:T(8,128)S(1)}, f32[8,128]{1,0:T(8,128)S(1)}, u32[]{:S(2)}, u32[]{:S(2)}) %collective-permute-start.29) | collective-permute-done | bytes 4128 | tf_op jit(solution)/shard_map/ppermute | solution.py:591
  114.0 3.1 %collective-permute-start.39 = (bf16[80,1024]{1,0:T(8,128)(2,1)S(1)}, bf16[80,1024]{1,0:T(8,128)(2,1)S(1)}, u32[]{:S(2)}, u32[]{:S(2)}) collective-permute-start(bf16[80,1024]{1,0:T(8,128)(2,1)S(1)} %get-tuple-element.163), channel_id=1, source_target_pairs={{0,24},{2,26},{4,28},{6,30},{8,16},{10,18},{12,20},{14,22},{16,8},... | collective-permute-start | bytes 491528 | tf_op jit(solution)/shard_map/ppermute | solution.py:591
  117.3 3.4 %collective-permute-done.30 = f32[8,128]{1,0:T(8,128)S(1)} collective-permute-done((f32[8,128]{1,0:T(8,128)S(1)}, f32[8,128]{1,0:T(8,128)S(1)}, u32[]{:S(2)}, u32[]{:S(2)}) %collective-permute-start.30) | collective-permute-done | bytes 4128 | tf_op jit(solution)/shard_map/ppermute | solution.py:587
  121.2 3.1 %collective-permute-done.31 = f32[8,128]{1,0:T(8,128)S(1)} collective-permute-done((f32[8,128]{1,0:T(8,128)S(1)}, f32[8,128]{1,0:T(8,128)S(1)}, u32[]{:S(2)}, u32[]{:S(2)}) %collective-permute-start.31) | collective-permute-done | bytes 4128 | tf_op jit(solution)/shard_map/ppermute | solution.py:587
  126.7 3.3 %collective-permute-start.45 = (bf16[80,1024]{1,0:T(8,128)(2,1)S(1)}, bf16[80,1024]{1,0:T(8,128)(2,1)S(1)}, u32[]{:S(2)}, u32[]{:S(2)}) collective-permute-start(bf16[80,1024]{1,0:T(8,128)(2,1)S(1)} %shard_map.139.refs_0_), channel_id=1, source_target_pairs={{0,16},{2,18},{4,20},{6,22},{8,24},{10,26},{12,28},{14,30},{16,0},... | collective-permute-start | bytes 491528 | tf_op jit(solution)/shard_map/ppermute | solution.py:591
  131.7 5.1 %collective-permute-done.45.refs_2_ = bf16[80,1024]{1,0:T(8,128)(2,1)S(1)} collective-permute-done((bf16[80,1024]{1,0:T(8,128)(2,1)S(1)}, bf16[80,1024]{1,0:T(8,128)(2,1)S(1)}, u32[]{:S(2)}, u32[]{:S(2)}) %collective-permute-start.45) | collective-permute-done | bytes 163872 | tf_op jit(solution)/shard_map/ppermute | solution.py:591
  140.9 1.9 %collective-permute-done.48.refs_3_ = bf16[80,1024]{1,0:T(8,128)(2,1)S(1)} collective-permute-done((bf16[80,1024]{1,0:T(8,128)(2,1)S(1)}, bf16[80,1024]{1,0:T(8,128)(2,1)S(1)}, u32[]{:S(2)}, u32[]{:S(2)}) %collective-permute-start.48) | collective-permute-done | bytes 163872 | tf_op jit(solution)/shard_map/ppermute | solution.py:591
  153.5 1.8 %shard_map.142 = (f32[4096,256]{1,0:T(8,128)}, f32[64,4096]{1,0:T(8,128)}) custom-call(s32[7]{0:T(128)S(1)} %stack.40.sp, bf16[80,1024]{1,0:T(8,128)(2,1)S(1)} %collective-permute-done.40.refs_0_, bf16[80,1024]{1,0:T(8,128)(2,1)S(1)} %collective-permute-done.51.refs_1_, ...), custom_call_target="tpu_custom_call", output_to_operand_aliasing={{0}: (5, {}), {1}: (6, {})} | custom-call | flops 1100000000 | tf_op jit(solution)/shard_map/pallas_call | solution.py:937
  157.4 1.8 %shard_map.143 = (f32[4096,256]{1,0:T(8,128)}, f32[64,4096]{1,0:T(8,128)}) custom-call(s32[7]{0:T(128)S(1)} %stack.40.sp, bf16[80,1024]{1,0:T(8,128)(2,1)S(1)} %collective-permute-done.41.refs_0_, bf16[80,1024]{1,0:T(8,128)(2,1)S(1)} %collective-permute-done.44.refs_1_, ...), custom_call_target="tpu_custom_call", output_to_operand_aliasing={{0}: (5, {}), {1}: (6, {})} | custom-call | flops 1100000000 | tf_op jit(solution)/shard_map/pallas_call | solution.py:937
  (125 shorter events, 57.8 us)
Async XLA Ops:
  3.5 17.1 %collective-permute-start.1 = (bf16[256,1024]{1,0:T(8,128)(2,1)}, bf16[256,1024]{1,0:T(8,128)(2,1)S(1)}, u32[]{:S(2)}, u32[]{:S(2)}) collective-permute-start(bf16[256,1024]{1,0:T(8,128)(2,1)} %get-tuple-element.93), channel_id=1, source_target_pairs={{0,6},{2,4},{4,2},{6,0},{8,14},{10,12},{12,10},{14,8},{16,22},{18,... | collective-permute-start | bytes 1572872 | tf_op jit(solution)/shard_map/ppermute | solution.py:587
  17.1 15.8 %collective-permute-start.2 = (bf16[144,1024]{1,0:T(8,128)(2,1)S(1)}, bf16[144,1024]{1,0:T(8,128)(2,1)S(1)}, u32[]{:S(2)}, u32[]{:S(2)}) collective-permute-start(bf16[144,1024]{1,0:T(8,128)(2,1)S(1)} %get-tuple-element.96), channel_id=1, source_target_pairs={{0,2},{2,0},{4,6},{6,4},{8,10},{10,8},{12,14},{14,12},{16,18},{18,... | collective-permute-start | bytes 884744 | tf_op jit(solution)/shard_map/ppermute | solution.py:587
  17.7 15.7 %collective-permute-start.3 = (bf16[144,1024]{1,0:T(8,128)(2,1)S(1)}, bf16[144,1024]{1,0:T(8,128)(2,1)S(1)}, u32[]{:S(2)}, u32[]{:S(2)}) collective-permute-start(bf16[144,1024]{1,0:T(8,128)(2,1)S(1)} %get-tuple-element.97), channel_id=1, source_target_pairs={{0,4},{2,6},{4,0},{6,2},{8,12},{10,14},{12,8},{14,10},{16,20},{18,... | collective-permute-start | bytes 884744 | tf_op jit(solution)/shard_map/ppermute | solution.py:587
  17.8 15.6 %collective-permute-start.4 = (bf16[144,1024]{1,0:T(8,128)(2,1)S(1)}, bf16[144,1024]{1,0:T(8,128)(2,1)S(1)}, u32[]{:S(2)}, u32[]{:S(2)}) collective-permute-start(bf16[144,1024]{1,0:T(8,128)(2,1)S(1)} %get-tuple-element.98), channel_id=1, source_target_pairs={{0,6},{2,4},{4,2},{6,0},{8,14},{10,12},{12,10},{14,8},{16,22},{18,... | collective-permute-start | bytes 884744 | tf_op jit(solution)/shard_map/ppermute | solution.py:587
  29.8 20.7 %collective-permute-start.5 = (bf16[176,1024]{1,0:T(8,128)(2,1)S(1)}, bf16[176,1024]{1,0:T(8,128)(2,1)S(1)}, u32[]{:S(2)}, u32[]{:S(2)}) collective-permute-start(bf16[176,1024]{1,0:T(8,128)(2,1)S(1)} %get-tuple-element.102), channel_id=1, source_target_pairs={{0,2},{2,0},{4,6},{6,4},{8,10},{10,8},{12,14},{14,12},{16,18},{18,... | collective-permute-start | bytes 1081352 | tf_op jit(solution)/shard_map/ppermute | solution.py:587
  31.7 19.6 %collective-permute-start.6 = (bf16[176,1024]{1,0:T(8,128)(2,1)S(1)}, bf16[176,1024]{1,0:T(8,128)(2,1)S(1)}, u32[]{:S(2)}, u32[]{:S(2)}) collective-permute-start(bf16[176,1024]{1,0:T(8,128)(2,1)S(1)} %get-tuple-element.103), channel_id=1, source_target_pairs={{0,4},{2,6},{4,0},{6,2},{8,12},{10,14},{12,8},{14,10},{16,20},{18,... | collective-permute-start | bytes 1081352 | tf_op jit(solution)/shard_map/ppermute | solution.py:587
  32.9 19.8 %collective-permute-start.7 = (bf16[176,1024]{1,0:T(8,128)(2,1)S(1)}, bf16[176,1024]{1,0:T(8,128)(2,1)S(1)}, u32[]{:S(2)}, u32[]{:S(2)}) collective-permute-start(bf16[176,1024]{1,0:T(8,128)(2,1)S(1)} %get-tuple-element.104), channel_id=1, source_target_pairs={{0,6},{2,4},{4,2},{6,0},{8,14},{10,12},{12,10},{14,8},{16,22},{18,... | collective-permute-start | bytes 1081352 | tf_op jit(solution)/shard_map/ppermute | solution.py:587
  46.8 9.6 %collective-permute-start.11 = (bf16[128,256]{1,0:T(8,128)(2,1)S(1)}, bf16[128,256]{1,0:T(8,128)(2,1)S(1)}, u32[]{:S(2)}, u32[]{:S(2)}) collective-permute-start(bf16[128,256]{1,0:T(8,128)(2,1)S(1)} %get-tuple-element.110), channel_id=1, source_target_pairs={{0,8},{2,10},{4,12},{6,14},{8,0},{10,2},{12,4},{14,6},{16,24},{18,... | collective-permute-start | bytes 196616 | tf_op jit(solution)/shard_map/ppermute | solution.py:591
  47.5 8.9 %collective-permute-start.12 = (bf16[128,256]{1,0:T(8,128)(2,1)S(1)}, bf16[128,256]{1,0:T(8,128)(2,1)S(1)}, u32[]{:S(2)}, u32[]{:S(2)}) collective-permute-start(bf16[128,256]{1,0:T(8,128)(2,1)S(1)} %get-tuple-element.111), channel_id=1, source_target_pairs={{0,16},{2,18},{4,20},{6,22},{8,24},{10,26},{12,28},{14,30},{16,0},... | collective-permute-start | bytes 196616 | tf_op jit(solution)/shard_map/ppermute | solution.py:591
  51.3 18.8 %collective-permute-start.20 = (bf16[256,1024]{1,0:T(8,128)(2,1)S(1)}, bf16[256,1024]{1,0:T(8,128)(2,1)S(1)}, u32[]{:S(2)}, u32[]{:S(2)}) collective-permute-start(bf16[256,1024]{1,0:T(8,128)(2,1)S(1)} %get-tuple-element.123), channel_id=1, source_target_pairs={{0,2},{2,0},{4,6},{6,4},{8,10},{10,8},{12,14},{14,12},{16,18},{18,... | collective-permute-start | bytes 1572872 | tf_op jit(solution)/shard_map/ppermute | solution.py:587
  52.7 17.4 %collective-permute-start.21 = (bf16[256,1024]{1,0:T(8,128)(2,1)S(1)}, bf16[256,1024]{1,0:T(8,128)(2,1)S(1)}, u32[]{:S(2)}, u32[]{:S(2)}) collective-permute-start(bf16[256,1024]{1,0:T(8,128)(2,1)S(1)} %get-tuple-element.124), channel_id=1, source_target_pairs={{0,4},{2,6},{4,0},{6,2},{8,12},{10,14},{12,8},{14,10},{16,20},{18,... | collective-permute-start | bytes 1572872 | tf_op jit(solution)/shard_map/ppermute | solution.py:587
  59.1 8.9 %collective-permute-start.18 = (bf16[128,256]{1,0:T(8,128)(2,1)S(1)}, bf16[128,256]{1,0:T(8,128)(2,1)S(1)}, u32[]{:S(2)}, u32[]{:S(2)}) collective-permute-start(bf16[128,256]{1,0:T(8,128)(2,1)S(1)} %get-tuple-element.121), channel_id=1, source_target_pairs={{0,16},{2,18},{4,20},{6,22},{8,24},{10,26},{12,28},{14,30},{16,0},... | collective-permute-start | bytes 196616 | tf_op jit(solution)/shard_map/ppermute | solution.py:591
  63.5 10.9 %collective-permute-start.16 = (bf16[128,1024]{1,0:T(8,128)(2,1)S(1)}, bf16[128,1024]{1,0:T(8,128)(2,1)S(1)}, u32[]{:S(2)}, u32[]{:S(2)}) collective-permute-start(bf16[128,1024]{1,0:T(8,128)(2,1)S(1)} %get-tuple-element.115), channel_id=1, source_target_pairs={{0,2},{2,0},{4,6},{6,4},{8,10},{10,8},{12,14},{14,12},{16,18},{18,... | collective-permute-start | bytes 786440 | tf_op jit(solution)/shard_map/ppermute | solution.py:587
  68.1 20.1 %collective-permute-start.14 = (bf16[128,1024]{1,0:T(8,128)(2,1)S(1)}, bf16[128,1024]{1,0:T(8,128)(2,1)S(1)}, u32[]{:S(2)}, u32[]{:S(2)}) collective-permute-start(bf16[128,1024]{1,0:T(8,128)(2,1)S(1)} %get-tuple-element.113), channel_id=1, source_target_pairs={{0,6},{2,4},{4,2},{6,0},{8,14},{10,12},{12,10},{14,8},{16,22},{18,... | collective-permute-start | bytes 786440 | tf_op jit(solution)/shard_map/ppermute | solution.py:587
  69.6 15.5 %collective-permute-start.15 = (bf16[128,1024]{1,0:T(8,128)(2,1)S(1)}, bf16[128,1024]{1,0:T(8,128)(2,1)S(1)}, u32[]{:S(2)}, u32[]{:S(2)}) collective-permute-start(bf16[128,1024]{1,0:T(8,128)(2,1)S(1)} %get-tuple-element.114), channel_id=1, source_target_pairs={{0,4},{2,6},{4,0},{6,2},{8,12},{10,14},{12,8},{14,10},{16,20},{18,... | collective-permute-start | bytes 786440 | tf_op jit(solution)/shard_map/ppermute | solution.py:587
  81.5 13.4 %collective-permute-start.25 = (bf16[128,1024]{1,0:T(8,128)(2,1)S(1)}, bf16[128,1024]{1,0:T(8,128)(2,1)S(1)}, u32[]{:S(2)}, u32[]{:S(2)}) collective-permute-start(bf16[128,1024]{1,0:T(8,128)(2,1)S(1)} %get-tuple-element.135), channel_id=1, source_target_pairs={{0,6},{2,4},{4,2},{6,0},{8,14},{10,12},{12,10},{14,8},{16,22},{18,... | collective-permute-start | bytes 786440 | tf_op jit(solution)/shard_map/ppermute | solution.py:587
  81.9 11.8 %collective-permute-start.26 = (bf16[128,1024]{1,0:T(8,128)(2,1)S(1)}, bf16[128,1024]{1,0:T(8,128)(2,1)S(1)}, u32[]{:S(2)}, u32[]{:S(2)}) collective-permute-start(bf16[128,1024]{1,0:T(8,128)(2,1)S(1)} %get-tuple-element.136), channel_id=1, source_target_pairs={{0,4},{2,6},{4,0},{6,2},{8,12},{10,14},{12,8},{14,10},{16,20},{18,... | collective-permute-start | bytes 786440 | tf_op jit(solution)/shard_map/ppermute | solution.py:587
  83.2 9.2 %collective-permute-start.27 = (bf16[128,1024]{1,0:T(8,128)(2,1)S(1)}, bf16[128,1024]{1,0:T(8,128)(2,1)S(1)}, u32[]{:S(2)}, u32[]{:S(2)}) collective-permute-start(bf16[128,1024]{1,0:T(8,128)(2,1)S(1)} %get-tuple-element.137), channel_id=1, source_target_pairs={{0,2},{2,0},{4,6},{6,4},{8,10},{10,8},{12,14},{14,12},{16,18},{18,... | collective-permute-start | bytes 786440 | tf_op jit(solution)/shard_map/ppermute | solution.py:587
  99.5 11.7 %collective-permute-start.36 = (bf16[320,256]{1,0:T(8,128)(2,1)S(1)}, bf16[320,256]{1,0:T(8,128)(2,1)S(1)}, u32[]{:S(2)}, u32[]{:S(2)}) collective-permute-start(bf16[320,256]{1,0:T(8,128)(2,1)S(1)} %shard_map.137.refs_0_), channel_id=1, source_target_pairs={{0,6},{2,4},{4,2},{6,0},{8,14},{10,12},{12,10},{14,8},{16,22},{18,... | collective-permute-start | bytes 491528 | tf_op jit(solution)/shard_map/ppermute | solution.py:587
  99.9 11.3 %collective-permute-start.35 = (bf16[320,256]{1,0:T(8,128)(2,1)S(1)}, bf16[320,256]{1,0:T(8,128)(2,1)S(1)}, u32[]{:S(2)}, u32[]{:S(2)}) collective-permute-start(bf16[320,256]{1,0:T(8,128)(2,1)S(1)} %shard_map.137.refs_0_), channel_id=1, source_target_pairs={{0,4},{2,6},{4,0},{6,2},{8,12},{10,14},{12,8},{14,10},{16,20},{18,... | collective-permute-start | bytes 491528 | tf_op jit(solution)/shard_map/ppermute | solution.py:587
  101.2 10.0 %collective-permute-start.34 = (bf16[320,256]{1,0:T(8,128)(2,1)S(1)}, bf16[320,256]{1,0:T(8,128)(2,1)S(1)}, u32[]{:S(2)}, u32[]{:S(2)}) collective-permute-start(bf16[320,256]{1,0:T(8,128)(2,1)S(1)} %shard_map.137.refs_0_), channel_id=1, source_target_pairs={{0,2},{2,0},{4,6},{6,4},{8,10},{10,8},{12,14},{14,12},{16,18},{18,... | collective-permute-start | bytes 491528 | tf_op jit(solution)/shard_map/ppermute | solution.py:587
  112.7 12.8 %collective-permute-start.37 = (bf16[80,1024]{1,0:T(8,128)(2,1)S(1)}, bf16[80,1024]{1,0:T(8,128)(2,1)S(1)}, u32[]{:S(2)}, u32[]{:S(2)}) collective-permute-start(bf16[80,1024]{1,0:T(8,128)(2,1)S(1)} %get-tuple-element.161), channel_id=1, source_target_pairs={{0,8},{2,10},{4,12},{6,14},{8,0},{10,2},{12,4},{14,6},{16,24},{18,... | collective-permute-start | bytes 491528 | tf_op jit(solution)/shard_map/ppermute | solution.py:591
  112.8 13.3 %collective-permute-start.38 = (bf16[80,1024]{1,0:T(8,128)(2,1)S(1)}, bf16[80,1024]{1,0:T(8,128)(2,1)S(1)}, u32[]{:S(2)}, u32[]{:S(2)}) collective-permute-start(bf16[80,1024]{1,0:T(8,128)(2,1)S(1)} %get-tuple-element.162), channel_id=1, source_target_pairs={{0,16},{2,18},{4,20},{6,22},{8,24},{10,26},{12,28},{14,30},{16,0},... | collective-permute-start | bytes 491528 | tf_op jit(solution)/shard_map/ppermute | solution.py:591
  114.0 12.0 %collective-permute-start.39 = (bf16[80,1024]{1,0:T(8,128)(2,1)S(1)}, bf16[80,1024]{1,0:T(8,128)(2,1)S(1)}, u32[]{:S(2)}, u32[]{:S(2)}) collective-permute-start(bf16[80,1024]{1,0:T(8,128)(2,1)S(1)} %get-tuple-element.163), channel_id=1, source_target_pairs={{0,24},{2,26},{4,28},{6,30},{8,16},{10,18},{12,20},{14,22},{16,8},... | collective-permute-start | bytes 491528 | tf_op jit(solution)/shard_map/ppermute | solution.py:591
  126.7 10.1 %collective-permute-start.45 = (bf16[80,1024]{1,0:T(8,128)(2,1)S(1)}, bf16[80,1024]{1,0:T(8,128)(2,1)S(1)}, u32[]{:S(2)}, u32[]{:S(2)}) collective-permute-start(bf16[80,1024]{1,0:T(8,128)(2,1)S(1)} %shard_map.139.refs_0_), channel_id=1, source_target_pairs={{0,16},{2,18},{4,20},{6,22},{8,24},{10,26},{12,28},{14,30},{16,0},... | collective-permute-start | bytes 491528 | tf_op jit(solution)/shard_map/ppermute | solution.py:591
  130.0 8.6 %collective-permute-start.53 = (bf16[80,1024]{1,0:T(8,128)(2,1)S(1)}, bf16[80,1024]{1,0:T(8,128)(2,1)S(1)}, u32[]{:S(2)}, u32[]{:S(2)}) collective-permute-start(bf16[80,1024]{1,0:T(8,128)(2,1)S(1)} %shard_map.139.refs_0_), channel_id=1, source_target_pairs={{0,2},{2,0},{4,6},{6,4},{8,10},{10,8},{12,14},{14,12},{16,18},{18,... | collective-permute-start | bytes 491528 | tf_op jit(solution)/shard_map/ppermute | solution.py:587
  131.5 9.1 %collective-permute-start.40 = (bf16[80,1024]{1,0:T(8,128)(2,1)S(1)}, bf16[80,1024]{1,0:T(8,128)(2,1)S(1)}, u32[]{:S(2)}, u32[]{:S(2)}) collective-permute-start(bf16[80,1024]{1,0:T(8,128)(2,1)S(1)} %shard_map.139.refs_0_), channel_id=1, source_target_pairs={{0,4},{2,6},{4,0},{6,2},{8,12},{10,14},{12,8},{14,10},{16,20},{18,... | collective-permute-start | bytes 491528 | tf_op jit(solution)/shard_map/ppermute | solution.py:587
  138.6 9.0 %collective-permute-start.46 = (bf16[80,1024]{1,0:T(8,128)(2,1)S(1)}, bf16[80,1024]{1,0:T(8,128)(2,1)S(1)}, u32[]{:S(2)}, u32[]{:S(2)}) collective-permute-start(bf16[80,1024]{1,0:T(8,128)(2,1)S(1)} %collective-permute-done.45.refs_2_), channel_id=1, source_target_pairs={{0,4},{2,6},{4,0},{6,2},{8,12},{10,14},{12,8},{14,10},{16,20},{18,... | collective-permute-start | bytes 491528 | tf_op jit(solution)/shard_map/ppermute | solution.py:587
  139.1 9.5 %collective-permute-start.51 = (bf16[80,1024]{1,0:T(8,128)(2,1)S(1)}, bf16[80,1024]{1,0:T(8,128)(2,1)S(1)}, u32[]{:S(2)}, u32[]{:S(2)}) collective-permute-start(bf16[80,1024]{1,0:T(8,128)(2,1)S(1)} %collective-permute-done.42.refs_1_), channel_id=1, source_target_pairs={{0,4},{2,6},{4,0},{6,2},{8,12},{10,14},{12,8},{14,10},{16,20},{18,... | collective-permute-start | bytes 491528 | tf_op jit(solution)/shard_map/ppermute | solution.py:587
  140.6 9.0 %collective-permute-start.43 = (bf16[80,1024]{1,0:T(8,128)(2,1)S(1)}, bf16[80,1024]{1,0:T(8,128)(2,1)S(1)}, u32[]{:S(2)}, u32[]{:S(2)}) collective-permute-start(bf16[80,1024]{1,0:T(8,128)(2,1)S(1)} %collective-permute-done.42.refs_1_), channel_id=1, source_target_pairs={{0,2},{2,0},{4,6},{6,4},{8,10},{10,8},{12,14},{14,12},{16,18},{18,... | collective-permute-start | bytes 491528 | tf_op jit(solution)/shard_map/ppermute | solution.py:587
  142.9 8.4 %collective-permute-start.49 = (bf16[80,1024]{1,0:T(8,128)(2,1)S(1)}, bf16[80,1024]{1,0:T(8,128)(2,1)S(1)}, u32[]{:S(2)}, u32[]{:S(2)}) collective-permute-start(bf16[80,1024]{1,0:T(8,128)(2,1)S(1)} %collective-permute-done.48.refs_3_), channel_id=1, source_target_pairs={{0,2},{2,0},{4,6},{6,4},{8,10},{10,8},{12,14},{14,12},{16,18},{18,... | collective-permute-start | bytes 491528 | tf_op jit(solution)/shard_map/ppermute | solution.py:587
  145.0 8.6 %collective-permute-start.52 = (bf16[80,1024]{1,0:T(8,128)(2,1)S(1)}, bf16[80,1024]{1,0:T(8,128)(2,1)S(1)}, u32[]{:S(2)}, u32[]{:S(2)}) collective-permute-start(bf16[80,1024]{1,0:T(8,128)(2,1)S(1)} %collective-permute-done.48.refs_3_), channel_id=1, source_target_pairs={{0,4},{2,6},{4,0},{6,2},{8,12},{10,14},{12,8},{14,10},{16,20},{18,... | collective-permute-start | bytes 491528 | tf_op jit(solution)/shard_map/ppermute | solution.py:587
  (29 other events, 171.3 us)

commit v6 on v5

--- a/solution.py
+++ b/solution.py
@@ -114,8 +114,8 @@
 
 def table_body(groups, local_heads, members, sp, *refs):
     projs = refs[:members]
-    u_ref, par_ref, bc_ref, rows_ref, cols_ref = refs[members : members + 5]
-    messages, dt_all, table_ref = refs[members + 5 : -2], refs[-2], refs[-1]
+    u_ref, par_ref, _, bc_ref, rows_ref, cols_ref = refs[members : members + 6]
+    messages, dt_all, table_ref = refs[members + 6 : -2], refs[-2], refs[-1]
     o = pl.program_id(0)
     q = o ^ sp[1]
     length = u_ref.shape[0]
@@ -646,7 +646,7 @@
     bc, rows, cols, *messages = call(
         functools.partial(table_body, groups, local_heads, dp_count),
         (groups,),
-        [whole((length, proj_width))] * dp_count + [group_wide, whole(params.shape)],
+        [whole((length, proj_width))] * dp_count + [group_wide, whole(params.shape), AFTER],
         [whole((length, bc_width)), group_rows, group_cols] + [whole(message_shape)] * groups,
         [
             shape_of((length, bc_width), BF16),
@@ -656,7 +656,7 @@
         + [shape_of(message_shape, BF16)] * groups,
         [pltpu.VMEM((LANE, length), F32), pltpu.VMEM((groups, TABLE, length), F32)],
         us=1,
-    )(sp, *projs, teacher_rows, params)
+    )(sp, *projs, teacher_rows, params, teacher_next)
     messages = exchanged(messages)
 
     err, *outs = call(

time: 161 us -> 162 us (level)
  starting transfers between devices: 64.3 us -> 68.1 us
  waiting for transfers between devices: 35.6 us -> 33.7 us
    ppermute x32, starting transfers between devices: 35.7 us -> 38.2 us  [in_plane(): return lax.ppermute(value, 'seq', pairs)]
  transfers between devices with their start and end apart: 55 -> 55, of which waited for: 19 -> 21; matrix products, arithmetic and copies ran while one was open for 1% -> 1% of each run, Pallas kernels for 28% -> 28%
where the time goes in v6:
time: 162 us
  starting transfers between devices  68.1 us (42%)
  Pallas kernels  54.8 us (34%)
  waiting for transfers between devices  33.7 us (21%)
  between operations  2.7 us (2%)
  local copies, waits for them, and re-layouts  1.79 us (1%)
    ppermute x32, starting transfers between devices, in_plane(): return lax.ppermute(value, 'seq', pairs)  38.2 us
    ppermute x20, starting transfers between devices, over_planes(): return lax.ppermute(value, 'seq', pairs)  29.7 us
    ppermute x20, waiting for transfers between devices, over_planes(): return lax.ppermute(value, 'seq', pairs)  21.4 us
    pallas_call x4, Pallas kernels, error_part(): call(functools.partial(error_body, o == 0, local_heads, o), (1,), [whole(...  11.9 us
    ppermute x32, waiting for transfers between devices, in_plane(): return lax.ppermute(value, 'seq', pairs)  7.91 us
    pallas_call x1, Pallas kernels, shards(): call(functools.partial(local_body, groups, local_heads), (groups,), [whol...  7.55 us
    pallas_call x4, Pallas kernels, shards(): call(functools.partial(spread_body, planes), (1,), [whole(share_shape)] *...  7.22 us
    pallas_call x2, Pallas kernels, project(): call(functools.partial(project_body, copies), (count,), [pl.BlockSpec((le...  6.73 us
  transfers between devices with their start and end apart: 55, of which 21 were waited for; matrix products, arithmetic and copies ran while one was open for 1% of the time, Pallas kernels for 28%

profile of v6, /device:TPU:0, one launch (start us, length us, event | category | flops | bytes accessed | tf_op | source)
XLA Modules:
  0.0 162.1 jit_solution(1509627480045224087)
XLA Ops:
  0.7 2.8 %shard_map.118 = (f32[256,384]{1,0:T(8,128)S(1)}, bf16[256,1024]{1,0:T(8,128)(2,1)}) custom-call(s32[7]{0:T(128)S(1)} %stack.40.sp, bf16[256,4096]{1,0:T(8,128)(2,1)} %refs_4_.5, bf16[8192,256]{1,0:T(8,128)(2,1)} %wb_ref.3, bf16[64,8192]{1,0:T(8,128)(2,1)} %bitcast.18), custom_call_target="tpu_custom_call" | custom-call | flops 1100000000 | tf_op jit(solution)/shard_map/pallas_call | solution.py:610
  3.5 4.0 %collective-permute-start.1 = (bf16[256,1024]{1,0:T(8,128)(2,1)}, bf16[256,1024]{1,0:T(8,128)(2,1)S(1)}, u32[]{:S(2)}, u32[]{:S(2)}) collective-permute-start(bf16[256,1024]{1,0:T(8,128)(2,1)} %get-tuple-element.93), channel_id=1, source_target_pairs={{0,6},{2,4},{4,2},{6,0},{8,14},{10,12},{12,10},{14,8},{16,22},{18,... | collective-permute-start | bytes 1572872 | tf_op jit(solution)/shard_map/ppermute | solution.py:587
  7.5 3.9 %shard_map.119.refs_0_ = f32[256,384]{1,0:T(8,128)S(1)} custom-call(s32[7]{0:T(128)S(1)} %stack.40.sp, bf16[256,4096]{1,0:T(8,128)(2,1)} %refs_4_.5, bf16[8192,256]{1,0:T(8,128)(2,1)} %wb_ref.3, bf16[64,8192]{1,0:T(8,128)(2,1)} %bitcast.19, f32[256,384]{1,0:T(8,128)S(1)} %get-tuple-element.89.refs_0_), custom_call_target="tpu_custom_call" | custom-call | flops 1100000000 | tf_op jit(solution)/shard_map/pallas_call | solution.py:610
  14.8 3.9 %shard_map.120 = (bf16[256,256]{1,0:T(8,128)(2,1)S(1)}, f32[4,48,256]{2,1,0:T(8,128)S(1)}, f32[4,256,128]{2,1,0:T(8,128)S(1)}, bf16[144,1024]{1,0:T(8,128)(2,1)S...) custom-call(s32[7]{0:T(128)S(1)} %stack.40.sp, ...), custom_call_target="tpu_custom_call" | custom-call | flops 1100000000 | tf_op jit(solution)/shard_map/pallas_call | solution.py:646
  19.4 2.9 %collective-permute-start.4 = (bf16[144,1024]{1,0:T(8,128)(2,1)S(1)}, bf16[144,1024]{1,0:T(8,128)(2,1)S(1)}, u32[]{:S(2)}, u32[]{:S(2)}) collective-permute-start(bf16[144,1024]{1,0:T(8,128)(2,1)S(1)} %get-tuple-element.98), channel_id=1, source_target_pairs={{0,6},{2,4},{4,2},{6,0},{8,14},{10,12},{12,10},{14,8},{16,22},{18,... | collective-permute-start | bytes 884744 | tf_op jit(solution)/shard_map/ppermute | solution.py:587
  22.3 7.5 %shard_map.121 = (f32[256,4096]{1,0:T(8,128)S(1)}, bf16[176,1024]{1,0:T(8,128)(2,1)S(1)}, bf16[176,1024]{1,0:T(8,128)(2,1)S(1)}, bf16[176,1024]{1,0:T(8,128)(2,1)S(1)}, bf16[176,1024]{1,0:T(8,128)(2,1)S(1)}) custom-call(s32[7]{0:T(128)S(1)} %stack.40.sp, bf16[256,256]{1,0:T(8,128)(2,1)S(1)} %get-tuple-element.90.bc_ref, ...), custom_call_target="tpu_custom_call" | custom-call | flops 7699999744 | tf_op jit(solution)/shard_map/pallas_call | solution.py:662
  30.5 2.9 %collective-permute-start.7 = (bf16[176,1024]{1,0:T(8,128)(2,1)S(1)}, bf16[176,1024]{1,0:T(8,128)(2,1)S(1)}, u32[]{:S(2)}, u32[]{:S(2)}) collective-permute-start(bf16[176,1024]{1,0:T(8,128)(2,1)S(1)} %get-tuple-element.104), channel_id=1, source_target_pairs={{0,6},{2,4},{4,2},{6,0},{8,14},{10,12},{12,10},{14,8},{16,22},{18,... | collective-permute-start | bytes 1081352 | tf_op jit(solution)/shard_map/ppermute | solution.py:587
  38.2 2.6 %collective-permute-start.9 = (bf16[144,256]{1,0:T(8,128)(2,1)S(1)}, bf16[144,256]{1,0:T(8,128)(2,1)S(1)}, u32[]{:S(2)}, u32[]{:S(2)}) collective-permute-start(bf16[144,256]{1,0:T(8,128)(2,1)S(1)} %get-tuple-element.107), channel_id=1, source_target_pairs={{0,16},{2,18},{4,20},{6,22},{8,24},{10,26},{12,28},{14,30},{16,0},... | collective-permute-start | bytes 221192 | tf_op jit(solution)/shard_map/ppermute | solution.py:591
  41.4 3.2 %collective-permute-start.10 = (bf16[144,256]{1,0:T(8,128)(2,1)S(1)}, bf16[144,256]{1,0:T(8,128)(2,1)S(1)}, u32[]{:S(2)}, u32[]{:S(2)}) collective-permute-start(bf16[144,256]{1,0:T(8,128)(2,1)S(1)} %get-tuple-element.108), channel_id=1, source_target_pairs={{0,24},{2,26},{4,28},{6,30},{8,16},{10,18},{12,20},{14,22},{16,8},... | collective-permute-start | bytes 221192 | tf_op jit(solution)/shard_map/ppermute | solution.py:591
  45.4 2.3 %collective-permute-done.10.refs_3_ = bf16[144,256]{1,0:T(8,128)(2,1)S(1)} collective-permute-done((bf16[144,256]{1,0:T(8,128)(2,1)S(1)}, bf16[144,256]{1,0:T(8,128)(2,1)S(1)}, u32[]{:S(2)}, u32[]{:S(2)}) %collective-permute-start.10) | collective-permute-done | bytes 73760 | tf_op jit(solution)/shard_map/ppermute | solution.py:591
  49.1 3.0 %collective-permute-start.12 = (bf16[128,256]{1,0:T(8,128)(2,1)S(1)}, bf16[128,256]{1,0:T(8,128)(2,1)S(1)}, u32[]{:S(2)}, u32[]{:S(2)}) collective-permute-start(bf16[128,256]{1,0:T(8,128)(2,1)S(1)} %get-tuple-element.111), channel_id=1, source_target_pairs={{0,16},{2,18},{4,20},{6,22},{8,24},{10,26},{12,28},{14,30},{16,0},... | collective-permute-start | bytes 196616 | tf_op jit(solution)/shard_map/ppermute | solution.py:591
  54.9 2.2 %shard_map.123.moment_ref = bf16[4,128,1024]{2,1,0:T(8,128)(2,1)S(1)} custom-call(s32[7]{0:T(128)S(1)} %stack.40.sp, bf16[176,1024]{1,0:T(8,128)(2,1)S(1)} %get-tuple-element.101.refs_0_.refs_4_, bf16[176,1024]{1,0:T(8,128)(2,1)S(1)} %collective-permute-done.5.refs_1_.refs_5_, bf16[176,1024]{1,0:T(8,128)(2,1)S(1)} %collective-permute-done.6.refs_2_.refs_6_, ...), custom_call_target="tpu_custom_call" | custom-call | flops 2200000000 | tf_op jit(solution)/shard_map/pallas_call | solution.py:695
  58.2 2.5 %shard_map.125 = (bf16[128,1024]{1,0:T(8,128)(2,1)S(1)}, bf16[128,1024]{1,0:T(8,128)(2,1)S(1)}, bf16[128,1024]{1,0:T(8,128)(2,1)S(1)}, bf16[128,1024]{1,0:T(8,12...) custom-call(s32[7]{0:T(128)S(1)} %stack.40.sp, ...), custom_call_target="tpu_custom_call" | custom-call | flops 2200000000 | tf_op jit(solution)/shard_map/pallas_call | solution.py:736
  60.7 2.8 %collective-permute-start.18 = (bf16[128,256]{1,0:T(8,128)(2,1)S(1)}, bf16[128,256]{1,0:T(8,128)(2,1)S(1)}, u32[]{:S(2)}, u32[]{:S(2)}) collective-permute-start(bf16[128,256]{1,0:T(8,128)(2,1)S(1)} %get-tuple-element.121), channel_id=1, source_target_pairs={{0,16},{2,18},{4,20},{6,22},{8,24},{10,26},{12,28},{14,30},{16,0},... | collective-permute-start | bytes 196616 | tf_op jit(solution)/shard_map/ppermute | solution.py:591
  67.4 2.9 %shard_map.126 = (f32[16,256]{1,0:T(8,128)S(1)}, f32[16,128]{1,0:T(8,128)S(1)}, f32[256,384]{1,0:T(8,128)S(1)}, f32[8,128]{1,0:T(8,128)S(1)}) custom-call(s32[7]{0:T(128)S(1)} %stack.40.sp, bf16[256,256]{1,0:T(8,128)(2,1)S(1)} %get-tuple-element.90.bc_ref, f32[4,48,256]{2,1,0:T(8,128)S(1)} %get-tuple-element.91.rows_ref, ...), custom_call_target="tpu_custom_call" | custom-call | flops 4400000000 | tf_op jit(solution)/shard_map/pallas_call | solution.py:777
  75.1 2.7 %collective-permute-start.24 = (bf16[128,256]{1,0:T(8,128)(2,1)S(1)}, bf16[128,256]{1,0:T(8,128)(2,1)S(1)}, u32[]{:S(2)}, u32[]{:S(2)}) collective-permute-start(bf16[128,256]{1,0:T(8,128)(2,1)S(1)} %get-tuple-element.130), channel_id=1, source_target_pairs={{0,24},{2,26},{4,28},{6,30},{8,16},{10,18},{12,20},{14,22},{16,8},... | collective-permute-start | bytes 196616 | tf_op jit(solution)/shard_map/ppermute | solution.py:591
  77.8 3.0 %shard_map.128 = (f32[16,256]{1,0:T(8,128)S(1)}, f32[16,128]{1,0:T(8,128)S(1)}, f32[256,384]{1,0:T(8,128)S(1)}, f32[8,128]{1,0:T(8,128)}) custom-call(s32[7]{0:T(128)S(1)} %stack.40.sp, bf16[256,256]{1,0:T(8,128)(2,1)S(1)} %get-tuple-element.90.bc_ref, f32[4,48,256]{2,1,0:T(8,128)S(1)} %get-tuple-element.91.rows_ref, ...), custom_call_target="tpu_custom_call" | custom-call | flops 4400000000 | tf_op jit(solution)/shard_map/pallas_call | solution.py:777
  85.7 3.1 %shard_map.130 = (f32[16,256]{1,0:T(8,128)S(1)}, f32[16,128]{1,0:T(8,128)S(1)}, f32[256,384]{1,0:T(8,128)S(1)}, f32[8,128]{1,0:T(8,128)}) custom-call(s32[7]{0:T(128)S(1)} %stack.40.sp, bf16[256,256]{1,0:T(8,128)(2,1)S(1)} %get-tuple-element.90.bc_ref, f32[4,48,256]{2,1,0:T(8,128)S(1)} %get-tuple-element.91.rows_ref, ...), custom_call_target="tpu_custom_call" | custom-call | flops 4400000000 | tf_op jit(solution)/shard_map/pallas_call | solution.py:777
  88.8 3.0 %shard_map.131 = (f32[16,256]{1,0:T(8,128)S(1)}, f32[16,128]{1,0:T(8,128)S(1)}, f32[256,384]{1,0:T(8,128)S(1)}, f32[8,128]{1,0:T(8,128)}) custom-call(s32[7]{0:T(128)S(1)} %stack.40.sp, bf16[256,256]{1,0:T(8,128)(2,1)S(1)} %get-tuple-element.90.bc_ref, f32[4,48,256]{2,1,0:T(8,128)S(1)} %get-tuple-element.91.rows_ref, ...), custom_call_target="tpu_custom_call" | custom-call | flops 4400000000 | tf_op jit(solution)/shard_map/pallas_call | solution.py:777
  103.7 3.6 %collective-permute-done.28 = f32[8,128]{1,0:T(8,128)S(1)} collective-permute-done((f32[8,128]{1,0:T(8,128)S(1)}, f32[8,128]{1,0:T(8,128)S(1)}, u32[]{:S(2)}, u32[]{:S(2)}) %collective-permute-start.28) | collective-permute-done | bytes 4128 | tf_op jit(solution)/shard_map/ppermute | solution.py:591
  108.5 3.3 %collective-permute-done.29 = f32[8,128]{1,0:T(8,128)S(1)} collective-permute-done((f32[8,128]{1,0:T(8,128)S(1)}, f32[8,128]{1,0:T(8,128)S(1)}, u32[]{:S(2)}, u32[]{:S(2)}) %collective-permute-start.29) | collective-permute-done | bytes 4128 | tf_op jit(solution)/shard_map/ppermute | solution.py:591
  113.7 2.9 %collective-permute-start.38 = (bf16[80,1024]{1,0:T(8,128)(2,1)S(1)}, bf16[80,1024]{1,0:T(8,128)(2,1)S(1)}, u32[]{:S(2)}, u32[]{:S(2)}) collective-permute-start(bf16[80,1024]{1,0:T(8,128)(2,1)S(1)} %get-tuple-element.162), channel_id=1, source_target_pairs={{0,16},{2,18},{4,20},{6,22},{8,24},{10,26},{12,28},{14,30},{16,0},... | collective-permute-start | bytes 491528 | tf_op jit(solution)/shard_map/ppermute | solution.py:591
  119.1 2.3 %collective-permute-done.30 = f32[8,128]{1,0:T(8,128)S(1)} collective-permute-done((f32[8,128]{1,0:T(8,128)S(1)}, f32[8,128]{1,0:T(8,128)S(1)}, u32[]{:S(2)}, u32[]{:S(2)}) %collective-permute-start.30) | collective-permute-done | bytes 4128 | tf_op jit(solution)/shard_map/ppermute | solution.py:587
  121.4 2.0 %collective-permute-start.31 = (f32[8,128]{1,0:T(8,128)S(1)}, f32[8,128]{1,0:T(8,128)S(1)}, u32[]{:S(2)}, u32[]{:S(2)}) collective-permute-start(f32[8,128]{1,0:T(8,128)S(1)} %add.23), channel_id=1, source_target_pairs={{0,4},{2,6},{4,0},{6,2},{8,12},{10,14},{12,8},{14,10},{16,20},{18,... | collective-permute-start | bytes 12296 | tf_op jit(solution)/shard_map/ppermute | solution.py:587
  126.2 2.4 %collective-permute-done.38.refs_1_ = bf16[80,1024]{1,0:T(8,128)(2,1)S(1)} collective-permute-done((bf16[80,1024]{1,0:T(8,128)(2,1)S(1)}, bf16[80,1024]{1,0:T(8,128)(2,1)S(1)}, u32[]{:S(2)}, u32[]{:S(2)}) %collective-permute-start.38) | collective-permute-done | bytes 163872 | tf_op jit(solution)/shard_map/ppermute | solution.py:591
  129.2 3.4 %collective-permute-start.45 = (bf16[80,1024]{1,0:T(8,128)(2,1)S(1)}, bf16[80,1024]{1,0:T(8,128)(2,1)S(1)}, u32[]{:S(2)}, u32[]{:S(2)}) collective-permute-start(bf16[80,1024]{1,0:T(8,128)(2,1)S(1)} %shard_map.139.refs_0_), channel_id=1, source_target_pairs={{0,16},{2,18},{4,20},{6,22},{8,24},{10,26},{12,28},{14,30},{16,0},... | collective-permute-start | bytes 491528 | tf_op jit(solution)/shard_map/ppermute | solution.py:591
  132.7 1.8 %collective-permute-start.40 = (bf16[80,1024]{1,0:T(8,128)(2,1)S(1)}, bf16[80,1024]{1,0:T(8,128)(2,1)S(1)}, u32[]{:S(2)}, u32[]{:S(2)}) collective-permute-start(bf16[80,1024]{1,0:T(8,128)(2,1)S(1)} %shard_map.139.refs_0_), channel_id=1, source_target_pairs={{0,4},{2,6},{4,0},{6,2},{8,12},{10,14},{12,8},{14,10},{16,20},{18,... | collective-permute-start | bytes 491528 | tf_op jit(solution)/shard_map/ppermute | solution.py:587
  134.5 4.6 %collective-permute-done.45.refs_2_ = bf16[80,1024]{1,0:T(8,128)(2,1)S(1)} collective-permute-done((bf16[80,1024]{1,0:T(8,128)(2,1)S(1)}, bf16[80,1024]{1,0:T(8,128)(2,1)S(1)}, u32[]{:S(2)}, u32[]{:S(2)}) %collective-permute-start.45) | collective-permute-done | bytes 163872 | tf_op jit(solution)/shard_map/ppermute | solution.py:591
  146.3 2.0 %collective-permute-start.52 = (bf16[80,1024]{1,0:T(8,128)(2,1)S(1)}, bf16[80,1024]{1,0:T(8,128)(2,1)S(1)}, u32[]{:S(2)}, u32[]{:S(2)}) collective-permute-start(bf16[80,1024]{1,0:T(8,128)(2,1)S(1)} %collective-permute-done.48.refs_3_), channel_id=1, source_target_pairs={{0,4},{2,6},{4,0},{6,2},{8,12},{10,14},{12,8},{14,10},{16,20},{18,... | collective-permute-start | bytes 491528 | tf_op jit(solution)/shard_map/ppermute | solution.py:587
  154.2 1.8 %shard_map.141 = (f32[4096,256]{1,0:T(8,128)}, f32[64,4096]{1,0:T(8,128)}) custom-call(s32[7]{0:T(128)S(1)} %stack.40.sp, bf16[80,1024]{1,0:T(8,128)(2,1)S(1)} %collective-permute-done.53.refs_0_, bf16[80,1024]{1,0:T(8,128)(2,1)S(1)} %collective-permute-done.43.refs_1_, ...), custom_call_target="tpu_custom_call", output_to_operand_aliasing={{0}: (5, {}), {1}: (6, {})} | custom-call | flops 1100000000 | tf_op jit(solution)/shard_map/pallas_call | solution.py:937
  156.0 1.8 %shard_map.142 = (f32[4096,256]{1,0:T(8,128)}, f32[64,4096]{1,0:T(8,128)}) custom-call(s32[7]{0:T(128)S(1)} %stack.40.sp, bf16[80,1024]{1,0:T(8,128)(2,1)S(1)} %collective-permute-done.40.refs_0_, bf16[80,1024]{1,0:T(8,128)(2,1)S(1)} %collective-permute-done.51.refs_1_, ...), custom_call_target="tpu_custom_call", output_to_operand_aliasing={{0}: (5, {}), {1}: (6, {})} | custom-call | flops 1100000000 | tf_op jit(solution)/shard_map/pallas_call | solution.py:937
  159.2 1.8 %shard_map.143 = (f32[4096,256]{1,0:T(8,128)}, f32[64,4096]{1,0:T(8,128)}) custom-call(s32[7]{0:T(128)S(1)} %stack.40.sp, bf16[80,1024]{1,0:T(8,128)(2,1)S(1)} %collective-permute-done.41.refs_0_, bf16[80,1024]{1,0:T(8,128)(2,1)S(1)} %collective-permute-done.44.refs_1_, ...), custom_call_target="tpu_custom_call", output_to_operand_aliasing={{0}: (5, {}), {1}: (6, {})} | custom-call | flops 1100000000 | tf_op jit(solution)/shard_map/pallas_call | solution.py:937
  (125 shorter events, 64.7 us)
Async XLA Ops:
  3.5 18.7 %collective-permute-start.1 = (bf16[256,1024]{1,0:T(8,128)(2,1)}, bf16[256,1024]{1,0:T(8,128)(2,1)S(1)}, u32[]{:S(2)}, u32[]{:S(2)}) collective-permute-start(bf16[256,1024]{1,0:T(8,128)(2,1)} %get-tuple-element.93), channel_id=1, source_target_pairs={{0,6},{2,4},{4,2},{6,0},{8,14},{10,12},{12,10},{14,8},{16,22},{18,... | collective-permute-start | bytes 1572872 | tf_op jit(solution)/shard_map/ppermute | solution.py:587
  18.7 11.8 %collective-permute-start.2 = (bf16[144,1024]{1,0:T(8,128)(2,1)S(1)}, bf16[144,1024]{1,0:T(8,128)(2,1)S(1)}, u32[]{:S(2)}, u32[]{:S(2)}) collective-permute-start(bf16[144,1024]{1,0:T(8,128)(2,1)S(1)} %get-tuple-element.96), channel_id=1, source_target_pairs={{0,2},{2,0},{4,6},{6,4},{8,10},{10,8},{12,14},{14,12},{16,18},{18,... | collective-permute-start | bytes 884744 | tf_op jit(solution)/shard_map/ppermute | solution.py:587
  19.3 14.8 %collective-permute-start.3 = (bf16[144,1024]{1,0:T(8,128)(2,1)S(1)}, bf16[144,1024]{1,0:T(8,128)(2,1)S(1)}, u32[]{:S(2)}, u32[]{:S(2)}) collective-permute-start(bf16[144,1024]{1,0:T(8,128)(2,1)S(1)} %get-tuple-element.97), channel_id=1, source_target_pairs={{0,4},{2,6},{4,0},{6,2},{8,12},{10,14},{12,8},{14,10},{16,20},{18,... | collective-permute-start | bytes 884744 | tf_op jit(solution)/shard_map/ppermute | solution.py:587
  19.4 15.5 %collective-permute-start.4 = (bf16[144,1024]{1,0:T(8,128)(2,1)S(1)}, bf16[144,1024]{1,0:T(8,128)(2,1)S(1)}, u32[]{:S(2)}, u32[]{:S(2)}) collective-permute-start(bf16[144,1024]{1,0:T(8,128)(2,1)S(1)} %get-tuple-element.98), channel_id=1, source_target_pairs={{0,6},{2,4},{4,2},{6,0},{8,14},{10,12},{12,10},{14,8},{16,22},{18,... | collective-permute-start | bytes 884744 | tf_op jit(solution)/shard_map/ppermute | solution.py:587
  29.8 22.3 %collective-permute-start.5 = (bf16[176,1024]{1,0:T(8,128)(2,1)S(1)}, bf16[176,1024]{1,0:T(8,128)(2,1)S(1)}, u32[]{:S(2)}, u32[]{:S(2)}) collective-permute-start(bf16[176,1024]{1,0:T(8,128)(2,1)S(1)} %get-tuple-element.102), channel_id=1, source_target_pairs={{0,2},{2,0},{4,6},{6,4},{8,10},{10,8},{12,14},{14,12},{16,18},{18,... | collective-permute-start | bytes 1081352 | tf_op jit(solution)/shard_map/ppermute | solution.py:587
  30.4 22.4 %collective-permute-start.6 = (bf16[176,1024]{1,0:T(8,128)(2,1)S(1)}, bf16[176,1024]{1,0:T(8,128)(2,1)S(1)}, u32[]{:S(2)}, u32[]{:S(2)}) collective-permute-start(bf16[176,1024]{1,0:T(8,128)(2,1)S(1)} %get-tuple-element.103), channel_id=1, source_target_pairs={{0,4},{2,6},{4,0},{6,2},{8,12},{10,14},{12,8},{14,10},{16,20},{18,... | collective-permute-start | bytes 1081352 | tf_op jit(solution)/shard_map/ppermute | solution.py:587
  30.5 24.0 %collective-permute-start.7 = (bf16[176,1024]{1,0:T(8,128)(2,1)S(1)}, bf16[176,1024]{1,0:T(8,128)(2,1)S(1)}, u32[]{:S(2)}, u32[]{:S(2)}) collective-permute-start(bf16[176,1024]{1,0:T(8,128)(2,1)S(1)} %get-tuple-element.104), channel_id=1, source_target_pairs={{0,6},{2,4},{4,2},{6,0},{8,14},{10,12},{12,10},{14,8},{16,22},{18,... | collective-permute-start | bytes 1081352 | tf_op jit(solution)/shard_map/ppermute | solution.py:587
  48.4 8.8 %collective-permute-start.11 = (bf16[128,256]{1,0:T(8,128)(2,1)S(1)}, bf16[128,256]{1,0:T(8,128)(2,1)S(1)}, u32[]{:S(2)}, u32[]{:S(2)}) collective-permute-start(bf16[128,256]{1,0:T(8,128)(2,1)S(1)} %get-tuple-element.110), channel_id=1, source_target_pairs={{0,8},{2,10},{4,12},{6,14},{8,0},{10,2},{12,4},{14,6},{16,24},{18,... | collective-permute-start | bytes 196616 | tf_op jit(solution)/shard_map/ppermute | solution.py:591
  49.1 8.1 %collective-permute-start.12 = (bf16[128,256]{1,0:T(8,128)(2,1)S(1)}, bf16[128,256]{1,0:T(8,128)(2,1)S(1)}, u32[]{:S(2)}, u32[]{:S(2)}) collective-permute-start(bf16[128,256]{1,0:T(8,128)(2,1)S(1)} %get-tuple-element.111), channel_id=1, source_target_pairs={{0,16},{2,18},{4,20},{6,22},{8,24},{10,26},{12,28},{14,30},{16,0},... | collective-permute-start | bytes 196616 | tf_op jit(solution)/shard_map/ppermute | solution.py:591
  52.9 19.8 %collective-permute-start.20 = (bf16[256,1024]{1,0:T(8,128)(2,1)S(1)}, bf16[256,1024]{1,0:T(8,128)(2,1)S(1)}, u32[]{:S(2)}, u32[]{:S(2)}) collective-permute-start(bf16[256,1024]{1,0:T(8,128)(2,1)S(1)} %get-tuple-element.123), channel_id=1, source_target_pairs={{0,2},{2,0},{4,6},{6,4},{8,10},{10,8},{12,14},{14,12},{16,18},{18,... | collective-permute-start | bytes 1572872 | tf_op jit(solution)/shard_map/ppermute | solution.py:587
  54.5 18.1 %collective-permute-start.21 = (bf16[256,1024]{1,0:T(8,128)(2,1)S(1)}, bf16[256,1024]{1,0:T(8,128)(2,1)S(1)}, u32[]{:S(2)}, u32[]{:S(2)}) collective-permute-start(bf16[256,1024]{1,0:T(8,128)(2,1)S(1)} %get-tuple-element.124), channel_id=1, source_target_pairs={{0,4},{2,6},{4,0},{6,2},{8,12},{10,14},{12,8},{14,10},{16,20},{18,... | collective-permute-start | bytes 1572872 | tf_op jit(solution)/shard_map/ppermute | solution.py:587
  60.7 9.6 %collective-permute-start.18 = (bf16[128,256]{1,0:T(8,128)(2,1)S(1)}, bf16[128,256]{1,0:T(8,128)(2,1)S(1)}, u32[]{:S(2)}, u32[]{:S(2)}) collective-permute-start(bf16[128,256]{1,0:T(8,128)(2,1)S(1)} %get-tuple-element.121), channel_id=1, source_target_pairs={{0,16},{2,18},{4,20},{6,22},{8,24},{10,26},{12,28},{14,30},{16,0},... | collective-permute-start | bytes 196616 | tf_op jit(solution)/shard_map/ppermute | solution.py:591
  66.2 8.9 %collective-permute-start.16 = (bf16[128,1024]{1,0:T(8,128)(2,1)S(1)}, bf16[128,1024]{1,0:T(8,128)(2,1)S(1)}, u32[]{:S(2)}, u32[]{:S(2)}) collective-permute-start(bf16[128,1024]{1,0:T(8,128)(2,1)S(1)} %get-tuple-element.115), channel_id=1, source_target_pairs={{0,2},{2,0},{4,6},{6,4},{8,10},{10,8},{12,14},{14,12},{16,18},{18,... | collective-permute-start | bytes 786440 | tf_op jit(solution)/shard_map/ppermute | solution.py:587
  70.3 18.5 %collective-permute-start.14 = (bf16[128,1024]{1,0:T(8,128)(2,1)S(1)}, bf16[128,1024]{1,0:T(8,128)(2,1)S(1)}, u32[]{:S(2)}, u32[]{:S(2)}) collective-permute-start(bf16[128,1024]{1,0:T(8,128)(2,1)S(1)} %get-tuple-element.113), channel_id=1, source_target_pairs={{0,6},{2,4},{4,2},{6,0},{8,14},{10,12},{12,10},{14,8},{16,22},{18,... | collective-permute-start | bytes 786440 | tf_op jit(solution)/shard_map/ppermute | solution.py:587
  71.0 14.7 %collective-permute-start.15 = (bf16[128,1024]{1,0:T(8,128)(2,1)S(1)}, bf16[128,1024]{1,0:T(8,128)(2,1)S(1)}, u32[]{:S(2)}, u32[]{:S(2)}) collective-permute-start(bf16[128,1024]{1,0:T(8,128)(2,1)S(1)} %get-tuple-element.114), channel_id=1, source_target_pairs={{0,4},{2,6},{4,0},{6,2},{8,12},{10,14},{12,8},{14,10},{16,20},{18,... | collective-permute-start | bytes 786440 | tf_op jit(solution)/shard_map/ppermute | solution.py:587
  82.2 13.4 %collective-permute-start.25 = (bf16[128,1024]{1,0:T(8,128)(2,1)S(1)}, bf16[128,1024]{1,0:T(8,128)(2,1)S(1)}, u32[]{:S(2)}, u32[]{:S(2)}) collective-permute-start(bf16[128,1024]{1,0:T(8,128)(2,1)S(1)} %get-tuple-element.135), channel_id=1, source_target_pairs={{0,6},{2,4},{4,2},{6,0},{8,14},{10,12},{12,10},{14,8},{16,22},{18,... | collective-permute-start | bytes 786440 | tf_op jit(solution)/shard_map/ppermute | solution.py:587
  83.7 10.6 %collective-permute-start.26 = (bf16[128,1024]{1,0:T(8,128)(2,1)S(1)}, bf16[128,1024]{1,0:T(8,128)(2,1)S(1)}, u32[]{:S(2)}, u32[]{:S(2)}) collective-permute-start(bf16[128,1024]{1,0:T(8,128)(2,1)S(1)} %get-tuple-element.136), channel_id=1, source_target_pairs={{0,4},{2,6},{4,0},{6,2},{8,12},{10,14},{12,8},{14,10},{16,20},{18,... | collective-permute-start | bytes 786440 | tf_op jit(solution)/shard_map/ppermute | solution.py:587
  85.0 8.1 %collective-permute-start.27 = (bf16[128,1024]{1,0:T(8,128)(2,1)S(1)}, bf16[128,1024]{1,0:T(8,128)(2,1)S(1)}, u32[]{:S(2)}, u32[]{:S(2)}) collective-permute-start(bf16[128,1024]{1,0:T(8,128)(2,1)S(1)} %get-tuple-element.137), channel_id=1, source_target_pairs={{0,2},{2,0},{4,6},{6,4},{8,10},{10,8},{12,14},{14,12},{16,18},{18,... | collective-permute-start | bytes 786440 | tf_op jit(solution)/shard_map/ppermute | solution.py:587
  100.1 11.7 %collective-permute-start.36 = (bf16[320,256]{1,0:T(8,128)(2,1)S(1)}, bf16[320,256]{1,0:T(8,128)(2,1)S(1)}, u32[]{:S(2)}, u32[]{:S(2)}) collective-permute-start(bf16[320,256]{1,0:T(8,128)(2,1)S(1)} %shard_map.137.refs_0_), channel_id=1, source_target_pairs={{0,6},{2,4},{4,2},{6,0},{8,14},{10,12},{12,10},{14,8},{16,22},{18,... | collective-permute-start | bytes 491528 | tf_op jit(solution)/shard_map/ppermute | solution.py:587
  101.7 10.1 %collective-permute-start.35 = (bf16[320,256]{1,0:T(8,128)(2,1)S(1)}, bf16[320,256]{1,0:T(8,128)(2,1)S(1)}, u32[]{:S(2)}, u32[]{:S(2)}) collective-permute-start(bf16[320,256]{1,0:T(8,128)(2,1)S(1)} %shard_map.137.refs_0_), channel_id=1, source_target_pairs={{0,4},{2,6},{4,0},{6,2},{8,12},{10,14},{12,8},{14,10},{16,20},{18,... | collective-permute-start | bytes 491528 | tf_op jit(solution)/shard_map/ppermute | solution.py:587
  103.0 8.9 %collective-permute-start.34 = (bf16[320,256]{1,0:T(8,128)(2,1)S(1)}, bf16[320,256]{1,0:T(8,128)(2,1)S(1)}, u32[]{:S(2)}, u32[]{:S(2)}) collective-permute-start(bf16[320,256]{1,0:T(8,128)(2,1)S(1)} %shard_map.137.refs_0_), channel_id=1, source_target_pairs={{0,2},{2,0},{4,6},{6,4},{8,10},{10,8},{12,14},{14,12},{16,18},{18,... | collective-permute-start | bytes 491528 | tf_op jit(solution)/shard_map/ppermute | solution.py:587
  113.3 12.8 %collective-permute-start.37 = (bf16[80,1024]{1,0:T(8,128)(2,1)S(1)}, bf16[80,1024]{1,0:T(8,128)(2,1)S(1)}, u32[]{:S(2)}, u32[]{:S(2)}) collective-permute-start(bf16[80,1024]{1,0:T(8,128)(2,1)S(1)} %get-tuple-element.161), channel_id=1, source_target_pairs={{0,8},{2,10},{4,12},{6,14},{8,0},{10,2},{12,4},{14,6},{16,24},{18,... | collective-permute-start | bytes 491528 | tf_op jit(solution)/shard_map/ppermute | solution.py:591
  113.7 14.8 %collective-permute-start.38 = (bf16[80,1024]{1,0:T(8,128)(2,1)S(1)}, bf16[80,1024]{1,0:T(8,128)(2,1)S(1)}, u32[]{:S(2)}, u32[]{:S(2)}) collective-permute-start(bf16[80,1024]{1,0:T(8,128)(2,1)S(1)} %get-tuple-element.162), channel_id=1, source_target_pairs={{0,16},{2,18},{4,20},{6,22},{8,24},{10,26},{12,28},{14,30},{16,0},... | collective-permute-start | bytes 491528 | tf_op jit(solution)/shard_map/ppermute | solution.py:591
  116.6 11.9 %collective-permute-start.39 = (bf16[80,1024]{1,0:T(8,128)(2,1)S(1)}, bf16[80,1024]{1,0:T(8,128)(2,1)S(1)}, u32[]{:S(2)}, u32[]{:S(2)}) collective-permute-start(bf16[80,1024]{1,0:T(8,128)(2,1)S(1)} %get-tuple-element.163), channel_id=1, source_target_pairs={{0,24},{2,26},{4,28},{6,30},{8,16},{10,18},{12,20},{14,22},{16,8},... | collective-permute-start | bytes 491528 | tf_op jit(solution)/shard_map/ppermute | solution.py:591
  129.2 10.0 %collective-permute-start.45 = (bf16[80,1024]{1,0:T(8,128)(2,1)S(1)}, bf16[80,1024]{1,0:T(8,128)(2,1)S(1)}, u32[]{:S(2)}, u32[]{:S(2)}) collective-permute-start(bf16[80,1024]{1,0:T(8,128)(2,1)S(1)} %shard_map.139.refs_0_), channel_id=1, source_target_pairs={{0,16},{2,18},{4,20},{6,22},{8,24},{10,26},{12,28},{14,30},{16,0},... | collective-permute-start | bytes 491528 | tf_op jit(solution)/shard_map/ppermute | solution.py:591
  132.7 8.5 %collective-permute-start.42 = (bf16[80,1024]{1,0:T(8,128)(2,1)S(1)}, bf16[80,1024]{1,0:T(8,128)(2,1)S(1)}, u32[]{:S(2)}, u32[]{:S(2)}) collective-permute-start(bf16[80,1024]{1,0:T(8,128)(2,1)S(1)} %shard_map.139.refs_0_), channel_id=1, source_target_pairs={{0,8},{2,10},{4,12},{6,14},{8,0},{10,2},{12,4},{14,6},{16,24},{18,... | collective-permute-start | bytes 491528 | tf_op jit(solution)/shard_map/ppermute | solution.py:591
  132.7 9.8 %collective-permute-start.40 = (bf16[80,1024]{1,0:T(8,128)(2,1)S(1)}, bf16[80,1024]{1,0:T(8,128)(2,1)S(1)}, u32[]{:S(2)}, u32[]{:S(2)}) collective-permute-start(bf16[80,1024]{1,0:T(8,128)(2,1)S(1)} %shard_map.139.refs_0_), channel_id=1, source_target_pairs={{0,4},{2,6},{4,0},{6,2},{8,12},{10,14},{12,8},{14,10},{16,20},{18,... | collective-permute-start | bytes 491528 | tf_op jit(solution)/shard_map/ppermute | solution.py:587
  140.1 10.0 %collective-permute-start.46 = (bf16[80,1024]{1,0:T(8,128)(2,1)S(1)}, bf16[80,1024]{1,0:T(8,128)(2,1)S(1)}, u32[]{:S(2)}, u32[]{:S(2)}) collective-permute-start(bf16[80,1024]{1,0:T(8,128)(2,1)S(1)} %collective-permute-done.45.refs_2_), channel_id=1, source_target_pairs={{0,4},{2,6},{4,0},{6,2},{8,12},{10,14},{12,8},{14,10},{16,20},{18,... | collective-permute-start | bytes 491528 | tf_op jit(solution)/shard_map/ppermute | solution.py:587
  141.1 9.6 %collective-permute-start.51 = (bf16[80,1024]{1,0:T(8,128)(2,1)S(1)}, bf16[80,1024]{1,0:T(8,128)(2,1)S(1)}, u32[]{:S(2)}, u32[]{:S(2)}) collective-permute-start(bf16[80,1024]{1,0:T(8,128)(2,1)S(1)} %collective-permute-done.42.refs_1_), channel_id=1, source_target_pairs={{0,4},{2,6},{4,0},{6,2},{8,12},{10,14},{12,8},{14,10},{16,20},{18,... | collective-permute-start | bytes 491528 | tf_op jit(solution)/shard_map/ppermute | solution.py:587
  142.5 9.6 %collective-permute-start.43 = (bf16[80,1024]{1,0:T(8,128)(2,1)S(1)}, bf16[80,1024]{1,0:T(8,128)(2,1)S(1)}, u32[]{:S(2)}, u32[]{:S(2)}) collective-permute-start(bf16[80,1024]{1,0:T(8,128)(2,1)S(1)} %collective-permute-done.42.refs_1_), channel_id=1, source_target_pairs={{0,2},{2,0},{4,6},{6,4},{8,10},{10,8},{12,14},{14,12},{16,18},{18,... | collective-permute-start | bytes 491528 | tf_op jit(solution)/shard_map/ppermute | solution.py:587
  144.4 8.8 %collective-permute-start.49 = (bf16[80,1024]{1,0:T(8,128)(2,1)S(1)}, bf16[80,1024]{1,0:T(8,128)(2,1)S(1)}, u32[]{:S(2)}, u32[]{:S(2)}) collective-permute-start(bf16[80,1024]{1,0:T(8,128)(2,1)S(1)} %collective-permute-done.48.refs_3_), channel_id=1, source_target_pairs={{0,2},{2,0},{4,6},{6,4},{8,10},{10,8},{12,14},{14,12},{16,18},{18,... | collective-permute-start | bytes 491528 | tf_op jit(solution)/shard_map/ppermute | solution.py:587
  146.3 9.7 %collective-permute-start.52 = (bf16[80,1024]{1,0:T(8,128)(2,1)S(1)}, bf16[80,1024]{1,0:T(8,128)(2,1)S(1)}, u32[]{:S(2)}, u32[]{:S(2)}) collective-permute-start(bf16[80,1024]{1,0:T(8,128)(2,1)S(1)} %collective-permute-done.48.refs_3_), channel_id=1, source_target_pairs={{0,4},{2,6},{4,0},{6,2},{8,12},{10,14},{12,8},{14,10},{16,20},{18,... | collective-permute-start | bytes 491528 | tf_op jit(solution)/shard_map/ppermute | solution.py:587
  (29 other events, 171.2 us)

commit v7 on v5

--- a/solution.py
+++ b/solution.py
@@ -669,6 +669,7 @@
         + [shape_of(local_shape, BF16)] * groups,
         [pltpu.VMEM((length, length), F32)],
         us=7,
+        vmem=48 * 1024 * 1024,
     )(sp, bc, rows, cols, teacher_rows, teacher_next, params, *far_rows.values())
     local_grads = exchanged(outs)
 
@@ -691,7 +692,7 @@
             shape_of((HEADS, span), F32),
         ]
         + [shape_of(sent_shape, BF16)] * count,
-    )(sp, *messages, err)
+    )(sp, *messages, local_grads[0])
     moments = call(
         functools.partial(moment_body, groups, length, states),
         (1,),

time: 161 us -> 160 us (level)
  transfers between devices with their start and end apart: 55 -> 55, of which waited for: 19 -> 19; matrix products, arithmetic and copies ran while one was open for 1% -> 1% of each run, Pallas kernels for 28% -> 29%
where the time goes in v7:
time: 160 us
  starting transfers between devices  65.4 us (41%)
  Pallas kernels  56.1 us (35%)
  waiting for transfers between devices  34.3 us (21%)
  between operations  2.7 us (2%)
    ppermute x32, starting transfers between devices, in_plane(): return lax.ppermute(value, 'seq', pairs)  37 us
    ppermute x20, starting transfers between devices, over_planes(): return lax.ppermute(value, 'seq', pairs)  28.2 us
    ppermute x20, waiting for transfers between devices, over_planes(): return lax.ppermute(value, 'seq', pairs)  21.1 us
    pallas_call x4, Pallas kernels, error_part(): call(functools.partial(error_body, o == 0, local_heads, o), (1,), [whole(...  11.9 us
    pallas_call x1, Pallas kernels, shards(): call(functools.partial(local_body, groups, local_heads), (groups,), [whol...  8.9 us
    ppermute x32, waiting for transfers between devices, in_plane(): return lax.ppermute(value, 'seq', pairs)  8.83 us
    pallas_call x4, Pallas kernels, shards(): call(functools.partial(spread_body, planes), (1,), [whole(share_shape)] *...  7.22 us
    pallas_call x2, Pallas kernels, project(): call(functools.partial(project_body, copies), (count,), [pl.BlockSpec((le...  6.73 us
  transfers between devices with their start and end apart: 55, of which 19 were waited for; matrix products, arithmetic and copies ran while one was open for 1% of the time, Pallas kernels for 29%

profile of v7, /device:TPU:0, one launch (start us, length us, event | category | flops | bytes accessed | tf_op | source)
XLA Modules:
  0.0 159.8 jit_solution(7436161121840963583)
XLA Ops:
  0.7 2.8 %shard_map.118 = (f32[256,384]{1,0:T(8,128)S(1)}, bf16[256,1024]{1,0:T(8,128)(2,1)}) custom-call(s32[7]{0:T(128)S(1)} %stack.40.sp, bf16[256,4096]{1,0:T(8,128)(2,1)} %refs_4_.3, bf16[8192,256]{1,0:T(8,128)(2,1)} %wb_ref.3, bf16[64,8192]{1,0:T(8,128)(2,1)} %bitcast.18), custom_call_target="tpu_custom_call" | custom-call | flops 1100000000 | tf_op jit(solution)/shard_map/pallas_call | solution.py:610
  3.5 4.0 %collective-permute-start.1 = (bf16[256,1024]{1,0:T(8,128)(2,1)}, bf16[256,1024]{1,0:T(8,128)(2,1)S(1)}, u32[]{:S(2)}, u32[]{:S(2)}) collective-permute-start(bf16[256,1024]{1,0:T(8,128)(2,1)} %get-tuple-element.93), channel_id=1, source_target_pairs={{0,6},{2,4},{4,2},{6,0},{8,14},{10,12},{12,10},{14,8},{16,22},{18,... | collective-permute-start | bytes 1572872 | tf_op jit(solution)/shard_map/ppermute | solution.py:587
  7.5 3.9 %shard_map.119.refs_0_ = f32[256,384]{1,0:T(8,128)S(1)} custom-call(s32[7]{0:T(128)S(1)} %stack.40.sp, bf16[256,4096]{1,0:T(8,128)(2,1)} %refs_4_.3, bf16[8192,256]{1,0:T(8,128)(2,1)} %wb_ref.3, bf16[64,8192]{1,0:T(8,128)(2,1)} %bitcast.19, f32[256,384]{1,0:T(8,128)S(1)} %get-tuple-element.89.refs_0_), custom_call_target="tpu_custom_call" | custom-call | flops 1100000000 | tf_op jit(solution)/shard_map/pallas_call | solution.py:610
  13.2 3.9 %shard_map.120 = (bf16[256,256]{1,0:T(8,128)(2,1)S(1)}, f32[4,48,256]{2,1,0:T(8,128)S(1)}, f32[4,256,128]{2,1,0:T(8,128)S(1)}, bf16[144,1024]{1,0:T(8,128)(2,1)S...) custom-call(s32[7]{0:T(128)S(1)} %stack.40.sp, ...), custom_call_target="tpu_custom_call" | custom-call | flops 1100000000 | tf_op jit(solution)/shard_map/pallas_call | solution.py:646
  17.8 2.9 %collective-permute-start.4 = (bf16[144,1024]{1,0:T(8,128)(2,1)S(1)}, bf16[144,1024]{1,0:T(8,128)(2,1)S(1)}, u32[]{:S(2)}, u32[]{:S(2)}) collective-permute-start(bf16[144,1024]{1,0:T(8,128)(2,1)S(1)} %get-tuple-element.98), channel_id=1, source_target_pairs={{0,6},{2,4},{4,2},{6,0},{8,14},{10,12},{12,10},{14,8},{16,22},{18,... | collective-permute-start | bytes 884744 | tf_op jit(solution)/shard_map/ppermute | solution.py:587
  20.7 8.9 %shard_map.121 = (f32[256,4096]{1,0:T(8,128)}, bf16[176,1024]{1,0:T(8,128)(2,1)S(1)}, bf16[176,1024]{1,0:T(8,128)(2,1)S(1)}, bf16[176,1024]{1,0:T(8,128)(2,1)S(1)}, bf16[176,1024]{1,0:T(8,128)(2,1)S(1)}) custom-call(s32[7]{0:T(128)S(1)} %stack.40.sp, bf16[256,256]{1,0:T(8,128)(2,1)S(1)} %get-tuple-element.90.bc_ref, ...), custom_call_target="tpu_custom_call" | custom-call | flops 7699999744 | tf_op jit(solution)/shard_map/pallas_call | solution.py:662
  36.6 2.6 %collective-permute-start.9 = (bf16[144,256]{1,0:T(8,128)(2,1)S(1)}, bf16[144,256]{1,0:T(8,128)(2,1)S(1)}, u32[]{:S(2)}, u32[]{:S(2)}) collective-permute-start(bf16[144,256]{1,0:T(8,128)(2,1)S(1)} %get-tuple-element.107), channel_id=1, source_target_pairs={{0,16},{2,18},{4,20},{6,22},{8,24},{10,26},{12,28},{14,30},{16,0},... | collective-permute-start | bytes 221192 | tf_op jit(solution)/shard_map/ppermute | solution.py:591
  39.9 3.1 %collective-permute-start.10 = (bf16[144,256]{1,0:T(8,128)(2,1)S(1)}, bf16[144,256]{1,0:T(8,128)(2,1)S(1)}, u32[]{:S(2)}, u32[]{:S(2)}) collective-permute-start(bf16[144,256]{1,0:T(8,128)(2,1)S(1)} %get-tuple-element.108), channel_id=1, source_target_pairs={{0,24},{2,26},{4,28},{6,30},{8,16},{10,18},{12,20},{14,22},{16,8},... | collective-permute-start | bytes 221192 | tf_op jit(solution)/shard_map/ppermute | solution.py:591
  43.8 2.3 %collective-permute-done.10.refs_3_ = bf16[144,256]{1,0:T(8,128)(2,1)S(1)} collective-permute-done((bf16[144,256]{1,0:T(8,128)(2,1)S(1)}, bf16[144,256]{1,0:T(8,128)(2,1)S(1)}, u32[]{:S(2)}, u32[]{:S(2)}) %collective-permute-start.10) | collective-permute-done | bytes 73760 | tf_op jit(solution)/shard_map/ppermute | solution.py:591
  47.5 3.0 %collective-permute-start.12 = (bf16[128,256]{1,0:T(8,128)(2,1)S(1)}, bf16[128,256]{1,0:T(8,128)(2,1)S(1)}, u32[]{:S(2)}, u32[]{:S(2)}) collective-permute-start(bf16[128,256]{1,0:T(8,128)(2,1)S(1)} %get-tuple-element.111), channel_id=1, source_target_pairs={{0,16},{2,18},{4,20},{6,22},{8,24},{10,26},{12,28},{14,30},{16,0},... | collective-permute-start | bytes 196616 | tf_op jit(solution)/shard_map/ppermute | solution.py:591
  54.2 2.2 %shard_map.123.moment_ref = bf16[4,128,1024]{2,1,0:T(8,128)(2,1)S(1)} custom-call(s32[7]{0:T(128)S(1)} %stack.40.sp, bf16[176,1024]{1,0:T(8,128)(2,1)S(1)} %get-tuple-element.99.refs_4_.refs_0_, bf16[176,1024]{1,0:T(8,128)(2,1)S(1)} %collective-permute-done.5.refs_1_.refs_5_, bf16[176,1024]{1,0:T(8,128)(2,1)S(1)} %collective-permute-done.6.refs_2_.refs_6_, ...), custom_call_target="tpu_custom_call" | custom-call | flops 2200000000 | tf_op jit(solution)/shard_map/pallas_call | solution.py:696
  56.6 2.5 %shard_map.125 = (bf16[128,1024]{1,0:T(8,128)(2,1)S(1)}, bf16[128,1024]{1,0:T(8,128)(2,1)S(1)}, bf16[128,1024]{1,0:T(8,128)(2,1)S(1)}, bf16[128,1024]{1,0:T(8,12...) custom-call(s32[7]{0:T(128)S(1)} %stack.40.sp, ...), custom_call_target="tpu_custom_call" | custom-call | flops 2200000000 | tf_op jit(solution)/shard_map/pallas_call | solution.py:737
  59.1 3.7 %collective-permute-start.18 = (bf16[128,256]{1,0:T(8,128)(2,1)S(1)}, bf16[128,256]{1,0:T(8,128)(2,1)S(1)}, u32[]{:S(2)}, u32[]{:S(2)}) collective-permute-start(bf16[128,256]{1,0:T(8,128)(2,1)S(1)} %get-tuple-element.121), channel_id=1, source_target_pairs={{0,16},{2,18},{4,20},{6,22},{8,24},{10,26},{12,28},{14,30},{16,0},... | collective-permute-start | bytes 196616 | tf_op jit(solution)/shard_map/ppermute | solution.py:591
  63.4 2.2 %collective-permute-start.16 = (bf16[128,1024]{1,0:T(8,128)(2,1)S(1)}, bf16[128,1024]{1,0:T(8,128)(2,1)S(1)}, u32[]{:S(2)}, u32[]{:S(2)}) collective-permute-start(bf16[128,1024]{1,0:T(8,128)(2,1)S(1)} %get-tuple-element.115), channel_id=1, source_target_pairs={{0,2},{2,0},{4,6},{6,4},{8,10},{10,8},{12,14},{14,12},{16,18},{18,... | collective-permute-start | bytes 786440 | tf_op jit(solution)/shard_map/ppermute | solution.py:587
  65.6 2.9 %shard_map.126 = (f32[16,256]{1,0:T(8,128)S(1)}, f32[16,128]{1,0:T(8,128)S(1)}, f32[256,384]{1,0:T(8,128)S(1)}, f32[8,128]{1,0:T(8,128)S(1)}) custom-call(s32[7]{0:T(128)S(1)} %stack.40.sp, bf16[256,256]{1,0:T(8,128)(2,1)S(1)} %get-tuple-element.90.bc_ref, f32[4,48,256]{2,1,0:T(8,128)S(1)} %get-tuple-element.91.rows_ref, ...), custom_call_target="tpu_custom_call" | custom-call | flops 4400000000 | tf_op jit(solution)/shard_map/pallas_call | solution.py:778
  71.2 3.1 %collective-permute-start.23 = (bf16[128,256]{1,0:T(8,128)(2,1)S(1)}, bf16[128,256]{1,0:T(8,128)(2,1)S(1)}, u32[]{:S(2)}, u32[]{:S(2)}) collective-permute-start(bf16[128,256]{1,0:T(8,128)(2,1)S(1)} %get-tuple-element.129), channel_id=1, source_target_pairs={{0,16},{2,18},{4,20},{6,22},{8,24},{10,26},{12,28},{14,30},{16,0},... | collective-permute-start | bytes 196616 | tf_op jit(solution)/shard_map/ppermute | solution.py:591
  75.6 3.0 %shard_map.128 = (f32[16,256]{1,0:T(8,128)S(1)}, f32[16,128]{1,0:T(8,128)S(1)}, f32[256,384]{1,0:T(8,128)S(1)}, f32[8,128]{1,0:T(8,128)}) custom-call(s32[7]{0:T(128)S(1)} %stack.40.sp, bf16[256,256]{1,0:T(8,128)(2,1)S(1)} %get-tuple-element.90.bc_ref, f32[4,48,256]{2,1,0:T(8,128)S(1)} %get-tuple-element.91.rows_ref, ...), custom_call_target="tpu_custom_call" | custom-call | flops 4400000000 | tf_op jit(solution)/shard_map/pallas_call | solution.py:778
  78.5 1.9 %collective-permute-done.24.refs_3_ = bf16[128,256]{1,0:T(8,128)(2,1)S(1)} collective-permute-done((bf16[128,256]{1,0:T(8,128)(2,1)S(1)}, bf16[128,256]{1,0:T(8,128)(2,1)S(1)}, u32[]{:S(2)}, u32[]{:S(2)}) %collective-permute-start.24) | collective-permute-done | bytes 65568 | tf_op jit(solution)/shard_map/ppermute | solution.py:591
  84.9 3.1 %shard_map.130 = (f32[16,256]{1,0:T(8,128)S(1)}, f32[16,128]{1,0:T(8,128)S(1)}, f32[256,384]{1,0:T(8,128)S(1)}, f32[8,128]{1,0:T(8,128)}) custom-call(s32[7]{0:T(128)S(1)} %stack.40.sp, bf16[256,256]{1,0:T(8,128)(2,1)S(1)} %get-tuple-element.90.bc_ref, f32[4,48,256]{2,1,0:T(8,128)S(1)} %get-tuple-element.91.rows_ref, ...), custom_call_target="tpu_custom_call" | custom-call | flops 4400000000 | tf_op jit(solution)/shard_map/pallas_call | solution.py:778
  88.0 3.0 %shard_map.131 = (f32[16,256]{1,0:T(8,128)S(1)}, f32[16,128]{1,0:T(8,128)S(1)}, f32[256,384]{1,0:T(8,128)S(1)}, f32[8,128]{1,0:T(8,128)}) custom-call(s32[7]{0:T(128)S(1)} %stack.40.sp, bf16[256,256]{1,0:T(8,128)(2,1)S(1)} %get-tuple-element.90.bc_ref, f32[4,48,256]{2,1,0:T(8,128)S(1)} %get-tuple-element.91.rows_ref, ...), custom_call_target="tpu_custom_call" | custom-call | flops 4400000000 | tf_op jit(solution)/shard_map/pallas_call | solution.py:778
  102.9 3.6 %collective-permute-done.28 = f32[8,128]{1,0:T(8,128)S(1)} collective-permute-done((f32[8,128]{1,0:T(8,128)S(1)}, f32[8,128]{1,0:T(8,128)S(1)}, u32[]{:S(2)}, u32[]{:S(2)}) %collective-permute-start.28) | collective-permute-done | bytes 4128 | tf_op jit(solution)/shard_map/ppermute | solution.py:591
  106.5 4.5 %collective-permute-done.29 = f32[8,128]{1,0:T(8,128)S(1)} collective-permute-done((f32[8,128]{1,0:T(8,128)S(1)}, f32[8,128]{1,0:T(8,128)S(1)}, u32[]{:S(2)}, u32[]{:S(2)}) %collective-permute-start.29) | collective-permute-done | bytes 4128 | tf_op jit(solution)/shard_map/ppermute | solution.py:591
  114.4 2.6 %collective-permute-start.39 = (bf16[80,1024]{1,0:T(8,128)(2,1)S(1)}, bf16[80,1024]{1,0:T(8,128)(2,1)S(1)}, u32[]{:S(2)}, u32[]{:S(2)}) collective-permute-start(bf16[80,1024]{1,0:T(8,128)(2,1)S(1)} %get-tuple-element.163), channel_id=1, source_target_pairs={{0,24},{2,26},{4,28},{6,30},{8,16},{10,18},{12,20},{14,22},{16,8},... | collective-permute-start | bytes 491528 | tf_op jit(solution)/shard_map/ppermute | solution.py:591
  117.4 3.2 %collective-permute-done.30 = f32[8,128]{1,0:T(8,128)S(1)} collective-permute-done((f32[8,128]{1,0:T(8,128)S(1)}, f32[8,128]{1,0:T(8,128)S(1)}, u32[]{:S(2)}, u32[]{:S(2)}) %collective-permute-start.30) | collective-permute-done | bytes 4128 | tf_op jit(solution)/shard_map/ppermute | solution.py:587
  121.7 2.5 %collective-permute-done.31 = f32[8,128]{1,0:T(8,128)S(1)} collective-permute-done((f32[8,128]{1,0:T(8,128)S(1)}, f32[8,128]{1,0:T(8,128)S(1)}, u32[]{:S(2)}, u32[]{:S(2)}) %collective-permute-start.31) | collective-permute-done | bytes 4128 | tf_op jit(solution)/shard_map/ppermute | solution.py:587
  127.1 3.2 %collective-permute-start.45 = (bf16[80,1024]{1,0:T(8,128)(2,1)S(1)}, bf16[80,1024]{1,0:T(8,128)(2,1)S(1)}, u32[]{:S(2)}, u32[]{:S(2)}) collective-permute-start(bf16[80,1024]{1,0:T(8,128)(2,1)S(1)} %shard_map.139.refs_0_), channel_id=1, source_target_pairs={{0,16},{2,18},{4,20},{6,22},{8,24},{10,26},{12,28},{14,30},{16,0},... | collective-permute-start | bytes 491528 | tf_op jit(solution)/shard_map/ppermute | solution.py:591
  132.4 4.6 %collective-permute-done.45.refs_2_ = bf16[80,1024]{1,0:T(8,128)(2,1)S(1)} collective-permute-done((bf16[80,1024]{1,0:T(8,128)(2,1)S(1)}, bf16[80,1024]{1,0:T(8,128)(2,1)S(1)}, u32[]{:S(2)}, u32[]{:S(2)}) %collective-permute-start.45) | collective-permute-done | bytes 163872 | tf_op jit(solution)/shard_map/ppermute | solution.py:591
  147.0 2.0 %collective-permute-start.41 = (bf16[80,1024]{1,0:T(8,128)(2,1)S(1)}, bf16[80,1024]{1,0:T(8,128)(2,1)S(1)}, u32[]{:S(2)}, u32[]{:S(2)}) collective-permute-start(bf16[80,1024]{1,0:T(8,128)(2,1)S(1)} %collective-permute-done.40.refs_0_), channel_id=1, source_target_pairs={{0,2},{2,0},{4,6},{6,4},{8,10},{10,8},{12,14},{14,12},{16,18},{18,... | collective-permute-start | bytes 491528 | tf_op jit(solution)/shard_map/ppermute | solution.py:587
  151.2 1.8 %shard_map.141 = (f32[4096,256]{1,0:T(8,128)}, f32[64,4096]{1,0:T(8,128)}) custom-call(s32[7]{0:T(128)S(1)} %stack.40.sp, bf16[80,1024]{1,0:T(8,128)(2,1)S(1)} %collective-permute-done.53.refs_0_, bf16[80,1024]{1,0:T(8,128)(2,1)S(1)} %collective-permute-done.43.refs_1_, ...), custom_call_target="tpu_custom_call", output_to_operand_aliasing={{0}: (5, {}), {1}: (6, {})} | custom-call | flops 1100000000 | tf_op jit(solution)/shard_map/pallas_call | solution.py:938
  153.0 1.8 %shard_map.142 = (f32[4096,256]{1,0:T(8,128)}, f32[64,4096]{1,0:T(8,128)}) custom-call(s32[7]{0:T(128)S(1)} %stack.40.sp, bf16[80,1024]{1,0:T(8,128)(2,1)S(1)} %collective-permute-done.40.refs_0_, bf16[80,1024]{1,0:T(8,128)(2,1)S(1)} %collective-permute-done.51.refs_1_, ...), custom_call_target="tpu_custom_call", output_to_operand_aliasing={{0}: (5, {}), {1}: (6, {})} | custom-call | flops 1100000000 | tf_op jit(solution)/shard_map/pallas_call | solution.py:938
  154.8 1.8 %collective-permute-done.47.refs_2_ = bf16[80,1024]{1,0:T(8,128)(2,1)S(1)} collective-permute-done((bf16[80,1024]{1,0:T(8,128)(2,1)S(1)}, bf16[80,1024]{1,0:T(8,128)(2,1)S(1)}, u32[]{:S(2)}, u32[]{:S(2)}) %collective-permute-start.47) | collective-permute-done | bytes 163872 | tf_op jit(solution)/shard_map/ppermute | solution.py:587
  156.8 1.8 %shard_map.143 = (f32[4096,256]{1,0:T(8,128)}, f32[64,4096]{1,0:T(8,128)}) custom-call(s32[7]{0:T(128)S(1)} %stack.40.sp, bf16[80,1024]{1,0:T(8,128)(2,1)S(1)} %collective-permute-done.41.refs_0_, bf16[80,1024]{1,0:T(8,128)(2,1)S(1)} %collective-permute-done.44.refs_1_, ...), custom_call_target="tpu_custom_call", output_to_operand_aliasing={{0}: (5, {}), {1}: (6, {})} | custom-call | flops 1100000000 | tf_op jit(solution)/shard_map/pallas_call | solution.py:938
  (125 shorter events, 58.9 us)
Async XLA Ops:
  3.5 17.1 %collective-permute-start.1 = (bf16[256,1024]{1,0:T(8,128)(2,1)}, bf16[256,1024]{1,0:T(8,128)(2,1)S(1)}, u32[]{:S(2)}, u32[]{:S(2)}) collective-permute-start(bf16[256,1024]{1,0:T(8,128)(2,1)} %get-tuple-element.93), channel_id=1, source_target_pairs={{0,6},{2,4},{4,2},{6,0},{8,14},{10,12},{12,10},{14,8},{16,22},{18,... | collective-permute-start | bytes 1572872 | tf_op jit(solution)/shard_map/ppermute | solution.py:587
  17.1 15.5 %collective-permute-start.2 = (bf16[144,1024]{1,0:T(8,128)(2,1)S(1)}, bf16[144,1024]{1,0:T(8,128)(2,1)S(1)}, u32[]{:S(2)}, u32[]{:S(2)}) collective-permute-start(bf16[144,1024]{1,0:T(8,128)(2,1)S(1)} %get-tuple-element.96), channel_id=1, source_target_pairs={{0,2},{2,0},{4,6},{6,4},{8,10},{10,8},{12,14},{14,12},{16,18},{18,... | collective-permute-start | bytes 884744 | tf_op jit(solution)/shard_map/ppermute | solution.py:587
  17.7 15.4 %collective-permute-start.3 = (bf16[144,1024]{1,0:T(8,128)(2,1)S(1)}, bf16[144,1024]{1,0:T(8,128)(2,1)S(1)}, u32[]{:S(2)}, u32[]{:S(2)}) collective-permute-start(bf16[144,1024]{1,0:T(8,128)(2,1)S(1)} %get-tuple-element.97), channel_id=1, source_target_pairs={{0,4},{2,6},{4,0},{6,2},{8,12},{10,14},{12,8},{14,10},{16,20},{18,... | collective-permute-start | bytes 884744 | tf_op jit(solution)/shard_map/ppermute | solution.py:587
  17.8 15.5 %collective-permute-start.4 = (bf16[144,1024]{1,0:T(8,128)(2,1)S(1)}, bf16[144,1024]{1,0:T(8,128)(2,1)S(1)}, u32[]{:S(2)}, u32[]{:S(2)}) collective-permute-start(bf16[144,1024]{1,0:T(8,128)(2,1)S(1)} %get-tuple-element.98), channel_id=1, source_target_pairs={{0,6},{2,4},{4,2},{6,0},{8,14},{10,12},{12,10},{14,8},{16,22},{18,... | collective-permute-start | bytes 884744 | tf_op jit(solution)/shard_map/ppermute | solution.py:587
  29.6 20.9 %collective-permute-start.5 = (bf16[176,1024]{1,0:T(8,128)(2,1)S(1)}, bf16[176,1024]{1,0:T(8,128)(2,1)S(1)}, u32[]{:S(2)}, u32[]{:S(2)}) collective-permute-start(bf16[176,1024]{1,0:T(8,128)(2,1)S(1)} %get-tuple-element.102), channel_id=1, source_target_pairs={{0,2},{2,0},{4,6},{6,4},{8,10},{10,8},{12,14},{14,12},{16,18},{18,... | collective-permute-start | bytes 1081352 | tf_op jit(solution)/shard_map/ppermute | solution.py:587
  31.4 19.9 %collective-permute-start.6 = (bf16[176,1024]{1,0:T(8,128)(2,1)S(1)}, bf16[176,1024]{1,0:T(8,128)(2,1)S(1)}, u32[]{:S(2)}, u32[]{:S(2)}) collective-permute-start(bf16[176,1024]{1,0:T(8,128)(2,1)S(1)} %get-tuple-element.103), channel_id=1, source_target_pairs={{0,4},{2,6},{4,0},{6,2},{8,12},{10,14},{12,8},{14,10},{16,20},{18,... | collective-permute-start | bytes 1081352 | tf_op jit(solution)/shard_map/ppermute | solution.py:587
  32.6 20.1 %collective-permute-start.7 = (bf16[176,1024]{1,0:T(8,128)(2,1)S(1)}, bf16[176,1024]{1,0:T(8,128)(2,1)S(1)}, u32[]{:S(2)}, u32[]{:S(2)}) collective-permute-start(bf16[176,1024]{1,0:T(8,128)(2,1)S(1)} %get-tuple-element.104), channel_id=1, source_target_pairs={{0,6},{2,4},{4,2},{6,0},{8,14},{10,12},{12,10},{14,8},{16,22},{18,... | collective-permute-start | bytes 1081352 | tf_op jit(solution)/shard_map/ppermute | solution.py:587
  46.8 9.6 %collective-permute-start.11 = (bf16[128,256]{1,0:T(8,128)(2,1)S(1)}, bf16[128,256]{1,0:T(8,128)(2,1)S(1)}, u32[]{:S(2)}, u32[]{:S(2)}) collective-permute-start(bf16[128,256]{1,0:T(8,128)(2,1)S(1)} %get-tuple-element.110), channel_id=1, source_target_pairs={{0,8},{2,10},{4,12},{6,14},{8,0},{10,2},{12,4},{14,6},{16,24},{18,... | collective-permute-start | bytes 196616 | tf_op jit(solution)/shard_map/ppermute | solution.py:591
  47.5 8.9 %collective-permute-start.12 = (bf16[128,256]{1,0:T(8,128)(2,1)S(1)}, bf16[128,256]{1,0:T(8,128)(2,1)S(1)}, u32[]{:S(2)}, u32[]{:S(2)}) collective-permute-start(bf16[128,256]{1,0:T(8,128)(2,1)S(1)} %get-tuple-element.111), channel_id=1, source_target_pairs={{0,16},{2,18},{4,20},{6,22},{8,24},{10,26},{12,28},{14,30},{16,0},... | collective-permute-start | bytes 196616 | tf_op jit(solution)/shard_map/ppermute | solution.py:591
  51.3 19.2 %collective-permute-start.20 = (bf16[256,1024]{1,0:T(8,128)(2,1)S(1)}, bf16[256,1024]{1,0:T(8,128)(2,1)S(1)}, u32[]{:S(2)}, u32[]{:S(2)}) collective-permute-start(bf16[256,1024]{1,0:T(8,128)(2,1)S(1)} %get-tuple-element.123), channel_id=1, source_target_pairs={{0,2},{2,0},{4,6},{6,4},{8,10},{10,8},{12,14},{14,12},{16,18},{18,... | collective-permute-start | bytes 1572872 | tf_op jit(solution)/shard_map/ppermute | solution.py:587
  52.7 17.7 %collective-permute-start.21 = (bf16[256,1024]{1,0:T(8,128)(2,1)S(1)}, bf16[256,1024]{1,0:T(8,128)(2,1)S(1)}, u32[]{:S(2)}, u32[]{:S(2)}) collective-permute-start(bf16[256,1024]{1,0:T(8,128)(2,1)S(1)} %get-tuple-element.124), channel_id=1, source_target_pairs={{0,4},{2,6},{4,0},{6,2},{8,12},{10,14},{12,8},{14,10},{16,20},{18,... | collective-permute-start | bytes 1572872 | tf_op jit(solution)/shard_map/ppermute | solution.py:587
  59.1 9.5 %collective-permute-start.18 = (bf16[128,256]{1,0:T(8,128)(2,1)S(1)}, bf16[128,256]{1,0:T(8,128)(2,1)S(1)}, u32[]{:S(2)}, u32[]{:S(2)}) collective-permute-start(bf16[128,256]{1,0:T(8,128)(2,1)S(1)} %get-tuple-element.121), channel_id=1, source_target_pairs={{0,16},{2,18},{4,20},{6,22},{8,24},{10,26},{12,28},{14,30},{16,0},... | collective-permute-start | bytes 196616 | tf_op jit(solution)/shard_map/ppermute | solution.py:591
  63.4 10.9 %collective-permute-start.16 = (bf16[128,1024]{1,0:T(8,128)(2,1)S(1)}, bf16[128,1024]{1,0:T(8,128)(2,1)S(1)}, u32[]{:S(2)}, u32[]{:S(2)}) collective-permute-start(bf16[128,1024]{1,0:T(8,128)(2,1)S(1)} %get-tuple-element.115), channel_id=1, source_target_pairs={{0,2},{2,0},{4,6},{6,4},{8,10},{10,8},{12,14},{14,12},{16,18},{18,... | collective-permute-start | bytes 786440 | tf_op jit(solution)/shard_map/ppermute | solution.py:587
  68.5 19.5 %collective-permute-start.14 = (bf16[128,1024]{1,0:T(8,128)(2,1)S(1)}, bf16[128,1024]{1,0:T(8,128)(2,1)S(1)}, u32[]{:S(2)}, u32[]{:S(2)}) collective-permute-start(bf16[128,1024]{1,0:T(8,128)(2,1)S(1)} %get-tuple-element.113), channel_id=1, source_target_pairs={{0,6},{2,4},{4,2},{6,0},{8,14},{10,12},{12,10},{14,8},{16,22},{18,... | collective-permute-start | bytes 786440 | tf_op jit(solution)/shard_map/ppermute | solution.py:587
  69.4 15.5 %collective-permute-start.15 = (bf16[128,1024]{1,0:T(8,128)(2,1)S(1)}, bf16[128,1024]{1,0:T(8,128)(2,1)S(1)}, u32[]{:S(2)}, u32[]{:S(2)}) collective-permute-start(bf16[128,1024]{1,0:T(8,128)(2,1)S(1)} %get-tuple-element.114), channel_id=1, source_target_pairs={{0,4},{2,6},{4,0},{6,2},{8,12},{10,14},{12,8},{14,10},{16,20},{18,... | collective-permute-start | bytes 786440 | tf_op jit(solution)/shard_map/ppermute | solution.py:587
  81.3 13.5 %collective-permute-start.25 = (bf16[128,1024]{1,0:T(8,128)(2,1)S(1)}, bf16[128,1024]{1,0:T(8,128)(2,1)S(1)}, u32[]{:S(2)}, u32[]{:S(2)}) collective-permute-start(bf16[128,1024]{1,0:T(8,128)(2,1)S(1)} %get-tuple-element.135), channel_id=1, source_target_pairs={{0,6},{2,4},{4,2},{6,0},{8,14},{10,12},{12,10},{14,8},{16,22},{18,... | collective-permute-start | bytes 786440 | tf_op jit(solution)/shard_map/ppermute | solution.py:587
  82.0 11.5 %collective-permute-start.26 = (bf16[128,1024]{1,0:T(8,128)(2,1)S(1)}, bf16[128,1024]{1,0:T(8,128)(2,1)S(1)}, u32[]{:S(2)}, u32[]{:S(2)}) collective-permute-start(bf16[128,1024]{1,0:T(8,128)(2,1)S(1)} %get-tuple-element.136), channel_id=1, source_target_pairs={{0,4},{2,6},{4,0},{6,2},{8,12},{10,14},{12,8},{14,10},{16,20},{18,... | collective-permute-start | bytes 786440 | tf_op jit(solution)/shard_map/ppermute | solution.py:587
  83.3 8.9 %collective-permute-start.27 = (bf16[128,1024]{1,0:T(8,128)(2,1)S(1)}, bf16[128,1024]{1,0:T(8,128)(2,1)S(1)}, u32[]{:S(2)}, u32[]{:S(2)}) collective-permute-start(bf16[128,1024]{1,0:T(8,128)(2,1)S(1)} %get-tuple-element.137), channel_id=1, source_target_pairs={{0,2},{2,0},{4,6},{6,4},{8,10},{10,8},{12,14},{14,12},{16,18},{18,... | collective-permute-start | bytes 786440 | tf_op jit(solution)/shard_map/ppermute | solution.py:587
  99.4 11.7 %collective-permute-start.36 = (bf16[320,256]{1,0:T(8,128)(2,1)S(1)}, bf16[320,256]{1,0:T(8,128)(2,1)S(1)}, u32[]{:S(2)}, u32[]{:S(2)}) collective-permute-start(bf16[320,256]{1,0:T(8,128)(2,1)S(1)} %shard_map.137.refs_0_), channel_id=1, source_target_pairs={{0,6},{2,4},{4,2},{6,0},{8,14},{10,12},{12,10},{14,8},{16,22},{18,... | collective-permute-start | bytes 491528 | tf_op jit(solution)/shard_map/ppermute | solution.py:587
  100.0 11.0 %collective-permute-start.35 = (bf16[320,256]{1,0:T(8,128)(2,1)S(1)}, bf16[320,256]{1,0:T(8,128)(2,1)S(1)}, u32[]{:S(2)}, u32[]{:S(2)}) collective-permute-start(bf16[320,256]{1,0:T(8,128)(2,1)S(1)} %shard_map.137.refs_0_), channel_id=1, source_target_pairs={{0,4},{2,6},{4,0},{6,2},{8,12},{10,14},{12,8},{14,10},{16,20},{18,... | collective-permute-start | bytes 491528 | tf_op jit(solution)/shard_map/ppermute | solution.py:587
  101.3 9.7 %collective-permute-start.34 = (bf16[320,256]{1,0:T(8,128)(2,1)S(1)}, bf16[320,256]{1,0:T(8,128)(2,1)S(1)}, u32[]{:S(2)}, u32[]{:S(2)}) collective-permute-start(bf16[320,256]{1,0:T(8,128)(2,1)S(1)} %shard_map.137.refs_0_), channel_id=1, source_target_pairs={{0,2},{2,0},{4,6},{6,4},{8,10},{10,8},{12,14},{14,12},{16,18},{18,... | collective-permute-start | bytes 491528 | tf_op jit(solution)/shard_map/ppermute | solution.py:587
  112.5 12.8 %collective-permute-start.37 = (bf16[80,1024]{1,0:T(8,128)(2,1)S(1)}, bf16[80,1024]{1,0:T(8,128)(2,1)S(1)}, u32[]{:S(2)}, u32[]{:S(2)}) collective-permute-start(bf16[80,1024]{1,0:T(8,128)(2,1)S(1)} %get-tuple-element.161), channel_id=1, source_target_pairs={{0,8},{2,10},{4,12},{6,14},{8,0},{10,2},{12,4},{14,6},{16,24},{18,... | collective-permute-start | bytes 491528 | tf_op jit(solution)/shard_map/ppermute | solution.py:591
  112.6 13.9 %collective-permute-start.38 = (bf16[80,1024]{1,0:T(8,128)(2,1)S(1)}, bf16[80,1024]{1,0:T(8,128)(2,1)S(1)}, u32[]{:S(2)}, u32[]{:S(2)}) collective-permute-start(bf16[80,1024]{1,0:T(8,128)(2,1)S(1)} %get-tuple-element.162), channel_id=1, source_target_pairs={{0,16},{2,18},{4,20},{6,22},{8,24},{10,26},{12,28},{14,30},{16,0},... | collective-permute-start | bytes 491528 | tf_op jit(solution)/shard_map/ppermute | solution.py:591
  114.4 12.1 %collective-permute-start.39 = (bf16[80,1024]{1,0:T(8,128)(2,1)S(1)}, bf16[80,1024]{1,0:T(8,128)(2,1)S(1)}, u32[]{:S(2)}, u32[]{:S(2)}) collective-permute-start(bf16[80,1024]{1,0:T(8,128)(2,1)S(1)} %get-tuple-element.163), channel_id=1, source_target_pairs={{0,24},{2,26},{4,28},{6,30},{8,16},{10,18},{12,20},{14,22},{16,8},... | collective-permute-start | bytes 491528 | tf_op jit(solution)/shard_map/ppermute | solution.py:591
  127.1 9.9 %collective-permute-start.45 = (bf16[80,1024]{1,0:T(8,128)(2,1)S(1)}, bf16[80,1024]{1,0:T(8,128)(2,1)S(1)}, u32[]{:S(2)}, u32[]{:S(2)}) collective-permute-start(bf16[80,1024]{1,0:T(8,128)(2,1)S(1)} %shard_map.139.refs_0_), channel_id=1, source_target_pairs={{0,16},{2,18},{4,20},{6,22},{8,24},{10,26},{12,28},{14,30},{16,0},... | collective-permute-start | bytes 491528 | tf_op jit(solution)/shard_map/ppermute | solution.py:591
  130.3 8.2 %collective-permute-start.53 = (bf16[80,1024]{1,0:T(8,128)(2,1)S(1)}, bf16[80,1024]{1,0:T(8,128)(2,1)S(1)}, u32[]{:S(2)}, u32[]{:S(2)}) collective-permute-start(bf16[80,1024]{1,0:T(8,128)(2,1)S(1)} %shard_map.139.refs_0_), channel_id=1, source_target_pairs={{0,2},{2,0},{4,6},{6,4},{8,10},{10,8},{12,14},{14,12},{16,18},{18,... | collective-permute-start | bytes 491528 | tf_op jit(solution)/shard_map/ppermute | solution.py:587
  131.2 9.3 %collective-permute-start.40 = (bf16[80,1024]{1,0:T(8,128)(2,1)S(1)}, bf16[80,1024]{1,0:T(8,128)(2,1)S(1)}, u32[]{:S(2)}, u32[]{:S(2)}) collective-permute-start(bf16[80,1024]{1,0:T(8,128)(2,1)S(1)} %shard_map.139.refs_0_), channel_id=1, source_target_pairs={{0,4},{2,6},{4,0},{6,2},{8,12},{10,14},{12,8},{14,10},{16,20},{18,... | collective-permute-start | bytes 491528 | tf_op jit(solution)/shard_map/ppermute | solution.py:587
  138.5 8.5 %collective-permute-start.46 = (bf16[80,1024]{1,0:T(8,128)(2,1)S(1)}, bf16[80,1024]{1,0:T(8,128)(2,1)S(1)}, u32[]{:S(2)}, u32[]{:S(2)}) collective-permute-start(bf16[80,1024]{1,0:T(8,128)(2,1)S(1)} %collective-permute-done.45.refs_2_), channel_id=1, source_target_pairs={{0,4},{2,6},{4,0},{6,2},{8,12},{10,14},{12,8},{14,10},{16,20},{18,... | collective-permute-start | bytes 491528 | tf_op jit(solution)/shard_map/ppermute | solution.py:587
  139.2 9.8 %collective-permute-start.51 = (bf16[80,1024]{1,0:T(8,128)(2,1)S(1)}, bf16[80,1024]{1,0:T(8,128)(2,1)S(1)}, u32[]{:S(2)}, u32[]{:S(2)}) collective-permute-start(bf16[80,1024]{1,0:T(8,128)(2,1)S(1)} %collective-permute-done.42.refs_1_), channel_id=1, source_target_pairs={{0,4},{2,6},{4,0},{6,2},{8,12},{10,14},{12,8},{14,10},{16,20},{18,... | collective-permute-start | bytes 491528 | tf_op jit(solution)/shard_map/ppermute | solution.py:587
  140.5 8.6 %collective-permute-start.43 = (bf16[80,1024]{1,0:T(8,128)(2,1)S(1)}, bf16[80,1024]{1,0:T(8,128)(2,1)S(1)}, u32[]{:S(2)}, u32[]{:S(2)}) collective-permute-start(bf16[80,1024]{1,0:T(8,128)(2,1)S(1)} %collective-permute-done.42.refs_1_), channel_id=1, source_target_pairs={{0,2},{2,0},{4,6},{6,4},{8,10},{10,8},{12,14},{14,12},{16,18},{18,... | collective-permute-start | bytes 491528 | tf_op jit(solution)/shard_map/ppermute | solution.py:587
  142.6 8.6 %collective-permute-start.49 = (bf16[80,1024]{1,0:T(8,128)(2,1)S(1)}, bf16[80,1024]{1,0:T(8,128)(2,1)S(1)}, u32[]{:S(2)}, u32[]{:S(2)}) collective-permute-start(bf16[80,1024]{1,0:T(8,128)(2,1)S(1)} %collective-permute-done.48.refs_3_), channel_id=1, source_target_pairs={{0,2},{2,0},{4,6},{6,4},{8,10},{10,8},{12,14},{14,12},{16,18},{18,... | collective-permute-start | bytes 491528 | tf_op jit(solution)/shard_map/ppermute | solution.py:587
  144.4 8.6 %collective-permute-start.52 = (bf16[80,1024]{1,0:T(8,128)(2,1)S(1)}, bf16[80,1024]{1,0:T(8,128)(2,1)S(1)}, u32[]{:S(2)}, u32[]{:S(2)}) collective-permute-start(bf16[80,1024]{1,0:T(8,128)(2,1)S(1)} %collective-permute-done.48.refs_3_), channel_id=1, source_target_pairs={{0,4},{2,6},{4,0},{6,2},{8,12},{10,14},{12,8},{14,10},{16,20},{18,... | collective-permute-start | bytes 491528 | tf_op jit(solution)/shard_map/ppermute | solution.py:587
  (29 other events, 177.9 us)

commit v8 on v7

--- a/solution.py
+++ b/solution.py
@@ -946,6 +946,7 @@
             [shape_of((local_width, bc_width), F32), shape_of((head_count, local_width), F32)],
             [pltpu.VMEM((padded, span), BF16)],
             aliases={1 + planes + i: i for i in range(len(results))},
+            us=3 if o == 0 else 1,
         )(sp, *[part[o] for part in pieces], *results)
     state_grad, step_grad = results
 

time: 160 us -> 162 us (1.012)
  starting transfers between devices: 65.4 us -> 68.1 us
  transfers between devices with their start and end apart: 55 -> 55, of which waited for: 19 -> 18; matrix products, arithmetic and copies ran while one was open for 1% -> 1% of each run, Pallas kernels for 29% -> 29%
where the time goes in v8:
time: 162 us
  starting transfers between devices  68.1 us (42%)
  Pallas kernels  56.1 us (35%)
  waiting for transfers between devices  33.3 us (21%)
  between operations  2.71 us (2%)
    ppermute x32, starting transfers between devices, in_plane(): return lax.ppermute(value, 'seq', pairs)  38.6 us
    ppermute x20, starting transfers between devices, over_planes(): return lax.ppermute(value, 'seq', pairs)  29.4 us
    ppermute x20, waiting for transfers between devices, over_planes(): return lax.ppermute(value, 'seq', pairs)  19.6 us
    pallas_call x4, Pallas kernels, error_part(): call(functools.partial(error_body, o == 0, local_heads, o), (1,), [whole(...  11.9 us
    ppermute x32, waiting for transfers between devices, in_plane(): return lax.ppermute(value, 'seq', pairs)  9.34 us
    pallas_call x1, Pallas kernels, shards(): call(functools.partial(local_body, groups, local_heads), (groups,), [whol...  8.9 us
    pallas_call x4, Pallas kernels, shards(): call(functools.partial(spread_body, planes), (1,), [whole(share_shape)] *...  7.22 us
    pallas_call x2, Pallas kernels, project(): call(functools.partial(project_body, copies), (count,), [pl.BlockSpec((le...  6.73 us
  transfers between devices with their start and end apart: 55, of which 18 were waited for; matrix products, arithmetic and copies ran while one was open for 1% of the time, Pallas kernels for 29%

profile of v8, /device:TPU:0, one launch (start us, length us, event | category | flops | bytes accessed | tf_op | source)
XLA Modules:
  0.0 161.6 jit_solution(5270531900513724237)
XLA Ops:
  0.7 2.8 %shard_map.118 = (f32[256,384]{1,0:T(8,128)S(1)}, bf16[256,1024]{1,0:T(8,128)(2,1)}) custom-call(s32[7]{0:T(128)S(1)} %stack.40.sp, bf16[256,4096]{1,0:T(8,128)(2,1)} %refs_4_.3, bf16[8192,256]{1,0:T(8,128)(2,1)} %wb_ref.3, bf16[64,8192]{1,0:T(8,128)(2,1)} %bitcast.18), custom_call_target="tpu_custom_call" | custom-call | flops 1100000000 | tf_op jit(solution)/shard_map/pallas_call | solution.py:610
  3.5 4.0 %collective-permute-start.1 = (bf16[256,1024]{1,0:T(8,128)(2,1)}, bf16[256,1024]{1,0:T(8,128)(2,1)S(1)}, u32[]{:S(2)}, u32[]{:S(2)}) collective-permute-start(bf16[256,1024]{1,0:T(8,128)(2,1)} %get-tuple-element.93), channel_id=1, source_target_pairs={{0,6},{2,4},{4,2},{6,0},{8,14},{10,12},{12,10},{14,8},{16,22},{18,... | collective-permute-start | bytes 1572872 | tf_op jit(solution)/shard_map/ppermute | solution.py:587
  7.5 3.9 %shard_map.119.refs_0_ = f32[256,384]{1,0:T(8,128)S(1)} custom-call(s32[7]{0:T(128)S(1)} %stack.40.sp, bf16[256,4096]{1,0:T(8,128)(2,1)} %refs_4_.3, bf16[8192,256]{1,0:T(8,128)(2,1)} %wb_ref.3, bf16[64,8192]{1,0:T(8,128)(2,1)} %bitcast.19, f32[256,384]{1,0:T(8,128)S(1)} %get-tuple-element.89.refs_0_), custom_call_target="tpu_custom_call" | custom-call | flops 1100000000 | tf_op jit(solution)/shard_map/pallas_call | solution.py:610
  13.2 3.9 %shard_map.120 = (bf16[256,256]{1,0:T(8,128)(2,1)S(1)}, f32[4,48,256]{2,1,0:T(8,128)S(1)}, f32[4,256,128]{2,1,0:T(8,128)S(1)}, bf16[144,1024]{1,0:T(8,128)(2,1)S...) custom-call(s32[7]{0:T(128)S(1)} %stack.40.sp, ...), custom_call_target="tpu_custom_call" | custom-call | flops 1100000000 | tf_op jit(solution)/shard_map/pallas_call | solution.py:646
  17.8 2.9 %collective-permute-start.4 = (bf16[144,1024]{1,0:T(8,128)(2,1)S(1)}, bf16[144,1024]{1,0:T(8,128)(2,1)S(1)}, u32[]{:S(2)}, u32[]{:S(2)}) collective-permute-start(bf16[144,1024]{1,0:T(8,128)(2,1)S(1)} %get-tuple-element.98), channel_id=1, source_target_pairs={{0,6},{2,4},{4,2},{6,0},{8,14},{10,12},{12,10},{14,8},{16,22},{18,... | collective-permute-start | bytes 884744 | tf_op jit(solution)/shard_map/ppermute | solution.py:587
  20.7 8.9 %shard_map.121 = (f32[256,4096]{1,0:T(8,128)}, bf16[176,1024]{1,0:T(8,128)(2,1)S(1)}, bf16[176,1024]{1,0:T(8,128)(2,1)S(1)}, bf16[176,1024]{1,0:T(8,128)(2,1)S(1)}, bf16[176,1024]{1,0:T(8,128)(2,1)S(1)}) custom-call(s32[7]{0:T(128)S(1)} %stack.40.sp, bf16[256,256]{1,0:T(8,128)(2,1)S(1)} %get-tuple-element.90.bc_ref, ...), custom_call_target="tpu_custom_call" | custom-call | flops 7699999744 | tf_op jit(solution)/shard_map/pallas_call | solution.py:662
  36.6 2.6 %collective-permute-start.9 = (bf16[144,256]{1,0:T(8,128)(2,1)S(1)}, bf16[144,256]{1,0:T(8,128)(2,1)S(1)}, u32[]{:S(2)}, u32[]{:S(2)}) collective-permute-start(bf16[144,256]{1,0:T(8,128)(2,1)S(1)} %get-tuple-element.107), channel_id=1, source_target_pairs={{0,16},{2,18},{4,20},{6,22},{8,24},{10,26},{12,28},{14,30},{16,0},... | collective-permute-start | bytes 221192 | tf_op jit(solution)/shard_map/ppermute | solution.py:591
  39.9 3.1 %collective-permute-start.10 = (bf16[144,256]{1,0:T(8,128)(2,1)S(1)}, bf16[144,256]{1,0:T(8,128)(2,1)S(1)}, u32[]{:S(2)}, u32[]{:S(2)}) collective-permute-start(bf16[144,256]{1,0:T(8,128)(2,1)S(1)} %get-tuple-element.108), channel_id=1, source_target_pairs={{0,24},{2,26},{4,28},{6,30},{8,16},{10,18},{12,20},{14,22},{16,8},... | collective-permute-start | bytes 221192 | tf_op jit(solution)/shard_map/ppermute | solution.py:591
  43.8 2.3 %collective-permute-done.10.refs_3_ = bf16[144,256]{1,0:T(8,128)(2,1)S(1)} collective-permute-done((bf16[144,256]{1,0:T(8,128)(2,1)S(1)}, bf16[144,256]{1,0:T(8,128)(2,1)S(1)}, u32[]{:S(2)}, u32[]{:S(2)}) %collective-permute-start.10) | collective-permute-done | bytes 73760 | tf_op jit(solution)/shard_map/ppermute | solution.py:591
  47.5 3.0 %collective-permute-start.12 = (bf16[128,256]{1,0:T(8,128)(2,1)S(1)}, bf16[128,256]{1,0:T(8,128)(2,1)S(1)}, u32[]{:S(2)}, u32[]{:S(2)}) collective-permute-start(bf16[128,256]{1,0:T(8,128)(2,1)S(1)} %get-tuple-element.111), channel_id=1, source_target_pairs={{0,16},{2,18},{4,20},{6,22},{8,24},{10,26},{12,28},{14,30},{16,0},... | collective-permute-start | bytes 196616 | tf_op jit(solution)/shard_map/ppermute | solution.py:591
  54.2 2.2 %shard_map.123.moment_ref = bf16[4,128,1024]{2,1,0:T(8,128)(2,1)S(1)} custom-call(s32[7]{0:T(128)S(1)} %stack.40.sp, bf16[176,1024]{1,0:T(8,128)(2,1)S(1)} %get-tuple-element.99.refs_4_.refs_0_, bf16[176,1024]{1,0:T(8,128)(2,1)S(1)} %collective-permute-done.5.refs_1_.refs_5_, bf16[176,1024]{1,0:T(8,128)(2,1)S(1)} %collective-permute-done.6.refs_2_.refs_6_, ...), custom_call_target="tpu_custom_call" | custom-call | flops 2200000000 | tf_op jit(solution)/shard_map/pallas_call | solution.py:696
  56.6 2.5 %shard_map.125 = (bf16[128,1024]{1,0:T(8,128)(2,1)S(1)}, bf16[128,1024]{1,0:T(8,128)(2,1)S(1)}, bf16[128,1024]{1,0:T(8,128)(2,1)S(1)}, bf16[128,1024]{1,0:T(8,12...) custom-call(s32[7]{0:T(128)S(1)} %stack.40.sp, ...), custom_call_target="tpu_custom_call" | custom-call | flops 2200000000 | tf_op jit(solution)/shard_map/pallas_call | solution.py:737
  59.1 3.7 %collective-permute-start.18 = (bf16[128,256]{1,0:T(8,128)(2,1)S(1)}, bf16[128,256]{1,0:T(8,128)(2,1)S(1)}, u32[]{:S(2)}, u32[]{:S(2)}) collective-permute-start(bf16[128,256]{1,0:T(8,128)(2,1)S(1)} %get-tuple-element.121), channel_id=1, source_target_pairs={{0,16},{2,18},{4,20},{6,22},{8,24},{10,26},{12,28},{14,30},{16,0},... | collective-permute-start | bytes 196616 | tf_op jit(solution)/shard_map/ppermute | solution.py:591
  63.4 2.2 %collective-permute-start.16 = (bf16[128,1024]{1,0:T(8,128)(2,1)S(1)}, bf16[128,1024]{1,0:T(8,128)(2,1)S(1)}, u32[]{:S(2)}, u32[]{:S(2)}) collective-permute-start(bf16[128,1024]{1,0:T(8,128)(2,1)S(1)} %get-tuple-element.115), channel_id=1, source_target_pairs={{0,2},{2,0},{4,6},{6,4},{8,10},{10,8},{12,14},{14,12},{16,18},{18,... | collective-permute-start | bytes 786440 | tf_op jit(solution)/shard_map/ppermute | solution.py:587
  65.6 2.9 %shard_map.126 = (f32[16,256]{1,0:T(8,128)S(1)}, f32[16,128]{1,0:T(8,128)S(1)}, f32[256,384]{1,0:T(8,128)S(1)}, f32[8,128]{1,0:T(8,128)S(1)}) custom-call(s32[7]{0:T(128)S(1)} %stack.40.sp, bf16[256,256]{1,0:T(8,128)(2,1)S(1)} %get-tuple-element.90.bc_ref, f32[4,48,256]{2,1,0:T(8,128)S(1)} %get-tuple-element.91.rows_ref, ...), custom_call_target="tpu_custom_call" | custom-call | flops 4400000000 | tf_op jit(solution)/shard_map/pallas_call | solution.py:778
  71.2 3.1 %collective-permute-start.23 = (bf16[128,256]{1,0:T(8,128)(2,1)S(1)}, bf16[128,256]{1,0:T(8,128)(2,1)S(1)}, u32[]{:S(2)}, u32[]{:S(2)}) collective-permute-start(bf16[128,256]{1,0:T(8,128)(2,1)S(1)} %get-tuple-element.129), channel_id=1, source_target_pairs={{0,16},{2,18},{4,20},{6,22},{8,24},{10,26},{12,28},{14,30},{16,0},... | collective-permute-start | bytes 196616 | tf_op jit(solution)/shard_map/ppermute | solution.py:591
  75.6 3.0 %shard_map.128 = (f32[16,256]{1,0:T(8,128)S(1)}, f32[16,128]{1,0:T(8,128)S(1)}, f32[256,384]{1,0:T(8,128)S(1)}, f32[8,128]{1,0:T(8,128)}) custom-call(s32[7]{0:T(128)S(1)} %stack.40.sp, bf16[256,256]{1,0:T(8,128)(2,1)S(1)} %get-tuple-element.90.bc_ref, f32[4,48,256]{2,1,0:T(8,128)S(1)} %get-tuple-element.91.rows_ref, ...), custom_call_target="tpu_custom_call" | custom-call | flops 4400000000 | tf_op jit(solution)/shard_map/pallas_call | solution.py:778
  78.5 1.9 %collective-permute-done.24.refs_3_ = bf16[128,256]{1,0:T(8,128)(2,1)S(1)} collective-permute-done((bf16[128,256]{1,0:T(8,128)(2,1)S(1)}, bf16[128,256]{1,0:T(8,128)(2,1)S(1)}, u32[]{:S(2)}, u32[]{:S(2)}) %collective-permute-start.24) | collective-permute-done | bytes 65568 | tf_op jit(solution)/shard_map/ppermute | solution.py:591
  84.9 3.1 %shard_map.130 = (f32[16,256]{1,0:T(8,128)S(1)}, f32[16,128]{1,0:T(8,128)S(1)}, f32[256,384]{1,0:T(8,128)S(1)}, f32[8,128]{1,0:T(8,128)}) custom-call(s32[7]{0:T(128)S(1)} %stack.40.sp, bf16[256,256]{1,0:T(8,128)(2,1)S(1)} %get-tuple-element.90.bc_ref, f32[4,48,256]{2,1,0:T(8,128)S(1)} %get-tuple-element.91.rows_ref, ...), custom_call_target="tpu_custom_call" | custom-call | flops 4400000000 | tf_op jit(solution)/shard_map/pallas_call | solution.py:778
  88.0 3.0 %shard_map.131 = (f32[16,256]{1,0:T(8,128)S(1)}, f32[16,128]{1,0:T(8,128)S(1)}, f32[256,384]{1,0:T(8,128)S(1)}, f32[8,128]{1,0:T(8,128)}) custom-call(s32[7]{0:T(128)S(1)} %stack.40.sp, bf16[256,256]{1,0:T(8,128)(2,1)S(1)} %get-tuple-element.90.bc_ref, f32[4,48,256]{2,1,0:T(8,128)S(1)} %get-tuple-element.91.rows_ref, ...), custom_call_target="tpu_custom_call" | custom-call | flops 4400000000 | tf_op jit(solution)/shard_map/pallas_call | solution.py:778
  102.9 3.6 %collective-permute-done.28 = f32[8,128]{1,0:T(8,128)S(1)} collective-permute-done((f32[8,128]{1,0:T(8,128)S(1)}, f32[8,128]{1,0:T(8,128)S(1)}, u32[]{:S(2)}, u32[]{:S(2)}) %collective-permute-start.28) | collective-permute-done | bytes 4128 | tf_op jit(solution)/shard_map/ppermute | solution.py:591
  106.5 4.5 %collective-permute-done.29 = f32[8,128]{1,0:T(8,128)S(1)} collective-permute-done((f32[8,128]{1,0:T(8,128)S(1)}, f32[8,128]{1,0:T(8,128)S(1)}, u32[]{:S(2)}, u32[]{:S(2)}) %collective-permute-start.29) | collective-permute-done | bytes 4128 | tf_op jit(solution)/shard_map/ppermute | solution.py:591
  114.4 2.6 %collective-permute-start.39 = (bf16[80,1024]{1,0:T(8,128)(2,1)S(1)}, bf16[80,1024]{1,0:T(8,128)(2,1)S(1)}, u32[]{:S(2)}, u32[]{:S(2)}) collective-permute-start(bf16[80,1024]{1,0:T(8,128)(2,1)S(1)} %get-tuple-element.163), channel_id=1, source_target_pairs={{0,24},{2,26},{4,28},{6,30},{8,16},{10,18},{12,20},{14,22},{16,8},... | collective-permute-start | bytes 491528 | tf_op jit(solution)/shard_map/ppermute | solution.py:591
  117.4 3.2 %collective-permute-done.30 = f32[8,128]{1,0:T(8,128)S(1)} collective-permute-done((f32[8,128]{1,0:T(8,128)S(1)}, f32[8,128]{1,0:T(8,128)S(1)}, u32[]{:S(2)}, u32[]{:S(2)}) %collective-permute-start.30) | collective-permute-done | bytes 4128 | tf_op jit(solution)/shard_map/ppermute | solution.py:587
  121.7 2.5 %collective-permute-done.31 = f32[8,128]{1,0:T(8,128)S(1)} collective-permute-done((f32[8,128]{1,0:T(8,128)S(1)}, f32[8,128]{1,0:T(8,128)S(1)}, u32[]{:S(2)}, u32[]{:S(2)}) %collective-permute-start.31) | collective-permute-done | bytes 4128 | tf_op jit(solution)/shard_map/ppermute | solution.py:587
  127.1 3.2 %collective-permute-start.45 = (bf16[80,1024]{1,0:T(8,128)(2,1)S(1)}, bf16[80,1024]{1,0:T(8,128)(2,1)S(1)}, u32[]{:S(2)}, u32[]{:S(2)}) collective-permute-start(bf16[80,1024]{1,0:T(8,128)(2,1)S(1)} %shard_map.139.refs_0_), channel_id=1, source_target_pairs={{0,16},{2,18},{4,20},{6,22},{8,24},{10,26},{12,28},{14,30},{16,0},... | collective-permute-start | bytes 491528 | tf_op jit(solution)/shard_map/ppermute | solution.py:591
  132.4 4.6 %collective-permute-done.45.refs_2_ = bf16[80,1024]{1,0:T(8,128)(2,1)S(1)} collective-permute-done((bf16[80,1024]{1,0:T(8,128)(2,1)S(1)}, bf16[80,1024]{1,0:T(8,128)(2,1)S(1)}, u32[]{:S(2)}, u32[]{:S(2)}) %collective-permute-start.45) | collective-permute-done | bytes 163872 | tf_op jit(solution)/shard_map/ppermute | solution.py:591
  145.4 1.8 %shard_map.140 = (f32[4096,256]{1,0:T(8,128)}, f32[64,4096]{1,0:T(8,128)}) custom-call(s32[7]{0:T(128)S(1)} %stack.40.sp, bf16[80,1024]{1,0:T(8,128)(2,1)S(1)} %shard_map.139.refs_0_, bf16[80,1024]{1,0:T(8,128)(2,1)S(1)} %collective-permute-done.42.refs_1_, bf16[80,1024]{1,0:T(8,128)(2,1)S(1)} %collective-permute-done.45.refs_2_, ...), custom_call_target="tpu_custom_call" | custom-call | flops 3300000000 | tf_op jit(solution)/shard_map/pallas_call | solution.py:938
  149.7 1.8 %collective-permute-start.47 = (bf16[80,1024]{1,0:T(8,128)(2,1)S(1)}, bf16[80,1024]{1,0:T(8,128)(2,1)S(1)}, u32[]{:S(2)}, u32[]{:S(2)}) collective-permute-start(bf16[80,1024]{1,0:T(8,128)(2,1)S(1)} %collective-permute-done.46.refs_2_), channel_id=1, source_target_pairs={{0,2},{2,0},{4,6},{6,4},{8,10},{10,8},{12,14},{14,12},{16,18},{18,... | collective-permute-start | bytes 491528 | tf_op jit(solution)/shard_map/ppermute | solution.py:587
  153.6 1.8 %shard_map.141 = (f32[4096,256]{1,0:T(8,128)}, f32[64,4096]{1,0:T(8,128)}) custom-call(s32[7]{0:T(128)S(1)} %stack.40.sp, bf16[80,1024]{1,0:T(8,128)(2,1)S(1)} %collective-permute-done.53.refs_0_, bf16[80,1024]{1,0:T(8,128)(2,1)S(1)} %collective-permute-done.43.refs_1_, ...), custom_call_target="tpu_custom_call", output_to_operand_aliasing={{0}: (5, {}), {1}: (6, {})} | custom-call | flops 1100000000 | tf_op jit(solution)/shard_map/pallas_call | solution.py:938
  155.4 1.8 %shard_map.142 = (f32[4096,256]{1,0:T(8,128)}, f32[64,4096]{1,0:T(8,128)}) custom-call(s32[7]{0:T(128)S(1)} %stack.40.sp, bf16[80,1024]{1,0:T(8,128)(2,1)S(1)} %collective-permute-done.40.refs_0_, bf16[80,1024]{1,0:T(8,128)(2,1)S(1)} %collective-permute-done.51.refs_1_, ...), custom_call_target="tpu_custom_call", output_to_operand_aliasing={{0}: (5, {}), {1}: (6, {})} | custom-call | flops 1100000000 | tf_op jit(solution)/shard_map/pallas_call | solution.py:938
  158.6 1.8 %shard_map.143 = (f32[4096,256]{1,0:T(8,128)}, f32[64,4096]{1,0:T(8,128)}) custom-call(s32[7]{0:T(128)S(1)} %stack.40.sp, bf16[80,1024]{1,0:T(8,128)(2,1)S(1)} %collective-permute-done.41.refs_0_, bf16[80,1024]{1,0:T(8,128)(2,1)S(1)} %collective-permute-done.44.refs_1_, ...), custom_call_target="tpu_custom_call", output_to_operand_aliasing={{0}: (5, {}), {1}: (6, {})} | custom-call | flops 1100000000 | tf_op jit(solution)/shard_map/pallas_call | solution.py:938
  (125 shorter events, 60.9 us)
Async XLA Ops:
  3.5 17.1 %collective-permute-start.1 = (bf16[256,1024]{1,0:T(8,128)(2,1)}, bf16[256,1024]{1,0:T(8,128)(2,1)S(1)}, u32[]{:S(2)}, u32[]{:S(2)}) collective-permute-start(bf16[256,1024]{1,0:T(8,128)(2,1)} %get-tuple-element.93), channel_id=1, source_target_pairs={{0,6},{2,4},{4,2},{6,0},{8,14},{10,12},{12,10},{14,8},{16,22},{18,... | collective-permute-start | bytes 1572872 | tf_op jit(solution)/shard_map/ppermute | solution.py:587
  17.1 15.5 %collective-permute-start.2 = (bf16[144,1024]{1,0:T(8,128)(2,1)S(1)}, bf16[144,1024]{1,0:T(8,128)(2,1)S(1)}, u32[]{:S(2)}, u32[]{:S(2)}) collective-permute-start(bf16[144,1024]{1,0:T(8,128)(2,1)S(1)} %get-tuple-element.96), channel_id=1, source_target_pairs={{0,2},{2,0},{4,6},{6,4},{8,10},{10,8},{12,14},{14,12},{16,18},{18,... | collective-permute-start | bytes 884744 | tf_op jit(solution)/shard_map/ppermute | solution.py:587
  17.7 15.4 %collective-permute-start.3 = (bf16[144,1024]{1,0:T(8,128)(2,1)S(1)}, bf16[144,1024]{1,0:T(8,128)(2,1)S(1)}, u32[]{:S(2)}, u32[]{:S(2)}) collective-permute-start(bf16[144,1024]{1,0:T(8,128)(2,1)S(1)} %get-tuple-element.97), channel_id=1, source_target_pairs={{0,4},{2,6},{4,0},{6,2},{8,12},{10,14},{12,8},{14,10},{16,20},{18,... | collective-permute-start | bytes 884744 | tf_op jit(solution)/shard_map/ppermute | solution.py:587
  17.8 15.5 %collective-permute-start.4 = (bf16[144,1024]{1,0:T(8,128)(2,1)S(1)}, bf16[144,1024]{1,0:T(8,128)(2,1)S(1)}, u32[]{:S(2)}, u32[]{:S(2)}) collective-permute-start(bf16[144,1024]{1,0:T(8,128)(2,1)S(1)} %get-tuple-element.98), channel_id=1, source_target_pairs={{0,6},{2,4},{4,2},{6,0},{8,14},{10,12},{12,10},{14,8},{16,22},{18,... | collective-permute-start | bytes 884744 | tf_op jit(solution)/shard_map/ppermute | solution.py:587
  29.6 20.9 %collective-permute-start.5 = (bf16[176,1024]{1,0:T(8,128)(2,1)S(1)}, bf16[176,1024]{1,0:T(8,128)(2,1)S(1)}, u32[]{:S(2)}, u32[]{:S(2)}) collective-permute-start(bf16[176,1024]{1,0:T(8,128)(2,1)S(1)} %get-tuple-element.102), channel_id=1, source_target_pairs={{0,2},{2,0},{4,6},{6,4},{8,10},{10,8},{12,14},{14,12},{16,18},{18,... | collective-permute-start | bytes 1081352 | tf_op jit(solution)/shard_map/ppermute | solution.py:587
  31.4 19.9 %collective-permute-start.6 = (bf16[176,1024]{1,0:T(8,128)(2,1)S(1)}, bf16[176,1024]{1,0:T(8,128)(2,1)S(1)}, u32[]{:S(2)}, u32[]{:S(2)}) collective-permute-start(bf16[176,1024]{1,0:T(8,128)(2,1)S(1)} %get-tuple-element.103), channel_id=1, source_target_pairs={{0,4},{2,6},{4,0},{6,2},{8,12},{10,14},{12,8},{14,10},{16,20},{18,... | collective-permute-start | bytes 1081352 | tf_op jit(solution)/shard_map/ppermute | solution.py:587
  32.6 20.1 %collective-permute-start.7 = (bf16[176,1024]{1,0:T(8,128)(2,1)S(1)}, bf16[176,1024]{1,0:T(8,128)(2,1)S(1)}, u32[]{:S(2)}, u32[]{:S(2)}) collective-permute-start(bf16[176,1024]{1,0:T(8,128)(2,1)S(1)} %get-tuple-element.104), channel_id=1, source_target_pairs={{0,6},{2,4},{4,2},{6,0},{8,14},{10,12},{12,10},{14,8},{16,22},{18,... | collective-permute-start | bytes 1081352 | tf_op jit(solution)/shard_map/ppermute | solution.py:587
  46.8 9.6 %collective-permute-start.11 = (bf16[128,256]{1,0:T(8,128)(2,1)S(1)}, bf16[128,256]{1,0:T(8,128)(2,1)S(1)}, u32[]{:S(2)}, u32[]{:S(2)}) collective-permute-start(bf16[128,256]{1,0:T(8,128)(2,1)S(1)} %get-tuple-element.110), channel_id=1, source_target_pairs={{0,8},{2,10},{4,12},{6,14},{8,0},{10,2},{12,4},{14,6},{16,24},{18,... | collective-permute-start | bytes 196616 | tf_op jit(solution)/shard_map/ppermute | solution.py:591
  47.5 8.9 %collective-permute-start.12 = (bf16[128,256]{1,0:T(8,128)(2,1)S(1)}, bf16[128,256]{1,0:T(8,128)(2,1)S(1)}, u32[]{:S(2)}, u32[]{:S(2)}) collective-permute-start(bf16[128,256]{1,0:T(8,128)(2,1)S(1)} %get-tuple-element.111), channel_id=1, source_target_pairs={{0,16},{2,18},{4,20},{6,22},{8,24},{10,26},{12,28},{14,30},{16,0},... | collective-permute-start | bytes 196616 | tf_op jit(solution)/shard_map/ppermute | solution.py:591
  51.3 19.2 %collective-permute-start.20 = (bf16[256,1024]{1,0:T(8,128)(2,1)S(1)}, bf16[256,1024]{1,0:T(8,128)(2,1)S(1)}, u32[]{:S(2)}, u32[]{:S(2)}) collective-permute-start(bf16[256,1024]{1,0:T(8,128)(2,1)S(1)} %get-tuple-element.123), channel_id=1, source_target_pairs={{0,2},{2,0},{4,6},{6,4},{8,10},{10,8},{12,14},{14,12},{16,18},{18,... | collective-permute-start | bytes 1572872 | tf_op jit(solution)/shard_map/ppermute | solution.py:587
  52.7 17.7 %collective-permute-start.21 = (bf16[256,1024]{1,0:T(8,128)(2,1)S(1)}, bf16[256,1024]{1,0:T(8,128)(2,1)S(1)}, u32[]{:S(2)}, u32[]{:S(2)}) collective-permute-start(bf16[256,1024]{1,0:T(8,128)(2,1)S(1)} %get-tuple-element.124), channel_id=1, source_target_pairs={{0,4},{2,6},{4,0},{6,2},{8,12},{10,14},{12,8},{14,10},{16,20},{18,... | collective-permute-start | bytes 1572872 | tf_op jit(solution)/shard_map/ppermute | solution.py:587
  59.1 9.5 %collective-permute-start.18 = (bf16[128,256]{1,0:T(8,128)(2,1)S(1)}, bf16[128,256]{1,0:T(8,128)(2,1)S(1)}, u32[]{:S(2)}, u32[]{:S(2)}) collective-permute-start(bf16[128,256]{1,0:T(8,128)(2,1)S(1)} %get-tuple-element.121), channel_id=1, source_target_pairs={{0,16},{2,18},{4,20},{6,22},{8,24},{10,26},{12,28},{14,30},{16,0},... | collective-permute-start | bytes 196616 | tf_op jit(solution)/shard_map/ppermute | solution.py:591
  63.4 10.9 %collective-permute-start.16 = (bf16[128,1024]{1,0:T(8,128)(2,1)S(1)}, bf16[128,1024]{1,0:T(8,128)(2,1)S(1)}, u32[]{:S(2)}, u32[]{:S(2)}) collective-permute-start(bf16[128,1024]{1,0:T(8,128)(2,1)S(1)} %get-tuple-element.115), channel_id=1, source_target_pairs={{0,2},{2,0},{4,6},{6,4},{8,10},{10,8},{12,14},{14,12},{16,18},{18,... | collective-permute-start | bytes 786440 | tf_op jit(solution)/shard_map/ppermute | solution.py:587
  68.5 19.5 %collective-permute-start.14 = (bf16[128,1024]{1,0:T(8,128)(2,1)S(1)}, bf16[128,1024]{1,0:T(8,128)(2,1)S(1)}, u32[]{:S(2)}, u32[]{:S(2)}) collective-permute-start(bf16[128,1024]{1,0:T(8,128)(2,1)S(1)} %get-tuple-element.113), channel_id=1, source_target_pairs={{0,6},{2,4},{4,2},{6,0},{8,14},{10,12},{12,10},{14,8},{16,22},{18,... | collective-permute-start | bytes 786440 | tf_op jit(solution)/shard_map/ppermute | solution.py:587
  69.4 15.5 %collective-permute-start.15 = (bf16[128,1024]{1,0:T(8,128)(2,1)S(1)}, bf16[128,1024]{1,0:T(8,128)(2,1)S(1)}, u32[]{:S(2)}, u32[]{:S(2)}) collective-permute-start(bf16[128,1024]{1,0:T(8,128)(2,1)S(1)} %get-tuple-element.114), channel_id=1, source_target_pairs={{0,4},{2,6},{4,0},{6,2},{8,12},{10,14},{12,8},{14,10},{16,20},{18,... | collective-permute-start | bytes 786440 | tf_op jit(solution)/shard_map/ppermute | solution.py:587
  81.3 13.5 %collective-permute-start.25 = (bf16[128,1024]{1,0:T(8,128)(2,1)S(1)}, bf16[128,1024]{1,0:T(8,128)(2,1)S(1)}, u32[]{:S(2)}, u32[]{:S(2)}) collective-permute-start(bf16[128,1024]{1,0:T(8,128)(2,1)S(1)} %get-tuple-element.135), channel_id=1, source_target_pairs={{0,6},{2,4},{4,2},{6,0},{8,14},{10,12},{12,10},{14,8},{16,22},{18,... | collective-permute-start | bytes 786440 | tf_op jit(solution)/shard_map/ppermute | solution.py:587
  82.0 11.5 %collective-permute-start.26 = (bf16[128,1024]{1,0:T(8,128)(2,1)S(1)}, bf16[128,1024]{1,0:T(8,128)(2,1)S(1)}, u32[]{:S(2)}, u32[]{:S(2)}) collective-permute-start(bf16[128,1024]{1,0:T(8,128)(2,1)S(1)} %get-tuple-element.136), channel_id=1, source_target_pairs={{0,4},{2,6},{4,0},{6,2},{8,12},{10,14},{12,8},{14,10},{16,20},{18,... | collective-permute-start | bytes 786440 | tf_op jit(solution)/shard_map/ppermute | solution.py:587
  83.3 8.9 %collective-permute-start.27 = (bf16[128,1024]{1,0:T(8,128)(2,1)S(1)}, bf16[128,1024]{1,0:T(8,128)(2,1)S(1)}, u32[]{:S(2)}, u32[]{:S(2)}) collective-permute-start(bf16[128,1024]{1,0:T(8,128)(2,1)S(1)} %get-tuple-element.137), channel_id=1, source_target_pairs={{0,2},{2,0},{4,6},{6,4},{8,10},{10,8},{12,14},{14,12},{16,18},{18,... | collective-permute-start | bytes 786440 | tf_op jit(solution)/shard_map/ppermute | solution.py:587
  99.4 11.7 %collective-permute-start.36 = (bf16[320,256]{1,0:T(8,128)(2,1)S(1)}, bf16[320,256]{1,0:T(8,128)(2,1)S(1)}, u32[]{:S(2)}, u32[]{:S(2)}) collective-permute-start(bf16[320,256]{1,0:T(8,128)(2,1)S(1)} %shard_map.137.refs_0_), channel_id=1, source_target_pairs={{0,6},{2,4},{4,2},{6,0},{8,14},{10,12},{12,10},{14,8},{16,22},{18,... | collective-permute-start | bytes 491528 | tf_op jit(solution)/shard_map/ppermute | solution.py:587
  100.0 11.0 %collective-permute-start.35 = (bf16[320,256]{1,0:T(8,128)(2,1)S(1)}, bf16[320,256]{1,0:T(8,128)(2,1)S(1)}, u32[]{:S(2)}, u32[]{:S(2)}) collective-permute-start(bf16[320,256]{1,0:T(8,128)(2,1)S(1)} %shard_map.137.refs_0_), channel_id=1, source_target_pairs={{0,4},{2,6},{4,0},{6,2},{8,12},{10,14},{12,8},{14,10},{16,20},{18,... | collective-permute-start | bytes 491528 | tf_op jit(solution)/shard_map/ppermute | solution.py:587
  101.3 9.7 %collective-permute-start.34 = (bf16[320,256]{1,0:T(8,128)(2,1)S(1)}, bf16[320,256]{1,0:T(8,128)(2,1)S(1)}, u32[]{:S(2)}, u32[]{:S(2)}) collective-permute-start(bf16[320,256]{1,0:T(8,128)(2,1)S(1)} %shard_map.137.refs_0_), channel_id=1, source_target_pairs={{0,2},{2,0},{4,6},{6,4},{8,10},{10,8},{12,14},{14,12},{16,18},{18,... | collective-permute-start | bytes 491528 | tf_op jit(solution)/shard_map/ppermute | solution.py:587
  112.5 12.8 %collective-permute-start.37 = (bf16[80,1024]{1,0:T(8,128)(2,1)S(1)}, bf16[80,1024]{1,0:T(8,128)(2,1)S(1)}, u32[]{:S(2)}, u32[]{:S(2)}) collective-permute-start(bf16[80,1024]{1,0:T(8,128)(2,1)S(1)} %get-tuple-element.161), channel_id=1, source_target_pairs={{0,8},{2,10},{4,12},{6,14},{8,0},{10,2},{12,4},{14,6},{16,24},{18,... | collective-permute-start | bytes 491528 | tf_op jit(solution)/shard_map/ppermute | solution.py:591
  112.6 13.9 %collective-permute-start.38 = (bf16[80,1024]{1,0:T(8,128)(2,1)S(1)}, bf16[80,1024]{1,0:T(8,128)(2,1)S(1)}, u32[]{:S(2)}, u32[]{:S(2)}) collective-permute-start(bf16[80,1024]{1,0:T(8,128)(2,1)S(1)} %get-tuple-element.162), channel_id=1, source_target_pairs={{0,16},{2,18},{4,20},{6,22},{8,24},{10,26},{12,28},{14,30},{16,0},... | collective-permute-start | bytes 491528 | tf_op jit(solution)/shard_map/ppermute | solution.py:591
  114.4 12.1 %collective-permute-start.39 = (bf16[80,1024]{1,0:T(8,128)(2,1)S(1)}, bf16[80,1024]{1,0:T(8,128)(2,1)S(1)}, u32[]{:S(2)}, u32[]{:S(2)}) collective-permute-start(bf16[80,1024]{1,0:T(8,128)(2,1)S(1)} %get-tuple-element.163), channel_id=1, source_target_pairs={{0,24},{2,26},{4,28},{6,30},{8,16},{10,18},{12,20},{14,22},{16,8},... | collective-permute-start | bytes 491528 | tf_op jit(solution)/shard_map/ppermute | solution.py:591
  127.1 9.9 %collective-permute-start.45 = (bf16[80,1024]{1,0:T(8,128)(2,1)S(1)}, bf16[80,1024]{1,0:T(8,128)(2,1)S(1)}, u32[]{:S(2)}, u32[]{:S(2)}) collective-permute-start(bf16[80,1024]{1,0:T(8,128)(2,1)S(1)} %shard_map.139.refs_0_), channel_id=1, source_target_pairs={{0,16},{2,18},{4,20},{6,22},{8,24},{10,26},{12,28},{14,30},{16,0},... | collective-permute-start | bytes 491528 | tf_op jit(solution)/shard_map/ppermute | solution.py:591
  130.3 9.9 %collective-permute-start.53 = (bf16[80,1024]{1,0:T(8,128)(2,1)S(1)}, bf16[80,1024]{1,0:T(8,128)(2,1)S(1)}, u32[]{:S(2)}, u32[]{:S(2)}) collective-permute-start(bf16[80,1024]{1,0:T(8,128)(2,1)S(1)} %shard_map.139.refs_0_), channel_id=1, source_target_pairs={{0,2},{2,0},{4,6},{6,4},{8,10},{10,8},{12,14},{14,12},{16,18},{18,... | collective-permute-start | bytes 491528 | tf_op jit(solution)/shard_map/ppermute | solution.py:587
  131.2 9.8 %collective-permute-start.42 = (bf16[80,1024]{1,0:T(8,128)(2,1)S(1)}, bf16[80,1024]{1,0:T(8,128)(2,1)S(1)}, u32[]{:S(2)}, u32[]{:S(2)}) collective-permute-start(bf16[80,1024]{1,0:T(8,128)(2,1)S(1)} %shard_map.139.refs_0_), channel_id=1, source_target_pairs={{0,8},{2,10},{4,12},{6,14},{8,0},{10,2},{12,4},{14,6},{16,24},{18,... | collective-permute-start | bytes 491528 | tf_op jit(solution)/shard_map/ppermute | solution.py:591
  131.2 11.2 %collective-permute-start.40 = (bf16[80,1024]{1,0:T(8,128)(2,1)S(1)}, bf16[80,1024]{1,0:T(8,128)(2,1)S(1)}, u32[]{:S(2)}, u32[]{:S(2)}) collective-permute-start(bf16[80,1024]{1,0:T(8,128)(2,1)S(1)} %shard_map.139.refs_0_), channel_id=1, source_target_pairs={{0,4},{2,6},{4,0},{6,2},{8,12},{10,14},{12,8},{14,10},{16,20},{18,... | collective-permute-start | bytes 491528 | tf_op jit(solution)/shard_map/ppermute | solution.py:587
  141.0 8.7 %collective-permute-start.51 = (bf16[80,1024]{1,0:T(8,128)(2,1)S(1)}, bf16[80,1024]{1,0:T(8,128)(2,1)S(1)}, u32[]{:S(2)}, u32[]{:S(2)}) collective-permute-start(bf16[80,1024]{1,0:T(8,128)(2,1)S(1)} %collective-permute-done.42.refs_1_), channel_id=1, source_target_pairs={{0,4},{2,6},{4,0},{6,2},{8,12},{10,14},{12,8},{14,10},{16,20},{18,... | collective-permute-start | bytes 491528 | tf_op jit(solution)/shard_map/ppermute | solution.py:587
  142.3 9.2 %collective-permute-start.43 = (bf16[80,1024]{1,0:T(8,128)(2,1)S(1)}, bf16[80,1024]{1,0:T(8,128)(2,1)S(1)}, u32[]{:S(2)}, u32[]{:S(2)}) collective-permute-start(bf16[80,1024]{1,0:T(8,128)(2,1)S(1)} %collective-permute-done.42.refs_1_), channel_id=1, source_target_pairs={{0,2},{2,0},{4,6},{6,4},{8,10},{10,8},{12,14},{14,12},{16,18},{18,... | collective-permute-start | bytes 491528 | tf_op jit(solution)/shard_map/ppermute | solution.py:587
  142.9 12.5 %collective-permute-start.52 = (bf16[80,1024]{1,0:T(8,128)(2,1)S(1)}, bf16[80,1024]{1,0:T(8,128)(2,1)S(1)}, u32[]{:S(2)}, u32[]{:S(2)}) collective-permute-start(bf16[80,1024]{1,0:T(8,128)(2,1)S(1)} %collective-permute-done.48.refs_3_), channel_id=1, source_target_pairs={{0,4},{2,6},{4,0},{6,2},{8,12},{10,14},{12,8},{14,10},{16,20},{18,... | collective-permute-start | bytes 491528 | tf_op jit(solution)/shard_map/ppermute | solution.py:587
  147.5 9.7 %collective-permute-start.41 = (bf16[80,1024]{1,0:T(8,128)(2,1)S(1)}, bf16[80,1024]{1,0:T(8,128)(2,1)S(1)}, u32[]{:S(2)}, u32[]{:S(2)}) collective-permute-start(bf16[80,1024]{1,0:T(8,128)(2,1)S(1)} %collective-permute-done.40.refs_0_), channel_id=1, source_target_pairs={{0,2},{2,0},{4,6},{6,4},{8,10},{10,8},{12,14},{14,12},{16,18},{18,... | collective-permute-start | bytes 491528 | tf_op jit(solution)/shard_map/ppermute | solution.py:587
  (29 other events, 175.8 us)
